TPU v7x, 512 devices: a whole 4x4x16 slice. The times are simulated.
512 devices in a mesh: rep: 4 (over y_lo, core), fsdp: 128 (over z, y_hi, x).
Axes of the slice: x: 4, y: 4 (y_hi: 2, y_lo: 2; y = y_hi * 2 + y_lo), z: 16, core: 2. Of those that a mesh axis runs over, the one named last changes fastest.
Arguments:
- hidden_in: bfloat16 [4, 24576, 8192], P('rep', 'fsdp'), may hold values from -6 to 6
- norm_gain: float32 [8192], replicated, may hold values from 0.1 to 1.9
- key_weight: bfloat16 [4, 8192, 512], P('rep', 'fsdp'), may hold values from -0.0625 to 0.0625
- fragment_index: int32 [1], replicated, may hold values from 0 to 6
- outer_params: float32 [7, 8192, 512], P(None, 'fsdp'), may hold values from -6 to 6
- outer_moment: float32 [7, 8192, 512], P(None, 'fsdp'), may hold values from -4 to 4
- inner_params: bfloat16 [4, 7, 8192, 512], P('rep', None, 'fsdp'), may hold values from -6 to 6
Outputs:
- keys: bfloat16 [4, 24576, 512], P('rep', 'fsdp')
- new_outer: float32 [8192, 512], P('fsdp')
- new_moment: float32 [8192, 512], P('fsdp')
- mixed_inner: bfloat16 [4, 8192, 512], P('rep', 'fsdp')
All inputs are finite; a program needn't handle non-finite values.
Results may differ from a plain program's by a relative error of at most 0.022.
Values may be sent and summed in bfloat16 or wider, within the bound.
No kernel may reach another device: no remote copies, remote signals or barrier semaphores. Data moves between devices by JAX's collectives and lax.ppermute only.
A program may use at most 64 MiB of HBM per device.

v0:
```python
import jax
import jax.numpy as jnp
from jax import lax
from jax.sharding import PartitionSpec as P

momentum_coef = 0.9
outer_rate = 0.7
mix_keep = 0.5
epsilon = 1e-05


def outer_update(averaged, outer_layer, moment_layer):
    new_moment = momentum_coef * moment_layer + averaged
    new_outer = outer_layer - outer_rate * (averaged + momentum_coef * new_moment)
    return (new_outer, new_moment)


def shards(
    hidden_in, norm_gain, key_weight, fragment_index, outer_params, outer_moment, inner_params
):
    replicas = lax.axis_size("rep")
    layer_idx = fragment_index[0]
    outer_layer = lax.dynamic_index_in_dim(outer_params, layer_idx, 0, keepdims=False)
    moment_layer = lax.dynamic_index_in_dim(outer_moment, layer_idx, 0, keepdims=False)
    inner_layer = lax.dynamic_index_in_dim(inner_params[0], layer_idx, 0, keepdims=False)
    pseudo_grad = (outer_layer - inner_layer.astype(jnp.float32)).astype(jnp.bfloat16)
    summed = lax.psum(pseudo_grad.astype(jnp.float32).astype(jnp.bfloat16), "rep").astype(
        jnp.float32
    )
    new_outer, new_moment = outer_update(summed / replicas, outer_layer, moment_layer)
    mixed_inner = (
        mix_keep * inner_layer.astype(jnp.float32) + (1.0 - mix_keep) * new_outer
    ).astype(jnp.bfloat16)
    hidden = hidden_in[0]
    hidden32 = hidden.astype(jnp.float32)
    mean_square = jnp.mean(hidden32 * hidden32, axis=-1, keepdims=True)
    normed = (hidden32 * lax.rsqrt(mean_square + epsilon) * norm_gain).astype(jnp.bfloat16)
    weight_shard = key_weight[0]
    full_weight = lax.all_gather(weight_shard, "fsdp", axis=0, tiled=True)
    key_sum = jnp.dot(normed, full_weight, preferred_element_type=jnp.float32)
    keys = key_sum.astype(jnp.bfloat16)[None]
    return (keys, new_outer, new_moment, mixed_inner[None])


def solution(mesh):
    placed = (
        P("rep", "fsdp", None),
        P(),
        P("rep", "fsdp", None),
        P(),
        P(None, "fsdp", None),
        P(None, "fsdp", None),
        P("rep", None, "fsdp", None),
    )
    return jax.shard_map(
        shards,
        mesh=mesh,
        in_specs=placed,
        out_specs=(
            P("rep", "fsdp", None),
            P("fsdp", None),
            P("fsdp", None),
            P("rep", "fsdp", None),
        ),
        check_vma=False,
    )
```

profile of v0, /device:TPU:38, one launch (start us, length us, event | category | flops | bytes accessed | tf_op | source)
XLA Modules:
  0.0 276.3 jit_solution(18413889619019784808)
XLA Ops:
  8.0 0.0 all-reduce.2.cloned.1.call-start
  8.7 1.6 fusion.19
  10.2 0.0 all-reduce.2.cloned.1.call-update
  10.3 0.0 all-gather.3.cloned.1.call-start
  10.3 0.5 all-gather.3.cloned.1.call-update
  10.9 2.6 fusion.2
  13.5 54.0 %all-reduce.2.cloned.1.call-done = bf16[64,512]{1,0:T(8,128)(2,1)} async-done(((bf16[64,512]{1,0:T(8,128)(2,1)}), bf16[64,512]{1,0:T(8,128)(2,1)}) %all-reduce.2.cloned.1.call-update) | async-done | bytes 65552 | tf_op jit(solution)/shard_map/psum | solution.py:27
  67.5 1.8 fusion.22
  69.3 192.7 %all-gather.3.cloned.1.call-done = bf16[1,8192,512]{2,1,0:T(8,128)(2,1)} async-done(((bf16[1,64,512]{2,1,0:T(8,128)(2,1)}), bf16[1,8192,512]{2,1,0:T(8,128)(2,1)}) %all-gather.3.cloned.1.call-update) | async-done | bytes 8388624 | tf_op jit(solution)/shard_map/all_gather | solution.py:39
  261.9 6.9 %fusion.14 = bf16[1,192,512]{2,1,0:T(8,128)(2,1)} fusion(bf16[1,8192,512]{2,1,0:T(8,128)(2,1)} %all-gather.3.cloned.1.call-done, bf16[1,192,8192]{2,1,0:T(8,128)(2,1)} %param.7, f32[8192]{0:T(1024)} %param.8, f32[192]{0:T(256)S(1)} %add_rsqrt_fusion), kind=kOutput, calls=%fused_computation.11 | convolution fusion | flops 1617002496 | bytes 11764480 | tf_op jit(solution)/shard_map/dot_general | solution.py:40
  (1 shorter events, 0.0 us)
Async XLA Ops:
  8.0 59.5 %all-reduce.2.cloned.1.call-start = ((), (), s32[]{:S(2)}) async-start(), calls=%async_computation | async-start | bytes 131072 | tf_op jit(solution)/shard_map/psum | solution.py:27
  10.3 251.7 %all-gather.3.cloned.1.call-start = ((), (), s32[]{:S(2)}) async-start(), calls=%async_computation.1 | async-start | bytes 8454144 | tf_op jit(solution)/shard_map/all_gather | solution.py:39
Sparse Core Ops, SparseCore 0:
  12.3 55.1 all-reduce.1
Sparse Core Ops, SparseCore 1:
  15.3 246.6 all-gather.2
where the time goes:
time: 276 us
  waiting for transfers between devices  247 us (89%)
  between operations  16.1 us (6%)
  matrix products  6.87 us (2%)
  other arithmetic  5.96 us (2%)
    all_gather x1, waiting for transfers between devices, shards(): full_weight = lax.all_gather(weight_shard, 'fsdp', axis=0, tiled=True)  193 us
    psum x1, waiting for transfers between devices, shards(): lax.psum(pseudo_grad.astype(jnp.float32).astype(jnp.bfloat16), 'rep')  54 us
    dot_general x1, matrix products, shards(): key_sum = jnp.dot(normed, full_weight, preferred_element_type=jnp.float32)  6.87 us
  transfers between devices with their start and end apart: 2, of which 2 were waited for; matrix products, arithmetic and copies ran while one was open for 2% of the time, Pallas kernels for 0%

commit v1 on v0

v1 whole, which is shorter than its diff:
```python
import jax
import jax.numpy as jnp
from jax import lax
from jax.experimental import pallas as pl
from jax.experimental.pallas import tpu as pltpu
from jax.sharding import Mesh, PartitionSpec as P

momentum_coef = 0.9
outer_rate = 0.7
mix_keep = 0.5
epsilon = 1e-05

Z, PLANE, REP = "z", ("yh", "x"), ("yl", "core")
PLANES, PEERS = 16, 8
ROWS = 32


def outer_update(averaged, outer_layer, moment_layer):
    new_moment = momentum_coef * moment_layer + averaged
    new_outer = outer_layer - outer_rate * (averaged + momentum_coef * new_moment)
    return (new_outer, new_moment)


def pack_kernel(hidden_ref, packed_ref, scale_ref):
    hidden = hidden_ref[...].astype(jnp.float32)
    features = hidden.shape[1]
    mean_square = jnp.sum(hidden * hidden, axis=-1, keepdims=True) / features
    scale_ref[...] = lax.rsqrt(mean_square + epsilon)
    low = lax.broadcasted_iota(jnp.int32, (hidden.shape[0], 128), 1) < 64
    for pair in range(PLANES // 2):
        for tile in range(PEERS // 2):
            start = pair * 1024 + tile * 128
            first = hidden[:, start : start + 128]
            second = hidden[:, start + 512 : start + 640]
            columns = slice(pair * 128, pair * 128 + 128)
            even = jnp.where(low, first, pltpu.roll(second, 64, 1))
            odd = jnp.where(low, pltpu.roll(first, 64, 1), second)
            packed_ref[2 * tile, :, columns] = even.astype(jnp.bfloat16)
            packed_ref[2 * tile + 1, :, columns] = odd.astype(jnp.bfloat16)


def pack(hidden):
    tokens, features = hidden.shape
    return pl.pallas_call(
        pack_kernel,
        grid=(tokens // ROWS,),
        in_specs=[pl.BlockSpec((ROWS, features), lambda i: (i, 0))],
        out_specs=[
            pl.BlockSpec((PEERS, ROWS, features // PEERS), lambda i: (0, i, 0)),
            pl.BlockSpec((ROWS, 1), lambda i: (i, 0)),
        ],
        out_shape=[
            jax.ShapeDtypeStruct((PEERS, tokens, features // PEERS), jnp.bfloat16),
            jax.ShapeDtypeStruct((tokens, 1), jnp.float32),
        ],
        compiler_params=pltpu.CompilerParams(vmem_limit_bytes=16 * 1024 * 1024),
        cost_estimate=pl.CostEstimate(
            flops=4 * tokens * features, bytes_accessed=4 * tokens * features, transcendentals=tokens
        ),
        name="pack_hidden",
    )(hidden)


def shards(
    hidden_in, norm_gain, key_weight, fragment_index, outer_params, outer_moment, inner_params
):
    replicas = 4
    layer_idx = fragment_index[0]
    outer_layer = lax.dynamic_index_in_dim(outer_params, layer_idx, 0, keepdims=False)
    moment_layer = lax.dynamic_index_in_dim(outer_moment, layer_idx, 0, keepdims=False)
    inner_layer = lax.dynamic_index_in_dim(inner_params[0], layer_idx, 0, keepdims=False)
    pseudo_grad = (outer_layer - inner_layer.astype(jnp.float32)).astype(jnp.bfloat16)
    every = lax.all_gather(pseudo_grad, REP, axis=0, tiled=False)
    summed = jnp.sum(every.astype(jnp.float32), axis=0)
    new_outer, new_moment = outer_update(summed / replicas, outer_layer, moment_layer)
    mixed_inner = (
        mix_keep * inner_layer.astype(jnp.float32) + (1.0 - mix_keep) * new_outer
    ).astype(jnp.bfloat16)

    weight = lax.all_gather(key_weight[0], Z, axis=0, tiled=True)
    packed, scale = pack(hidden_in[0])
    gathered = lax.all_to_all(packed, PLANE, 0, 0, tiled=True)
    mine = lax.axis_index(PLANE)
    gain = lax.dynamic_index_in_dim(norm_gain.reshape(PLANES, PEERS, 64), mine, 1, keepdims=False)
    weight = (weight.astype(jnp.float32) * gain.reshape(-1, 1)).astype(jnp.bfloat16)
    tokens = gathered.reshape(-1, gathered.shape[-1])
    partial = jnp.dot(tokens, weight, preferred_element_type=jnp.float32).astype(jnp.bfloat16)
    partial = partial.reshape(PEERS, -1, partial.shape[-1])
    partial = lax.all_to_all(partial, PLANE, 0, 0, tiled=True)
    keys = (jnp.sum(partial.astype(jnp.float32), axis=0) * scale).astype(jnp.bfloat16)
    return (keys[None], new_outer, new_moment, mixed_inner[None])


def solution(mesh):
    fine = Mesh(mesh.devices.reshape(2, 2, 16, 2, 4), ("yl", "core", "z", "yh", "x"))
    fsdp = ("z", "yh", "x")
    placed = (
        P(REP, fsdp, None),
        P(),
        P(REP, fsdp, None),
        P(),
        P(None, fsdp, None),
        P(None, fsdp, None),
        P(REP, None, fsdp, None),
    )
    return jax.shard_map(
        shards,
        mesh=fine,
        in_specs=placed,
        out_specs=(
            P(REP, fsdp, None),
            P(fsdp, None),
            P(fsdp, None),
            P(REP, fsdp, None),
        ),
        check_vma=False,
    )
```

time: 276 us -> 138 us (0.50)
  the two profiles are of different devices: /device:TPU:38 before, /device:TPU:1 now
where the time goes in v1:
time: 138 us; the launch traced here: 137 us
  waiting for transfers between devices  69.6 us (50%)
  blocking collectives  20.1 us (15%)
  between operations  14.7 us (11%)
  starting transfers between devices  13.9 us (10%)
  other arithmetic  5.41 us (4%)
  local copies, waits for them, and re-layouts  4.66 us (3%)
  matrix products  4.46 us (3%)
  Pallas kernels  3.68 us (3%)
    all_gather x1, waiting for transfers between devices, shards(): weight = lax.all_gather(key_weight[0], Z, axis=0, tiled=True)  69 us
    all_gather x1, blocking collectives, shards(): every = lax.all_gather(pseudo_grad, REP, axis=0, tiled=False)  20.1 us
    all_to_all x1, starting transfers between devices, shards(): gathered = lax.all_to_all(packed, PLANE, 0, 0, tiled=True)  7.61 us
    all_to_all x1, starting transfers between devices, shards(): partial = lax.all_to_all(partial, PLANE, 0, 0, tiled=True)  6.24 us
    dot_general x1, matrix products, shards(): jnp.dot(tokens, weight, preferred_element_type=jnp.float32)  4.46 us
    pallas_call x1, Pallas kernels, pack(): pl.pallas_call(pack_kernel, grid=(tokens // ROWS,), in_specs=[pl.BlockSpe...  3.68 us
  transfers between devices with their start and end apart: 3, of which 1 were waited for; matrix products, arithmetic and copies ran while one was open for 3% of the time, Pallas kernels for 0%

profile of v1, /device:TPU:1, one launch (start us, length us, event | category | flops | bytes accessed | tf_op | source)
XLA Modules:
  0.0 136.6 jit_solution(2005356687940530197)
XLA Ops:
  7.2 0.0 copy-start
  7.2 1.9 %copy-done = bf16[1,192,8192]{2,1,0:T(8,128)(2,1)S(1)} copy-done((bf16[1,192,8192]{2,1,0:T(8,128)(2,1)S(1)}, bf16[1,192,8192]{2,1,0:T(8,128)(2,1)}, u32[]{:S(2)}) %copy-start) | copy-done | bytes 3145752
  9.1 3.7 %pack_hidden.1 = (bf16[8,192,1024]{2,1,0:T(8,128)(2,1)}, f32[192,1]{1,0:T(8,128)S(1)}) custom-call(bf16[192,8192]{1,0:T(8,128)(2,1)S(1)} %bitcast.42), custom_call_target="tpu_custom_call" | custom-call | flops 6291456 | bytes 6291456 | tf_op jit(solution)/shard_map/pack_hidden/pallas_call | solution.py:44
  12.7 0.0 copy-start.1
  12.7 7.6 %all-to-all-start = ((bf16[8,192,1024]{2,1,0:T(8,128)(2,1)}), bf16[8,192,1024]{2,1,0:T(8,128)(2,1)S(1)}, u32[]{:S(2)}, u32[]{:S(2)}) async-start(bf16[8,192,1024]{2,1,0:T(8,128)(2,1)} %get-tuple-element.6), calls=%async_computation | async-start | bytes 6291456 | tf_op jit(solution)/shard_map/all_to_all | solution.py:82
  20.3 0.0 all-gather.3.cloned.1.call-start
  20.4 0.7 all-gather.3.cloned.1.call-update
  21.1 0.0 copy-done.1
  21.1 0.1 reshape.84
  21.2 0.1 mul.59
  21.3 69.0 %all-gather.3.cloned.1.call-done = bf16[1,1024,512]{2,1,0:T(8,128)(2,1)} async-done(((bf16[1,64,512]{2,1,0:T(8,128)(2,1)}), bf16[1,1024,512]{2,1,0:T(8,128)(2,1)}) %all-gather.3.cloned.1.call-update) | async-done | bytes 1048592 | tf_op jit(solution)/shard_map/all_gather | solution.py:80
  90.2 0.0 all-to-all-done
  90.2 4.5 %fusion = bf16[1536,512]{0,1:T(8,128)(2,1)} fusion(bf16[1536,1024]{1,0:T(8,128)(2,1)S(1)} %bitcast.43, bf16[1,1024,512]{2,1,0:T(8,128)(2,1)} %all-gather.3.cloned.1.call-done, f32[1024]{0:T(1024)S(1)} %mul.59), kind=kOutput, calls=%fused_computation.2 | convolution fusion | flops 1612972032 | bytes 5771264 | tf_op jit(solution)/shard_map/dot_general | solution.py:87
  94.7 2.6 %copy.12 = bf16[1536,512]{1,0:T(8,128)(2,1)} copy(bf16[1536,512]{0,1:T(8,128)(2,1)} %fusion) | data formatting | bytes 3145728 | tf_op jit(solution)/shard_map/convert_element_type | solution.py:87
  97.3 6.2 %all-to-all-start.1 = ((bf16[8,192,512]{2,1,0:T(8,128)(2,1)}), bf16[8,192,512]{2,1,0:T(8,128)(2,1)S(1)}, u32[]{:S(2)}, u32[]{:S(2)}) async-start(bf16[8,192,512]{2,1,0:T(8,128)(2,1)} %bitcast.4), calls=%async_computation.1 | async-start | bytes 3145728 | tf_op jit(solution)/shard_map/all_to_all | solution.py:89
  104.2 0.1 reduce.1
  104.3 0.9 fusion.6
  105.2 20.1 %all_gather.8 = bf16[4,64,512]{2,1,0:T(8,128)(2,1)S(1)} all-gather(bf16[1,64,512]{2,1,0:T(8,128)(2,1)S(1)} %fusion.6), channel_id=1, replica_groups=mesh['yl'=2,'core'=2,'z'=16,'yh'=2,'x'=4] {'yl','core'}, dimensions={0}, use_global_device_ids=true | all-gather | bytes 327680 | tf_op jit(solution)/shard_map/all_gather | solution.py:73
  125.4 1.7 %fusion.8 = bf16[1,64,512]{2,1,0:T(8,128)(2,1)} fusion(f32[64,512]{1,0:T(8,128)S(1)} %convert_reduce_fusion.1, f32[7,64,512]{2,1,0:T(8,128)} %param.12, s32[]{:T(128)S(6)} %select_n.12, f32[7,64,512]{2,1,0:T(8,128)} %param.11, bf16[1,7,64,512]{3,2,1,0:T(8,128)(2,1)} %param.13), kind=kLoop, calls=%fused_computation.14 | loop fusion | flops 360448 | bytes 524292 | tf_op jit(solution)/shard_map/convert_element_type | solution.py:78
  127.0 1.7 %bitcast_subtract_fusion = (f32[64,512]{1,0:T(8,128)}, f32[64,512]{1,0:T(8,128)}) fusion(f32[64,512]{1,0:T(8,128)S(1)} %convert_reduce_fusion.1, f32[7,64,512]{2,1,0:T(8,128)} %param.11, s32[]{:T(128)S(6)} %select_n.12, f32[7,64,512]{2,1,0:T(8,128)} %param.12), kind=kLoop, calls=%fused_computation.21 | loop fusion | flops 229376 | bytes 655364 | tf_op jit(solution)/shard_map/sub | solution.py:20
  128.7 0.0 all-to-all-done.1
  128.7 0.2 convert_reduce_fusion
  128.9 0.8 fusion.5
  (2 shorter events, 0.1 us)
Async XLA Ops:
  7.2 1.9 %copy-start = (bf16[1,192,8192]{2,1,0:T(8,128)(2,1)S(1)}, bf16[1,192,8192]{2,1,0:T(8,128)(2,1)}, u32[]{:S(2)}) copy-start(bf16[1,192,8192]{2,1,0:T(8,128)(2,1)} %param.7) | copy-start | bytes 9437188
  12.7 8.4 %copy-start.1 = (f32[8192]{0:T(1024)S(1)}, f32[8192]{0:T(1024)}, u32[]{:S(2)}) copy-start(f32[8192]{0:T(1024)} %param.8) | copy-start | bytes 98308
  12.7 77.5 %all-to-all-start = ((bf16[8,192,1024]{2,1,0:T(8,128)(2,1)}), bf16[8,192,1024]{2,1,0:T(8,128)(2,1)S(1)}, u32[]{:S(2)}, u32[]{:S(2)}) async-start(bf16[8,192,1024]{2,1,0:T(8,128)(2,1)} %get-tuple-element.6), calls=%async_computation | async-start | bytes 6291456 | tf_op jit(solution)/shard_map/all_to_all | solution.py:82
  20.3 69.9 %all-gather.3.cloned.1.call-start = ((), (), s32[]{:S(2)}) async-start(), calls=%async_computation.2 | async-start | bytes 1114112 | tf_op jit(solution)/shard_map/all_gather | solution.py:80
  97.3 31.4 %all-to-all-start.1 = ((bf16[8,192,512]{2,1,0:T(8,128)(2,1)}), bf16[8,192,512]{2,1,0:T(8,128)(2,1)S(1)}, u32[]{:S(2)}, u32[]{:S(2)}) async-start(bf16[8,192,512]{2,1,0:T(8,128)(2,1)} %bitcast.4), calls=%async_computation.1 | async-start | bytes 3145728 | tf_op jit(solution)/shard_map/all_to_all | solution.py:89
Sparse Core Ops, SparseCore 0:
  23.3 66.9 all-gather.2

commit v2 on v1

--- a/solution.py
+++ b/solution.py
@@ -21,17 +21,18 @@
     return (new_outer, new_moment)
 
 
-def pack_kernel(hidden_ref, packed_ref, scale_ref):
+def pack_kernel(hidden_ref, gain_ref, packed_ref, scale_ref):
     hidden = hidden_ref[...].astype(jnp.float32)
     features = hidden.shape[1]
     mean_square = jnp.sum(hidden * hidden, axis=-1, keepdims=True) / features
     scale_ref[...] = lax.rsqrt(mean_square + epsilon)
+    gained = hidden * gain_ref[...]
     low = lax.broadcasted_iota(jnp.int32, (hidden.shape[0], 128), 1) < 64
     for pair in range(PLANES // 2):
         for tile in range(PEERS // 2):
             start = pair * 1024 + tile * 128
-            first = hidden[:, start : start + 128]
-            second = hidden[:, start + 512 : start + 640]
+            first = gained[:, start : start + 128]
+            second = gained[:, start + 512 : start + 640]
             columns = slice(pair * 128, pair * 128 + 128)
             even = jnp.where(low, first, pltpu.roll(second, 64, 1))
             odd = jnp.where(low, pltpu.roll(first, 64, 1), second)
@@ -39,12 +40,15 @@
             packed_ref[2 * tile + 1, :, columns] = odd.astype(jnp.bfloat16)
 
 
-def pack(hidden):
+def pack(hidden, gain):
     tokens, features = hidden.shape
     return pl.pallas_call(
         pack_kernel,
         grid=(tokens // ROWS,),
-        in_specs=[pl.BlockSpec((ROWS, features), lambda i: (i, 0))],
+        in_specs=[
+            pl.BlockSpec((ROWS, features), lambda i: (i, 0)),
+            pl.BlockSpec((1, features), lambda i: (0, 0)),
+        ],
         out_specs=[
             pl.BlockSpec((PEERS, ROWS, features // PEERS), lambda i: (0, i, 0)),
             pl.BlockSpec((ROWS, 1), lambda i: (i, 0)),
@@ -58,7 +62,66 @@
             flops=4 * tokens * features, bytes_accessed=4 * tokens * features, transcendentals=tokens
         ),
         name="pack_hidden",
-    )(hidden)
+    )(hidden, gain)
+
+
+HELD = ((0, -4, 4, 8), (-1, -5, 3, 7), (1, -3, 5, 9), (-2, -6), (2, 6))
+
+
+def project_kernel(place_ref, tokens_ref, *refs):
+    held_refs, (out_ref, weight) = refs[: len(HELD)], refs[len(HELD) :]
+
+    @pl.when(pl.program_id(0) == 0)
+    def _():
+        for held_ref, offsets in zip(held_refs, HELD, strict=True):
+            for at, offset in enumerate(offsets):
+                plane = lax.rem(place_ref[0] + offset + PLANES, PLANES)
+                rows = pl.ds(pl.multiple_of(plane * 64, 64), 64)
+                weight[rows, :] = held_ref[at * 64 : at * 64 + 64, :]
+
+    out_ref[0] = jnp.dot(tokens_ref[0], weight[...], preferred_element_type=jnp.float32).astype(
+        jnp.bfloat16
+    )
+
+
+def project(place, tokens, held):
+    peers, rows, features = tokens.shape
+    width = held[0].shape[1]
+    whole = [pl.BlockSpec(part.shape, lambda i, place: (0, 0)) for part in held]
+    return pl.pallas_call(
+        project_kernel,
+        grid_spec=pltpu.PrefetchScalarGridSpec(
+            num_scalar_prefetch=1,
+            grid=(peers,),
+            in_specs=[pl.BlockSpec((1, rows, features), lambda i, place: (i, 0, 0)), *whole],
+            out_specs=pl.BlockSpec((1, rows, width), lambda i, place: (i, 0, 0)),
+            scratch_shapes=[pltpu.VMEM((features, width), jnp.bfloat16)],
+        ),
+        out_shape=jax.ShapeDtypeStruct((peers, rows, width), jnp.bfloat16),
+        compiler_params=pltpu.CompilerParams(vmem_limit_bytes=16 * 1024 * 1024),
+        cost_estimate=pl.CostEstimate(
+            flops=2 * peers * rows * features * width,
+            bytes_accessed=2 * (peers * rows * (features + width) + features * width),
+            transcendentals=0,
+        ),
+        name="project_keys",
+    )(place, tokens, *held)
+
+
+def moved(block, steps):
+    return lax.ppermute(block, Z, [(z, (z + steps) % PLANES) for z in range(PLANES)])
+
+
+def weight_blocks(block):
+    below, above, across = moved(block, 4), moved(block, -4), moved(block, 8)
+    own = jnp.concatenate([block, below, above, across], axis=0)
+    return (
+        own,
+        moved(own, 1),
+        moved(own, -1),
+        moved(jnp.concatenate([block, below], axis=0), 2),
+        moved(jnp.concatenate([block, above], axis=0), -2),
+    )
 
 
 def shards(
@@ -77,16 +140,14 @@
         mix_keep * inner_layer.astype(jnp.float32) + (1.0 - mix_keep) * new_outer
     ).astype(jnp.bfloat16)
 
-    weight = lax.all_gather(key_weight[0], Z, axis=0, tiled=True)
-    packed, scale = pack(hidden_in[0])
-    gathered = lax.all_to_all(packed, PLANE, 0, 0, tiled=True)
-    mine = lax.axis_index(PLANE)
-    gain = lax.dynamic_index_in_dim(norm_gain.reshape(PLANES, PEERS, 64), mine, 1, keepdims=False)
-    weight = (weight.astype(jnp.float32) * gain.reshape(-1, 1)).astype(jnp.bfloat16)
-    tokens = gathered.reshape(-1, gathered.shape[-1])
-    partial = jnp.dot(tokens, weight, preferred_element_type=jnp.float32).astype(jnp.bfloat16)
-    partial = partial.reshape(PEERS, -1, partial.shape[-1])
-    partial = lax.all_to_all(partial, PLANE, 0, 0, tiled=True)
+    held = weight_blocks(key_weight[0])
+    packed, scale = pack(hidden_in[0], norm_gain[None])
+    tokens = lax.all_to_all(packed, PLANE, 0, 0, tiled=True)
+    tokens, new_outer, new_moment, mixed_inner = lax.optimization_barrier(
+        (tokens, new_outer, new_moment, mixed_inner)
+    )
+    place = lax.axis_index(Z).astype(jnp.int32)[None]
+    partial = lax.all_to_all(project(place, tokens, held), PLANE, 0, 0, tiled=True)
     keys = (jnp.sum(partial.astype(jnp.float32), axis=0) * scale).astype(jnp.bfloat16)
     return (keys[None], new_outer, new_moment, mixed_inner[None])
 

time: 138 us -> 121 us (0.88)
  starting transfers between devices: 13.9 us -> 58.8 us
  waiting for transfers between devices: 69.6 us -> 26.4 us
  between operations: 14.7 us -> 1.44 us
  blocking collectives: 20.1 us -> 14.2 us
  matrix products: 4.46 us -> 0 us
  Pallas kernels: 3.68 us -> 6.6 us
  local copies, waits for them, and re-layouts: 4.66 us -> 6.66 us
    all_gather x1 -> x0, waiting for transfers between devices: 69 us -> none  [shards(): weight = lax.all_gather(key_weight[0], Z, axis=0, tiled=True)]
    ppermute x0 -> x7, starting transfers between devices: none -> 38.5 us  [moved(): lax.ppermute(block, Z, [(z, (z + steps) % PLANES) for z in range(PLANES)])]
    all_to_all x2, waiting for transfers between devices: 0.01 us -> 22.8 us  [the longest x1 22.8 us: shards(): lax.all_to_all(project(place, tokens, held), PLANE, 0, 0, tiled=True)]
    all_to_all x2, starting transfers between devices: 13.9 us -> 20.3 us  [the longest x1 12.7 us: shards(): lax.all_to_all(project(place, tokens, held), PLANE, 0, 0, tiled=True)]
    all_gather x1, blocking collectives: 20.1 us -> 14.2 us  [shards(): every = lax.all_gather(pseudo_grad, REP, axis=0, tiled=False)]
    unnamed x4 -> x14, local copies, waits for them, and re-layouts: 1.89 us -> 6.66 us
    dot_general x1 -> x0, matrix products: 4.46 us -> none  [shards(): jnp.dot(tokens, weight, preferred_element_type=jnp.float32)]
    pallas_call x0 -> x1, Pallas kernels: none -> 4.42 us  [project(): pl.pallas_call(project_kernel, grid_spec=pltpu.PrefetchScalarGridSpec(num...]
  transfers between devices with their start and end apart: 3 -> 9, of which waited for: 1 -> 3; matrix products, arithmetic and copies ran while one was open for 3% -> 4% of each run, Pallas kernels for 0% -> 0%
where the time goes in v2:
time: 121 us; the launch traced here: 120 us
  starting transfers between devices  58.8 us (49%)
  waiting for transfers between devices  26.4 us (22%)
  blocking collectives  14.2 us (12%)
  local copies, waits for them, and re-layouts  6.66 us (6%)
  Pallas kernels  6.6 us (5%)
  other arithmetic  6.38 us (5%)
  between operations  1.44 us (1%)
    ppermute x7, starting transfers between devices, moved(): lax.ppermute(block, Z, [(z, (z + steps) % PLANES) for z in range(PLANES)])  38.5 us
    all_to_all x1, waiting for transfers between devices, shards(): lax.all_to_all(project(place, tokens, held), PLANE, 0, 0, tiled=True)  22.8 us
    all_gather x1, blocking collectives, shards(): every = lax.all_gather(pseudo_grad, REP, axis=0, tiled=False)  14.2 us
    all_to_all x1, starting transfers between devices, shards(): lax.all_to_all(project(place, tokens, held), PLANE, 0, 0, tiled=True)  12.7 us
    all_to_all x1, starting transfers between devices, shards(): tokens = lax.all_to_all(packed, PLANE, 0, 0, tiled=True)  7.61 us
    unnamed x14, local copies, waits for them, and re-layouts  6.66 us
    pallas_call x1, Pallas kernels, project(): pl.pallas_call(project_kernel, grid_spec=pltpu.PrefetchScalarGridSpec(num...  4.42 us
    ppermute x7, waiting for transfers between devices, moved(): lax.ppermute(block, Z, [(z, (z + steps) % PLANES) for z in range(PLANES)])  3.52 us
  transfers between devices with their start and end apart: 9, of which 3 were waited for; matrix products, arithmetic and copies ran while one was open for 4% of the time, Pallas kernels for 0%

profile of v2, /device:TPU:1, one launch (start us, length us, event | category | flops | bytes accessed | tf_op | source)
XLA Modules:
  0.0 120.5 jit_solution(10547055038092691301)
XLA Ops:
  0.6 0.0 copy-start
  0.6 1.9 %copy-done = bf16[1,192,8192]{2,1,0:T(8,128)(2,1)S(1)} copy-done((bf16[1,192,8192]{2,1,0:T(8,128)(2,1)S(1)}, bf16[1,192,8192]{2,1,0:T(8,128)(2,1)}, u32[]{:S(2)}) %copy-start) | copy-done | bytes 3145752
  2.5 0.0 copy-start.3
  2.5 0.8 copy-done.3
  3.3 2.2 %pack_hidden.1 = (bf16[8,192,1024]{2,1,0:T(8,128)(2,1)S(1)}, f32[192,1]{1,0:T(8,128)S(1)}) custom-call(bf16[192,8192]{1,0:T(8,128)(2,1)S(1)} %bitcast.35, f32[1,8192]{1,0:T(1,128)S(1)} %bitcast.36), custom_call_target="tpu_custom_call" | custom-call | flops 6291456 | bytes 6291456 | tf_op jit(solution)/shard_map/pack_hidden/pallas_call | solution.py:45
  5.5 0.0 copy-start.1
  5.5 1.6 %copy-done.1 = bf16[8,192,1024]{2,1,0:T(8,128)(2,1)} copy-done((bf16[8,192,1024]{2,1,0:T(8,128)(2,1)}, bf16[8,192,1024]{2,1,0:T(8,128)(2,1)S(1)}, u32[]{:S(2)}) %copy-start.1) | copy-done | bytes 3145752
  7.1 0.0 copy-start.4
  7.1 7.6 %all-to-all-start = ((bf16[8,192,1024]{2,1,0:T(8,128)(2,1)}), bf16[8,192,1024]{2,1,0:T(8,128)(2,1)S(1)}, u32[]{:S(2)}, u32[]{:S(2)}) async-start(bf16[8,192,1024]{2,1,0:T(8,128)(2,1)} %copy-done.1), calls=%async_computation | async-start | bytes 6291456 | tf_op jit(solution)/shard_map/all_to_all | solution.py:145
  14.7 0.0 copy-done.4
  14.7 15.4 %collective-permute-start.2 = (bf16[64,512]{1,0:T(8,128)(2,1)S(1)}, bf16[64,512]{1,0:T(8,128)(2,1)S(1)}, u32[]{:S(2)}, u32[]{:S(2)}) collective-permute-start(bf16[64,512]{1,0:T(8,128)(2,1)S(1)} %bitcast.39), channel_id=1, source_target_pairs={{0,64},{8,72},{16,80},{24,88},{32,96},{40,104},{48,112},{56,120},{... | collective-permute-start | bytes 196616 | tf_op jit(solution)/shard_map/ppermute | solution.py:112
  30.2 1.9 %collective-permute-start.1 = (bf16[64,512]{1,0:T(8,128)(2,1)S(1)}, bf16[64,512]{1,0:T(8,128)(2,1)S(1)}, u32[]{:S(2)}, u32[]{:S(2)}) collective-permute-start(bf16[64,512]{1,0:T(8,128)(2,1)S(1)} %bitcast.40), channel_id=1, source_target_pairs={{0,96},{8,104},{16,112},{24,120},{32,0},{40,8},{48,16},{56,24},{64... | collective-permute-start | bytes 196616 | tf_op jit(solution)/shard_map/ppermute | solution.py:112
  32.1 7.3 %collective-permute-start = (bf16[64,512]{1,0:T(8,128)(2,1)S(1)}, bf16[64,512]{1,0:T(8,128)(2,1)}, u32[]{:S(2)}, u32[]{:S(2)}) collective-permute-start(bf16[64,512]{1,0:T(8,128)(2,1)S(1)} %bitcast.41), channel_id=1, source_target_pairs={{0,32},{8,40},{16,48},{24,56},{32,64},{40,72},{48,80},{56,88},{64,... | collective-permute-start | bytes 196616 | tf_op jit(solution)/shard_map/ppermute | solution.py:112
  40.0 0.9 fusion.2
  41.0 14.2 %all_gather.4 = bf16[4,64,512]{2,1,0:T(8,128)(2,1)S(1)} all-gather(bf16[1,64,512]{2,1,0:T(8,128)(2,1)S(1)} %fusion.2), channel_id=1, replica_groups=mesh['yl'=2,'core'=2,'z'=16,'yh'=2,'x'=4] {'yl','core'}, dimensions={0}, use_global_device_ids=true | all-gather | bytes 327680 | tf_op jit(solution)/shard_map/all_gather | solution.py:136
  55.2 0.0 collective-permute-done.2
  55.2 0.0 copy-start.6
  55.2 0.0 collective-permute-done.1
  55.2 0.6 copy-done.6
  55.8 0.0 copy-start.5
  55.8 0.6 copy-done.5
  56.4 0.0 collective-permute-done
  56.4 1.0 pad_maximum_fusion.refs_0_
  57.4 3.3 %collective-permute-start.3 = (bf16[256,512]{1,0:T(8,128)(2,1)S(1)}, bf16[256,512]{1,0:T(8,128)(2,1)}, u32[]{:S(2)}, u32[]{:S(2)}) collective-permute-start(bf16[256,512]{1,0:T(8,128)(2,1)S(1)} %pad_maximum_fusion.refs_0_), channel_id=1, source_target_pairs={{0,8},{8,16},{16,24},{24,32},{32,40},{40,48},{48,56},{56,64},{64,7... | collective-permute-start | bytes 786440 | tf_op jit(solution)/shard_map/ppermute | solution.py:112
  60.7 3.2 %collective-permute-start.4 = (bf16[256,512]{1,0:T(8,128)(2,1)S(1)}, bf16[256,512]{1,0:T(8,128)(2,1)}, u32[]{:S(2)}, u32[]{:S(2)}) collective-permute-start(bf16[256,512]{1,0:T(8,128)(2,1)S(1)} %pad_maximum_fusion.refs_0_), channel_id=1, source_target_pairs={{0,120},{8,0},{16,8},{24,16},{32,24},{40,32},{48,40},{56,48},{64,5... | collective-permute-start | bytes 786440 | tf_op jit(solution)/shard_map/ppermute | solution.py:112
  63.9 1.6 %pad_maximum_fusion.1 = (bf16[128,512]{1,0:T(8,128)(2,1)}, bf16[128,512]{1,0:T(8,128)(2,1)}) fusion(bf16[64,512]{1,0:T(8,128)(2,1)} %bitcast.38, bf16[64,512]{1,0:T(8,128)(2,1)} %copy-done.5, bf16[64,512]{1,0:T(8,128)(2,1)} %collective-permute-done), kind=kLoop, calls=%fused_computation.7 | loop fusion | flops 458752 | bytes 458752 | tf_op jit(solution)/shard_map/concatenate | solution.py:123
  65.5 3.0 %collective-permute-start.5 = (bf16[128,512]{1,0:T(8,128)(2,1)}, bf16[128,512]{1,0:T(8,128)(2,1)}, u32[]{:S(2)}, u32[]{:S(2)}) collective-permute-start(bf16[128,512]{1,0:T(8,128)(2,1)} %get-tuple-element.20), channel_id=1, source_target_pairs={{0,16},{8,24},{16,32},{24,40},{32,48},{40,56},{48,64},{56,72},{64,... | collective-permute-start | bytes 393224 | tf_op jit(solution)/shard_map/ppermute | solution.py:112
  68.5 4.4 %collective-permute-start.6 = (bf16[128,512]{1,0:T(8,128)(2,1)}, bf16[128,512]{1,0:T(8,128)(2,1)}, u32[]{:S(2)}, u32[]{:S(2)}) collective-permute-start(bf16[128,512]{1,0:T(8,128)(2,1)} %get-tuple-element.19), channel_id=1, source_target_pairs={{0,112},{8,120},{16,0},{24,8},{32,16},{40,24},{48,32},{56,40},{64,... | collective-permute-start | bytes 393224 | tf_op jit(solution)/shard_map/ppermute | solution.py:112
  72.9 1.8 %fusion.5 = (bf16[64,512]{1,0:T(8,128)(2,1)}, f32[64,512]{1,0:T(8,128)}, f32[64,512]{1,0:T(8,128)}) fusion(bf16[1,7,64,512]{3,2,1,0:T(8,128)(2,1)} %param.13, s32[]{:T(128)S(6)} %select_n.7, f32[7,64,512]{2,1,0:T(8,128)} %param.12, f32[64,512]{1,0:T(8,128)S(1)} %convert_reduce_fusion.1, f32[7,64,512]{2,1,0:T(8,128)} %param.11), kind=kLoop, calls=%fused_computation.13 | loop fusion | flops 360448 | bytes 786436 | tf_op jit(solution)/shard_map/convert_element_type | solution.py:141
  74.7 0.0 all-to-all-done.tokens_ref
  74.7 1.1 collective-permute-done.5.refs_3_
  75.8 2.4 %collective-permute-done.6.refs_4_ = bf16[128,512]{1,0:T(8,128)(2,1)} collective-permute-done((bf16[128,512]{1,0:T(8,128)(2,1)}, bf16[128,512]{1,0:T(8,128)(2,1)}, u32[]{:S(2)}, u32[]{:S(2)}) %collective-permute-start.6) | collective-permute-done | bytes 131104 | tf_op jit(solution)/shard_map/ppermute | solution.py:112
  78.2 0.0 collective-permute-done.3.refs_1_
  78.2 0.0 collective-permute-done.4.refs_2_
  78.2 4.4 %project_keys.1 = bf16[8,192,512]{2,1,0:T(8,128)(2,1)S(1)} custom-call(s32[1]{0:T(128)} %bitcast.place_ref, bf16[8,192,1024]{2,1,0:T(8,128)(2,1)S(1)} %all-to-all-done.tokens_ref, bf16[256,512]{1,0:T(8,128)(2,1)S(1)} %pad_maximum_fusion.refs_0_, bf16[256,512]{1,0:T(8,128)(2,1)} %collective-permute-done.3.refs_1_, ...), custom_call_target="tpu_custom_call" | custom-call | flops 1610612736 | bytes 5767168 | tf_op jit(solution)/shard_map/project_keys/pallas_call | solution.py:91
  82.6 0.0 copy-start.2
  82.6 1.2 copy-done.2
  83.8 12.7 %all-to-all-start.1 = ((bf16[8,192,512]{2,1,0:T(8,128)(2,1)}), bf16[8,192,512]{2,1,0:T(8,128)(2,1)S(1)}, u32[]{:S(2)}, u32[]{:S(2)}) async-start(bf16[8,192,512]{2,1,0:T(8,128)(2,1)} %copy-done.2), calls=%async_computation.1 | async-start | bytes 3145728 | tf_op jit(solution)/shard_map/all_to_all | solution.py:150
  96.5 0.1 reduce
  96.6 22.8 %all-to-all-done.1 = bf16[8,192,512]{2,1,0:T(8,128)(2,1)S(1)} async-done(((bf16[8,192,512]{2,1,0:T(8,128)(2,1)}), bf16[8,192,512]{2,1,0:T(8,128)(2,1)S(1)}, u32[]{:S(2)}, u32[]{:S(2)}) %all-to-all-start.1) | async-done | bytes 1572896 | tf_op jit(solution)/shard_map/all_to_all | solution.py:150
  119.5 0.2 convert_reduce_fusion
  119.7 0.8 fusion
  (1 shorter events, 0.0 us)
Async XLA Ops:
  0.6 1.9 %copy-start = (bf16[1,192,8192]{2,1,0:T(8,128)(2,1)S(1)}, bf16[1,192,8192]{2,1,0:T(8,128)(2,1)}, u32[]{:S(2)}) copy-start(bf16[1,192,8192]{2,1,0:T(8,128)(2,1)} %param.7) | copy-start | bytes 9437188
  2.5 0.8 copy-start.3
  5.5 1.6 %copy-start.1 = (bf16[8,192,1024]{2,1,0:T(8,128)(2,1)}, bf16[8,192,1024]{2,1,0:T(8,128)(2,1)S(1)}, u32[]{:S(2)}) copy-start(bf16[8,192,1024]{2,1,0:T(8,128)(2,1)S(1)} %get-tuple-element.10) | copy-start | bytes 9437188
  7.1 7.6 %copy-start.4 = (bf16[1,64,512]{2,1,0:T(8,128)(2,1)S(1)}, bf16[1,64,512]{2,1,0:T(8,128)(2,1)}, u32[]{:S(2)}) copy-start(bf16[1,64,512]{2,1,0:T(8,128)(2,1)} %param.9) | copy-start | bytes 196612
  7.1 67.6 %all-to-all-start = ((bf16[8,192,1024]{2,1,0:T(8,128)(2,1)}), bf16[8,192,1024]{2,1,0:T(8,128)(2,1)S(1)}, u32[]{:S(2)}, u32[]{:S(2)}) async-start(bf16[8,192,1024]{2,1,0:T(8,128)(2,1)} %copy-done.1), calls=%async_computation | async-start | bytes 6291456 | tf_op jit(solution)/shard_map/all_to_all | solution.py:145
  14.7 40.5 %collective-permute-start.2 = (bf16[64,512]{1,0:T(8,128)(2,1)S(1)}, bf16[64,512]{1,0:T(8,128)(2,1)S(1)}, u32[]{:S(2)}, u32[]{:S(2)}) collective-permute-start(bf16[64,512]{1,0:T(8,128)(2,1)S(1)} %bitcast.39), channel_id=1, source_target_pairs={{0,64},{8,72},{16,80},{24,88},{32,96},{40,104},{48,112},{56,120},{... | collective-permute-start | bytes 196616 | tf_op jit(solution)/shard_map/ppermute | solution.py:112
  30.2 25.0 %collective-permute-start.1 = (bf16[64,512]{1,0:T(8,128)(2,1)S(1)}, bf16[64,512]{1,0:T(8,128)(2,1)S(1)}, u32[]{:S(2)}, u32[]{:S(2)}) collective-permute-start(bf16[64,512]{1,0:T(8,128)(2,1)S(1)} %bitcast.40), channel_id=1, source_target_pairs={{0,96},{8,104},{16,112},{24,120},{32,0},{40,8},{48,16},{56,24},{64... | collective-permute-start | bytes 196616 | tf_op jit(solution)/shard_map/ppermute | solution.py:112
  32.1 24.3 %collective-permute-start = (bf16[64,512]{1,0:T(8,128)(2,1)S(1)}, bf16[64,512]{1,0:T(8,128)(2,1)}, u32[]{:S(2)}, u32[]{:S(2)}) collective-permute-start(bf16[64,512]{1,0:T(8,128)(2,1)S(1)} %bitcast.41), channel_id=1, source_target_pairs={{0,32},{8,40},{16,48},{24,56},{32,64},{40,72},{48,80},{56,88},{64,... | collective-permute-start | bytes 196616 | tf_op jit(solution)/shard_map/ppermute | solution.py:112
  55.2 0.6 copy-start.6
  55.8 0.6 copy-start.5
  57.4 20.8 %collective-permute-start.3 = (bf16[256,512]{1,0:T(8,128)(2,1)S(1)}, bf16[256,512]{1,0:T(8,128)(2,1)}, u32[]{:S(2)}, u32[]{:S(2)}) collective-permute-start(bf16[256,512]{1,0:T(8,128)(2,1)S(1)} %pad_maximum_fusion.refs_0_), channel_id=1, source_target_pairs={{0,8},{8,16},{16,24},{24,32},{32,40},{40,48},{48,56},{56,64},{64,7... | collective-permute-start | bytes 786440 | tf_op jit(solution)/shard_map/ppermute | solution.py:112
  60.7 17.5 %collective-permute-start.4 = (bf16[256,512]{1,0:T(8,128)(2,1)S(1)}, bf16[256,512]{1,0:T(8,128)(2,1)}, u32[]{:S(2)}, u32[]{:S(2)}) collective-permute-start(bf16[256,512]{1,0:T(8,128)(2,1)S(1)} %pad_maximum_fusion.refs_0_), channel_id=1, source_target_pairs={{0,120},{8,0},{16,8},{24,16},{32,24},{40,32},{48,40},{56,48},{64,5... | collective-permute-start | bytes 786440 | tf_op jit(solution)/shard_map/ppermute | solution.py:112
  65.5 10.3 %collective-permute-start.5 = (bf16[128,512]{1,0:T(8,128)(2,1)}, bf16[128,512]{1,0:T(8,128)(2,1)}, u32[]{:S(2)}, u32[]{:S(2)}) collective-permute-start(bf16[128,512]{1,0:T(8,128)(2,1)} %get-tuple-element.20), channel_id=1, source_target_pairs={{0,16},{8,24},{16,32},{24,40},{32,48},{40,56},{48,64},{56,72},{64,... | collective-permute-start | bytes 393224 | tf_op jit(solution)/shard_map/ppermute | solution.py:112
  68.5 9.7 %collective-permute-start.6 = (bf16[128,512]{1,0:T(8,128)(2,1)}, bf16[128,512]{1,0:T(8,128)(2,1)}, u32[]{:S(2)}, u32[]{:S(2)}) collective-permute-start(bf16[128,512]{1,0:T(8,128)(2,1)} %get-tuple-element.19), channel_id=1, source_target_pairs={{0,112},{8,120},{16,0},{24,8},{32,16},{40,24},{48,32},{56,40},{64,... | collective-permute-start | bytes 393224 | tf_op jit(solution)/shard_map/ppermute | solution.py:112
  82.6 1.2 copy-start.2
  83.8 35.7 %all-to-all-start.1 = ((bf16[8,192,512]{2,1,0:T(8,128)(2,1)}), bf16[8,192,512]{2,1,0:T(8,128)(2,1)S(1)}, u32[]{:S(2)}, u32[]{:S(2)}) async-start(bf16[8,192,512]{2,1,0:T(8,128)(2,1)} %copy-done.2), calls=%async_computation.1 | async-start | bytes 3145728 | tf_op jit(solution)/shard_map/all_to_all | solution.py:150

commit v3 on v2

--- a/solution.py
+++ b/solution.py
@@ -12,7 +12,7 @@
 
 Z, PLANE, REP = "z", ("yh", "x"), ("yl", "core")
 PLANES, PEERS = 16, 8
-ROWS = 32
+ROWS, SOURCES = 32, 2
 
 
 def outer_update(averaged, outer_layer, moment_layer):
@@ -79,9 +79,9 @@
                 rows = pl.ds(pl.multiple_of(plane * 64, 64), 64)
                 weight[rows, :] = held_ref[at * 64 : at * 64 + 64, :]
 
-    out_ref[0] = jnp.dot(tokens_ref[0], weight[...], preferred_element_type=jnp.float32).astype(
-        jnp.bfloat16
-    )
+    tokens = tokens_ref[...].reshape(-1, tokens_ref.shape[-1])
+    product = jnp.dot(tokens, weight[...], preferred_element_type=jnp.float32)
+    out_ref[...] = product.astype(jnp.bfloat16).reshape(out_ref.shape)
 
 
 def project(place, tokens, held):
@@ -92,9 +92,9 @@
         project_kernel,
         grid_spec=pltpu.PrefetchScalarGridSpec(
             num_scalar_prefetch=1,
-            grid=(peers,),
-            in_specs=[pl.BlockSpec((1, rows, features), lambda i, place: (i, 0, 0)), *whole],
-            out_specs=pl.BlockSpec((1, rows, width), lambda i, place: (i, 0, 0)),
+            grid=(peers // SOURCES,),
+            in_specs=[pl.BlockSpec((SOURCES, rows, features), lambda i, place: (i, 0, 0)), *whole],
+            out_specs=pl.BlockSpec((SOURCES, rows, width), lambda i, place: (i, 0, 0)),
             scratch_shapes=[pltpu.VMEM((features, width), jnp.bfloat16)],
         ),
         out_shape=jax.ShapeDtypeStruct((peers, rows, width), jnp.bfloat16),
@@ -133,21 +133,19 @@
     moment_layer = lax.dynamic_index_in_dim(outer_moment, layer_idx, 0, keepdims=False)
     inner_layer = lax.dynamic_index_in_dim(inner_params[0], layer_idx, 0, keepdims=False)
     pseudo_grad = (outer_layer - inner_layer.astype(jnp.float32)).astype(jnp.bfloat16)
+    held = weight_blocks(key_weight[0])
+    packed, scale = pack(hidden_in[0], norm_gain[None])
+    tokens = lax.all_to_all(packed, PLANE, 0, 0, tiled=True)
+    place = lax.axis_index(Z).astype(jnp.int32)[None]
+    partial = project(place, tokens, held)
+    partial, pseudo_grad = lax.optimization_barrier((partial, pseudo_grad))
+    partial = lax.all_to_all(partial, PLANE, 0, 0, tiled=True)
     every = lax.all_gather(pseudo_grad, REP, axis=0, tiled=False)
     summed = jnp.sum(every.astype(jnp.float32), axis=0)
     new_outer, new_moment = outer_update(summed / replicas, outer_layer, moment_layer)
     mixed_inner = (
         mix_keep * inner_layer.astype(jnp.float32) + (1.0 - mix_keep) * new_outer
     ).astype(jnp.bfloat16)
-
-    held = weight_blocks(key_weight[0])
-    packed, scale = pack(hidden_in[0], norm_gain[None])
-    tokens = lax.all_to_all(packed, PLANE, 0, 0, tiled=True)
-    tokens, new_outer, new_moment, mixed_inner = lax.optimization_barrier(
-        (tokens, new_outer, new_moment, mixed_inner)
-    )
-    place = lax.axis_index(Z).astype(jnp.int32)[None]
-    partial = lax.all_to_all(project(place, tokens, held), PLANE, 0, 0, tiled=True)
     keys = (jnp.sum(partial.astype(jnp.float32), axis=0) * scale).astype(jnp.bfloat16)
     return (keys[None], new_outer, new_moment, mixed_inner[None])
 

time: 121 us -> 104 us (0.86)
  the two profiles are of different devices: /device:TPU:1 before, /device:TPU:19 now
where the time goes in v3:
time: 104 us; the launch traced here: 103 us
  starting transfers between devices  52.8 us (51%)
  blocking collectives  22.6 us (22%)
  other arithmetic  8.46 us (8%)
  waiting for transfers between devices  6.42 us (6%)
  Pallas kernels  5.73 us (6%)
  local copies, waits for them, and re-layouts  5.41 us (5%)
  between operations  1.43 us (1%)
    ppermute x7, starting transfers between devices, moved(): lax.ppermute(block, Z, [(z, (z + steps) % PLANES) for z in range(PLANES)])  39.2 us
    all_gather x1, blocking collectives, shards(): every = lax.all_gather(pseudo_grad, REP, axis=0, tiled=False)  22.6 us
    all_to_all x1, starting transfers between devices, shards(): tokens = lax.all_to_all(packed, PLANE, 0, 0, tiled=True)  6.81 us
    all_to_all x1, starting transfers between devices, shards(): partial = lax.all_to_all(partial, PLANE, 0, 0, tiled=True)  6.78 us
    ppermute x7, waiting for transfers between devices, moved(): lax.ppermute(block, Z, [(z, (z + steps) % PLANES) for z in range(PLANES)])  6.41 us
    unnamed x12, local copies, waits for them, and re-layouts  5.41 us
    pallas_call x1, Pallas kernels, project(): pl.pallas_call(project_kernel, grid_spec=pltpu.PrefetchScalarGridSpec(num...  3.55 us
    pallas_call x1, Pallas kernels, pack(): pl.pallas_call(pack_kernel, grid=(tokens // ROWS,), in_specs=[pl.BlockSpe...  2.18 us
  transfers between devices with their start and end apart: 9, of which 3 were waited for; matrix products, arithmetic and copies ran while one was open for 7% of the time, Pallas kernels for 0%

profile of v3, /device:TPU:19, one launch (start us, length us, event | category | flops | bytes accessed | tf_op | source)
XLA Modules:
  0.0 102.8 jit_solution(2275669017445031051)
XLA Ops:
  0.6 0.0 copy-start
  0.6 1.9 %copy-done = bf16[1,192,8192]{2,1,0:T(8,128)(2,1)S(1)} copy-done((bf16[1,192,8192]{2,1,0:T(8,128)(2,1)S(1)}, bf16[1,192,8192]{2,1,0:T(8,128)(2,1)}, u32[]{:S(2)}) %copy-start) | copy-done | bytes 3145752
  2.5 0.0 copy-start.3
  2.5 0.8 copy-done.3
  3.3 2.2 %pack_hidden.1 = (bf16[8,192,1024]{2,1,0:T(8,128)(2,1)S(1)}, f32[192,1]{1,0:T(8,128)S(1)}) custom-call(bf16[192,8192]{1,0:T(8,128)(2,1)S(1)} %bitcast.47, f32[1,8192]{1,0:T(1,128)S(1)} %bitcast.48), custom_call_target="tpu_custom_call" | custom-call | flops 6291456 | bytes 6291456 | tf_op jit(solution)/shard_map/pack_hidden/pallas_call | solution.py:45
  5.5 0.0 copy-start.1
  5.5 1.6 %copy-done.1 = bf16[8,192,1024]{2,1,0:T(8,128)(2,1)} copy-done((bf16[8,192,1024]{2,1,0:T(8,128)(2,1)}, bf16[8,192,1024]{2,1,0:T(8,128)(2,1)S(1)}, u32[]{:S(2)}) %copy-start.1) | copy-done | bytes 3145752
  7.1 0.0 copy-start.5
  7.1 6.8 %all-to-all-start = ((bf16[8,192,1024]{2,1,0:T(8,128)(2,1)}), bf16[8,192,1024]{2,1,0:T(8,128)(2,1)S(1)}, u32[]{:S(2)}, u32[]{:S(2)}) async-start(bf16[8,192,1024]{2,1,0:T(8,128)(2,1)} %copy-done.1), calls=%async_computation | async-start | bytes 6291456 | tf_op jit(solution)/shard_map/all_to_all | solution.py:138
  13.9 0.0 copy-done.5
  13.9 15.4 %collective-permute-start.2 = (bf16[64,512]{1,0:T(8,128)(2,1)S(1)}, bf16[64,512]{1,0:T(8,128)(2,1)S(1)}, u32[]{:S(2)}, u32[]{:S(2)}) collective-permute-start(bf16[64,512]{1,0:T(8,128)(2,1)S(1)} %bitcast.52), channel_id=1, source_target_pairs={{0,64},{8,72},{16,80},{24,88},{32,96},{40,104},{48,112},{56,120},{... | collective-permute-start | bytes 196616 | tf_op jit(solution)/shard_map/ppermute | solution.py:112
  29.3 1.9 %collective-permute-start.1 = (bf16[64,512]{1,0:T(8,128)(2,1)S(1)}, bf16[64,512]{1,0:T(8,128)(2,1)S(1)}, u32[]{:S(2)}, u32[]{:S(2)}) collective-permute-start(bf16[64,512]{1,0:T(8,128)(2,1)S(1)} %bitcast.53), channel_id=1, source_target_pairs={{0,96},{8,104},{16,112},{24,120},{32,0},{40,8},{48,16},{56,24},{64... | collective-permute-start | bytes 196616 | tf_op jit(solution)/shard_map/ppermute | solution.py:112
  31.3 7.3 %collective-permute-start = (bf16[64,512]{1,0:T(8,128)(2,1)S(1)}, bf16[64,512]{1,0:T(8,128)(2,1)S(1)}, u32[]{:S(2)}, u32[]{:S(2)}) collective-permute-start(bf16[64,512]{1,0:T(8,128)(2,1)S(1)} %bitcast.54), channel_id=1, source_target_pairs={{0,32},{8,40},{16,48},{24,56},{32,64},{40,72},{48,80},{56,88},{64,... | collective-permute-start | bytes 196616 | tf_op jit(solution)/shard_map/ppermute | solution.py:112
  38.5 0.0 collective-permute-done.2
  38.6 3.4 %collective-permute-done.1 = bf16[64,512]{1,0:T(8,128)(2,1)S(1)} collective-permute-done((bf16[64,512]{1,0:T(8,128)(2,1)S(1)}, bf16[64,512]{1,0:T(8,128)(2,1)S(1)}, u32[]{:S(2)}, u32[]{:S(2)}) %collective-permute-start.1) | collective-permute-done | bytes 65568 | tf_op jit(solution)/shard_map/ppermute | solution.py:112
  42.0 0.0 collective-permute-done
  42.0 0.9 pad_maximum_fusion.refs_0_
  42.8 4.0 %collective-permute-start.3 = (bf16[256,512]{1,0:T(8,128)(2,1)S(1)}, bf16[256,512]{1,0:T(8,128)(2,1)}, u32[]{:S(2)}, u32[]{:S(2)}) collective-permute-start(bf16[256,512]{1,0:T(8,128)(2,1)S(1)} %pad_maximum_fusion.refs_0_), channel_id=1, source_target_pairs={{0,8},{8,16},{16,24},{24,32},{32,40},{40,48},{48,56},{56,64},{64,7... | collective-permute-start | bytes 786440 | tf_op jit(solution)/shard_map/ppermute | solution.py:112
  46.9 3.2 %collective-permute-start.4 = (bf16[256,512]{1,0:T(8,128)(2,1)S(1)}, bf16[256,512]{1,0:T(8,128)(2,1)}, u32[]{:S(2)}, u32[]{:S(2)}) collective-permute-start(bf16[256,512]{1,0:T(8,128)(2,1)S(1)} %pad_maximum_fusion.refs_0_), channel_id=1, source_target_pairs={{0,120},{8,0},{16,8},{24,16},{32,24},{40,32},{48,40},{56,48},{64,5... | collective-permute-start | bytes 786440 | tf_op jit(solution)/shard_map/ppermute | solution.py:112
  50.1 1.6 %pad_maximum_fusion.1 = (bf16[128,512]{1,0:T(8,128)(2,1)}, bf16[128,512]{1,0:T(8,128)(2,1)}) fusion(bf16[64,512]{1,0:T(8,128)(2,1)} %bitcast.51, bf16[64,512]{1,0:T(8,128)(2,1)S(1)} %collective-permute-done.1, bf16[64,512]{1,0:T(8,128)(2,1)S(1)} %collective-permute-done), kind=kLoop, calls=%fused_computation.7 | loop fusion | flops 458752 | bytes 458752 | tf_op jit(solution)/shard_map/concatenate | solution.py:123
  51.6 3.9 %collective-permute-start.5 = (bf16[128,512]{1,0:T(8,128)(2,1)}, bf16[128,512]{1,0:T(8,128)(2,1)}, u32[]{:S(2)}, u32[]{:S(2)}) collective-permute-start(bf16[128,512]{1,0:T(8,128)(2,1)} %get-tuple-element.15), channel_id=1, source_target_pairs={{0,16},{8,24},{16,32},{24,40},{32,48},{40,56},{48,64},{56,72},{64,... | collective-permute-start | bytes 393224 | tf_op jit(solution)/shard_map/ppermute | solution.py:112
  55.6 3.4 %collective-permute-start.6 = (bf16[128,512]{1,0:T(8,128)(2,1)}, bf16[128,512]{1,0:T(8,128)(2,1)}, u32[]{:S(2)}, u32[]{:S(2)}) collective-permute-start(bf16[128,512]{1,0:T(8,128)(2,1)} %get-tuple-element.14), channel_id=1, source_target_pairs={{0,112},{8,120},{16,0},{24,8},{32,16},{40,24},{48,32},{56,40},{64,... | collective-permute-start | bytes 393224 | tf_op jit(solution)/shard_map/ppermute | solution.py:112
  59.7 1.6 %fusion.2 = bf16[64,512]{1,0:T(8,128)(2,1)} fusion(f32[7,64,512]{2,1,0:T(8,128)} %param.11, s32[]{:T(128)S(6)} %select_n.7, bf16[1,7,64,512]{3,2,1,0:T(8,128)(2,1)} %param.13), kind=kLoop, calls=%fused_computation.10 | loop fusion | flops 98304 | bytes 262148 | tf_op jit(solution)/shard_map/convert_element_type | solution.py:135
  61.2 1.4 %collective-permute-done.5.refs_3_ = bf16[128,512]{1,0:T(8,128)(2,1)} collective-permute-done((bf16[128,512]{1,0:T(8,128)(2,1)}, bf16[128,512]{1,0:T(8,128)(2,1)}, u32[]{:S(2)}, u32[]{:S(2)}) %collective-permute-start.5) | collective-permute-done | bytes 131104 | tf_op jit(solution)/shard_map/ppermute | solution.py:112
  62.7 1.5 %collective-permute-done.6.refs_4_ = bf16[128,512]{1,0:T(8,128)(2,1)} collective-permute-done((bf16[128,512]{1,0:T(8,128)(2,1)}, bf16[128,512]{1,0:T(8,128)(2,1)}, u32[]{:S(2)}, u32[]{:S(2)}) %collective-permute-start.6) | collective-permute-done | bytes 131104 | tf_op jit(solution)/shard_map/ppermute | solution.py:112
  64.2 0.0 collective-permute-done.3.refs_1_
  64.2 0.0 collective-permute-done.4.refs_2_
  64.2 0.0 all-to-all-done.tokens_ref
  64.2 3.6 %project_keys.1 = bf16[8,192,512]{2,1,0:T(8,128)(2,1)S(1)} custom-call(s32[1]{0:T(128)} %bitcast.place_ref, bf16[8,192,1024]{2,1,0:T(8,128)(2,1)S(1)} %all-to-all-done.tokens_ref, bf16[256,512]{1,0:T(8,128)(2,1)S(1)} %pad_maximum_fusion.refs_0_, bf16[256,512]{1,0:T(8,128)(2,1)} %collective-permute-done.3.refs_1_, ...), custom_call_target="tpu_custom_call" | custom-call | flops 1610612736 | bytes 5767168 | tf_op jit(solution)/shard_map/project_keys/pallas_call | solution.py:91
  67.8 0.0 copy-start.2
  67.8 1.1 %copy-done.2 = bf16[8,192,512]{2,1,0:T(8,128)(2,1)} copy-done((bf16[8,192,512]{2,1,0:T(8,128)(2,1)}, bf16[8,192,512]{2,1,0:T(8,128)(2,1)S(1)}, u32[]{:S(2)}) %copy-start.2) | copy-done | bytes 1572888
  69.0 0.0 copy-start.4
  69.0 6.8 %all-to-all-start.1 = ((bf16[8,192,512]{2,1,0:T(8,128)(2,1)}), bf16[8,192,512]{2,1,0:T(8,128)(2,1)S(1)}, u32[]{:S(2)}, u32[]{:S(2)}) async-start(bf16[8,192,512]{2,1,0:T(8,128)(2,1)} %copy-done.2), calls=%async_computation.1 | async-start | bytes 3145728 | tf_op jit(solution)/shard_map/all_to_all | solution.py:142
  75.7 0.1 reduce
  75.8 0.0 copy-done.4
  75.9 22.6 %all-gather = bf16[256,512]{1,0:T(8,128)(2,1)S(1)} all-gather(bf16[64,512]{1,0:T(8,128)(2,1)S(1)} %copy-done.4), channel_id=2, replica_groups=mesh['yl'=2,'core'=2,'z'=16,'yh'=2,'x'=4] {'yl','core'}, dimensions={0}, use_global_device_ids=true | all-gather | bytes 327680 | tf_op jit(solution)/shard_map/all_gather | solution.py:143
  98.5 1.7 %fusion.5 = bf16[1,64,512]{2,1,0:T(8,128)(2,1)} fusion(f32[64,512]{1,0:T(8,128)S(1)} %convert_reduce_fusion.1, f32[7,64,512]{2,1,0:T(8,128)} %param.12, s32[]{:T(128)S(6)} %select_n.7, f32[7,64,512]{2,1,0:T(8,128)} %param.11, bf16[1,7,64,512]{3,2,1,0:T(8,128)(2,1)} %param.13), kind=kLoop, calls=%fused_computation.13 | loop fusion | flops 360448 | bytes 524292 | tf_op jit(solution)/shard_map/convert_element_type | solution.py:148
  100.1 1.7 %bitcast_subtract_fusion = (f32[64,512]{1,0:T(8,128)}, f32[64,512]{1,0:T(8,128)}) fusion(f32[64,512]{1,0:T(8,128)S(1)} %convert_reduce_fusion.1, f32[7,64,512]{2,1,0:T(8,128)} %param.11, s32[]{:T(128)S(6)} %select_n.7, f32[7,64,512]{2,1,0:T(8,128)} %param.12), kind=kLoop, calls=%fused_computation.20 | loop fusion | flops 229376 | bytes 655364 | tf_op jit(solution)/shard_map/sub | solution.py:20
  101.8 0.0 all-to-all-done.1
  101.8 0.2 convert_reduce_fusion
  102.0 0.8 fusion
  (1 shorter events, 0.0 us)
Async XLA Ops:
  0.6 1.9 %copy-start = (bf16[1,192,8192]{2,1,0:T(8,128)(2,1)S(1)}, bf16[1,192,8192]{2,1,0:T(8,128)(2,1)}, u32[]{:S(2)}) copy-start(bf16[1,192,8192]{2,1,0:T(8,128)(2,1)} %param.7) | copy-start | bytes 9437188
  2.5 0.8 copy-start.3
  5.5 1.6 %copy-start.1 = (bf16[8,192,1024]{2,1,0:T(8,128)(2,1)}, bf16[8,192,1024]{2,1,0:T(8,128)(2,1)S(1)}, u32[]{:S(2)}) copy-start(bf16[8,192,1024]{2,1,0:T(8,128)(2,1)S(1)} %get-tuple-element.8) | copy-start | bytes 9437188
  7.1 6.8 %copy-start.5 = (bf16[1,64,512]{2,1,0:T(8,128)(2,1)S(1)}, bf16[1,64,512]{2,1,0:T(8,128)(2,1)}, u32[]{:S(2)}) copy-start(bf16[1,64,512]{2,1,0:T(8,128)(2,1)} %param.9) | copy-start | bytes 196612
  7.1 57.1 %all-to-all-start = ((bf16[8,192,1024]{2,1,0:T(8,128)(2,1)}), bf16[8,192,1024]{2,1,0:T(8,128)(2,1)S(1)}, u32[]{:S(2)}, u32[]{:S(2)}) async-start(bf16[8,192,1024]{2,1,0:T(8,128)(2,1)} %copy-done.1), calls=%async_computation | async-start | bytes 6291456 | tf_op jit(solution)/shard_map/all_to_all | solution.py:138
  13.9 24.6 %collective-permute-start.2 = (bf16[64,512]{1,0:T(8,128)(2,1)S(1)}, bf16[64,512]{1,0:T(8,128)(2,1)S(1)}, u32[]{:S(2)}, u32[]{:S(2)}) collective-permute-start(bf16[64,512]{1,0:T(8,128)(2,1)S(1)} %bitcast.52), channel_id=1, source_target_pairs={{0,64},{8,72},{16,80},{24,88},{32,96},{40,104},{48,112},{56,120},{... | collective-permute-start | bytes 196616 | tf_op jit(solution)/shard_map/ppermute | solution.py:112
  29.3 12.6 %collective-permute-start.1 = (bf16[64,512]{1,0:T(8,128)(2,1)S(1)}, bf16[64,512]{1,0:T(8,128)(2,1)S(1)}, u32[]{:S(2)}, u32[]{:S(2)}) collective-permute-start(bf16[64,512]{1,0:T(8,128)(2,1)S(1)} %bitcast.53), channel_id=1, source_target_pairs={{0,96},{8,104},{16,112},{24,120},{32,0},{40,8},{48,16},{56,24},{64... | collective-permute-start | bytes 196616 | tf_op jit(solution)/shard_map/ppermute | solution.py:112
  31.3 10.7 %collective-permute-start = (bf16[64,512]{1,0:T(8,128)(2,1)S(1)}, bf16[64,512]{1,0:T(8,128)(2,1)S(1)}, u32[]{:S(2)}, u32[]{:S(2)}) collective-permute-start(bf16[64,512]{1,0:T(8,128)(2,1)S(1)} %bitcast.54), channel_id=1, source_target_pairs={{0,32},{8,40},{16,48},{24,56},{32,64},{40,72},{48,80},{56,88},{64,... | collective-permute-start | bytes 196616 | tf_op jit(solution)/shard_map/ppermute | solution.py:112
  42.8 21.4 %collective-permute-start.3 = (bf16[256,512]{1,0:T(8,128)(2,1)S(1)}, bf16[256,512]{1,0:T(8,128)(2,1)}, u32[]{:S(2)}, u32[]{:S(2)}) collective-permute-start(bf16[256,512]{1,0:T(8,128)(2,1)S(1)} %pad_maximum_fusion.refs_0_), channel_id=1, source_target_pairs={{0,8},{8,16},{16,24},{24,32},{32,40},{40,48},{48,56},{56,64},{64,7... | collective-permute-start | bytes 786440 | tf_op jit(solution)/shard_map/ppermute | solution.py:112
  46.9 17.4 %collective-permute-start.4 = (bf16[256,512]{1,0:T(8,128)(2,1)S(1)}, bf16[256,512]{1,0:T(8,128)(2,1)}, u32[]{:S(2)}, u32[]{:S(2)}) collective-permute-start(bf16[256,512]{1,0:T(8,128)(2,1)S(1)} %pad_maximum_fusion.refs_0_), channel_id=1, source_target_pairs={{0,120},{8,0},{16,8},{24,16},{32,24},{40,32},{48,40},{56,48},{64,5... | collective-permute-start | bytes 786440 | tf_op jit(solution)/shard_map/ppermute | solution.py:112
  51.6 11.0 %collective-permute-start.5 = (bf16[128,512]{1,0:T(8,128)(2,1)}, bf16[128,512]{1,0:T(8,128)(2,1)}, u32[]{:S(2)}, u32[]{:S(2)}) collective-permute-start(bf16[128,512]{1,0:T(8,128)(2,1)} %get-tuple-element.15), channel_id=1, source_target_pairs={{0,16},{8,24},{16,32},{24,40},{32,48},{40,56},{48,64},{56,72},{64,... | collective-permute-start | bytes 393224 | tf_op jit(solution)/shard_map/ppermute | solution.py:112
  55.6 8.6 %collective-permute-start.6 = (bf16[128,512]{1,0:T(8,128)(2,1)}, bf16[128,512]{1,0:T(8,128)(2,1)}, u32[]{:S(2)}, u32[]{:S(2)}) collective-permute-start(bf16[128,512]{1,0:T(8,128)(2,1)} %get-tuple-element.14), channel_id=1, source_target_pairs={{0,112},{8,120},{16,0},{24,8},{32,16},{40,24},{48,32},{56,40},{64,... | collective-permute-start | bytes 393224 | tf_op jit(solution)/shard_map/ppermute | solution.py:112
  67.8 1.2 %copy-start.2 = (bf16[8,192,512]{2,1,0:T(8,128)(2,1)}, bf16[8,192,512]{2,1,0:T(8,128)(2,1)S(1)}, u32[]{:S(2)}) copy-start(bf16[8,192,512]{2,1,0:T(8,128)(2,1)S(1)} %project_keys.1) | copy-start | bytes 4718596
  69.0 6.9 %copy-start.4 = (bf16[64,512]{1,0:T(8,128)(2,1)S(1)}, bf16[64,512]{1,0:T(8,128)(2,1)}, u32[]{:S(2)}) copy-start(bf16[64,512]{1,0:T(8,128)(2,1)} %fusion.2) | copy-start | bytes 196612
  69.0 32.9 %all-to-all-start.1 = ((bf16[8,192,512]{2,1,0:T(8,128)(2,1)}), bf16[8,192,512]{2,1,0:T(8,128)(2,1)S(1)}, u32[]{:S(2)}, u32[]{:S(2)}) async-start(bf16[8,192,512]{2,1,0:T(8,128)(2,1)} %copy-done.2), calls=%async_computation.1 | async-start | bytes 3145728 | tf_op jit(solution)/shard_map/all_to_all | solution.py:142

commit v4 on v3

--- a/solution.py
+++ b/solution.py
@@ -13,6 +13,7 @@
 Z, PLANE, REP = "z", ("yh", "x"), ("yl", "core")
 PLANES, PEERS = 16, 8
 ROWS, SOURCES = 32, 2
+PACK_VMEM, PROJECT_VMEM = 60 * 1024 * 1024, 60 * 1024 * 1024
 
 
 def outer_update(averaged, outer_layer, moment_layer):
@@ -57,7 +58,7 @@
             jax.ShapeDtypeStruct((PEERS, tokens, features // PEERS), jnp.bfloat16),
             jax.ShapeDtypeStruct((tokens, 1), jnp.float32),
         ],
-        compiler_params=pltpu.CompilerParams(vmem_limit_bytes=16 * 1024 * 1024),
+        compiler_params=pltpu.CompilerParams(vmem_limit_bytes=PACK_VMEM),
         cost_estimate=pl.CostEstimate(
             flops=4 * tokens * features, bytes_accessed=4 * tokens * features, transcendentals=tokens
         ),
@@ -65,7 +66,8 @@
     )(hidden, gain)
 
 
-HELD = ((0, -4, 4, 8), (-1, -5, 3, 7), (1, -3, 5, 9), (-2, -6), (2, 6))
+NEAR = (0, -4, 4, 8)
+HELD = (0, -1, 1, None)
 
 
 def project_kernel(place_ref, tokens_ref, *refs):
@@ -73,9 +75,12 @@
 
     @pl.when(pl.program_id(0) == 0)
     def _():
-        for held_ref, offsets in zip(held_refs, HELD, strict=True):
-            for at, offset in enumerate(offsets):
-                plane = lax.rem(place_ref[0] + offset + PLANES, PLANES)
+        here = place_ref[0]
+        for held_ref, offset in zip(held_refs, HELD, strict=True):
+            if offset is None:
+                offset = jnp.where(lax.rem(here, 2) == 0, -2, 2)
+            for at, further in enumerate(NEAR):
+                plane = lax.rem(here + offset + further + PLANES, PLANES)
                 rows = pl.ds(pl.multiple_of(plane * 64, 64), 64)
                 weight[rows, :] = held_ref[at * 64 : at * 64 + 64, :]
 
@@ -98,7 +103,7 @@
             scratch_shapes=[pltpu.VMEM((features, width), jnp.bfloat16)],
         ),
         out_shape=jax.ShapeDtypeStruct((peers, rows, width), jnp.bfloat16),
-        compiler_params=pltpu.CompilerParams(vmem_limit_bytes=16 * 1024 * 1024),
+        compiler_params=pltpu.CompilerParams(vmem_limit_bytes=PROJECT_VMEM),
         cost_estimate=pl.CostEstimate(
             flops=2 * peers * rows * features * width,
             bytes_accessed=2 * (peers * rows * (features + width) + features * width),
@@ -108,38 +113,36 @@
     )(place, tokens, *held)
 
 
-def moved(block, steps):
-    return lax.ppermute(block, Z, [(z, (z + steps) % PLANES) for z in range(PLANES)])
-
-
-def weight_blocks(block):
-    below, above, across = moved(block, 4), moved(block, -4), moved(block, 8)
-    own = jnp.concatenate([block, below, above, across], axis=0)
-    return (
-        own,
-        moved(own, 1),
-        moved(own, -1),
-        moved(jnp.concatenate([block, below], axis=0), 2),
-        moved(jnp.concatenate([block, above], axis=0), -2),
-    )
+def moved(block, target):
+    return lax.ppermute(block, Z, [(z, target(z) % PLANES) for z in range(PLANES)])
 
 
 def shards(
     hidden_in, norm_gain, key_weight, fragment_index, outer_params, outer_moment, inner_params
 ):
     replicas = 4
+    block = key_weight[0]
+    below, above = moved(block, lambda z: z + 4), moved(block, lambda z: z - 4)
+    packed, scale = pack(hidden_in[0], norm_gain[None])
+    packed, below, above, later = lax.optimization_barrier((packed, below, above, block))
+    tokens = lax.all_to_all(packed, PLANE, 0, 0, tiled=True)
+    across = moved(later, lambda z: z + 8)
+    own = jnp.concatenate([block, below, above, across], axis=0)
+    held = (
+        own,
+        moved(own, lambda z: z + 1),
+        moved(own, lambda z: z - 1),
+        moved(own, lambda z: z + 2 if z % 2 == 0 else z - 2),
+    )
+    place = lax.axis_index(Z).astype(jnp.int32)[None]
+    partial = project(place, tokens, held)
+    partial, fragment_index = lax.optimization_barrier((partial, fragment_index))
+    partial = lax.all_to_all(partial, PLANE, 0, 0, tiled=True)
     layer_idx = fragment_index[0]
     outer_layer = lax.dynamic_index_in_dim(outer_params, layer_idx, 0, keepdims=False)
     moment_layer = lax.dynamic_index_in_dim(outer_moment, layer_idx, 0, keepdims=False)
     inner_layer = lax.dynamic_index_in_dim(inner_params[0], layer_idx, 0, keepdims=False)
     pseudo_grad = (outer_layer - inner_layer.astype(jnp.float32)).astype(jnp.bfloat16)
-    held = weight_blocks(key_weight[0])
-    packed, scale = pack(hidden_in[0], norm_gain[None])
-    tokens = lax.all_to_all(packed, PLANE, 0, 0, tiled=True)
-    place = lax.axis_index(Z).astype(jnp.int32)[None]
-    partial = project(place, tokens, held)
-    partial, pseudo_grad = lax.optimization_barrier((partial, pseudo_grad))
-    partial = lax.all_to_all(partial, PLANE, 0, 0, tiled=True)
     every = lax.all_gather(pseudo_grad, REP, axis=0, tiled=False)
     summed = jnp.sum(every.astype(jnp.float32), axis=0)
     new_outer, new_moment = outer_update(summed / replicas, outer_layer, moment_layer)

time: 104 us -> 116 us (1.12)
  the two profiles are of different devices: /device:TPU:19 before, /device:TPU:17 now
where the time goes in v4:
time: 116 us; the launch traced here: 115 us
  starting transfers between devices  49 us (42%)
  waiting for transfers between devices  24.1 us (21%)
  blocking collectives  20.9 us (18%)
  Pallas kernels  11.4 us (10%)
  other arithmetic  6.27 us (5%)
  local copies, waits for them, and re-layouts  2.28 us (2%)
  between operations  1.39 us (1%)
    ppermute x6, starting transfers between devices, moved(): lax.ppermute(block, Z, [(z, target(z) % PLANES) for z in range(PLANES)])  30.3 us
    all_gather x1, blocking collectives, shards(): every = lax.all_gather(pseudo_grad, REP, axis=0, tiled=False)  20.9 us
    ppermute x6, waiting for transfers between devices, moved(): lax.ppermute(block, Z, [(z, target(z) % PLANES) for z in range(PLANES)])  19.3 us
    all_to_all x1, starting transfers between devices, shards(): partial = lax.all_to_all(partial, PLANE, 0, 0, tiled=True)  11.9 us
    all_to_all x1, starting transfers between devices, shards(): tokens = lax.all_to_all(packed, PLANE, 0, 0, tiled=True)  6.83 us
    pallas_call x1, Pallas kernels, pack(): pl.pallas_call(pack_kernel, grid=(tokens // ROWS,), in_specs=[pl.BlockSpe...  6.01 us
    pallas_call x1, Pallas kernels, project(): pl.pallas_call(project_kernel, grid_spec=pltpu.PrefetchScalarGridSpec(num...  5.44 us
    all_to_all x1, waiting for transfers between devices, shards(): tokens = lax.all_to_all(packed, PLANE, 0, 0, tiled=True)  4.74 us
  transfers between devices with their start and end apart: 8, of which 6 were waited for; matrix products, arithmetic and copies ran while one was open for 5% of the time, Pallas kernels for 5%

profile of v4, /device:TPU:17, one launch (start us, length us, event | category | flops | bytes accessed | tf_op | source)
XLA Modules:
  0.0 115.4 jit_solution(16953490117383984408)
XLA Ops:
  0.6 8.8 %collective-permute-start = (bf16[64,512]{1,0:T(8,128)(2,1)}, bf16[64,512]{1,0:T(8,128)(2,1)S(1)}, u32[]{:S(2)}, u32[]{:S(2)}) collective-permute-start(bf16[64,512]{1,0:T(8,128)(2,1)} %bitcast.35), channel_id=1, source_target_pairs={{0,32},{8,40},{16,48},{24,56},{32,64},{40,72},{48,80},{56,88},{64,... | collective-permute-start | bytes 196616 | tf_op jit(solution)/shard_map/ppermute | solution.py:117
  9.5 5.6 %collective-permute-start.1 = (bf16[64,512]{1,0:T(8,128)(2,1)}, bf16[64,512]{1,0:T(8,128)(2,1)S(1)}, u32[]{:S(2)}, u32[]{:S(2)}) collective-permute-start(bf16[64,512]{1,0:T(8,128)(2,1)} %bitcast.36), channel_id=1, source_target_pairs={{0,96},{8,104},{16,112},{24,120},{32,0},{40,8},{48,16},{56,24},{64... | collective-permute-start | bytes 196616 | tf_op jit(solution)/shard_map/ppermute | solution.py:117
  15.0 6.0 %pack_hidden.1 = (bf16[8,192,1024]{2,1,0:T(8,128)(2,1)}, f32[192,1]{1,0:T(8,128)}) custom-call(bf16[192,8192]{1,0:T(8,128)(2,1)} %bitcast.34, f32[1,8192]{1,0:T(1,128)} %bitcast.39), custom_call_target="tpu_custom_call" | custom-call | flops 6291456 | bytes 6291456 | tf_op jit(solution)/shard_map/pack_hidden/pallas_call | solution.py:46
  21.0 0.0 collective-permute-done
  21.0 3.8 %collective-permute-done.1 = bf16[64,512]{1,0:T(8,128)(2,1)S(1)} collective-permute-done((bf16[64,512]{1,0:T(8,128)(2,1)}, bf16[64,512]{1,0:T(8,128)(2,1)S(1)}, u32[]{:S(2)}, u32[]{:S(2)}) %collective-permute-start.1) | collective-permute-done | bytes 65568 | tf_op jit(solution)/shard_map/ppermute | solution.py:117
  24.8 0.0 copy-start.4
  24.8 0.6 copy-done.4
  25.4 0.0 copy-start.3
  25.4 6.8 %all-to-all-start = ((bf16[8,192,1024]{2,1,0:T(8,128)(2,1)}), bf16[8,192,1024]{2,1,0:T(8,128)(2,1)S(1)}, u32[]{:S(2)}, u32[]{:S(2)}) async-start(bf16[8,192,1024]{2,1,0:T(8,128)(2,1)} %get-tuple-element.13), calls=%async_computation | async-start | bytes 6291456 | tf_op jit(solution)/shard_map/all_to_all | solution.py:128
  32.3 0.0 copy-done.3
  32.3 7.5 %collective-permute-start.2 = (bf16[64,512]{1,0:T(8,128)(2,1)S(1)}, bf16[64,512]{1,0:T(8,128)(2,1)S(1)}, u32[]{:S(2)}, u32[]{:S(2)}) collective-permute-start(bf16[64,512]{1,0:T(8,128)(2,1)S(1)} %bitcast.37), channel_id=1, source_target_pairs={{0,64},{8,72},{16,80},{24,88},{32,96},{40,104},{48,112},{56,120},{... | collective-permute-start | bytes 196616 | tf_op jit(solution)/shard_map/ppermute | solution.py:117
  39.8 8.0 %collective-permute-done.2 = bf16[64,512]{1,0:T(8,128)(2,1)S(1)} collective-permute-done((bf16[64,512]{1,0:T(8,128)(2,1)S(1)}, bf16[64,512]{1,0:T(8,128)(2,1)S(1)}, u32[]{:S(2)}, u32[]{:S(2)}) %collective-permute-start.2) | collective-permute-done | bytes 65568 | tf_op jit(solution)/shard_map/ppermute | solution.py:117
  47.7 0.9 pad_maximum_fusion.refs_0_
  48.6 0.0 copy-start.1
  48.6 1.9 %collective-permute-start.3 = (bf16[256,512]{1,0:T(8,128)(2,1)S(1)}, bf16[256,512]{1,0:T(8,128)(2,1)}, u32[]{:S(2)}, u32[]{:S(2)}) collective-permute-start(bf16[256,512]{1,0:T(8,128)(2,1)S(1)} %pad_maximum_fusion.refs_0_), channel_id=1, source_target_pairs={{0,8},{8,16},{16,24},{24,32},{32,40},{40,48},{48,56},{56,64},{64,7... | collective-permute-start | bytes 786440 | tf_op jit(solution)/shard_map/ppermute | solution.py:117
  50.5 4.6 %collective-permute-start.4 = (bf16[256,512]{1,0:T(8,128)(2,1)S(1)}, bf16[256,512]{1,0:T(8,128)(2,1)}, u32[]{:S(2)}, u32[]{:S(2)}) collective-permute-start(bf16[256,512]{1,0:T(8,128)(2,1)S(1)} %pad_maximum_fusion.refs_0_), channel_id=1, source_target_pairs={{0,120},{8,0},{16,8},{24,16},{32,24},{40,32},{48,40},{56,48},{64,5... | collective-permute-start | bytes 786440 | tf_op jit(solution)/shard_map/ppermute | solution.py:117
  55.1 1.9 %collective-permute-start.5 = (bf16[256,512]{1,0:T(8,128)(2,1)S(1)}, bf16[256,512]{1,0:T(8,128)(2,1)}, u32[]{:S(2)}, u32[]{:S(2)}) collective-permute-start(bf16[256,512]{1,0:T(8,128)(2,1)S(1)} %pad_maximum_fusion.refs_0_), channel_id=1, source_target_pairs={{0,16},{8,120},{16,32},{24,8},{32,48},{40,24},{48,64},{56,40},{64,... | collective-permute-start | bytes 786440 | tf_op jit(solution)/shard_map/ppermute | solution.py:117
  57.0 0.2 collective-permute-done.3.refs_1_
  57.2 1.2 %collective-permute-done.4.refs_2_ = bf16[256,512]{1,0:T(8,128)(2,1)} collective-permute-done((bf16[256,512]{1,0:T(8,128)(2,1)S(1)}, bf16[256,512]{1,0:T(8,128)(2,1)}, u32[]{:S(2)}, u32[]{:S(2)}) %collective-permute-start.4) | collective-permute-done | bytes 262176 | tf_op jit(solution)/shard_map/ppermute | solution.py:117
  58.4 6.2 %collective-permute-done.5.refs_3_ = bf16[256,512]{1,0:T(8,128)(2,1)} collective-permute-done((bf16[256,512]{1,0:T(8,128)(2,1)S(1)}, bf16[256,512]{1,0:T(8,128)(2,1)}, u32[]{:S(2)}, u32[]{:S(2)}) %collective-permute-start.5) | collective-permute-done | bytes 262176 | tf_op jit(solution)/shard_map/ppermute | solution.py:117
  64.6 4.7 %all-to-all-done.tokens_ref = bf16[8,192,1024]{2,1,0:T(8,128)(2,1)S(1)} async-done(((bf16[8,192,1024]{2,1,0:T(8,128)(2,1)}), bf16[8,192,1024]{2,1,0:T(8,128)(2,1)S(1)}, u32[]{:S(2)}, u32[]{:S(2)}) %all-to-all-start) | async-done | bytes 3145760 | tf_op jit(solution)/shard_map/all_to_all | solution.py:128
  69.4 0.0 copy-start
  69.4 0.0 copy-done.1
  69.4 1.6 %copy-done = bf16[8,192,1024]{2,1,0:T(8,128)(2,1)} copy-done((bf16[8,192,1024]{2,1,0:T(8,128)(2,1)}, bf16[8,192,1024]{2,1,0:T(8,128)(2,1)S(1)}, u32[]{:S(2)}) %copy-start) | copy-done | bytes 3145752
  71.0 0.0 copy-start.2
  71.0 5.4 %project_keys.1 = bf16[8,192,512]{2,1,0:T(8,128)(2,1)} custom-call(s32[1]{0:T(128)} %bitcast.place_ref, bf16[8,192,1024]{2,1,0:T(8,128)(2,1)} %copy-done, bf16[256,512]{1,0:T(8,128)(2,1)} %copy-done.1, bf16[256,512]{1,0:T(8,128)(2,1)} %collective-permute-done.3.refs_1_, bf16[256,512]{1,0:T(8,128)(2,1)} %collective-permute-done.4.refs_2_, ...), custom_call_target="tpu_custom_call" | custom-call | flops 1610612736 | bytes 5767168 | tf_op jit(solution)/shard_map/project_keys/pallas_call | solution.py:96
  76.5 11.9 %all-to-all-start.1 = ((bf16[8,192,512]{2,1,0:T(8,128)(2,1)}), bf16[8,192,512]{2,1,0:T(8,128)(2,1)S(1)}, u32[]{:S(2)}, u32[]{:S(2)}) async-start(bf16[8,192,512]{2,1,0:T(8,128)(2,1)} %project_keys.1), calls=%async_computation.1 | async-start | bytes 3145728 | tf_op jit(solution)/shard_map/all_to_all | solution.py:140
  89.0 0.0 copy-done.2
  89.0 0.1 reduce
  89.1 0.9 fusion.1
  90.1 20.9 %all_gather.4 = bf16[4,64,512]{2,1,0:T(8,128)(2,1)S(1)} all-gather(bf16[1,64,512]{2,1,0:T(8,128)(2,1)S(1)} %fusion.1), channel_id=1, replica_groups=mesh['yl'=2,'core'=2,'z'=16,'yh'=2,'x'=4] {'yl','core'}, dimensions={0}, use_global_device_ids=true | all-gather | bytes 327680 | tf_op jit(solution)/shard_map/all_gather | solution.py:146
  111.0 1.7 %fusion.3 = bf16[1,64,512]{2,1,0:T(8,128)(2,1)} fusion(f32[64,512]{1,0:T(8,128)S(1)} %convert_reduce_fusion.1, f32[7,64,512]{2,1,0:T(8,128)} %param.12, s32[]{:T(128)S(6)} %select_n.7, f32[7,64,512]{2,1,0:T(8,128)} %param.11, bf16[1,7,64,512]{3,2,1,0:T(8,128)(2,1)} %param.13), kind=kLoop, calls=%fused_computation.9 | loop fusion | flops 360448 | bytes 524292 | tf_op jit(solution)/shard_map/convert_element_type | solution.py:151
  112.7 1.7 %bitcast_subtract_fusion = (f32[64,512]{1,0:T(8,128)}, f32[64,512]{1,0:T(8,128)}) fusion(f32[64,512]{1,0:T(8,128)S(1)} %convert_reduce_fusion.1, f32[7,64,512]{2,1,0:T(8,128)} %param.11, s32[]{:T(128)S(6)} %select_n.7, f32[7,64,512]{2,1,0:T(8,128)} %param.12), kind=kLoop, calls=%fused_computation.16 | loop fusion | flops 229376 | bytes 655364 | tf_op jit(solution)/shard_map/sub | solution.py:21
  114.4 0.0 all-to-all-done.1
  114.4 0.2 convert_reduce_fusion
  114.6 0.8 fusion
  (1 shorter events, 0.0 us)
Async XLA Ops:
  0.6 20.4 %collective-permute-start = (bf16[64,512]{1,0:T(8,128)(2,1)}, bf16[64,512]{1,0:T(8,128)(2,1)S(1)}, u32[]{:S(2)}, u32[]{:S(2)}) collective-permute-start(bf16[64,512]{1,0:T(8,128)(2,1)} %bitcast.35), channel_id=1, source_target_pairs={{0,32},{8,40},{16,48},{24,56},{32,64},{40,72},{48,80},{56,88},{64,... | collective-permute-start | bytes 196616 | tf_op jit(solution)/shard_map/ppermute | solution.py:117
  9.5 15.4 %collective-permute-start.1 = (bf16[64,512]{1,0:T(8,128)(2,1)}, bf16[64,512]{1,0:T(8,128)(2,1)S(1)}, u32[]{:S(2)}, u32[]{:S(2)}) collective-permute-start(bf16[64,512]{1,0:T(8,128)(2,1)} %bitcast.36), channel_id=1, source_target_pairs={{0,96},{8,104},{16,112},{24,120},{32,0},{40,8},{48,16},{56,24},{64... | collective-permute-start | bytes 196616 | tf_op jit(solution)/shard_map/ppermute | solution.py:117
  24.8 0.6 copy-start.4
  25.4 6.8 %copy-start.3 = (bf16[1,64,512]{2,1,0:T(8,128)(2,1)S(1)}, bf16[1,64,512]{2,1,0:T(8,128)(2,1)}, u32[]{:S(2)}) copy-start(bf16[1,64,512]{2,1,0:T(8,128)(2,1)} %param.9) | copy-start | bytes 196612
  25.4 43.9 %all-to-all-start = ((bf16[8,192,1024]{2,1,0:T(8,128)(2,1)}), bf16[8,192,1024]{2,1,0:T(8,128)(2,1)S(1)}, u32[]{:S(2)}, u32[]{:S(2)}) async-start(bf16[8,192,1024]{2,1,0:T(8,128)(2,1)} %get-tuple-element.13), calls=%async_computation | async-start | bytes 6291456 | tf_op jit(solution)/shard_map/all_to_all | solution.py:128
  32.3 15.4 %collective-permute-start.2 = (bf16[64,512]{1,0:T(8,128)(2,1)S(1)}, bf16[64,512]{1,0:T(8,128)(2,1)S(1)}, u32[]{:S(2)}, u32[]{:S(2)}) collective-permute-start(bf16[64,512]{1,0:T(8,128)(2,1)S(1)} %bitcast.37), channel_id=1, source_target_pairs={{0,64},{8,72},{16,80},{24,88},{32,96},{40,104},{48,112},{56,120},{... | collective-permute-start | bytes 196616 | tf_op jit(solution)/shard_map/ppermute | solution.py:117
  48.6 20.8 %copy-start.1 = (bf16[256,512]{1,0:T(8,128)(2,1)}, bf16[256,512]{1,0:T(8,128)(2,1)S(1)}, u32[]{:S(2)}) copy-start(bf16[256,512]{1,0:T(8,128)(2,1)S(1)} %pad_maximum_fusion.refs_0_) | copy-start | bytes 786436
  48.6 8.6 %collective-permute-start.3 = (bf16[256,512]{1,0:T(8,128)(2,1)S(1)}, bf16[256,512]{1,0:T(8,128)(2,1)}, u32[]{:S(2)}, u32[]{:S(2)}) collective-permute-start(bf16[256,512]{1,0:T(8,128)(2,1)S(1)} %pad_maximum_fusion.refs_0_), channel_id=1, source_target_pairs={{0,8},{8,16},{16,24},{24,32},{32,40},{40,48},{48,56},{56,64},{64,7... | collective-permute-start | bytes 786440 | tf_op jit(solution)/shard_map/ppermute | solution.py:117
  50.5 7.9 %collective-permute-start.4 = (bf16[256,512]{1,0:T(8,128)(2,1)S(1)}, bf16[256,512]{1,0:T(8,128)(2,1)}, u32[]{:S(2)}, u32[]{:S(2)}) collective-permute-start(bf16[256,512]{1,0:T(8,128)(2,1)S(1)} %pad_maximum_fusion.refs_0_), channel_id=1, source_target_pairs={{0,120},{8,0},{16,8},{24,16},{32,24},{40,32},{48,40},{56,48},{64,5... | collective-permute-start | bytes 786440 | tf_op jit(solution)/shard_map/ppermute | solution.py:117
  55.1 9.5 %collective-permute-start.5 = (bf16[256,512]{1,0:T(8,128)(2,1)S(1)}, bf16[256,512]{1,0:T(8,128)(2,1)}, u32[]{:S(2)}, u32[]{:S(2)}) collective-permute-start(bf16[256,512]{1,0:T(8,128)(2,1)S(1)} %pad_maximum_fusion.refs_0_), channel_id=1, source_target_pairs={{0,16},{8,120},{16,32},{24,8},{32,48},{40,24},{48,64},{56,40},{64,... | collective-permute-start | bytes 786440 | tf_op jit(solution)/shard_map/ppermute | solution.py:117
  69.4 1.6 %copy-start = (bf16[8,192,1024]{2,1,0:T(8,128)(2,1)}, bf16[8,192,1024]{2,1,0:T(8,128)(2,1)S(1)}, u32[]{:S(2)}) copy-start(bf16[8,192,1024]{2,1,0:T(8,128)(2,1)S(1)} %all-to-all-done.tokens_ref) | copy-start | bytes 9437188
  71.0 18.0 %copy-start.2 = (f32[192,1]{1,0:T(8,128)S(1)}, f32[192,1]{1,0:T(8,128)}, u32[]{:S(2)}) copy-start(f32[192,1]{1,0:T(8,128)} %get-tuple-element.18) | copy-start | bytes 2308
  76.5 38.0 %all-to-all-start.1 = ((bf16[8,192,512]{2,1,0:T(8,128)(2,1)}), bf16[8,192,512]{2,1,0:T(8,128)(2,1)S(1)}, u32[]{:S(2)}, u32[]{:S(2)}) async-start(bf16[8,192,512]{2,1,0:T(8,128)(2,1)} %project_keys.1), calls=%async_computation.1 | async-start | bytes 3145728 | tf_op jit(solution)/shard_map/all_to_all | solution.py:140

commit v5 on v4

--- a/solution.py
+++ b/solution.py
@@ -12,8 +12,8 @@
 
 Z, PLANE, REP = "z", ("yh", "x"), ("yl", "core")
 PLANES, PEERS = 16, 8
-ROWS, SOURCES = 32, 2
-PACK_VMEM, PROJECT_VMEM = 60 * 1024 * 1024, 60 * 1024 * 1024
+ROWS, SOURCES = 64, 4
+KERNEL_VMEM = 24 * 1024 * 1024
 
 
 def outer_update(averaged, outer_layer, moment_layer):
@@ -55,10 +55,10 @@
             pl.BlockSpec((ROWS, 1), lambda i: (i, 0)),
         ],
         out_shape=[
-            jax.ShapeDtypeStruct((PEERS, tokens, features // PEERS), jnp.bfloat16),
+            pltpu.HBM((PEERS, tokens, features // PEERS), jnp.bfloat16),
             jax.ShapeDtypeStruct((tokens, 1), jnp.float32),
         ],
-        compiler_params=pltpu.CompilerParams(vmem_limit_bytes=PACK_VMEM),
+        compiler_params=pltpu.CompilerParams(vmem_limit_bytes=KERNEL_VMEM),
         cost_estimate=pl.CostEstimate(
             flops=4 * tokens * features, bytes_accessed=4 * tokens * features, transcendentals=tokens
         ),
@@ -102,8 +102,8 @@
             out_specs=pl.BlockSpec((SOURCES, rows, width), lambda i, place: (i, 0, 0)),
             scratch_shapes=[pltpu.VMEM((features, width), jnp.bfloat16)],
         ),
-        out_shape=jax.ShapeDtypeStruct((peers, rows, width), jnp.bfloat16),
-        compiler_params=pltpu.CompilerParams(vmem_limit_bytes=PROJECT_VMEM),
+        out_shape=pltpu.HBM((peers, rows, width), jnp.bfloat16),
+        compiler_params=pltpu.CompilerParams(vmem_limit_bytes=KERNEL_VMEM),
         cost_estimate=pl.CostEstimate(
             flops=2 * peers * rows * features * width,
             bytes_accessed=2 * (peers * rows * (features + width) + features * width),
@@ -121,12 +121,11 @@
     hidden_in, norm_gain, key_weight, fragment_index, outer_params, outer_moment, inner_params
 ):
     replicas = 4
-    block = key_weight[0]
+    packed, scale = pack(hidden_in[0], norm_gain[None])
+    packed, block = lax.optimization_barrier((packed, key_weight[0]))
+    tokens = lax.all_to_all(packed, PLANE, 0, 0, tiled=True)
     below, above = moved(block, lambda z: z + 4), moved(block, lambda z: z - 4)
-    packed, scale = pack(hidden_in[0], norm_gain[None])
-    packed, below, above, later = lax.optimization_barrier((packed, below, above, block))
-    tokens = lax.all_to_all(packed, PLANE, 0, 0, tiled=True)
-    across = moved(later, lambda z: z + 8)
+    across = moved(block, lambda z: z + 8)
     own = jnp.concatenate([block, below, above, across], axis=0)
     held = (
         own,
@@ -143,8 +142,10 @@
     moment_layer = lax.dynamic_index_in_dim(outer_moment, layer_idx, 0, keepdims=False)
     inner_layer = lax.dynamic_index_in_dim(inner_params[0], layer_idx, 0, keepdims=False)
     pseudo_grad = (outer_layer - inner_layer.astype(jnp.float32)).astype(jnp.bfloat16)
-    every = lax.all_gather(pseudo_grad, REP, axis=0, tiled=False)
-    summed = jnp.sum(every.astype(jnp.float32), axis=0)
+    summed = pseudo_grad.astype(jnp.float32)
+    for other in range(1, replicas):
+        pairs = [(replica, replica ^ other) for replica in range(replicas)]
+        summed += lax.ppermute(pseudo_grad, REP, pairs).astype(jnp.float32)
     new_outer, new_moment = outer_update(summed / replicas, outer_layer, moment_layer)
     mixed_inner = (
         mix_keep * inner_layer.astype(jnp.float32) + (1.0 - mix_keep) * new_outer

time: 116 us -> 99.9 us (0.86)
  the two profiles are of different devices: /device:TPU:17 before, /device:TPU:1 now
where the time goes in v5:
time: 99.9 us; the launch traced here: 99 us
  starting transfers between devices  61.8 us (62%)
  waiting for transfers between devices  21.2 us (21%)
  Pallas kernels  7.3 us (7%)
  other arithmetic  3.8 us (4%)
  local copies, waits for them, and re-layouts  3.51 us (4%)
  between operations  1.41 us (1%)
    ppermute x6, starting transfers between devices, moved(): lax.ppermute(block, Z, [(z, target(z) % PLANES) for z in range(PLANES)])  37.6 us
    ppermute x6, waiting for transfers between devices, moved(): lax.ppermute(block, Z, [(z, target(z) % PLANES) for z in range(PLANES)])  11.1 us
    ppermute x3, waiting for transfers between devices, shards(): summed += lax.ppermute(pseudo_grad, REP, pairs).astype(jnp.float32)  10.1 us
    ppermute x3, starting transfers between devices, shards(): summed += lax.ppermute(pseudo_grad, REP, pairs).astype(jnp.float32)  9.97 us
    all_to_all x1, starting transfers between devices, shards(): tokens = lax.all_to_all(packed, PLANE, 0, 0, tiled=True)  7.48 us
    all_to_all x1, starting transfers between devices, shards(): partial = lax.all_to_all(partial, PLANE, 0, 0, tiled=True)  6.8 us
    pallas_call x1, Pallas kernels, project(): pl.pallas_call(project_kernel, grid_spec=pltpu.PrefetchScalarGridSpec(num...  4.12 us
    unnamed x7, local copies, waits for them, and re-layouts  3.51 us
  transfers between devices with their start and end apart: 11, of which 5 were waited for; matrix products, arithmetic and copies ran while one was open for 4% of the time, Pallas kernels for 0%

profile of v5, /device:TPU:1, one launch (start us, length us, event | category | flops | bytes accessed | tf_op | source)
XLA Modules:
  0.0 99.0 jit_solution(11146467427764355991)
XLA Ops:
  0.6 0.0 copy-start
  0.6 1.9 %copy-done = bf16[1,192,8192]{2,1,0:T(8,128)(2,1)S(1)} copy-done((bf16[1,192,8192]{2,1,0:T(8,128)(2,1)S(1)}, bf16[1,192,8192]{2,1,0:T(8,128)(2,1)}, u32[]{:S(2)}) %copy-start) | copy-done | bytes 3145752
  2.5 0.0 copy-start.1
  2.5 0.8 copy-done.1
  3.3 3.2 %pack_hidden.1 = (bf16[8,192,1024]{2,1,0:T(8,128)(2,1)}, f32[192,1]{1,0:T(8,128)S(1)}) custom-call(bf16[192,8192]{1,0:T(8,128)(2,1)S(1)} %bitcast.25, f32[1,8192]{1,0:T(1,128)S(1)} %bitcast.26), custom_call_target="tpu_custom_call" | custom-call | flops 6291456 | bytes 6291456 | tf_op jit(solution)/shard_map/pack_hidden/pallas_call | solution.py:46
  6.5 7.5 %all-to-all-start = ((bf16[8,192,1024]{2,1,0:T(8,128)(2,1)}), bf16[8,192,1024]{2,1,0:T(8,128)(2,1)S(1)}, u32[]{:S(2)}, u32[]{:S(2)}) async-start(bf16[8,192,1024]{2,1,0:T(8,128)(2,1)} %get-tuple-element.11), calls=%async_computation | async-start | bytes 6291456 | tf_op jit(solution)/shard_map/all_to_all | solution.py:126
  13.9 8.8 %collective-permute-start = (bf16[64,512]{1,0:T(8,128)(2,1)}, bf16[64,512]{1,0:T(8,128)(2,1)S(1)}, u32[]{:S(2)}, u32[]{:S(2)}) collective-permute-start(bf16[64,512]{1,0:T(8,128)(2,1)} %bitcast.3), channel_id=1, source_target_pairs={{0,32},{8,40},{16,48},{24,56},{32,64},{40,72},{48,80},{56,88},{64,... | collective-permute-start | bytes 196616 | tf_op jit(solution)/shard_map/ppermute | solution.py:117
  22.8 5.6 %collective-permute-start.1 = (bf16[64,512]{1,0:T(8,128)(2,1)}, bf16[64,512]{1,0:T(8,128)(2,1)S(1)}, u32[]{:S(2)}, u32[]{:S(2)}) collective-permute-start(bf16[64,512]{1,0:T(8,128)(2,1)} %bitcast.3), channel_id=1, source_target_pairs={{0,96},{8,104},{16,112},{24,120},{32,0},{40,8},{48,16},{56,24},{64... | collective-permute-start | bytes 196616 | tf_op jit(solution)/shard_map/ppermute | solution.py:117
  28.3 10.3 %collective-permute-start.2 = (bf16[64,512]{1,0:T(8,128)(2,1)}, bf16[64,512]{1,0:T(8,128)(2,1)S(1)}, u32[]{:S(2)}, u32[]{:S(2)}) collective-permute-start(bf16[64,512]{1,0:T(8,128)(2,1)} %bitcast.3), channel_id=1, source_target_pairs={{0,64},{8,72},{16,80},{24,88},{32,96},{40,104},{48,112},{56,120},{... | collective-permute-start | bytes 196616 | tf_op jit(solution)/shard_map/ppermute | solution.py:117
  38.6 0.9 constant_dynamic-update-slice_fusion.3
  39.5 0.0 collective-permute-done
  39.5 0.0 collective-permute-done.1
  39.5 2.9 %collective-permute-done.2 = bf16[64,512]{1,0:T(8,128)(2,1)S(1)} collective-permute-done((bf16[64,512]{1,0:T(8,128)(2,1)}, bf16[64,512]{1,0:T(8,128)(2,1)S(1)}, u32[]{:S(2)}, u32[]{:S(2)}) %collective-permute-start.2) | collective-permute-done | bytes 65568 | tf_op jit(solution)/shard_map/ppermute | solution.py:117
  42.4 4.2 %collective-permute-start.3 = (bf16[256,512]{1,0:T(8,128)(2,1)S(1)}, bf16[256,512]{1,0:T(8,128)(2,1)}, u32[]{:S(2)}, u32[]{:S(2)}) collective-permute-start(bf16[256,512]{1,0:T(8,128)(2,1)S(1)} %constant_dynamic-update-slice_fusion.refs_0_), channel_id=1, source_target_pairs={{0,8},{8,16},{16,24},{24,32},{32,40},{40,48},{48,56},{56,64},{64,7... | collective-permute-start | bytes 786440 | tf_op jit(solution)/shard_map/ppermute | solution.py:117
  46.6 6.8 %collective-permute-start.4 = (bf16[256,512]{1,0:T(8,128)(2,1)S(1)}, bf16[256,512]{1,0:T(8,128)(2,1)}, u32[]{:S(2)}, u32[]{:S(2)}) collective-permute-start(bf16[256,512]{1,0:T(8,128)(2,1)S(1)} %constant_dynamic-update-slice_fusion.refs_0_), channel_id=1, source_target_pairs={{0,120},{8,0},{16,8},{24,16},{32,24},{40,32},{48,40},{56,48},{64,5... | collective-permute-start | bytes 786440 | tf_op jit(solution)/shard_map/ppermute | solution.py:117
  53.4 1.9 %collective-permute-start.5 = (bf16[256,512]{1,0:T(8,128)(2,1)S(1)}, bf16[256,512]{1,0:T(8,128)(2,1)}, u32[]{:S(2)}, u32[]{:S(2)}) collective-permute-start(bf16[256,512]{1,0:T(8,128)(2,1)S(1)} %constant_dynamic-update-slice_fusion.refs_0_), channel_id=1, source_target_pairs={{0,16},{8,120},{16,32},{24,8},{32,48},{40,24},{48,64},{56,40},{64,... | collective-permute-start | bytes 786440 | tf_op jit(solution)/shard_map/ppermute | solution.py:117
  55.4 1.3 %collective-permute-done.3.refs_1_ = bf16[256,512]{1,0:T(8,128)(2,1)} collective-permute-done((bf16[256,512]{1,0:T(8,128)(2,1)S(1)}, bf16[256,512]{1,0:T(8,128)(2,1)}, u32[]{:S(2)}, u32[]{:S(2)}) %collective-permute-start.3) | collective-permute-done | bytes 262176 | tf_op jit(solution)/shard_map/ppermute | solution.py:117
  56.7 0.8 collective-permute-done.4.refs_2_
  57.5 6.1 %collective-permute-done.5.refs_3_ = bf16[256,512]{1,0:T(8,128)(2,1)} collective-permute-done((bf16[256,512]{1,0:T(8,128)(2,1)S(1)}, bf16[256,512]{1,0:T(8,128)(2,1)}, u32[]{:S(2)}, u32[]{:S(2)}) %collective-permute-start.5) | collective-permute-done | bytes 262176 | tf_op jit(solution)/shard_map/ppermute | solution.py:117
  63.5 0.0 all-to-all-done.tokens_ref
  63.5 4.1 %project_keys.1 = bf16[8,192,512]{2,1,0:T(8,128)(2,1)} custom-call(s32[1]{0:T(128)} %bitcast.place_ref, bf16[8,192,1024]{2,1,0:T(8,128)(2,1)S(1)} %all-to-all-done.tokens_ref, bf16[256,512]{1,0:T(8,128)(2,1)S(1)} %constant_dynamic-update-slice_fusion.refs_0_, bf16[256,512]{1,0:T(8,128)(2,1)} %collective-permute-done.3.refs_1_, ...), custom_call_target="tpu_custom_call" | custom-call | flops 1610612736 | bytes 5767168 | tf_op jit(solution)/shard_map/project_keys/pallas_call | solution.py:96
  67.7 6.8 %all-to-all-start.1 = ((bf16[8,192,512]{2,1,0:T(8,128)(2,1)}), bf16[8,192,512]{2,1,0:T(8,128)(2,1)S(1)}, u32[]{:S(2)}, u32[]{:S(2)}) async-start(bf16[8,192,512]{2,1,0:T(8,128)(2,1)} %project_keys.1), calls=%async_computation.1 | async-start | bytes 3145728 | tf_op jit(solution)/shard_map/all_to_all | solution.py:139
  75.1 0.9 fusion.1
  76.1 5.1 %collective-permute-start.8 = (bf16[64,512]{1,0:T(8,128)(2,1)S(1)}, bf16[64,512]{1,0:T(8,128)(2,1)S(1)}, u32[]{:S(2)}, u32[]{:S(2)}) collective-permute-start(bf16[64,512]{1,0:T(8,128)(2,1)S(1)} %fusion.1), channel_id=1, source_target_pairs={{0,384},{128,256},{256,128},{384,0},{1,385},{129,257},{257,129},{3... | collective-permute-start | bytes 196616 | tf_op jit(solution)/shard_map/ppermute | solution.py:148
  81.1 3.0 %collective-permute-start.7 = (bf16[64,512]{1,0:T(8,128)(2,1)S(1)}, bf16[64,512]{1,0:T(8,128)(2,1)S(1)}, u32[]{:S(2)}, u32[]{:S(2)}) collective-permute-start(bf16[64,512]{1,0:T(8,128)(2,1)S(1)} %fusion.1), channel_id=1, source_target_pairs={{0,256},{128,384},{256,0},{384,128},{1,257},{129,385},{257,1},{385... | collective-permute-start | bytes 196616 | tf_op jit(solution)/shard_map/ppermute | solution.py:148
  84.1 1.9 %collective-permute-start.6 = (bf16[64,512]{1,0:T(8,128)(2,1)S(1)}, bf16[64,512]{1,0:T(8,128)(2,1)S(1)}, u32[]{:S(2)}, u32[]{:S(2)}) collective-permute-start(bf16[64,512]{1,0:T(8,128)(2,1)S(1)} %fusion.1), channel_id=1, source_target_pairs={{0,128},{128,0},{256,384},{384,256},{1,129},{129,1},{257,385},{385... | collective-permute-start | bytes 196616 | tf_op jit(solution)/shard_map/ppermute | solution.py:148
  86.1 0.1 reduce
  86.2 10.1 %collective-permute-done.8 = bf16[64,512]{1,0:T(8,128)(2,1)S(1)} collective-permute-done((bf16[64,512]{1,0:T(8,128)(2,1)S(1)}, bf16[64,512]{1,0:T(8,128)(2,1)S(1)}, u32[]{:S(2)}, u32[]{:S(2)}) %collective-permute-start.8) | collective-permute-done | bytes 65568 | tf_op jit(solution)/shard_map/ppermute | solution.py:148
  96.2 0.0 collective-permute-done.7
  96.2 0.0 collective-permute-done.6
  96.2 1.8 %fusion.4 = (bf16[1,64,512]{2,1,0:T(8,128)(2,1)}, f32[64,512]{1,0:T(8,128)}, f32[64,512]{1,0:T(8,128)}) fusion(bf16[1,7,64,512]{3,2,1,0:T(8,128)(2,1)} %param.13, s32[]{:T(128)S(6)} %select_n.7, bf16[64,512]{1,0:T(8,128)(2,1)S(1)} %collective-permute-done.8, bf16[64,512]{1,0:T(8,128)(2,1)S(1)} %collective-permute-done.7, ...), kind=kLoop, calls=%fused_computation.11 | loop fusion | flops 589824 | bytes 917508 | tf_op jit(solution)/shard_map/broadcast_in_dim | solution.py:154
  98.0 0.0 all-to-all-done.1
  98.0 0.2 convert_reduce_fusion
  98.2 0.8 fusion
  (3 shorter events, 0.0 us)
Async XLA Ops:
  0.6 1.9 %copy-start = (bf16[1,192,8192]{2,1,0:T(8,128)(2,1)S(1)}, bf16[1,192,8192]{2,1,0:T(8,128)(2,1)}, u32[]{:S(2)}) copy-start(bf16[1,192,8192]{2,1,0:T(8,128)(2,1)} %param.7) | copy-start | bytes 9437188
  2.5 0.8 copy-start.1
  6.5 57.1 %all-to-all-start = ((bf16[8,192,1024]{2,1,0:T(8,128)(2,1)}), bf16[8,192,1024]{2,1,0:T(8,128)(2,1)S(1)}, u32[]{:S(2)}, u32[]{:S(2)}) async-start(bf16[8,192,1024]{2,1,0:T(8,128)(2,1)} %get-tuple-element.11), calls=%async_computation | async-start | bytes 6291456 | tf_op jit(solution)/shard_map/all_to_all | solution.py:126
  13.9 25.5 %collective-permute-start = (bf16[64,512]{1,0:T(8,128)(2,1)}, bf16[64,512]{1,0:T(8,128)(2,1)S(1)}, u32[]{:S(2)}, u32[]{:S(2)}) collective-permute-start(bf16[64,512]{1,0:T(8,128)(2,1)} %bitcast.3), channel_id=1, source_target_pairs={{0,32},{8,40},{16,48},{24,56},{32,64},{40,72},{48,80},{56,88},{64,... | collective-permute-start | bytes 196616 | tf_op jit(solution)/shard_map/ppermute | solution.py:117
  22.8 16.7 %collective-permute-start.1 = (bf16[64,512]{1,0:T(8,128)(2,1)}, bf16[64,512]{1,0:T(8,128)(2,1)S(1)}, u32[]{:S(2)}, u32[]{:S(2)}) collective-permute-start(bf16[64,512]{1,0:T(8,128)(2,1)} %bitcast.3), channel_id=1, source_target_pairs={{0,96},{8,104},{16,112},{24,120},{32,0},{40,8},{48,16},{56,24},{64... | collective-permute-start | bytes 196616 | tf_op jit(solution)/shard_map/ppermute | solution.py:117
  28.3 14.0 %collective-permute-start.2 = (bf16[64,512]{1,0:T(8,128)(2,1)}, bf16[64,512]{1,0:T(8,128)(2,1)S(1)}, u32[]{:S(2)}, u32[]{:S(2)}) collective-permute-start(bf16[64,512]{1,0:T(8,128)(2,1)} %bitcast.3), channel_id=1, source_target_pairs={{0,64},{8,72},{16,80},{24,88},{32,96},{40,104},{48,112},{56,120},{... | collective-permute-start | bytes 196616 | tf_op jit(solution)/shard_map/ppermute | solution.py:117
  42.4 14.3 %collective-permute-start.3 = (bf16[256,512]{1,0:T(8,128)(2,1)S(1)}, bf16[256,512]{1,0:T(8,128)(2,1)}, u32[]{:S(2)}, u32[]{:S(2)}) collective-permute-start(bf16[256,512]{1,0:T(8,128)(2,1)S(1)} %constant_dynamic-update-slice_fusion.refs_0_), channel_id=1, source_target_pairs={{0,8},{8,16},{16,24},{24,32},{32,40},{40,48},{48,56},{56,64},{64,7... | collective-permute-start | bytes 786440 | tf_op jit(solution)/shard_map/ppermute | solution.py:117
  46.6 10.9 %collective-permute-start.4 = (bf16[256,512]{1,0:T(8,128)(2,1)S(1)}, bf16[256,512]{1,0:T(8,128)(2,1)}, u32[]{:S(2)}, u32[]{:S(2)}) collective-permute-start(bf16[256,512]{1,0:T(8,128)(2,1)S(1)} %constant_dynamic-update-slice_fusion.refs_0_), channel_id=1, source_target_pairs={{0,120},{8,0},{16,8},{24,16},{32,24},{40,32},{48,40},{56,48},{64,5... | collective-permute-start | bytes 786440 | tf_op jit(solution)/shard_map/ppermute | solution.py:117
  53.4 10.1 %collective-permute-start.5 = (bf16[256,512]{1,0:T(8,128)(2,1)S(1)}, bf16[256,512]{1,0:T(8,128)(2,1)}, u32[]{:S(2)}, u32[]{:S(2)}) collective-permute-start(bf16[256,512]{1,0:T(8,128)(2,1)S(1)} %constant_dynamic-update-slice_fusion.refs_0_), channel_id=1, source_target_pairs={{0,16},{8,120},{16,32},{24,8},{32,48},{40,24},{48,64},{56,40},{64,... | collective-permute-start | bytes 786440 | tf_op jit(solution)/shard_map/ppermute | solution.py:117
  67.7 30.4 %all-to-all-start.1 = ((bf16[8,192,512]{2,1,0:T(8,128)(2,1)}), bf16[8,192,512]{2,1,0:T(8,128)(2,1)S(1)}, u32[]{:S(2)}, u32[]{:S(2)}) async-start(bf16[8,192,512]{2,1,0:T(8,128)(2,1)} %project_keys.1), calls=%async_computation.1 | async-start | bytes 3145728 | tf_op jit(solution)/shard_map/all_to_all | solution.py:139
  76.1 20.2 %collective-permute-start.8 = (bf16[64,512]{1,0:T(8,128)(2,1)S(1)}, bf16[64,512]{1,0:T(8,128)(2,1)S(1)}, u32[]{:S(2)}, u32[]{:S(2)}) collective-permute-start(bf16[64,512]{1,0:T(8,128)(2,1)S(1)} %fusion.1), channel_id=1, source_target_pairs={{0,384},{128,256},{256,128},{384,0},{1,385},{129,257},{257,129},{3... | collective-permute-start | bytes 196616 | tf_op jit(solution)/shard_map/ppermute | solution.py:148
  81.1 15.1 %collective-permute-start.7 = (bf16[64,512]{1,0:T(8,128)(2,1)S(1)}, bf16[64,512]{1,0:T(8,128)(2,1)S(1)}, u32[]{:S(2)}, u32[]{:S(2)}) collective-permute-start(bf16[64,512]{1,0:T(8,128)(2,1)S(1)} %fusion.1), channel_id=1, source_target_pairs={{0,256},{128,384},{256,0},{384,128},{1,257},{129,385},{257,1},{385... | collective-permute-start | bytes 196616 | tf_op jit(solution)/shard_map/ppermute | solution.py:148
  84.1 12.1 %collective-permute-start.6 = (bf16[64,512]{1,0:T(8,128)(2,1)S(1)}, bf16[64,512]{1,0:T(8,128)(2,1)S(1)}, u32[]{:S(2)}, u32[]{:S(2)}) collective-permute-start(bf16[64,512]{1,0:T(8,128)(2,1)S(1)} %fusion.1), channel_id=1, source_target_pairs={{0,128},{128,0},{256,384},{384,256},{1,129},{129,1},{257,385},{385... | collective-permute-start | bytes 196616 | tf_op jit(solution)/shard_map/ppermute | solution.py:148

commit v6 on v5

--- a/solution.py
+++ b/solution.py
@@ -10,7 +10,7 @@
 mix_keep = 0.5
 epsilon = 1e-05
 
-Z, PLANE, REP = "z", ("yh", "x"), ("yl", "core")
+Z, PLANE, REP = ("zh", "zl"), ("yh", "x"), ("yl", "core")
 PLANES, PEERS = 16, 8
 ROWS, SOURCES = 64, 4
 KERNEL_VMEM = 24 * 1024 * 1024
@@ -66,40 +66,36 @@
     )(hidden, gain)
 
 
-NEAR = (0, -4, 4, 8)
-HELD = (0, -1, 1, None)
+HALF = PLANES // 2
 
 
-def project_kernel(place_ref, tokens_ref, *refs):
-    held_refs, (out_ref, weight) = refs[: len(HELD)], refs[len(HELD) :]
-
+def project_kernel(parity_ref, tokens_ref, own_ref, first_ref, second_ref, out_ref, weight):
     @pl.when(pl.program_id(0) == 0)
     def _():
-        here = place_ref[0]
-        for held_ref, offset in zip(held_refs, HELD, strict=True):
-            if offset is None:
-                offset = jnp.where(lax.rem(here, 2) == 0, -2, 2)
-            for at, further in enumerate(NEAR):
-                plane = lax.rem(here + offset + further + PLANES, PLANES)
-                rows = pl.ds(pl.multiple_of(plane * 64, 64), 64)
-                weight[rows, :] = held_ref[at * 64 : at * 64 + 64, :]
+        same = parity_ref[0]
+        for at in range(HALF):
+            other_ref, row = (first_ref, at) if at < HALF // 2 else (second_ref, at - HALF // 2)
+            mine = pl.ds(pl.multiple_of((2 * at + same) * 64, 64), 64)
+            weight[mine, :] = own_ref[at * 64 : at * 64 + 64, :]
+            others = pl.ds(pl.multiple_of((2 * at + 1 - same) * 64, 64), 64)
+            weight[others, :] = other_ref[row * 64 : row * 64 + 64, :]
 
     tokens = tokens_ref[...].reshape(-1, tokens_ref.shape[-1])
     product = jnp.dot(tokens, weight[...], preferred_element_type=jnp.float32)
     out_ref[...] = product.astype(jnp.bfloat16).reshape(out_ref.shape)
 
 
-def project(place, tokens, held):
+def project(parity, tokens, held):
     peers, rows, features = tokens.shape
     width = held[0].shape[1]
-    whole = [pl.BlockSpec(part.shape, lambda i, place: (0, 0)) for part in held]
+    whole = [pl.BlockSpec(part.shape, lambda i, parity: (0, 0)) for part in held]
     return pl.pallas_call(
         project_kernel,
         grid_spec=pltpu.PrefetchScalarGridSpec(
             num_scalar_prefetch=1,
             grid=(peers // SOURCES,),
-            in_specs=[pl.BlockSpec((SOURCES, rows, features), lambda i, place: (i, 0, 0)), *whole],
-            out_specs=pl.BlockSpec((SOURCES, rows, width), lambda i, place: (i, 0, 0)),
+            in_specs=[pl.BlockSpec((SOURCES, rows, features), lambda i, parity: (i, 0, 0)), *whole],
+            out_specs=pl.BlockSpec((SOURCES, rows, width), lambda i, parity: (i, 0, 0)),
             scratch_shapes=[pltpu.VMEM((features, width), jnp.bfloat16)],
         ),
         out_shape=pltpu.HBM((peers, rows, width), jnp.bfloat16),
@@ -110,7 +106,7 @@
             transcendentals=0,
         ),
         name="project_keys",
-    )(place, tokens, *held)
+    )(parity, tokens, *held)
 
 
 def moved(block, target):
@@ -124,17 +120,11 @@
     packed, scale = pack(hidden_in[0], norm_gain[None])
     packed, block = lax.optimization_barrier((packed, key_weight[0]))
     tokens = lax.all_to_all(packed, PLANE, 0, 0, tiled=True)
-    below, above = moved(block, lambda z: z + 4), moved(block, lambda z: z - 4)
-    across = moved(block, lambda z: z + 8)
-    own = jnp.concatenate([block, below, above, across], axis=0)
-    held = (
-        own,
-        moved(own, lambda z: z + 1),
-        moved(own, lambda z: z - 1),
-        moved(own, lambda z: z + 2 if z % 2 == 0 else z - 2),
-    )
-    place = lax.axis_index(Z).astype(jnp.int32)[None]
-    partial = project(place, tokens, held)
+    own = lax.all_gather(block, "zh", axis=0, tiled=True)
+    middle = own.shape[0] // 2
+    first, second = moved(own[:middle], lambda z: z + 1), moved(own[middle:], lambda z: z - 1)
+    parity = lax.axis_index("zl").astype(jnp.int32)[None]
+    partial = project(parity, tokens, (own, first, second))
     partial, fragment_index = lax.optimization_barrier((partial, fragment_index))
     partial = lax.all_to_all(partial, PLANE, 0, 0, tiled=True)
     layer_idx = fragment_index[0]
@@ -155,8 +145,8 @@
 
 
 def solution(mesh):
-    fine = Mesh(mesh.devices.reshape(2, 2, 16, 2, 4), ("yl", "core", "z", "yh", "x"))
-    fsdp = ("z", "yh", "x")
+    fine = Mesh(mesh.devices.reshape(2, 2, 8, 2, 2, 4), ("yl", "core", "zh", "zl", "yh", "x"))
+    fsdp = ("zh", "zl", "yh", "x")
     placed = (
         P(REP, fsdp, None),
         P(),

time: 99.9 us -> 96.8 us (0.969)
  blocking collectives: 0 us -> 32.9 us
  starting transfers between devices: 61.8 us -> 34.2 us
  waiting for transfers between devices: 21.2 us -> 11.4 us
  local copies, waits for them, and re-layouts: 3.51 us -> 5.33 us
    all_gather x0 -> x1, blocking collectives: none -> 32.9 us  [shards(): own = lax.all_gather(block, 'zh', axis=0, tiled=True)]
    ppermute x6 -> x2, starting transfers between devices: 37.6 us -> 6.48 us  [moved(): lax.ppermute(block, Z, [(z, target(z) % PLANES) for z in range(PLANES)])]
    ppermute x6 -> x2, waiting for transfers between devices: 11.1 us -> 4.47 us  [moved(): lax.ppermute(block, Z, [(z, target(z) % PLANES) for z in range(PLANES)])]
    ppermute x3, starting transfers between devices: 9.97 us -> 14.3 us  [shards(): summed += lax.ppermute(pseudo_grad, REP, pairs).astype(jnp.float32)]
    ppermute x3, waiting for transfers between devices: 10.1 us -> 6.92 us  [shards(): summed += lax.ppermute(pseudo_grad, REP, pairs).astype(jnp.float32)]
    unnamed x7 -> x10, local copies, waits for them, and re-layouts: 3.51 us -> 4.51 us
  transfers between devices with their start and end apart: 11 -> 7, of which waited for: 5 -> 4; matrix products, arithmetic and copies ran while one was open for 4% -> 4% of each run, Pallas kernels for 0% -> 0%
where the time goes in v6:
time: 96.8 us; the launch traced here: 96.1 us
  starting transfers between devices  34.2 us (35%)
  blocking collectives  32.9 us (34%)
  waiting for transfers between devices  11.4 us (12%)
  Pallas kernels  7.11 us (7%)
  local copies, waits for them, and re-layouts  5.33 us (6%)
  other arithmetic  3.79 us (4%)
  between operations  1.37 us (1%)
    all_gather x1, blocking collectives, shards(): own = lax.all_gather(block, 'zh', axis=0, tiled=True)  32.9 us
    ppermute x3, starting transfers between devices, shards(): summed += lax.ppermute(pseudo_grad, REP, pairs).astype(jnp.float32)  14.3 us
    all_to_all x1, starting transfers between devices, shards(): tokens = lax.all_to_all(packed, PLANE, 0, 0, tiled=True)  7.61 us
    ppermute x3, waiting for transfers between devices, shards(): summed += lax.ppermute(pseudo_grad, REP, pairs).astype(jnp.float32)  6.92 us
    ppermute x2, starting transfers between devices, moved(): lax.ppermute(block, Z, [(z, target(z) % PLANES) for z in range(PLANES)])  6.48 us
    all_to_all x1, starting transfers between devices, shards(): partial = lax.all_to_all(partial, PLANE, 0, 0, tiled=True)  5.81 us
    unnamed x10, local copies, waits for them, and re-layouts  4.51 us
    ppermute x2, waiting for transfers between devices, moved(): lax.ppermute(block, Z, [(z, target(z) % PLANES) for z in range(PLANES)])  4.47 us
  transfers between devices with their start and end apart: 7, of which 4 were waited for; matrix products, arithmetic and copies ran while one was open for 4% of the time, Pallas kernels for 0%

profile of v6, /device:TPU:1, one launch (start us, length us, event | category | flops | bytes accessed | tf_op | source)
XLA Modules:
  0.0 96.1 jit_solution(9101778177260909120)
XLA Ops:
  0.6 0.0 copy-start
  0.6 1.9 %copy-done = bf16[1,192,8192]{2,1,0:T(8,128)(2,1)S(1)} copy-done((bf16[1,192,8192]{2,1,0:T(8,128)(2,1)S(1)}, bf16[1,192,8192]{2,1,0:T(8,128)(2,1)}, u32[]{:S(2)}) %copy-start) | copy-done | bytes 3145752
  2.5 0.0 copy-start.3
  2.5 0.8 copy-done.3
  3.3 3.2 %pack_hidden.1 = (bf16[8,192,1024]{2,1,0:T(8,128)(2,1)}, f32[192,1]{1,0:T(8,128)S(1)}) custom-call(bf16[192,8192]{1,0:T(8,128)(2,1)S(1)} %bitcast.25, f32[1,8192]{1,0:T(1,128)S(1)} %bitcast.26), custom_call_target="tpu_custom_call" | custom-call | flops 6291456 | bytes 6291456 | tf_op jit(solution)/shard_map/pack_hidden/pallas_call | solution.py:46
  6.5 0.0 copy-start.4
  6.5 7.6 %all-to-all-start = ((bf16[8,192,1024]{2,1,0:T(8,128)(2,1)}), bf16[8,192,1024]{2,1,0:T(8,128)(2,1)S(1)}, u32[]{:S(2)}, u32[]{:S(2)}) async-start(bf16[8,192,1024]{2,1,0:T(8,128)(2,1)} %get-tuple-element.11), calls=%async_computation | async-start | bytes 6291456 | tf_op jit(solution)/shard_map/all_to_all | solution.py:122
  14.1 0.0 copy-done.4
  14.1 32.9 %all_gather.3.own_ref = bf16[512,512]{1,0:T(8,128)(2,1)S(1)} all-gather(bf16[64,512]{1,0:T(8,128)(2,1)S(1)} %bitcast.27), channel_id=1, replica_groups=mesh['yl'=2,'core'=2,'zh'=8,'zl'=2,'yh'=2,'x'=4] {'zh'}, dimensions={0}, use_global_device_ids=true | all-gather | bytes 589824 | tf_op jit(solution)/shard_map/all_gather | solution.py:123
  47.0 0.8 fusion.5
  47.8 0.0 copy-start.1
  47.8 0.8 copy-done.1
  48.6 3.5 %collective-permute-start = (bf16[256,512]{1,0:T(8,128)(2,1)}, bf16[256,512]{1,0:T(8,128)(2,1)S(1)}, u32[]{:S(2)}, u32[]{:S(2)}) collective-permute-start(bf16[256,512]{1,0:T(8,128)(2,1)} %get-tuple-element.20), channel_id=1, source_target_pairs={{0,8},{8,16},{16,24},{24,32},{32,40},{40,48},{48,56},{56,64},{64,7... | collective-permute-start | bytes 786440 | tf_op jit(solution)/shard_map/ppermute | solution.py:113
  52.2 3.0 %collective-permute-start.1 = (bf16[256,512]{1,0:T(8,128)(2,1)}, bf16[256,512]{1,0:T(8,128)(2,1)}, u32[]{:S(2)}, u32[]{:S(2)}) collective-permute-start(bf16[256,512]{1,0:T(8,128)(2,1)} %get-tuple-element.19), channel_id=1, source_target_pairs={{0,120},{8,0},{16,8},{24,16},{32,24},{40,32},{48,40},{56,48},{64,5... | collective-permute-start | bytes 786440 | tf_op jit(solution)/shard_map/ppermute | solution.py:113
  55.1 2.0 %collective-permute-done.first_ref = bf16[256,512]{1,0:T(8,128)(2,1)S(1)} collective-permute-done((bf16[256,512]{1,0:T(8,128)(2,1)}, bf16[256,512]{1,0:T(8,128)(2,1)S(1)}, u32[]{:S(2)}, u32[]{:S(2)}) %collective-permute-start) | collective-permute-done | bytes 262176 | tf_op jit(solution)/shard_map/ppermute | solution.py:113
  57.2 2.4 %collective-permute-done.1.second_ref = bf16[256,512]{1,0:T(8,128)(2,1)} collective-permute-done((bf16[256,512]{1,0:T(8,128)(2,1)}, bf16[256,512]{1,0:T(8,128)(2,1)}, u32[]{:S(2)}, u32[]{:S(2)}) %collective-permute-start.1) | collective-permute-done | bytes 262176 | tf_op jit(solution)/shard_map/ppermute | solution.py:113
  59.6 0.0 all-to-all-done.tokens_ref
  59.6 0.0 copy-start.2
  59.6 1.0 %copy-done.2 = bf16[512,512]{1,0:T(8,128)(2,1)S(1)} copy-done((bf16[512,512]{1,0:T(8,128)(2,1)S(1)}, bf16[512,512]{1,0:T(8,128)(2,1)}, u32[]{:S(2)}) %copy-start.2) | copy-done | bytes 524312
  60.7 3.9 %project_keys.1 = bf16[8,192,512]{2,1,0:T(8,128)(2,1)} custom-call(s32[1]{0:T(128)} %bitcast.parity_ref, bf16[8,192,1024]{2,1,0:T(8,128)(2,1)S(1)} %all-to-all-done.tokens_ref, bf16[512,512]{1,0:T(8,128)(2,1)S(1)} %copy-done.2, bf16[256,512]{1,0:T(8,128)(2,1)S(1)} %collective-permute-done.first_ref, bf16[256,512]{1,0:T(8,128)(2,1)} %collective-permute-done.1.second_ref), custom_call_target="tpu_custom_call" | custom-call | flops 1610612736 | bytes 5767168 | tf_op jit(solution)/shard_map/project_keys/pallas_call | solution.py:92
  64.6 5.8 %all-to-all-start.1 = ((bf16[8,192,512]{2,1,0:T(8,128)(2,1)}), bf16[8,192,512]{2,1,0:T(8,128)(2,1)S(1)}, u32[]{:S(2)}, u32[]{:S(2)}) async-start(bf16[8,192,512]{2,1,0:T(8,128)(2,1)} %project_keys.1), calls=%async_computation.1 | async-start | bytes 3145728 | tf_op jit(solution)/shard_map/all_to_all | solution.py:129
  71.0 0.9 fusion.1
  72.0 9.6 %collective-permute-start.4 = (bf16[64,512]{1,0:T(8,128)(2,1)S(1)}, bf16[64,512]{1,0:T(8,128)(2,1)S(1)}, u32[]{:S(2)}, u32[]{:S(2)}) collective-permute-start(bf16[64,512]{1,0:T(8,128)(2,1)S(1)} %fusion.1), channel_id=1, source_target_pairs={{0,384},{128,256},{256,128},{384,0},{1,385},{129,257},{257,129},{3... | collective-permute-start | bytes 196616 | tf_op jit(solution)/shard_map/ppermute | solution.py:138
  81.6 2.8 %collective-permute-start.3 = (bf16[64,512]{1,0:T(8,128)(2,1)S(1)}, bf16[64,512]{1,0:T(8,128)(2,1)S(1)}, u32[]{:S(2)}, u32[]{:S(2)}) collective-permute-start(bf16[64,512]{1,0:T(8,128)(2,1)S(1)} %fusion.1), channel_id=1, source_target_pairs={{0,256},{128,384},{256,0},{384,128},{1,257},{129,385},{257,1},{385... | collective-permute-start | bytes 196616 | tf_op jit(solution)/shard_map/ppermute | solution.py:138
  84.4 1.9 %collective-permute-start.2 = (bf16[64,512]{1,0:T(8,128)(2,1)S(1)}, bf16[64,512]{1,0:T(8,128)(2,1)S(1)}, u32[]{:S(2)}, u32[]{:S(2)}) collective-permute-start(bf16[64,512]{1,0:T(8,128)(2,1)S(1)} %fusion.1), channel_id=1, source_target_pairs={{0,128},{128,0},{256,384},{384,256},{1,129},{129,1},{257,385},{385... | collective-permute-start | bytes 196616 | tf_op jit(solution)/shard_map/ppermute | solution.py:138
  86.3 0.1 reduce
  86.4 5.6 %collective-permute-done.4 = bf16[64,512]{1,0:T(8,128)(2,1)S(1)} collective-permute-done((bf16[64,512]{1,0:T(8,128)(2,1)S(1)}, bf16[64,512]{1,0:T(8,128)(2,1)S(1)}, u32[]{:S(2)}, u32[]{:S(2)}) %collective-permute-start.4) | collective-permute-done | bytes 65568 | tf_op jit(solution)/shard_map/ppermute | solution.py:138
  92.0 1.3 %collective-permute-done.3 = bf16[64,512]{1,0:T(8,128)(2,1)S(1)} collective-permute-done((bf16[64,512]{1,0:T(8,128)(2,1)S(1)}, bf16[64,512]{1,0:T(8,128)(2,1)S(1)}, u32[]{:S(2)}, u32[]{:S(2)}) %collective-permute-start.3) | collective-permute-done | bytes 65568 | tf_op jit(solution)/shard_map/ppermute | solution.py:138
  93.3 0.0 collective-permute-done.2
  93.3 1.8 %fusion.4 = (bf16[1,64,512]{2,1,0:T(8,128)(2,1)}, f32[64,512]{1,0:T(8,128)}, f32[64,512]{1,0:T(8,128)}) fusion(bf16[1,7,64,512]{3,2,1,0:T(8,128)(2,1)} %param.13, s32[]{:T(128)S(6)} %select_n.7, bf16[64,512]{1,0:T(8,128)(2,1)S(1)} %collective-permute-done.4, bf16[64,512]{1,0:T(8,128)(2,1)S(1)} %collective-permute-done.3, ...), kind=kLoop, calls=%fused_computation.11 | loop fusion | flops 589824 | bytes 917508 | tf_op jit(solution)/shard_map/broadcast_in_dim | solution.py:144
  95.1 0.0 all-to-all-done.1
  95.1 0.2 convert_reduce_fusion
  95.3 0.8 fusion
Async XLA Ops:
  0.6 1.9 %copy-start = (bf16[1,192,8192]{2,1,0:T(8,128)(2,1)S(1)}, bf16[1,192,8192]{2,1,0:T(8,128)(2,1)}, u32[]{:S(2)}) copy-start(bf16[1,192,8192]{2,1,0:T(8,128)(2,1)} %param.7) | copy-start | bytes 9437188
  2.5 0.8 copy-start.3
  6.5 7.6 %copy-start.4 = (bf16[1,64,512]{2,1,0:T(8,128)(2,1)S(1)}, bf16[1,64,512]{2,1,0:T(8,128)(2,1)}, u32[]{:S(2)}) copy-start(bf16[1,64,512]{2,1,0:T(8,128)(2,1)} %param.9) | copy-start | bytes 196612
  6.5 53.1 %all-to-all-start = ((bf16[8,192,1024]{2,1,0:T(8,128)(2,1)}), bf16[8,192,1024]{2,1,0:T(8,128)(2,1)S(1)}, u32[]{:S(2)}, u32[]{:S(2)}) async-start(bf16[8,192,1024]{2,1,0:T(8,128)(2,1)} %get-tuple-element.11), calls=%async_computation | async-start | bytes 6291456 | tf_op jit(solution)/shard_map/all_to_all | solution.py:122
  47.8 0.8 copy-start.1
  48.6 8.5 %collective-permute-start = (bf16[256,512]{1,0:T(8,128)(2,1)}, bf16[256,512]{1,0:T(8,128)(2,1)S(1)}, u32[]{:S(2)}, u32[]{:S(2)}) collective-permute-start(bf16[256,512]{1,0:T(8,128)(2,1)} %get-tuple-element.20), channel_id=1, source_target_pairs={{0,8},{8,16},{16,24},{24,32},{32,40},{40,48},{48,56},{56,64},{64,7... | collective-permute-start | bytes 786440 | tf_op jit(solution)/shard_map/ppermute | solution.py:113
  52.2 7.4 %collective-permute-start.1 = (bf16[256,512]{1,0:T(8,128)(2,1)}, bf16[256,512]{1,0:T(8,128)(2,1)}, u32[]{:S(2)}, u32[]{:S(2)}) collective-permute-start(bf16[256,512]{1,0:T(8,128)(2,1)} %get-tuple-element.19), channel_id=1, source_target_pairs={{0,120},{8,0},{16,8},{24,16},{32,24},{40,32},{48,40},{56,48},{64,5... | collective-permute-start | bytes 786440 | tf_op jit(solution)/shard_map/ppermute | solution.py:113
  59.6 1.0 %copy-start.2 = (bf16[512,512]{1,0:T(8,128)(2,1)S(1)}, bf16[512,512]{1,0:T(8,128)(2,1)}, u32[]{:S(2)}) copy-start(bf16[512,512]{1,0:T(8,128)(2,1)} %copy-done.1) | copy-start | bytes 1572868
  64.6 30.5 %all-to-all-start.1 = ((bf16[8,192,512]{2,1,0:T(8,128)(2,1)}), bf16[8,192,512]{2,1,0:T(8,128)(2,1)S(1)}, u32[]{:S(2)}, u32[]{:S(2)}) async-start(bf16[8,192,512]{2,1,0:T(8,128)(2,1)} %project_keys.1), calls=%async_computation.1 | async-start | bytes 3145728 | tf_op jit(solution)/shard_map/all_to_all | solution.py:129
  72.0 20.1 %collective-permute-start.4 = (bf16[64,512]{1,0:T(8,128)(2,1)S(1)}, bf16[64,512]{1,0:T(8,128)(2,1)S(1)}, u32[]{:S(2)}, u32[]{:S(2)}) collective-permute-start(bf16[64,512]{1,0:T(8,128)(2,1)S(1)} %fusion.1), channel_id=1, source_target_pairs={{0,384},{128,256},{256,128},{384,0},{1,385},{129,257},{257,129},{3... | collective-permute-start | bytes 196616 | tf_op jit(solution)/shard_map/ppermute | solution.py:138
  81.6 11.8 %collective-permute-start.3 = (bf16[64,512]{1,0:T(8,128)(2,1)S(1)}, bf16[64,512]{1,0:T(8,128)(2,1)S(1)}, u32[]{:S(2)}, u32[]{:S(2)}) collective-permute-start(bf16[64,512]{1,0:T(8,128)(2,1)S(1)} %fusion.1), channel_id=1, source_target_pairs={{0,256},{128,384},{256,0},{384,128},{1,257},{129,385},{257,1},{385... | collective-permute-start | bytes 196616 | tf_op jit(solution)/shard_map/ppermute | solution.py:138
  84.4 9.0 %collective-permute-start.2 = (bf16[64,512]{1,0:T(8,128)(2,1)S(1)}, bf16[64,512]{1,0:T(8,128)(2,1)S(1)}, u32[]{:S(2)}, u32[]{:S(2)}) collective-permute-start(bf16[64,512]{1,0:T(8,128)(2,1)S(1)} %fusion.1), channel_id=1, source_target_pairs={{0,128},{128,0},{256,384},{384,256},{1,129},{129,1},{257,385},{385... | collective-permute-start | bytes 196616 | tf_op jit(solution)/shard_map/ppermute | solution.py:138

commit v7 on v5

--- a/solution.py
+++ b/solution.py
@@ -10,7 +10,7 @@
 mix_keep = 0.5
 epsilon = 1e-05
 
-Z, PLANE, REP = "z", ("yh", "x"), ("yl", "core")
+Z, PLANE, REP = ("zh", "zl"), ("yh", "x"), ("yl", "core")
 PLANES, PEERS = 16, 8
 ROWS, SOURCES = 64, 4
 KERNEL_VMEM = 24 * 1024 * 1024
@@ -66,22 +66,19 @@
     )(hidden, gain)
 
 
-NEAR = (0, -4, 4, 8)
-HELD = (0, -1, 1, None)
+STEPS = 4
+HELD = (0, -1, 1, 2)
 
 
-def project_kernel(place_ref, tokens_ref, *refs):
+def project_kernel(residue_ref, tokens_ref, *refs):
     held_refs, (out_ref, weight) = refs[: len(HELD)], refs[len(HELD) :]
 
     @pl.when(pl.program_id(0) == 0)
     def _():
-        here = place_ref[0]
-        for held_ref, offset in zip(held_refs, HELD, strict=True):
-            if offset is None:
-                offset = jnp.where(lax.rem(here, 2) == 0, -2, 2)
-            for at, further in enumerate(NEAR):
-                plane = lax.rem(here + offset + further + PLANES, PLANES)
-                rows = pl.ds(pl.multiple_of(plane * 64, 64), 64)
+        for held_ref, above in zip(held_refs, HELD, strict=True):
+            residue = lax.rem(residue_ref[0] + above + STEPS, STEPS)
+            for at in range(PLANES // STEPS):
+                rows = pl.ds(pl.multiple_of((at * STEPS + residue) * 64, 64), 64)
                 weight[rows, :] = held_ref[at * 64 : at * 64 + 64, :]
 
     tokens = tokens_ref[...].reshape(-1, tokens_ref.shape[-1])
@@ -89,17 +86,17 @@
     out_ref[...] = product.astype(jnp.bfloat16).reshape(out_ref.shape)
 
 
-def project(place, tokens, held):
+def project(residue, tokens, held):
     peers, rows, features = tokens.shape
     width = held[0].shape[1]
-    whole = [pl.BlockSpec(part.shape, lambda i, place: (0, 0)) for part in held]
+    whole = [pl.BlockSpec(part.shape, lambda i, residue: (0, 0)) for part in held]
     return pl.pallas_call(
         project_kernel,
         grid_spec=pltpu.PrefetchScalarGridSpec(
             num_scalar_prefetch=1,
             grid=(peers // SOURCES,),
-            in_specs=[pl.BlockSpec((SOURCES, rows, features), lambda i, place: (i, 0, 0)), *whole],
-            out_specs=pl.BlockSpec((SOURCES, rows, width), lambda i, place: (i, 0, 0)),
+            in_specs=[pl.BlockSpec((SOURCES, rows, features), lambda i, residue: (i, 0, 0)), *whole],
+            out_specs=pl.BlockSpec((SOURCES, rows, width), lambda i, residue: (i, 0, 0)),
             scratch_shapes=[pltpu.VMEM((features, width), jnp.bfloat16)],
         ),
         out_shape=pltpu.HBM((peers, rows, width), jnp.bfloat16),
@@ -110,7 +107,7 @@
             transcendentals=0,
         ),
         name="project_keys",
-    )(place, tokens, *held)
+    )(residue, tokens, *held)
 
 
 def moved(block, target):
@@ -124,17 +121,15 @@
     packed, scale = pack(hidden_in[0], norm_gain[None])
     packed, block = lax.optimization_barrier((packed, key_weight[0]))
     tokens = lax.all_to_all(packed, PLANE, 0, 0, tiled=True)
-    below, above = moved(block, lambda z: z + 4), moved(block, lambda z: z - 4)
-    across = moved(block, lambda z: z + 8)
-    own = jnp.concatenate([block, below, above, across], axis=0)
+    own = lax.all_gather(block, "zh", axis=0, tiled=True)
     held = (
         own,
         moved(own, lambda z: z + 1),
         moved(own, lambda z: z - 1),
         moved(own, lambda z: z + 2 if z % 2 == 0 else z - 2),
     )
-    place = lax.axis_index(Z).astype(jnp.int32)[None]
-    partial = project(place, tokens, held)
+    residue = lax.axis_index("zl").astype(jnp.int32)[None]
+    partial = project(residue, tokens, held)
     partial, fragment_index = lax.optimization_barrier((partial, fragment_index))
     partial = lax.all_to_all(partial, PLANE, 0, 0, tiled=True)
     layer_idx = fragment_index[0]
@@ -155,8 +150,8 @@
 
 
 def solution(mesh):
-    fine = Mesh(mesh.devices.reshape(2, 2, 16, 2, 4), ("yl", "core", "z", "yh", "x"))
-    fsdp = ("z", "yh", "x")
+    fine = Mesh(mesh.devices.reshape(2, 2, 4, 4, 2, 4), ("yl", "core", "zh", "zl", "yh", "x"))
+    fsdp = ("zh", "zl", "yh", "x")
     placed = (
         P(REP, fsdp, None),
         P(),

time: 99.9 us -> 93.4 us (0.935)
  the two profiles are of different devices: /device:TPU:1 before, /device:TPU:464 now
where the time goes in v7:
time: 93.4 us; the launch traced here: 92.8 us
  starting transfers between devices  40.7 us (44%)
  blocking collectives  18.6 us (20%)
  waiting for transfers between devices  18.4 us (20%)
  Pallas kernels  7.3 us (8%)
  other arithmetic  3.79 us (4%)
  local copies, waits for them, and re-layouts  2.64 us (3%)
  between operations  1.37 us (1%)
    all_gather x1, blocking collectives, shards(): own = lax.all_gather(block, 'zh', axis=0, tiled=True)  18.6 us
    all_to_all x1, starting transfers between devices, shards(): partial = lax.all_to_all(partial, PLANE, 0, 0, tiled=True)  14.9 us
    ppermute x3, waiting for transfers between devices, shards(): summed += lax.ppermute(pseudo_grad, REP, pairs).astype(jnp.float32)  11.3 us
    ppermute x3, starting transfers between devices, moved(): lax.ppermute(block, Z, [(z, target(z) % PLANES) for z in range(PLANES)])  10.9 us
    ppermute x3, starting transfers between devices, shards(): summed += lax.ppermute(pseudo_grad, REP, pairs).astype(jnp.float32)  7.59 us
    all_to_all x1, starting transfers between devices, shards(): tokens = lax.all_to_all(packed, PLANE, 0, 0, tiled=True)  7.26 us
    ppermute x3, waiting for transfers between devices, moved(): lax.ppermute(block, Z, [(z, target(z) % PLANES) for z in range(PLANES)])  4.88 us
    pallas_call x1, Pallas kernels, project(): pl.pallas_call(project_kernel, grid_spec=pltpu.PrefetchScalarGridSpec(num...  4.07 us
  transfers between devices with their start and end apart: 8, of which 5 were waited for; matrix products, arithmetic and copies ran while one was open for 3% of the time, Pallas kernels for 0%

profile of v7, /device:TPU:464, one launch (start us, length us, event | category | flops | bytes accessed | tf_op | source)
XLA Modules:
  0.0 92.8 jit_solution(7663720059532784410)
XLA Ops:
  0.6 0.0 copy-start
  0.6 1.9 %copy-done = bf16[1,192,8192]{2,1,0:T(8,128)(2,1)S(1)} copy-done((bf16[1,192,8192]{2,1,0:T(8,128)(2,1)S(1)}, bf16[1,192,8192]{2,1,0:T(8,128)(2,1)}, u32[]{:S(2)}) %copy-start) | copy-done | bytes 3145752
  2.5 0.0 copy-start.1
  2.5 0.8 copy-done.1
  3.3 3.2 %pack_hidden.1 = (bf16[8,192,1024]{2,1,0:T(8,128)(2,1)}, f32[192,1]{1,0:T(8,128)S(1)}) custom-call(bf16[192,8192]{1,0:T(8,128)(2,1)S(1)} %bitcast.25, f32[1,8192]{1,0:T(1,128)S(1)} %bitcast.26), custom_call_target="tpu_custom_call" | custom-call | flops 6291456 | bytes 6291456 | tf_op jit(solution)/shard_map/pack_hidden/pallas_call | solution.py:46
  6.5 7.3 %all-to-all-start = ((bf16[8,192,1024]{2,1,0:T(8,128)(2,1)}), bf16[8,192,1024]{2,1,0:T(8,128)(2,1)S(1)}, u32[]{:S(2)}, u32[]{:S(2)}) async-start(bf16[8,192,1024]{2,1,0:T(8,128)(2,1)} %get-tuple-element.11), calls=%async_computation | async-start | bytes 6291456 | tf_op jit(solution)/shard_map/all_to_all | solution.py:123
  13.8 18.6 %all_gather.3.refs_0_ = bf16[256,512]{1,0:T(8,128)(2,1)S(1)} all-gather(bf16[64,512]{1,0:T(8,128)(2,1)} %bitcast.27), channel_id=1, replica_groups=mesh['yl'=2,'core'=2,'zh'=4,'zl'=4,'yh'=2,'x'=4] {'zh'}, dimensions={0}, use_global_device_ids=true | all-gather | bytes 327680 | tf_op jit(solution)/shard_map/all_gather | solution.py:124
  32.4 3.9 %collective-permute-start = (bf16[256,512]{1,0:T(8,128)(2,1)S(1)}, bf16[256,512]{1,0:T(8,128)(2,1)}, u32[]{:S(2)}, u32[]{:S(2)}) collective-permute-start(bf16[256,512]{1,0:T(8,128)(2,1)S(1)} %all_gather.3.refs_0_), channel_id=1, source_target_pairs={{0,8},{8,16},{16,24},{24,32},{32,40},{40,48},{48,56},{56,64},{64,7... | collective-permute-start | bytes 786440 | tf_op jit(solution)/shard_map/ppermute | solution.py:114
  36.3 2.0 %collective-permute-start.1 = (bf16[256,512]{1,0:T(8,128)(2,1)S(1)}, bf16[256,512]{1,0:T(8,128)(2,1)}, u32[]{:S(2)}, u32[]{:S(2)}) collective-permute-start(bf16[256,512]{1,0:T(8,128)(2,1)S(1)} %all_gather.3.refs_0_), channel_id=1, source_target_pairs={{0,120},{8,0},{16,8},{24,16},{32,24},{40,32},{48,40},{56,48},{64,5... | collective-permute-start | bytes 786440 | tf_op jit(solution)/shard_map/ppermute | solution.py:114
  38.3 5.1 %collective-permute-start.2 = (bf16[256,512]{1,0:T(8,128)(2,1)S(1)}, bf16[256,512]{1,0:T(8,128)(2,1)}, u32[]{:S(2)}, u32[]{:S(2)}) collective-permute-start(bf16[256,512]{1,0:T(8,128)(2,1)S(1)} %all_gather.3.refs_0_), channel_id=1, source_target_pairs={{0,16},{8,120},{16,32},{24,8},{32,48},{40,24},{48,64},{56,40},{64,... | collective-permute-start | bytes 786440 | tf_op jit(solution)/shard_map/ppermute | solution.py:114
  43.4 0.0 collective-permute-done.refs_1_
  43.4 2.6 %collective-permute-done.1.refs_2_ = bf16[256,512]{1,0:T(8,128)(2,1)} collective-permute-done((bf16[256,512]{1,0:T(8,128)(2,1)S(1)}, bf16[256,512]{1,0:T(8,128)(2,1)}, u32[]{:S(2)}, u32[]{:S(2)}) %collective-permute-start.1) | collective-permute-done | bytes 262176 | tf_op jit(solution)/shard_map/ppermute | solution.py:114
  46.0 2.3 %collective-permute-done.2.refs_3_ = bf16[256,512]{1,0:T(8,128)(2,1)} collective-permute-done((bf16[256,512]{1,0:T(8,128)(2,1)S(1)}, bf16[256,512]{1,0:T(8,128)(2,1)}, u32[]{:S(2)}, u32[]{:S(2)}) %collective-permute-start.2) | collective-permute-done | bytes 262176 | tf_op jit(solution)/shard_map/ppermute | solution.py:114
  48.3 2.2 %all-to-all-done.tokens_ref = bf16[8,192,1024]{2,1,0:T(8,128)(2,1)S(1)} async-done(((bf16[8,192,1024]{2,1,0:T(8,128)(2,1)}), bf16[8,192,1024]{2,1,0:T(8,128)(2,1)S(1)}, u32[]{:S(2)}, u32[]{:S(2)}) %all-to-all-start) | async-done | bytes 3145760 | tf_op jit(solution)/shard_map/all_to_all | solution.py:123
  50.5 4.1 %project_keys.1 = bf16[8,192,512]{2,1,0:T(8,128)(2,1)} custom-call(s32[1]{0:T(128)} %bitcast.residue_ref, bf16[8,192,1024]{2,1,0:T(8,128)(2,1)S(1)} %all-to-all-done.tokens_ref, bf16[256,512]{1,0:T(8,128)(2,1)S(1)} %all_gather.3.refs_0_, bf16[256,512]{1,0:T(8,128)(2,1)} %collective-permute-done.refs_1_, bf16[256,512]{1,0:T(8,128)(2,1)} %collective-permute-done.1.refs_2_, ...), custom_call_target="tpu_custom_call" | custom-call | flops 1610612736 | bytes 5767168 | tf_op jit(solution)/shard_map/project_keys/pallas_call | solution.py:93
  54.6 14.9 %all-to-all-start.1 = ((bf16[8,192,512]{2,1,0:T(8,128)(2,1)}), bf16[8,192,512]{2,1,0:T(8,128)(2,1)S(1)}, u32[]{:S(2)}, u32[]{:S(2)}) async-start(bf16[8,192,512]{2,1,0:T(8,128)(2,1)} %project_keys.1), calls=%async_computation.1 | async-start | bytes 3145728 | tf_op jit(solution)/shard_map/all_to_all | solution.py:134
  70.1 0.9 fusion.1
  71.1 1.9 %collective-permute-start.5 = (bf16[64,512]{1,0:T(8,128)(2,1)S(1)}, bf16[64,512]{1,0:T(8,128)(2,1)S(1)}, u32[]{:S(2)}, u32[]{:S(2)}) collective-permute-start(bf16[64,512]{1,0:T(8,128)(2,1)S(1)} %fusion.1), channel_id=1, source_target_pairs={{0,384},{128,256},{256,128},{384,0},{1,385},{129,257},{257,129},{3... | collective-permute-start | bytes 196616 | tf_op jit(solution)/shard_map/ppermute | solution.py:143
  73.0 3.2 %collective-permute-start.4 = (bf16[64,512]{1,0:T(8,128)(2,1)S(1)}, bf16[64,512]{1,0:T(8,128)(2,1)S(1)}, u32[]{:S(2)}, u32[]{:S(2)}) collective-permute-start(bf16[64,512]{1,0:T(8,128)(2,1)S(1)} %fusion.1), channel_id=1, source_target_pairs={{0,256},{128,384},{256,0},{384,128},{1,257},{129,385},{257,1},{385... | collective-permute-start | bytes 196616 | tf_op jit(solution)/shard_map/ppermute | solution.py:143
  76.2 2.5 %collective-permute-start.3 = (bf16[64,512]{1,0:T(8,128)(2,1)S(1)}, bf16[64,512]{1,0:T(8,128)(2,1)S(1)}, u32[]{:S(2)}, u32[]{:S(2)}) collective-permute-start(bf16[64,512]{1,0:T(8,128)(2,1)S(1)} %fusion.1), channel_id=1, source_target_pairs={{0,128},{128,0},{256,384},{384,256},{1,129},{129,1},{257,385},{385... | collective-permute-start | bytes 196616 | tf_op jit(solution)/shard_map/ppermute | solution.py:143
  78.7 0.1 reduce
  78.8 8.9 %collective-permute-done.5 = bf16[64,512]{1,0:T(8,128)(2,1)S(1)} collective-permute-done((bf16[64,512]{1,0:T(8,128)(2,1)S(1)}, bf16[64,512]{1,0:T(8,128)(2,1)S(1)}, u32[]{:S(2)}, u32[]{:S(2)}) %collective-permute-start.5) | collective-permute-done | bytes 65568 | tf_op jit(solution)/shard_map/ppermute | solution.py:143
  87.6 2.4 %collective-permute-done.4 = bf16[64,512]{1,0:T(8,128)(2,1)S(1)} collective-permute-done((bf16[64,512]{1,0:T(8,128)(2,1)S(1)}, bf16[64,512]{1,0:T(8,128)(2,1)S(1)}, u32[]{:S(2)}, u32[]{:S(2)}) %collective-permute-start.4) | collective-permute-done | bytes 65568 | tf_op jit(solution)/shard_map/ppermute | solution.py:143
  90.1 0.0 collective-permute-done.3
  90.1 1.8 %fusion.4 = (bf16[1,64,512]{2,1,0:T(8,128)(2,1)}, f32[64,512]{1,0:T(8,128)}, f32[64,512]{1,0:T(8,128)}) fusion(bf16[1,7,64,512]{3,2,1,0:T(8,128)(2,1)} %param.13, s32[]{:T(128)S(6)} %select_n.7, bf16[64,512]{1,0:T(8,128)(2,1)S(1)} %collective-permute-done.5, bf16[64,512]{1,0:T(8,128)(2,1)S(1)} %collective-permute-done.4, ...), kind=kLoop, calls=%fused_computation.11 | loop fusion | flops 589824 | bytes 917508 | tf_op jit(solution)/shard_map/broadcast_in_dim | solution.py:149
  91.8 0.0 all-to-all-done.1
  91.8 0.2 convert_reduce_fusion
  92.1 0.8 fusion
Async XLA Ops:
  0.6 1.9 %copy-start = (bf16[1,192,8192]{2,1,0:T(8,128)(2,1)S(1)}, bf16[1,192,8192]{2,1,0:T(8,128)(2,1)}, u32[]{:S(2)}) copy-start(bf16[1,192,8192]{2,1,0:T(8,128)(2,1)} %param.7) | copy-start | bytes 9437188
  2.5 0.8 copy-start.1
  6.5 44.0 %all-to-all-start = ((bf16[8,192,1024]{2,1,0:T(8,128)(2,1)}), bf16[8,192,1024]{2,1,0:T(8,128)(2,1)S(1)}, u32[]{:S(2)}, u32[]{:S(2)}) async-start(bf16[8,192,1024]{2,1,0:T(8,128)(2,1)} %get-tuple-element.11), calls=%async_computation | async-start | bytes 6291456 | tf_op jit(solution)/shard_map/all_to_all | solution.py:123
  32.4 11.0 %collective-permute-start = (bf16[256,512]{1,0:T(8,128)(2,1)S(1)}, bf16[256,512]{1,0:T(8,128)(2,1)}, u32[]{:S(2)}, u32[]{:S(2)}) collective-permute-start(bf16[256,512]{1,0:T(8,128)(2,1)S(1)} %all_gather.3.refs_0_), channel_id=1, source_target_pairs={{0,8},{8,16},{16,24},{24,32},{32,40},{40,48},{48,56},{56,64},{64,7... | collective-permute-start | bytes 786440 | tf_op jit(solution)/shard_map/ppermute | solution.py:114
  36.3 9.7 %collective-permute-start.1 = (bf16[256,512]{1,0:T(8,128)(2,1)S(1)}, bf16[256,512]{1,0:T(8,128)(2,1)}, u32[]{:S(2)}, u32[]{:S(2)}) collective-permute-start(bf16[256,512]{1,0:T(8,128)(2,1)S(1)} %all_gather.3.refs_0_), channel_id=1, source_target_pairs={{0,120},{8,0},{16,8},{24,16},{32,24},{40,32},{48,40},{56,48},{64,5... | collective-permute-start | bytes 786440 | tf_op jit(solution)/shard_map/ppermute | solution.py:114
  38.3 10.0 %collective-permute-start.2 = (bf16[256,512]{1,0:T(8,128)(2,1)S(1)}, bf16[256,512]{1,0:T(8,128)(2,1)}, u32[]{:S(2)}, u32[]{:S(2)}) collective-permute-start(bf16[256,512]{1,0:T(8,128)(2,1)S(1)} %all_gather.3.refs_0_), channel_id=1, source_target_pairs={{0,16},{8,120},{16,32},{24,8},{32,48},{40,24},{48,64},{56,40},{64,... | collective-permute-start | bytes 786440 | tf_op jit(solution)/shard_map/ppermute | solution.py:114
  54.6 37.3 %all-to-all-start.1 = ((bf16[8,192,512]{2,1,0:T(8,128)(2,1)}), bf16[8,192,512]{2,1,0:T(8,128)(2,1)S(1)}, u32[]{:S(2)}, u32[]{:S(2)}) async-start(bf16[8,192,512]{2,1,0:T(8,128)(2,1)} %project_keys.1), calls=%async_computation.1 | async-start | bytes 3145728 | tf_op jit(solution)/shard_map/all_to_all | solution.py:134
  71.1 16.6 %collective-permute-start.5 = (bf16[64,512]{1,0:T(8,128)(2,1)S(1)}, bf16[64,512]{1,0:T(8,128)(2,1)S(1)}, u32[]{:S(2)}, u32[]{:S(2)}) collective-permute-start(bf16[64,512]{1,0:T(8,128)(2,1)S(1)} %fusion.1), channel_id=1, source_target_pairs={{0,384},{128,256},{256,128},{384,0},{1,385},{129,257},{257,129},{3... | collective-permute-start | bytes 196616 | tf_op jit(solution)/shard_map/ppermute | solution.py:143
  73.0 17.1 %collective-permute-start.4 = (bf16[64,512]{1,0:T(8,128)(2,1)S(1)}, bf16[64,512]{1,0:T(8,128)(2,1)S(1)}, u32[]{:S(2)}, u32[]{:S(2)}) collective-permute-start(bf16[64,512]{1,0:T(8,128)(2,1)S(1)} %fusion.1), channel_id=1, source_target_pairs={{0,256},{128,384},{256,0},{384,128},{1,257},{129,385},{257,1},{385... | collective-permute-start | bytes 196616 | tf_op jit(solution)/shard_map/ppermute | solution.py:143
  76.2 13.9 %collective-permute-start.3 = (bf16[64,512]{1,0:T(8,128)(2,1)S(1)}, bf16[64,512]{1,0:T(8,128)(2,1)S(1)}, u32[]{:S(2)}, u32[]{:S(2)}) collective-permute-start(bf16[64,512]{1,0:T(8,128)(2,1)S(1)} %fusion.1), channel_id=1, source_target_pairs={{0,128},{128,0},{256,384},{384,256},{1,129},{129,1},{257,385},{385... | collective-permute-start | bytes 196616 | tf_op jit(solution)/shard_map/ppermute | solution.py:143

commit v8 on v7

--- a/solution.py
+++ b/solution.py
@@ -118,29 +118,34 @@
     hidden_in, norm_gain, key_weight, fragment_index, outer_params, outer_moment, inner_params
 ):
     replicas = 4
+    layer_idx = fragment_index[0]
+    outer_layer = lax.dynamic_index_in_dim(outer_params, layer_idx, 0, keepdims=False)
+    inner_layer = lax.dynamic_index_in_dim(inner_params[0], layer_idx, 0, keepdims=False)
+    pseudo_grad = (outer_layer - inner_layer.astype(jnp.float32)).astype(jnp.bfloat16)
+
     packed, scale = pack(hidden_in[0], norm_gain[None])
     packed, block = lax.optimization_barrier((packed, key_weight[0]))
     tokens = lax.all_to_all(packed, PLANE, 0, 0, tiled=True)
     own = lax.all_gather(block, "zh", axis=0, tiled=True)
+    own, pseudo_grad = lax.optimization_barrier((own, pseudo_grad))
     held = (
         own,
         moved(own, lambda z: z + 1),
         moved(own, lambda z: z - 1),
         moved(own, lambda z: z + 2 if z % 2 == 0 else z - 2),
     )
+    others = []
+    for other in range(1, replicas):
+        pairs = [(replica, replica ^ other) for replica in range(replicas)]
+        others.append(lax.ppermute(pseudo_grad, REP, pairs))
     residue = lax.axis_index("zl").astype(jnp.int32)[None]
     partial = project(residue, tokens, held)
-    partial, fragment_index = lax.optimization_barrier((partial, fragment_index))
+    partial, layer_idx, others = lax.optimization_barrier((partial, layer_idx, others))
     partial = lax.all_to_all(partial, PLANE, 0, 0, tiled=True)
-    layer_idx = fragment_index[0]
     outer_layer = lax.dynamic_index_in_dim(outer_params, layer_idx, 0, keepdims=False)
     moment_layer = lax.dynamic_index_in_dim(outer_moment, layer_idx, 0, keepdims=False)
     inner_layer = lax.dynamic_index_in_dim(inner_params[0], layer_idx, 0, keepdims=False)
-    pseudo_grad = (outer_layer - inner_layer.astype(jnp.float32)).astype(jnp.bfloat16)
-    summed = pseudo_grad.astype(jnp.float32)
-    for other in range(1, replicas):
-        pairs = [(replica, replica ^ other) for replica in range(replicas)]
-        summed += lax.ppermute(pseudo_grad, REP, pairs).astype(jnp.float32)
+    summed = pseudo_grad.astype(jnp.float32) + sum(part.astype(jnp.float32) for part in others)
     new_outer, new_moment = outer_update(summed / replicas, outer_layer, moment_layer)
     mixed_inner = (
         mix_keep * inner_layer.astype(jnp.float32) + (1.0 - mix_keep) * new_outer

time: 93.4 us -> 96.3 us (1.031)
  the two profiles are of different devices: /device:TPU:464 before, /device:TPU:1 now
where the time goes in v8:
time: 96.3 us; the launch traced here: 95.7 us
  starting transfers between devices  33.9 us (35%)
  blocking collectives  24.9 us (26%)
  waiting for transfers between devices  21 us (22%)
  Pallas kernels  7.33 us (8%)
  other arithmetic  4.56 us (5%)
  local copies, waits for them, and re-layouts  2.64 us (3%)
  between operations  1.4 us (1%)
    all_gather x1, blocking collectives, shards(): own = lax.all_gather(block, 'zh', axis=0, tiled=True)  24.9 us
    all_to_all x1, waiting for transfers between devices, shards(): partial = lax.all_to_all(partial, PLANE, 0, 0, tiled=True)  21 us
    ppermute x3, starting transfers between devices, shards(): others.append(lax.ppermute(pseudo_grad, REP, pairs))  10.6 us
    ppermute x3, starting transfers between devices, moved(): lax.ppermute(block, Z, [(z, target(z) % PLANES) for z in range(PLANES)])  8.56 us
    all_to_all x1, starting transfers between devices, shards(): tokens = lax.all_to_all(packed, PLANE, 0, 0, tiled=True)  7.48 us
    all_to_all x1, starting transfers between devices, shards(): partial = lax.all_to_all(partial, PLANE, 0, 0, tiled=True)  7.24 us
    pallas_call x1, Pallas kernels, project(): pl.pallas_call(project_kernel, grid_spec=pltpu.PrefetchScalarGridSpec(num...  4.1 us
    pallas_call x1, Pallas kernels, pack(): pl.pallas_call(pack_kernel, grid=(tokens // ROWS,), in_specs=[pl.BlockSpe...  3.23 us
  transfers between devices with their start and end apart: 8, of which 1 were waited for; matrix products, arithmetic and copies ran while one was open for 4% of the time, Pallas kernels for 4%

profile of v8, /device:TPU:1, one launch (start us, length us, event | category | flops | bytes accessed | tf_op | source)
XLA Modules:
  0.0 95.7 jit_solution(12387222519229811688)
XLA Ops:
  0.6 0.0 copy-start
  0.6 1.9 %copy-done = bf16[1,192,8192]{2,1,0:T(8,128)(2,1)S(1)} copy-done((bf16[1,192,8192]{2,1,0:T(8,128)(2,1)S(1)}, bf16[1,192,8192]{2,1,0:T(8,128)(2,1)}, u32[]{:S(2)}) %copy-start) | copy-done | bytes 3145752
  2.5 0.0 copy-start.1
  2.5 0.8 copy-done.1
  3.3 3.2 %pack_hidden.1 = (bf16[8,192,1024]{2,1,0:T(8,128)(2,1)}, f32[192,1]{1,0:T(8,128)S(1)}) custom-call(bf16[192,8192]{1,0:T(8,128)(2,1)S(1)} %bitcast.31, f32[1,8192]{1,0:T(1,128)S(1)} %bitcast.32), custom_call_target="tpu_custom_call" | custom-call | flops 6291456 | bytes 6291456 | tf_op jit(solution)/shard_map/pack_hidden/pallas_call | solution.py:46
  6.5 7.5 %all-to-all-start = ((bf16[8,192,1024]{2,1,0:T(8,128)(2,1)}), bf16[8,192,1024]{2,1,0:T(8,128)(2,1)S(1)}, u32[]{:S(2)}, u32[]{:S(2)}) async-start(bf16[8,192,1024]{2,1,0:T(8,128)(2,1)} %get-tuple-element.16), calls=%async_computation | async-start | bytes 6291456 | tf_op jit(solution)/shard_map/all_to_all | solution.py:128
  14.6 24.9 %all_gather.3.refs_0_ = bf16[256,512]{1,0:T(8,128)(2,1)S(1)} all-gather(bf16[64,512]{1,0:T(8,128)(2,1)} %bitcast.33), channel_id=1, replica_groups=mesh['yl'=2,'core'=2,'zh'=4,'zl'=4,'yh'=2,'x'=4] {'zh'}, dimensions={0}, use_global_device_ids=true | all-gather | bytes 327680 | tf_op jit(solution)/shard_map/all_gather | solution.py:129
  39.6 1.6 %fusion.3 = bf16[64,512]{1,0:T(8,128)(2,1)} fusion(f32[7,64,512]{2,1,0:T(8,128)} %param.11, s32[]{:T(128)S(6)} %select_n.11, bf16[1,7,64,512]{3,2,1,0:T(8,128)(2,1)} %param.13), kind=kLoop, calls=%fused_computation.7 | loop fusion | flops 98304 | bytes 262148 | tf_op jit(solution)/shard_map/convert_element_type | solution.py:124
  41.1 3.3 %collective-permute-start.2 = (bf16[256,512]{1,0:T(8,128)(2,1)S(1)}, bf16[256,512]{1,0:T(8,128)(2,1)}, u32[]{:S(2)}, u32[]{:S(2)}) collective-permute-start(bf16[256,512]{1,0:T(8,128)(2,1)S(1)} %all_gather.3.refs_0_), channel_id=1, source_target_pairs={{0,16},{8,120},{16,32},{24,8},{32,48},{40,24},{48,64},{56,40},{64,... | collective-permute-start | bytes 786440 | tf_op jit(solution)/shard_map/ppermute | solution.py:114
  44.4 2.4 %collective-permute-start.1 = (bf16[256,512]{1,0:T(8,128)(2,1)S(1)}, bf16[256,512]{1,0:T(8,128)(2,1)}, u32[]{:S(2)}, u32[]{:S(2)}) collective-permute-start(bf16[256,512]{1,0:T(8,128)(2,1)S(1)} %all_gather.3.refs_0_), channel_id=1, source_target_pairs={{0,120},{8,0},{16,8},{24,16},{32,24},{40,32},{48,40},{56,48},{64,5... | collective-permute-start | bytes 786440 | tf_op jit(solution)/shard_map/ppermute | solution.py:114
  46.8 2.8 %collective-permute-start = (bf16[256,512]{1,0:T(8,128)(2,1)S(1)}, bf16[256,512]{1,0:T(8,128)(2,1)}, u32[]{:S(2)}, u32[]{:S(2)}) collective-permute-start(bf16[256,512]{1,0:T(8,128)(2,1)S(1)} %all_gather.3.refs_0_), channel_id=1, source_target_pairs={{0,8},{8,16},{16,24},{24,32},{32,40},{40,48},{48,56},{56,64},{64,7... | collective-permute-start | bytes 786440 | tf_op jit(solution)/shard_map/ppermute | solution.py:114
  49.7 5.7 %collective-permute-start.5 = (bf16[64,512]{1,0:T(8,128)(2,1)}, bf16[64,512]{1,0:T(8,128)(2,1)}, u32[]{:S(2)}, u32[]{:S(2)}) collective-permute-start(bf16[64,512]{1,0:T(8,128)(2,1)} %fusion.3), channel_id=1, source_target_pairs={{0,384},{128,256},{256,128},{384,0},{1,385},{129,257},{257,129},{3... | collective-permute-start | bytes 196616 | tf_op jit(solution)/shard_map/ppermute | solution.py:140
  55.4 3.0 %collective-permute-start.4 = (bf16[64,512]{1,0:T(8,128)(2,1)}, bf16[64,512]{1,0:T(8,128)(2,1)}, u32[]{:S(2)}, u32[]{:S(2)}) collective-permute-start(bf16[64,512]{1,0:T(8,128)(2,1)} %fusion.3), channel_id=1, source_target_pairs={{0,256},{128,384},{256,0},{384,128},{1,257},{129,385},{257,1},{385... | collective-permute-start | bytes 196616 | tf_op jit(solution)/shard_map/ppermute | solution.py:140
  58.4 0.0 collective-permute-done.2.refs_3_
  58.4 1.9 %collective-permute-start.3 = (bf16[64,512]{1,0:T(8,128)(2,1)}, bf16[64,512]{1,0:T(8,128)(2,1)}, u32[]{:S(2)}, u32[]{:S(2)}) collective-permute-start(bf16[64,512]{1,0:T(8,128)(2,1)} %fusion.3), channel_id=1, source_target_pairs={{0,128},{128,0},{256,384},{384,256},{1,129},{129,1},{257,385},{385... | collective-permute-start | bytes 196616 | tf_op jit(solution)/shard_map/ppermute | solution.py:140
  60.3 0.0 collective-permute-done.1.refs_2_
  60.4 0.0 collective-permute-done.refs_1_
  60.4 0.0 all-to-all-done.tokens_ref
  60.4 4.1 %project_keys.1 = bf16[8,192,512]{2,1,0:T(8,128)(2,1)} custom-call(s32[1]{0:T(128)} %bitcast.residue_ref, bf16[8,192,1024]{2,1,0:T(8,128)(2,1)S(1)} %all-to-all-done.tokens_ref, bf16[256,512]{1,0:T(8,128)(2,1)S(1)} %all_gather.3.refs_0_, bf16[256,512]{1,0:T(8,128)(2,1)} %collective-permute-done.refs_1_, bf16[256,512]{1,0:T(8,128)(2,1)} %collective-permute-done.1.refs_2_, ...), custom_call_target="tpu_custom_call" | custom-call | flops 1610612736 | bytes 5767168 | tf_op jit(solution)/shard_map/project_keys/pallas_call | solution.py:93
  64.5 0.0 collective-permute-done.5
  64.5 0.0 collective-permute-done.4
  64.5 0.0 collective-permute-done.3
  64.5 7.2 %all-to-all-start.1 = ((bf16[8,192,512]{2,1,0:T(8,128)(2,1)}), bf16[8,192,512]{2,1,0:T(8,128)(2,1)S(1)}, u32[]{:S(2)}, u32[]{:S(2)}) async-start(bf16[8,192,512]{2,1,0:T(8,128)(2,1)} %project_keys.1), calls=%async_computation.1 | async-start | bytes 3145728 | tf_op jit(solution)/shard_map/all_to_all | solution.py:144
  71.7 0.1 reduce
  71.8 1.9 %fusion.4 = (bf16[1,64,512]{2,1,0:T(8,128)(2,1)}, f32[64,512]{1,0:T(8,128)}, f32[64,512]{1,0:T(8,128)}) fusion(bf16[1,7,64,512]{3,2,1,0:T(8,128)(2,1)} %param.13, s32[]{:T(128)S(6)} %select_n.12, bf16[64,512]{1,0:T(8,128)(2,1)} %collective-permute-done.5, bf16[64,512]{1,0:T(8,128)(2,1)} %collective-permute-done.4, ...), kind=kLoop, calls=%fused_computation.11 | loop fusion | flops 589824 | bytes 917508 | tf_op jit(solution)/shard_map/broadcast_in_dim | solution.py:154
  73.8 21.0 %all-to-all-done.1 = bf16[8,192,512]{2,1,0:T(8,128)(2,1)S(1)} async-done(((bf16[8,192,512]{2,1,0:T(8,128)(2,1)}), bf16[8,192,512]{2,1,0:T(8,128)(2,1)S(1)}, u32[]{:S(2)}, u32[]{:S(2)}) %all-to-all-start.1) | async-done | bytes 1572896 | tf_op jit(solution)/shard_map/all_to_all | solution.py:144
  94.7 0.2 convert_reduce_fusion
  95.0 0.8 fusion
Async XLA Ops:
  0.6 1.9 %copy-start = (bf16[1,192,8192]{2,1,0:T(8,128)(2,1)S(1)}, bf16[1,192,8192]{2,1,0:T(8,128)(2,1)}, u32[]{:S(2)}) copy-start(bf16[1,192,8192]{2,1,0:T(8,128)(2,1)} %param.7) | copy-start | bytes 9437188
  2.5 0.8 copy-start.1
  6.5 53.9 %all-to-all-start = ((bf16[8,192,1024]{2,1,0:T(8,128)(2,1)}), bf16[8,192,1024]{2,1,0:T(8,128)(2,1)S(1)}, u32[]{:S(2)}, u32[]{:S(2)}) async-start(bf16[8,192,1024]{2,1,0:T(8,128)(2,1)} %get-tuple-element.16), calls=%async_computation | async-start | bytes 6291456 | tf_op jit(solution)/shard_map/all_to_all | solution.py:128
  41.1 17.3 %collective-permute-start.2 = (bf16[256,512]{1,0:T(8,128)(2,1)S(1)}, bf16[256,512]{1,0:T(8,128)(2,1)}, u32[]{:S(2)}, u32[]{:S(2)}) collective-permute-start(bf16[256,512]{1,0:T(8,128)(2,1)S(1)} %all_gather.3.refs_0_), channel_id=1, source_target_pairs={{0,16},{8,120},{16,32},{24,8},{32,48},{40,24},{48,64},{56,40},{64,... | collective-permute-start | bytes 786440 | tf_op jit(solution)/shard_map/ppermute | solution.py:114
  44.4 16.0 %collective-permute-start.1 = (bf16[256,512]{1,0:T(8,128)(2,1)S(1)}, bf16[256,512]{1,0:T(8,128)(2,1)}, u32[]{:S(2)}, u32[]{:S(2)}) collective-permute-start(bf16[256,512]{1,0:T(8,128)(2,1)S(1)} %all_gather.3.refs_0_), channel_id=1, source_target_pairs={{0,120},{8,0},{16,8},{24,16},{32,24},{40,32},{48,40},{56,48},{64,5... | collective-permute-start | bytes 786440 | tf_op jit(solution)/shard_map/ppermute | solution.py:114
  46.8 13.5 %collective-permute-start = (bf16[256,512]{1,0:T(8,128)(2,1)S(1)}, bf16[256,512]{1,0:T(8,128)(2,1)}, u32[]{:S(2)}, u32[]{:S(2)}) collective-permute-start(bf16[256,512]{1,0:T(8,128)(2,1)S(1)} %all_gather.3.refs_0_), channel_id=1, source_target_pairs={{0,8},{8,16},{16,24},{24,32},{32,40},{40,48},{48,56},{56,64},{64,7... | collective-permute-start | bytes 786440 | tf_op jit(solution)/shard_map/ppermute | solution.py:114
  49.7 14.8 %collective-permute-start.5 = (bf16[64,512]{1,0:T(8,128)(2,1)}, bf16[64,512]{1,0:T(8,128)(2,1)}, u32[]{:S(2)}, u32[]{:S(2)}) collective-permute-start(bf16[64,512]{1,0:T(8,128)(2,1)} %fusion.3), channel_id=1, source_target_pairs={{0,384},{128,256},{256,128},{384,0},{1,385},{129,257},{257,129},{3... | collective-permute-start | bytes 196616 | tf_op jit(solution)/shard_map/ppermute | solution.py:140
  55.4 9.1 %collective-permute-start.4 = (bf16[64,512]{1,0:T(8,128)(2,1)}, bf16[64,512]{1,0:T(8,128)(2,1)}, u32[]{:S(2)}, u32[]{:S(2)}) collective-permute-start(bf16[64,512]{1,0:T(8,128)(2,1)} %fusion.3), channel_id=1, source_target_pairs={{0,256},{128,384},{256,0},{384,128},{1,257},{129,385},{257,1},{385... | collective-permute-start | bytes 196616 | tf_op jit(solution)/shard_map/ppermute | solution.py:140
  58.4 6.1 %collective-permute-start.3 = (bf16[64,512]{1,0:T(8,128)(2,1)}, bf16[64,512]{1,0:T(8,128)(2,1)}, u32[]{:S(2)}, u32[]{:S(2)}) collective-permute-start(bf16[64,512]{1,0:T(8,128)(2,1)} %fusion.3), channel_id=1, source_target_pairs={{0,128},{128,0},{256,384},{384,256},{1,129},{129,1},{257,385},{385... | collective-permute-start | bytes 196616 | tf_op jit(solution)/shard_map/ppermute | solution.py:140
  64.5 30.2 %all-to-all-start.1 = ((bf16[8,192,512]{2,1,0:T(8,128)(2,1)}), bf16[8,192,512]{2,1,0:T(8,128)(2,1)S(1)}, u32[]{:S(2)}, u32[]{:S(2)}) async-start(bf16[8,192,512]{2,1,0:T(8,128)(2,1)} %project_keys.1), calls=%async_computation.1 | async-start | bytes 3145728 | tf_op jit(solution)/shard_map/all_to_all | solution.py:144

commit v9 on v8

v9 whole, which is shorter than its diff:
```python
import jax
import jax.numpy as jnp
from jax import lax
from jax.experimental import pallas as pl
from jax.experimental.pallas import tpu as pltpu
from jax.sharding import Mesh, PartitionSpec as P

momentum_coef = 0.9
outer_rate = 0.7
mix_keep = 0.5
epsilon = 1e-05

REP, LINE = ("yl", "core"), ("core", "zh", "zl", "yh", "x")
PLANES, SIDES, COLUMNS = 16, 2, 4
CLASSES, ROWS, SOURCES = 4, 64, 2
KERNEL_VMEM = 24 * 1024 * 1024


def place_of(core, z, yh, x):
    return ((core * PLANES + z % PLANES) * SIDES + yh) * COLUMNS + x


def class_of(core, z, x):
    along = x // 2 if core == 0 else int(x in (1, 2))
    return along + 2 * (z % 2)


def exchange_groups():
    groups = []
    for core in range(2):
        starts = range(core, PLANES, 2)
        pairs = ((0, 3), (1, 2)) if core == 0 else ((0, 1), (2, 3))
        for z in starts:
            for yh in range(SIDES):
                for pair in pairs:
                    members = [(core, at % PLANES, yh, x) for at in (z, z + 1) for x in pair]
                    members.sort(key=lambda m: class_of(m[0], m[1], m[3]))
                    groups.append([place_of(*m) for m in members])
    return groups


def flipped(block, across_x, across_y):
    pairs = []
    for core in range(2):
        for z in range(PLANES):
            for yh in range(SIDES):
                for x in range(COLUMNS):
                    other = x ^ (1 if core == 0 else 3) if across_x else x
                    pairs.append((place_of(core, z, yh, x), place_of(core, z, yh ^ across_y, other)))
    return lax.ppermute(block, LINE, pairs)


def outer_update(averaged, outer_layer, moment_layer):
    new_moment = momentum_coef * moment_layer + averaged
    new_outer = outer_layer - outer_rate * (averaged + momentum_coef * new_moment)
    return (new_outer, new_moment)


def pack_kernel(core_ref, hidden_ref, gain_ref, packed_ref, scale_ref):
    hidden = hidden_ref[...].astype(jnp.float32)
    features = hidden.shape[1]
    mean_square = jnp.sum(hidden * hidden, axis=-1, keepdims=True) / features
    scale_ref[...] = lax.rsqrt(mean_square + epsilon)
    gained = hidden * gain_ref[...]
    lane = lax.broadcasted_iota(jnp.int32, (hidden.shape[0], 128), 1)
    swapped = jnp.logical_and(lane >= 64, core_ref[0] == 1)
    for z in range(PLANES):
        for yh in range(SIDES):
            start = z * 512 + yh * 256
            first, second = gained[:, start : start + 128], gained[:, start + 128 : start + 256]
            place = ((z // 2) * SIDES + yh) * 128
            columns, parity = slice(place, place + 128), z % 2
            packed_ref[2 * parity, :, columns] = jnp.where(swapped, second, first).astype(jnp.bfloat16)
            packed_ref[2 * parity + 1, :, columns] = jnp.where(swapped, first, second).astype(
                jnp.bfloat16
            )


def pack(core, hidden, gain):
    tokens, features = hidden.shape
    return pl.pallas_call(
        pack_kernel,
        grid_spec=pltpu.PrefetchScalarGridSpec(
            num_scalar_prefetch=1,
            grid=(tokens // ROWS,),
            in_specs=[
                pl.BlockSpec((ROWS, features), lambda i, core: (i, 0)),
                pl.BlockSpec((1, features), lambda i, core: (0, 0)),
            ],
            out_specs=[
                pl.BlockSpec((CLASSES, ROWS, features // CLASSES), lambda i, core: (0, i, 0)),
                pl.BlockSpec((ROWS, 1), lambda i, core: (i, 0)),
            ],
        ),
        out_shape=[
            pltpu.HBM((CLASSES, tokens, features // CLASSES), jnp.bfloat16),
            jax.ShapeDtypeStruct((tokens, 1), jnp.float32),
        ],
        compiler_params=pltpu.CompilerParams(vmem_limit_bytes=KERNEL_VMEM),
        cost_estimate=pl.CostEstimate(
            flops=4 * tokens * features, bytes_accessed=4 * tokens * features, transcendentals=tokens
        ),
        name="pack_hidden",
    )(core, hidden, gain)


def project_kernel(place_ref, tokens_ref, own_ref, x_ref, y_ref, both_ref, out_ref, weight):
    @pl.when(pl.program_id(0) == 0)
    def _():
        side, half = place_ref[0], place_ref[1]
        held = ((own_ref, side, half), (x_ref, side, 1 - half), (y_ref, 1 - side, half), (both_ref, 1 - side, 1 - half))
        for held_ref, at_side, at_half in held:
            offset = at_side * 128 + at_half * 64
            for at in range(PLANES // 2):
                rows = pl.ds(pl.multiple_of(at * 256 + offset, 64), 64)
                weight[rows, :] = held_ref[at * 64 : at * 64 + 64, :]

    tokens = tokens_ref[...].reshape(-1, tokens_ref.shape[-1])
    product = jnp.dot(tokens, weight[...], preferred_element_type=jnp.float32)
    out_ref[...] = product.astype(jnp.bfloat16).reshape(out_ref.shape)


def project(place, tokens, held):
    sources, rows, features = tokens.shape
    width = held[0].shape[1]
    whole = [pl.BlockSpec(part.shape, lambda i, place: (0, 0)) for part in held]
    return pl.pallas_call(
        project_kernel,
        grid_spec=pltpu.PrefetchScalarGridSpec(
            num_scalar_prefetch=1,
            grid=(sources // SOURCES,),
            in_specs=[pl.BlockSpec((SOURCES, rows, features), lambda i, place: (i, 0, 0)), *whole],
            out_specs=pl.BlockSpec((SOURCES, rows, width), lambda i, place: (i, 0, 0)),
            scratch_shapes=[pltpu.VMEM((features, width), jnp.bfloat16)],
        ),
        out_shape=pltpu.HBM((sources, rows, width), jnp.bfloat16),
        compiler_params=pltpu.CompilerParams(vmem_limit_bytes=KERNEL_VMEM),
        cost_estimate=pl.CostEstimate(
            flops=2 * sources * rows * features * width,
            bytes_accessed=2 * (sources * rows * (features + width) + features * width),
            transcendentals=0,
        ),
        name="project_keys",
    )(place, tokens, *held)


def shards(
    hidden_in, norm_gain, key_weight, fragment_index, outer_params, outer_moment, inner_params
):
    replicas = 4
    layer_idx = fragment_index[0]
    outer_layer = lax.dynamic_index_in_dim(outer_params, layer_idx, 0, keepdims=False)
    inner_layer = lax.dynamic_index_in_dim(inner_params[0], layer_idx, 0, keepdims=False)
    pseudo_grad = (outer_layer - inner_layer.astype(jnp.float32)).astype(jnp.bfloat16)

    core, yh, x = (lax.axis_index(axis).astype(jnp.int32) for axis in ("core", "yh", "x"))
    own = lax.all_gather(key_weight[0], "zh", axis=0, tiled=True)
    own, gain = lax.optimization_barrier((own, norm_gain))
    packed, scale = pack(core[None], hidden_in[0], gain[None])
    packed, own, pseudo_grad = lax.optimization_barrier((packed, own, pseudo_grad))
    groups = exchange_groups()
    tokens = lax.all_to_all(packed, LINE, 0, 0, axis_index_groups=groups, tiled=True)
    held = (own, flipped(own, 1, 0), flipped(own, 0, 1), flipped(own, 1, 1))
    others = []
    for other in range(1, replicas):
        pairs = [(replica, replica ^ other) for replica in range(replicas)]
        others.append(lax.ppermute(pseudo_grad, REP, pairs))
    partial = project(jnp.stack([yh, lax.rem(x, 2)]), tokens, held)
    partial, layer_idx, others = lax.optimization_barrier((partial, layer_idx, others))
    partial = lax.all_to_all(partial, LINE, 0, 0, axis_index_groups=groups, tiled=True)
    outer_layer = lax.dynamic_index_in_dim(outer_params, layer_idx, 0, keepdims=False)
    moment_layer = lax.dynamic_index_in_dim(outer_moment, layer_idx, 0, keepdims=False)
    inner_layer = lax.dynamic_index_in_dim(inner_params[0], layer_idx, 0, keepdims=False)
    summed = pseudo_grad.astype(jnp.float32) + sum(part.astype(jnp.float32) for part in others)
    new_outer, new_moment = outer_update(summed / replicas, outer_layer, moment_layer)
    mixed_inner = (
        mix_keep * inner_layer.astype(jnp.float32) + (1.0 - mix_keep) * new_outer
    ).astype(jnp.bfloat16)
    keys = (jnp.sum(partial.astype(jnp.float32), axis=0) * scale).astype(jnp.bfloat16)
    return (keys[None], new_outer, new_moment, mixed_inner[None])


def solution(mesh):
    fine = Mesh(mesh.devices.reshape(2, 2, 8, 2, 2, 4), ("yl", "core", "zh", "zl", "yh", "x"))
    fsdp = ("zh", "zl", "yh", "x")
    placed = (
        P(REP, fsdp, None),
        P(),
        P(REP, fsdp, None),
        P(),
        P(None, fsdp, None),
        P(None, fsdp, None),
        P(REP, None, fsdp, None),
    )
    return jax.shard_map(
        shards,
        mesh=fine,
        in_specs=placed,
        out_specs=(
            P(REP, fsdp, None),
            P(fsdp, None),
            P(fsdp, None),
            P(REP, fsdp, None),
        ),
        check_vma=False,
    )
```

time: 96.3 us -> 103 us (1.070)
  blocking collectives: 24.9 us -> 34.6 us
  waiting for transfers between devices: 21 us -> 17.3 us
  local copies, waits for them, and re-layouts: 2.64 us -> 3.68 us
    all_to_all x2, waiting for transfers between devices: 21 us -> 6.44 us  [the longest x1 6.44 us: shards(): lax.all_to_all(partial, LINE, 0, 0, axis_index_groups=groups, tiled=True)]
    ppermute x3, waiting for transfers between devices: 0.01 us -> 10.9 us  [flipped(): return lax.ppermute(block, LINE, pairs)]
    all_gather x1, blocking collectives: 24.9 us -> 34.6 us  [shards(): own = lax.all_gather(key_weight[0], 'zh', axis=0, tiled=True)]
    all_to_all x2, starting transfers between devices: 14.7 us -> 7.68 us  [the longest x1 3.98 us: shards(): lax.all_to_all(partial, LINE, 0, 0, axis_index_groups=groups, tiled=True)]
    ppermute x3, starting transfers between devices: 10.6 us -> 14.4 us  [shards(): others.append(lax.ppermute(pseudo_grad, REP, pairs))]
    ppermute x3, starting transfers between devices: 8.56 us -> 11.1 us  [flipped(): return lax.ppermute(block, LINE, pairs)]
    unnamed x4 -> x6, local copies, waits for them, and re-layouts: 2.64 us -> 3.68 us
  transfers between devices with their start and end apart: 8 -> 8, of which waited for: 1 -> 3; matrix products, arithmetic and copies ran while one was open for 4% -> 2% of each run, Pallas kernels for 4% -> 5%
where the time goes in v9:
time: 103 us; the launch traced here: 102 us
  blocking collectives  34.6 us (34%)
  starting transfers between devices  33.2 us (32%)
  waiting for transfers between devices  17.3 us (17%)
  Pallas kernels  8.06 us (8%)
  other arithmetic  3.76 us (4%)
  local copies, waits for them, and re-layouts  3.68 us (4%)
  between operations  1.38 us (1%)
    all_gather x1, blocking collectives, shards(): own = lax.all_gather(key_weight[0], 'zh', axis=0, tiled=True)  34.6 us
    ppermute x3, starting transfers between devices, shards(): others.append(lax.ppermute(pseudo_grad, REP, pairs))  14.4 us
    ppermute x3, starting transfers between devices, flipped(): return lax.ppermute(block, LINE, pairs)  11.1 us
    ppermute x3, waiting for transfers between devices, flipped(): return lax.ppermute(block, LINE, pairs)  10.9 us
    all_to_all x1, waiting for transfers between devices, shards(): lax.all_to_all(partial, LINE, 0, 0, axis_index_groups=groups, tiled=True)  6.44 us
    pallas_call x1, Pallas kernels, project(): pl.pallas_call(project_kernel, grid_spec=pltpu.PrefetchScalarGridSpec(num...  4.82 us
    all_to_all x1, starting transfers between devices, shards(): lax.all_to_all(partial, LINE, 0, 0, axis_index_groups=groups, tiled=True)  3.98 us
    all_to_all x1, starting transfers between devices, shards(): lax.all_to_all(packed, LINE, 0, 0, axis_index_groups=groups, tiled=True)  3.71 us
  transfers between devices with their start and end apart: 8, of which 3 were waited for; matrix products, arithmetic and copies ran while one was open for 2% of the time, Pallas kernels for 5%

profile of v9, /device:TPU:1, one launch (start us, length us, event | category | flops | bytes accessed | tf_op | source)
XLA Modules:
  0.0 102.0 jit_solution(15507130674001876454)
XLA Ops:
  1.3 34.6 %all-gather = bf16[1,512,512]{2,1,0:T(8,128)(2,1)} all-gather(bf16[1,64,512]{2,1,0:T(8,128)(2,1)} %param.9), channel_id=2, replica_groups=mesh['yl'=2,'core'=2,'zh'=8,'zl'=2,'yh'=2,'x'=4] {'zh'}, dimensions={1}, use_global_device_ids=true | all-gather | bytes 589824 | tf_op jit(solution)/shard_map/all_gather | solution.py:157
  35.9 0.9 fusion.3
  36.8 0.0 copy-start
  36.8 1.9 %copy-done = bf16[1,192,8192]{2,1,0:T(8,128)(2,1)S(1)} copy-done((bf16[1,192,8192]{2,1,0:T(8,128)(2,1)S(1)}, bf16[1,192,8192]{2,1,0:T(8,128)(2,1)}, u32[]{:S(2)}) %copy-start) | copy-done | bytes 3145752
  38.7 0.0 copy-start.2
  38.7 0.8 copy-done.2
  39.5 3.2 %pack_hidden.1 = (bf16[4,192,2048]{2,1,0:T(8,128)(2,1)}, f32[192,1]{1,0:T(8,128)S(1)}) custom-call(s32[1]{0:T(128)} %bitcast.2.core_ref, bf16[192,8192]{1,0:T(8,128)(2,1)S(1)} %bitcast.33, f32[1,8192]{1,0:T(1,128)S(1)} %bitcast.38), custom_call_target="tpu_custom_call" | custom-call | flops 6291456 | bytes 6291456 | tf_op jit(solution)/shard_map/pack_hidden/pallas_call | solution.py:81
  42.7 3.7 %all-to-all-start = ((bf16[4,192,2048]{2,1,0:T(8,128)(2,1)}), bf16[4,192,2048]{2,1,0:T(8,128)(2,1)S(1)}, u32[]{:S(2)}, u32[]{:S(2)}) async-start(bf16[4,192,2048]{2,1,0:T(8,128)(2,1)} %get-tuple-element.19), calls=%async_computation | async-start | bytes 6291456 | tf_op jit(solution)/shard_map/all_to_all | solution.py:162
  46.4 7.0 %collective-permute-start.2 = (bf16[512,512]{1,0:T(8,128)(2,1)}, bf16[512,512]{1,0:T(8,128)(2,1)}, u32[]{:S(2)}, u32[]{:S(2)}) collective-permute-start(bf16[512,512]{1,0:T(8,128)(2,1)} %bitcast.34), channel_id=1, source_target_pairs={{0,5},{1,4},{2,7},{3,6},{4,1},{5,0},{6,3},{7,2},{8,13},{9,12},{10,... | collective-permute-start | bytes 1572872 | tf_op jit(solution)/shard_map/ppermute | solution.py:50
  53.5 2.0 %collective-permute-start.1 = (bf16[512,512]{1,0:T(8,128)(2,1)}, bf16[512,512]{1,0:T(8,128)(2,1)}, u32[]{:S(2)}, u32[]{:S(2)}) collective-permute-start(bf16[512,512]{1,0:T(8,128)(2,1)} %bitcast.35), channel_id=1, source_target_pairs={{0,4},{1,5},{2,6},{3,7},{4,0},{5,1},{6,2},{7,3},{8,12},{9,13},{10,... | collective-permute-start | bytes 1572872 | tf_op jit(solution)/shard_map/ppermute | solution.py:50
  55.4 2.1 %collective-permute-start = (bf16[512,512]{1,0:T(8,128)(2,1)}, bf16[512,512]{1,0:T(8,128)(2,1)}, u32[]{:S(2)}, u32[]{:S(2)}) collective-permute-start(bf16[512,512]{1,0:T(8,128)(2,1)} %bitcast.36), channel_id=1, source_target_pairs={{0,1},{1,0},{2,3},{3,2},{4,5},{5,4},{6,7},{7,6},{8,9},{9,8},{10,11... | collective-permute-start | bytes 1572872 | tf_op jit(solution)/shard_map/ppermute | solution.py:50
  57.6 9.7 %collective-permute-start.5 = (bf16[64,512]{1,0:T(8,128)(2,1)S(1)}, bf16[64,512]{1,0:T(8,128)(2,1)S(1)}, u32[]{:S(2)}, u32[]{:S(2)}) collective-permute-start(bf16[64,512]{1,0:T(8,128)(2,1)S(1)} %fusion.3), channel_id=1, source_target_pairs={{0,384},{128,256},{256,128},{384,0},{1,385},{129,257},{257,129},{3... | collective-permute-start | bytes 196616 | tf_op jit(solution)/shard_map/ppermute | solution.py:167
  67.3 2.1 %collective-permute-start.4 = (bf16[64,512]{1,0:T(8,128)(2,1)S(1)}, bf16[64,512]{1,0:T(8,128)(2,1)S(1)}, u32[]{:S(2)}, u32[]{:S(2)}) collective-permute-start(bf16[64,512]{1,0:T(8,128)(2,1)S(1)} %fusion.3), channel_id=1, source_target_pairs={{0,256},{128,384},{256,0},{384,128},{1,257},{129,385},{257,1},{385... | collective-permute-start | bytes 196616 | tf_op jit(solution)/shard_map/ppermute | solution.py:167
  69.4 0.1 pad_add_fusion.place_ref
  69.5 4.2 %collective-permute-done.2.both_ref = bf16[512,512]{1,0:T(8,128)(2,1)} collective-permute-done((bf16[512,512]{1,0:T(8,128)(2,1)}, bf16[512,512]{1,0:T(8,128)(2,1)}, u32[]{:S(2)}, u32[]{:S(2)}) %collective-permute-start.2) | collective-permute-done | bytes 524320 | tf_op jit(solution)/shard_map/ppermute | solution.py:50
  73.7 2.6 %collective-permute-start.3 = (bf16[64,512]{1,0:T(8,128)(2,1)S(1)}, bf16[64,512]{1,0:T(8,128)(2,1)S(1)}, u32[]{:S(2)}, u32[]{:S(2)}) collective-permute-start(bf16[64,512]{1,0:T(8,128)(2,1)S(1)} %fusion.3), channel_id=1, source_target_pairs={{0,128},{128,0},{256,384},{384,256},{1,129},{129,1},{257,385},{385... | collective-permute-start | bytes 196616 | tf_op jit(solution)/shard_map/ppermute | solution.py:167
  76.3 0.0 collective-permute-done.1.y_ref
  76.3 6.6 %collective-permute-done.x_ref = bf16[512,512]{1,0:T(8,128)(2,1)} collective-permute-done((bf16[512,512]{1,0:T(8,128)(2,1)}, bf16[512,512]{1,0:T(8,128)(2,1)}, u32[]{:S(2)}, u32[]{:S(2)}) %collective-permute-start) | collective-permute-done | bytes 524320 | tf_op jit(solution)/shard_map/ppermute | solution.py:50
  82.9 0.0 all-to-all-done.tokens_ref
  83.0 0.0 copy-start.1
  83.0 1.0 %copy-done.1 = bf16[1,512,512]{2,1,0:T(8,128)(2,1)S(1)} copy-done((bf16[1,512,512]{2,1,0:T(8,128)(2,1)S(1)}, bf16[1,512,512]{2,1,0:T(8,128)(2,1)}, u32[]{:S(2)}) %copy-start.1) | copy-done | bytes 524312
  84.0 4.8 %project_keys.1 = bf16[4,192,512]{2,1,0:T(8,128)(2,1)} custom-call(s32[2]{0:T(128)S(1)} %pad_add_fusion.place_ref, bf16[4,192,2048]{2,1,0:T(8,128)(2,1)S(1)} %all-to-all-done.tokens_ref, bf16[512,512]{1,0:T(8,128)(2,1)S(1)} %bitcast.37, bf16[512,512]{1,0:T(8,128)(2,1)} %collective-permute-done.x_ref, bf16[512,512]{1,0:T(8,128)(2,1)} %collective-permute-done.1.y_ref, ...), custom_call_target="tpu_custom_call" | custom-call | flops 1610612736 | bytes 6029312 | tf_op jit(solution)/shard_map/project_keys/pallas_call | solution.py:127
  88.8 0.0 collective-permute-done.5
  88.8 0.0 collective-permute-done.4
  88.8 0.0 collective-permute-done.3
  88.8 4.0 %all-to-all-start.1 = ((bf16[4,192,512]{2,1,0:T(8,128)(2,1)}), bf16[4,192,512]{2,1,0:T(8,128)(2,1)S(1)}, u32[]{:S(2)}, u32[]{:S(2)}) async-start(bf16[4,192,512]{2,1,0:T(8,128)(2,1)} %project_keys.1), calls=%async_computation.1 | async-start | bytes 1572864 | tf_op jit(solution)/shard_map/all_to_all | solution.py:170
  92.8 0.1 reduce
  92.9 1.8 %fusion.4 = (bf16[1,64,512]{2,1,0:T(8,128)(2,1)}, f32[64,512]{1,0:T(8,128)}, f32[64,512]{1,0:T(8,128)}) fusion(bf16[1,7,64,512]{3,2,1,0:T(8,128)(2,1)} %param.13, s32[]{:T(128)S(6)} %select_n.12, bf16[64,512]{1,0:T(8,128)(2,1)S(1)} %collective-permute-done.5, bf16[64,512]{1,0:T(8,128)(2,1)S(1)} %collective-permute-done.4, ...), kind=kLoop, calls=%fused_computation.11 | loop fusion | flops 589824 | bytes 917508 | tf_op jit(solution)/shard_map/broadcast_in_dim | solution.py:180
  94.7 6.4 %all-to-all-done.1 = bf16[4,192,512]{2,1,0:T(8,128)(2,1)S(1)} async-done(((bf16[4,192,512]{2,1,0:T(8,128)(2,1)}), bf16[4,192,512]{2,1,0:T(8,128)(2,1)S(1)}, u32[]{:S(2)}, u32[]{:S(2)}) %all-to-all-start.1) | async-done | bytes 786464 | tf_op jit(solution)/shard_map/all_to_all | solution.py:170
  101.1 0.1 convert_reduce_fusion
  101.3 0.8 fusion
Async XLA Ops:
  36.8 1.9 %copy-start = (bf16[1,192,8192]{2,1,0:T(8,128)(2,1)S(1)}, bf16[1,192,8192]{2,1,0:T(8,128)(2,1)}, u32[]{:S(2)}) copy-start(bf16[1,192,8192]{2,1,0:T(8,128)(2,1)} %param.7) | copy-start | bytes 9437188
  38.7 0.8 copy-start.2
  42.7 40.2 %all-to-all-start = ((bf16[4,192,2048]{2,1,0:T(8,128)(2,1)}), bf16[4,192,2048]{2,1,0:T(8,128)(2,1)S(1)}, u32[]{:S(2)}, u32[]{:S(2)}) async-start(bf16[4,192,2048]{2,1,0:T(8,128)(2,1)} %get-tuple-element.19), calls=%async_computation | async-start | bytes 6291456 | tf_op jit(solution)/shard_map/all_to_all | solution.py:162
  46.4 27.3 %collective-permute-start.2 = (bf16[512,512]{1,0:T(8,128)(2,1)}, bf16[512,512]{1,0:T(8,128)(2,1)}, u32[]{:S(2)}, u32[]{:S(2)}) collective-permute-start(bf16[512,512]{1,0:T(8,128)(2,1)} %bitcast.34), channel_id=1, source_target_pairs={{0,5},{1,4},{2,7},{3,6},{4,1},{5,0},{6,3},{7,2},{8,13},{9,12},{10,... | collective-permute-start | bytes 1572872 | tf_op jit(solution)/shard_map/ppermute | solution.py:50
  53.5 22.9 %collective-permute-start.1 = (bf16[512,512]{1,0:T(8,128)(2,1)}, bf16[512,512]{1,0:T(8,128)(2,1)}, u32[]{:S(2)}, u32[]{:S(2)}) collective-permute-start(bf16[512,512]{1,0:T(8,128)(2,1)} %bitcast.35), channel_id=1, source_target_pairs={{0,4},{1,5},{2,6},{3,7},{4,0},{5,1},{6,2},{7,3},{8,12},{9,13},{10,... | collective-permute-start | bytes 1572872 | tf_op jit(solution)/shard_map/ppermute | solution.py:50
  55.4 27.5 %collective-permute-start = (bf16[512,512]{1,0:T(8,128)(2,1)}, bf16[512,512]{1,0:T(8,128)(2,1)}, u32[]{:S(2)}, u32[]{:S(2)}) collective-permute-start(bf16[512,512]{1,0:T(8,128)(2,1)} %bitcast.36), channel_id=1, source_target_pairs={{0,1},{1,0},{2,3},{3,2},{4,5},{5,4},{6,7},{7,6},{8,9},{9,8},{10,11... | collective-permute-start | bytes 1572872 | tf_op jit(solution)/shard_map/ppermute | solution.py:50
  57.6 31.2 %collective-permute-start.5 = (bf16[64,512]{1,0:T(8,128)(2,1)S(1)}, bf16[64,512]{1,0:T(8,128)(2,1)S(1)}, u32[]{:S(2)}, u32[]{:S(2)}) collective-permute-start(bf16[64,512]{1,0:T(8,128)(2,1)S(1)} %fusion.3), channel_id=1, source_target_pairs={{0,384},{128,256},{256,128},{384,0},{1,385},{129,257},{257,129},{3... | collective-permute-start | bytes 196616 | tf_op jit(solution)/shard_map/ppermute | solution.py:167
  67.3 21.5 %collective-permute-start.4 = (bf16[64,512]{1,0:T(8,128)(2,1)S(1)}, bf16[64,512]{1,0:T(8,128)(2,1)S(1)}, u32[]{:S(2)}, u32[]{:S(2)}) collective-permute-start(bf16[64,512]{1,0:T(8,128)(2,1)S(1)} %fusion.3), channel_id=1, source_target_pairs={{0,256},{128,384},{256,0},{384,128},{1,257},{129,385},{257,1},{385... | collective-permute-start | bytes 196616 | tf_op jit(solution)/shard_map/ppermute | solution.py:167
  73.7 15.1 %collective-permute-start.3 = (bf16[64,512]{1,0:T(8,128)(2,1)S(1)}, bf16[64,512]{1,0:T(8,128)(2,1)S(1)}, u32[]{:S(2)}, u32[]{:S(2)}) collective-permute-start(bf16[64,512]{1,0:T(8,128)(2,1)S(1)} %fusion.3), channel_id=1, source_target_pairs={{0,128},{128,0},{256,384},{384,256},{1,129},{129,1},{257,385},{385... | collective-permute-start | bytes 196616 | tf_op jit(solution)/shard_map/ppermute | solution.py:167
  83.0 1.0 %copy-start.1 = (bf16[1,512,512]{2,1,0:T(8,128)(2,1)S(1)}, bf16[1,512,512]{2,1,0:T(8,128)(2,1)}, u32[]{:S(2)}) copy-start(bf16[1,512,512]{2,1,0:T(8,128)(2,1)} %all-gather) | copy-start | bytes 1572868
  88.8 12.3 %all-to-all-start.1 = ((bf16[4,192,512]{2,1,0:T(8,128)(2,1)}), bf16[4,192,512]{2,1,0:T(8,128)(2,1)S(1)}, u32[]{:S(2)}, u32[]{:S(2)}) async-start(bf16[4,192,512]{2,1,0:T(8,128)(2,1)} %project_keys.1), calls=%async_computation.1 | async-start | bytes 1572864 | tf_op jit(solution)/shard_map/all_to_all | solution.py:170

commit v10 on v9

--- a/solution.py
+++ b/solution.py
@@ -10,7 +10,7 @@
 mix_keep = 0.5
 epsilon = 1e-05
 
-REP, LINE = ("yl", "core"), ("core", "zh", "zl", "yh", "x")
+REP, LINE = ("yl", "core"), ("core", "zh", "zm", "zl", "yh", "x")
 PLANES, SIDES, COLUMNS = 16, 2, 4
 CLASSES, ROWS, SOURCES = 4, 64, 2
 KERNEL_VMEM = 24 * 1024 * 1024
@@ -112,7 +112,8 @@
         for held_ref, at_side, at_half in held:
             offset = at_side * 128 + at_half * 64
             for at in range(PLANES // 2):
-                rows = pl.ds(pl.multiple_of(at * 256 + offset, 64), 64)
+                middle = place_ref[2] if at % 2 == 0 else 1 - place_ref[2]
+                rows = pl.ds(pl.multiple_of((at // 2 * 2 + middle) * 256 + offset, 64), 64)
                 weight[rows, :] = held_ref[at * 64 : at * 64 + 64, :]
 
     tokens = tokens_ref[...].reshape(-1, tokens_ref.shape[-1])
@@ -153,19 +154,21 @@
     inner_layer = lax.dynamic_index_in_dim(inner_params[0], layer_idx, 0, keepdims=False)
     pseudo_grad = (outer_layer - inner_layer.astype(jnp.float32)).astype(jnp.bfloat16)
 
-    core, yh, x = (lax.axis_index(axis).astype(jnp.int32) for axis in ("core", "yh", "x"))
-    own = lax.all_gather(key_weight[0], "zh", axis=0, tiled=True)
-    own, gain = lax.optimization_barrier((own, norm_gain))
-    packed, scale = pack(core[None], hidden_in[0], gain[None])
-    packed, own, pseudo_grad = lax.optimization_barrier((packed, own, pseudo_grad))
+    core, middle, yh, x = (lax.axis_index(axis).astype(jnp.int32) for axis in ("core", "zm", "yh", "x"))
+    block = key_weight[0]
+    block = jnp.concatenate([block, lax.ppermute(block, "zm", [(0, 1), (1, 0)])], axis=0)
+    packed, scale = pack(core[None], hidden_in[0], norm_gain[None])
+    packed, block, pseudo_grad = lax.optimization_barrier((packed, block, pseudo_grad))
     groups = exchange_groups()
     tokens = lax.all_to_all(packed, LINE, 0, 0, axis_index_groups=groups, tiled=True)
+    own = lax.all_gather(block, "zh", axis=0, tiled=True)
+    own, pseudo_grad = lax.optimization_barrier((own, pseudo_grad))
     held = (own, flipped(own, 1, 0), flipped(own, 0, 1), flipped(own, 1, 1))
     others = []
     for other in range(1, replicas):
         pairs = [(replica, replica ^ other) for replica in range(replicas)]
         others.append(lax.ppermute(pseudo_grad, REP, pairs))
-    partial = project(jnp.stack([yh, lax.rem(x, 2)]), tokens, held)
+    partial = project(jnp.stack([yh, lax.rem(x, 2), middle]), tokens, held)
     partial, layer_idx, others = lax.optimization_barrier((partial, layer_idx, others))
     partial = lax.all_to_all(partial, LINE, 0, 0, axis_index_groups=groups, tiled=True)
     outer_layer = lax.dynamic_index_in_dim(outer_params, layer_idx, 0, keepdims=False)
@@ -181,8 +184,8 @@
 
 
 def solution(mesh):
-    fine = Mesh(mesh.devices.reshape(2, 2, 8, 2, 2, 4), ("yl", "core", "zh", "zl", "yh", "x"))
-    fsdp = ("zh", "zl", "yh", "x")
+    fine = Mesh(mesh.devices.reshape(2, 2, 4, 2, 2, 2, 4), ("yl", "core", "zh", "zm", "zl", "yh", "x"))
+    fsdp = ("zh", "zm", "zl", "yh", "x")
     placed = (
         P(REP, fsdp, None),
         P(),

time: 103 us -> 116 us (1.13)
  starting transfers between devices: 33.2 us -> 47.5 us
  waiting for transfers between devices: 17.3 us -> 14.7 us
    all_to_all x1, starting transfers between devices: 3.71 us -> 9.6 us  [shards(): lax.all_to_all(packed, LINE, 0, 0, axis_index_groups=groups, tiled=True)]
    ppermute x0 -> x1, starting transfers between devices: none -> 5.73 us  [shards(): lax.ppermute(block, 'zm', [(0, 1), (1, 0)])]
    ppermute x3, starting transfers between devices: 14.4 us -> 9.99 us  [shards(): others.append(lax.ppermute(pseudo_grad, REP, pairs))]
    all_to_all x1, starting transfers between devices: 3.98 us -> 7.88 us  [shards(): lax.all_to_all(partial, LINE, 0, 0, axis_index_groups=groups, tiled=True)]
    ppermute x3, starting transfers between devices: 11.1 us -> 14.3 us  [flipped(): return lax.ppermute(block, LINE, pairs)]
    ppermute x3, waiting for transfers between devices: 10.9 us -> 8.58 us  [flipped(): return lax.ppermute(block, LINE, pairs)]
  transfers between devices with their start and end apart: 8 -> 9, of which waited for: 3 -> 2; matrix products, arithmetic and copies ran while one was open for 2% -> 3% of each run, Pallas kernels for 5% -> 7%
where the time goes in v10:
time: 116 us; the launch traced here: 114 us
  starting transfers between devices  47.5 us (41%)
  blocking collectives  35.7 us (31%)
  waiting for transfers between devices  14.7 us (13%)
  Pallas kernels  8.23 us (7%)
  other arithmetic  3.77 us (3%)
  local copies, waits for them, and re-layouts  2.64 us (2%)
  between operations  1.42 us (1%)
    all_gather x1, blocking collectives, shards(): own = lax.all_gather(block, 'zh', axis=0, tiled=True)  35.7 us
    ppermute x3, starting transfers between devices, flipped(): return lax.ppermute(block, LINE, pairs)  14.3 us
    ppermute x3, starting transfers between devices, shards(): others.append(lax.ppermute(pseudo_grad, REP, pairs))  9.99 us
    all_to_all x1, starting transfers between devices, shards(): lax.all_to_all(packed, LINE, 0, 0, axis_index_groups=groups, tiled=True)  9.6 us
    ppermute x3, waiting for transfers between devices, flipped(): return lax.ppermute(block, LINE, pairs)  8.58 us
    all_to_all x1, starting transfers between devices, shards(): lax.all_to_all(partial, LINE, 0, 0, axis_index_groups=groups, tiled=True)  7.88 us
    all_to_all x1, waiting for transfers between devices, shards(): lax.all_to_all(partial, LINE, 0, 0, axis_index_groups=groups, tiled=True)  6.15 us
    ppermute x1, starting transfers between devices, shards(): lax.ppermute(block, 'zm', [(0, 1), (1, 0)])  5.73 us
  transfers between devices with their start and end apart: 9, of which 2 were waited for; matrix products, arithmetic and copies ran while one was open for 3% of the time, Pallas kernels for 7%

profile of v10, /device:TPU:1, one launch (start us, length us, event | category | flops | bytes accessed | tf_op | source)
XLA Modules:
  0.0 114.0 jit_solution(14987337472015527286)
XLA Ops:
  0.6 5.7 %collective-permute-start = (bf16[64,512]{1,0:T(8,128)(2,1)}, bf16[64,512]{1,0:T(8,128)(2,1)S(1)}, u32[]{:S(2)}, u32[]{:S(2)}) collective-permute-start(bf16[64,512]{1,0:T(8,128)(2,1)} %bitcast.36), channel_id=1, source_target_pairs={{0,16},{16,0},{1,17},{17,1},{2,18},{18,2},{3,19},{19,3},{4,20},{20... | collective-permute-start | bytes 196616 | tf_op jit(solution)/shard_map/ppermute | solution.py:159
  7.0 0.0 copy-start
  7.0 1.9 %copy-done = bf16[1,192,8192]{2,1,0:T(8,128)(2,1)S(1)} copy-done((bf16[1,192,8192]{2,1,0:T(8,128)(2,1)S(1)}, bf16[1,192,8192]{2,1,0:T(8,128)(2,1)}, u32[]{:S(2)}) %copy-start) | copy-done | bytes 3145752
  8.9 0.0 copy-start.1
  8.9 0.8 copy-done.1
  9.7 0.0 copy-start.2
  9.7 3.2 %pack_hidden.1 = (bf16[4,192,2048]{2,1,0:T(8,128)(2,1)}, f32[192,1]{1,0:T(8,128)S(1)}) custom-call(s32[1]{0:T(128)} %bitcast.3.core_ref, bf16[192,8192]{1,0:T(8,128)(2,1)S(1)} %bitcast.34, f32[1,8192]{1,0:T(1,128)S(1)} %bitcast.35), custom_call_target="tpu_custom_call" | custom-call | flops 6291456 | bytes 6291456 | tf_op jit(solution)/shard_map/pack_hidden/pallas_call | solution.py:81
  12.9 0.9 fusion.3
  13.8 0.0 collective-permute-done
  13.9 0.0 copy-done.2
  13.9 9.6 %all-to-all-start = ((bf16[4,192,2048]{2,1,0:T(8,128)(2,1)}), bf16[4,192,2048]{2,1,0:T(8,128)(2,1)S(1)}, u32[]{:S(2)}, u32[]{:S(2)}) async-start(bf16[4,192,2048]{2,1,0:T(8,128)(2,1)} %get-tuple-element.17), calls=%async_computation | async-start | bytes 6291456 | tf_op jit(solution)/shard_map/all_to_all | solution.py:163
  23.5 35.7 %all_gather.3.own_ref = bf16[512,512]{1,0:T(8,128)(2,1)} all-gather(bf16[128,512]{1,0:T(8,128)(2,1)S(1)} %pad_maximum_fusion), channel_id=1, replica_groups=mesh['yl'=2,'core'=2,'zh'=4,'zm'=2,'zl'=2,'yh'=2,'x'=4] {'zh'}, dimensions={0}, use_global_device_ids=true | all-gather | bytes 655360 | tf_op jit(solution)/shard_map/all_gather | solution.py:164
  59.2 6.8 %collective-permute-start.3 = (bf16[512,512]{1,0:T(8,128)(2,1)}, bf16[512,512]{1,0:T(8,128)(2,1)}, u32[]{:S(2)}, u32[]{:S(2)}) collective-permute-start(bf16[512,512]{1,0:T(8,128)(2,1)} %all_gather.3.own_ref), channel_id=1, source_target_pairs={{0,5},{1,4},{2,7},{3,6},{4,1},{5,0},{6,3},{7,2},{8,13},{9,12},{10,... | collective-permute-start | bytes 1572872 | tf_op jit(solution)/shard_map/ppermute | solution.py:50
  66.0 3.1 %collective-permute-start.2 = (bf16[512,512]{1,0:T(8,128)(2,1)}, bf16[512,512]{1,0:T(8,128)(2,1)}, u32[]{:S(2)}, u32[]{:S(2)}) collective-permute-start(bf16[512,512]{1,0:T(8,128)(2,1)} %all_gather.3.own_ref), channel_id=1, source_target_pairs={{0,4},{1,5},{2,6},{3,7},{4,0},{5,1},{6,2},{7,3},{8,12},{9,13},{10,... | collective-permute-start | bytes 1572872 | tf_op jit(solution)/shard_map/ppermute | solution.py:50
  69.2 4.3 %collective-permute-start.1 = (bf16[512,512]{1,0:T(8,128)(2,1)}, bf16[512,512]{1,0:T(8,128)(2,1)}, u32[]{:S(2)}, u32[]{:S(2)}) collective-permute-start(bf16[512,512]{1,0:T(8,128)(2,1)} %all_gather.3.own_ref), channel_id=1, source_target_pairs={{0,1},{1,0},{2,3},{3,2},{4,5},{5,4},{6,7},{7,6},{8,9},{9,8},{10,11... | collective-permute-start | bytes 1572872 | tf_op jit(solution)/shard_map/ppermute | solution.py:50
  73.5 0.1 pad_add_fusion.place_ref
  73.6 5.0 %collective-permute-start.6 = (bf16[64,512]{1,0:T(8,128)(2,1)S(1)}, bf16[64,512]{1,0:T(8,128)(2,1)S(1)}, u32[]{:S(2)}, u32[]{:S(2)}) collective-permute-start(bf16[64,512]{1,0:T(8,128)(2,1)S(1)} %fusion.3), channel_id=1, source_target_pairs={{0,384},{128,256},{256,128},{384,0},{1,385},{129,257},{257,129},{3... | collective-permute-start | bytes 196616 | tf_op jit(solution)/shard_map/ppermute | solution.py:170
  78.6 3.0 %collective-permute-start.5 = (bf16[64,512]{1,0:T(8,128)(2,1)S(1)}, bf16[64,512]{1,0:T(8,128)(2,1)S(1)}, u32[]{:S(2)}, u32[]{:S(2)}) collective-permute-start(bf16[64,512]{1,0:T(8,128)(2,1)S(1)} %fusion.3), channel_id=1, source_target_pairs={{0,256},{128,384},{256,0},{384,128},{1,257},{129,385},{257,1},{385... | collective-permute-start | bytes 196616 | tf_op jit(solution)/shard_map/ppermute | solution.py:170
  81.7 0.0 collective-permute-done.3.both_ref
  81.7 1.9 %collective-permute-start.4 = (bf16[64,512]{1,0:T(8,128)(2,1)S(1)}, bf16[64,512]{1,0:T(8,128)(2,1)S(1)}, u32[]{:S(2)}, u32[]{:S(2)}) collective-permute-start(bf16[64,512]{1,0:T(8,128)(2,1)S(1)} %fusion.3), channel_id=1, source_target_pairs={{0,128},{128,0},{256,384},{384,256},{1,129},{129,1},{257,385},{385... | collective-permute-start | bytes 196616 | tf_op jit(solution)/shard_map/ppermute | solution.py:170
  83.6 8.6 %collective-permute-done.2.y_ref = bf16[512,512]{1,0:T(8,128)(2,1)} collective-permute-done((bf16[512,512]{1,0:T(8,128)(2,1)}, bf16[512,512]{1,0:T(8,128)(2,1)}, u32[]{:S(2)}, u32[]{:S(2)}) %collective-permute-start.2) | collective-permute-done | bytes 524320 | tf_op jit(solution)/shard_map/ppermute | solution.py:50
  92.2 0.0 collective-permute-done.1.x_ref
  92.2 0.0 all-to-all-done.tokens_ref
  92.2 5.0 %project_keys.1 = bf16[4,192,512]{2,1,0:T(8,128)(2,1)} custom-call(s32[3]{0:T(128)S(1)} %pad_add_fusion.place_ref, bf16[4,192,2048]{2,1,0:T(8,128)(2,1)S(1)} %all-to-all-done.tokens_ref, bf16[512,512]{1,0:T(8,128)(2,1)} %all_gather.3.own_ref, bf16[512,512]{1,0:T(8,128)(2,1)} %collective-permute-done.1.x_ref, bf16[512,512]{1,0:T(8,128)(2,1)} %collective-permute-done.2.y_ref, ...), custom_call_target="tpu_custom_call" | custom-call | flops 1610612736 | bytes 6029312 | tf_op jit(solution)/shard_map/project_keys/pallas_call | solution.py:128
  97.2 0.0 collective-permute-done.6
  97.2 0.0 collective-permute-done.5
  97.2 0.0 collective-permute-done.4
  97.2 7.9 %all-to-all-start.1 = ((bf16[4,192,512]{2,1,0:T(8,128)(2,1)}), bf16[4,192,512]{2,1,0:T(8,128)(2,1)S(1)}, u32[]{:S(2)}, u32[]{:S(2)}) async-start(bf16[4,192,512]{2,1,0:T(8,128)(2,1)} %project_keys.1), calls=%async_computation.1 | async-start | bytes 1572864 | tf_op jit(solution)/shard_map/all_to_all | solution.py:173
  105.1 0.1 reduce
  105.2 1.8 %fusion.4 = (bf16[1,64,512]{2,1,0:T(8,128)(2,1)}, f32[64,512]{1,0:T(8,128)}, f32[64,512]{1,0:T(8,128)}) fusion(bf16[1,7,64,512]{3,2,1,0:T(8,128)(2,1)} %param.13, s32[]{:T(128)S(6)} %select_n.12, bf16[64,512]{1,0:T(8,128)(2,1)S(1)} %collective-permute-done.6, bf16[64,512]{1,0:T(8,128)(2,1)S(1)} %collective-permute-done.5, ...), kind=kLoop, calls=%fused_computation.12 | loop fusion | flops 589824 | bytes 917508 | tf_op jit(solution)/shard_map/broadcast_in_dim | solution.py:183
  107.0 6.1 %all-to-all-done.1 = bf16[4,192,512]{2,1,0:T(8,128)(2,1)S(1)} async-done(((bf16[4,192,512]{2,1,0:T(8,128)(2,1)}), bf16[4,192,512]{2,1,0:T(8,128)(2,1)S(1)}, u32[]{:S(2)}, u32[]{:S(2)}) %all-to-all-start.1) | async-done | bytes 786464 | tf_op jit(solution)/shard_map/all_to_all | solution.py:173
  113.1 0.1 convert_reduce_fusion
  113.2 0.8 fusion
  (1 shorter events, 0.0 us)
Async XLA Ops:
  0.6 13.2 %collective-permute-start = (bf16[64,512]{1,0:T(8,128)(2,1)}, bf16[64,512]{1,0:T(8,128)(2,1)S(1)}, u32[]{:S(2)}, u32[]{:S(2)}) collective-permute-start(bf16[64,512]{1,0:T(8,128)(2,1)} %bitcast.36), channel_id=1, source_target_pairs={{0,16},{16,0},{1,17},{17,1},{2,18},{18,2},{3,19},{19,3},{4,20},{20... | collective-permute-start | bytes 196616 | tf_op jit(solution)/shard_map/ppermute | solution.py:159
  7.0 1.9 %copy-start = (bf16[1,192,8192]{2,1,0:T(8,128)(2,1)S(1)}, bf16[1,192,8192]{2,1,0:T(8,128)(2,1)}, u32[]{:S(2)}) copy-start(bf16[1,192,8192]{2,1,0:T(8,128)(2,1)} %param.7) | copy-start | bytes 9437188
  8.9 0.8 copy-start.1
  9.7 4.2 %copy-start.2 = (bf16[1,64,512]{2,1,0:T(8,128)(2,1)S(1)}, bf16[1,64,512]{2,1,0:T(8,128)(2,1)}, u32[]{:S(2)}) copy-start(bf16[1,64,512]{2,1,0:T(8,128)(2,1)} %param.9) | copy-start | bytes 196612
  13.9 78.3 %all-to-all-start = ((bf16[4,192,2048]{2,1,0:T(8,128)(2,1)}), bf16[4,192,2048]{2,1,0:T(8,128)(2,1)S(1)}, u32[]{:S(2)}, u32[]{:S(2)}) async-start(bf16[4,192,2048]{2,1,0:T(8,128)(2,1)} %get-tuple-element.17), calls=%async_computation | async-start | bytes 6291456 | tf_op jit(solution)/shard_map/all_to_all | solution.py:163
  59.2 22.5 %collective-permute-start.3 = (bf16[512,512]{1,0:T(8,128)(2,1)}, bf16[512,512]{1,0:T(8,128)(2,1)}, u32[]{:S(2)}, u32[]{:S(2)}) collective-permute-start(bf16[512,512]{1,0:T(8,128)(2,1)} %all_gather.3.own_ref), channel_id=1, source_target_pairs={{0,5},{1,4},{2,7},{3,6},{4,1},{5,0},{6,3},{7,2},{8,13},{9,12},{10,... | collective-permute-start | bytes 1572872 | tf_op jit(solution)/shard_map/ppermute | solution.py:50
  66.0 26.1 %collective-permute-start.2 = (bf16[512,512]{1,0:T(8,128)(2,1)}, bf16[512,512]{1,0:T(8,128)(2,1)}, u32[]{:S(2)}, u32[]{:S(2)}) collective-permute-start(bf16[512,512]{1,0:T(8,128)(2,1)} %all_gather.3.own_ref), channel_id=1, source_target_pairs={{0,4},{1,5},{2,6},{3,7},{4,0},{5,1},{6,2},{7,3},{8,12},{9,13},{10,... | collective-permute-start | bytes 1572872 | tf_op jit(solution)/shard_map/ppermute | solution.py:50
  69.2 23.0 %collective-permute-start.1 = (bf16[512,512]{1,0:T(8,128)(2,1)}, bf16[512,512]{1,0:T(8,128)(2,1)}, u32[]{:S(2)}, u32[]{:S(2)}) collective-permute-start(bf16[512,512]{1,0:T(8,128)(2,1)} %all_gather.3.own_ref), channel_id=1, source_target_pairs={{0,1},{1,0},{2,3},{3,2},{4,5},{5,4},{6,7},{7,6},{8,9},{9,8},{10,11... | collective-permute-start | bytes 1572872 | tf_op jit(solution)/shard_map/ppermute | solution.py:50
  73.6 23.6 %collective-permute-start.6 = (bf16[64,512]{1,0:T(8,128)(2,1)S(1)}, bf16[64,512]{1,0:T(8,128)(2,1)S(1)}, u32[]{:S(2)}, u32[]{:S(2)}) collective-permute-start(bf16[64,512]{1,0:T(8,128)(2,1)S(1)} %fusion.3), channel_id=1, source_target_pairs={{0,384},{128,256},{256,128},{384,0},{1,385},{129,257},{257,129},{3... | collective-permute-start | bytes 196616 | tf_op jit(solution)/shard_map/ppermute | solution.py:170
  78.6 18.6 %collective-permute-start.5 = (bf16[64,512]{1,0:T(8,128)(2,1)S(1)}, bf16[64,512]{1,0:T(8,128)(2,1)S(1)}, u32[]{:S(2)}, u32[]{:S(2)}) collective-permute-start(bf16[64,512]{1,0:T(8,128)(2,1)S(1)} %fusion.3), channel_id=1, source_target_pairs={{0,256},{128,384},{256,0},{384,128},{1,257},{129,385},{257,1},{385... | collective-permute-start | bytes 196616 | tf_op jit(solution)/shard_map/ppermute | solution.py:170
  81.7 15.5 %collective-permute-start.4 = (bf16[64,512]{1,0:T(8,128)(2,1)S(1)}, bf16[64,512]{1,0:T(8,128)(2,1)S(1)}, u32[]{:S(2)}, u32[]{:S(2)}) collective-permute-start(bf16[64,512]{1,0:T(8,128)(2,1)S(1)} %fusion.3), channel_id=1, source_target_pairs={{0,128},{128,0},{256,384},{384,256},{1,129},{129,1},{257,385},{385... | collective-permute-start | bytes 196616 | tf_op jit(solution)/shard_map/ppermute | solution.py:170
  97.2 15.9 %all-to-all-start.1 = ((bf16[4,192,512]{2,1,0:T(8,128)(2,1)}), bf16[4,192,512]{2,1,0:T(8,128)(2,1)S(1)}, u32[]{:S(2)}, u32[]{:S(2)}) async-start(bf16[4,192,512]{2,1,0:T(8,128)(2,1)} %project_keys.1), calls=%async_computation.1 | async-start | bytes 1572864 | tf_op jit(solution)/shard_map/all_to_all | solution.py:173

commit v11 on v8

--- a/solution.py
+++ b/solution.py
@@ -10,9 +10,9 @@
 mix_keep = 0.5
 epsilon = 1e-05
 
-Z, PLANE, REP = ("zh", "zl"), ("yh", "x"), ("yl", "core")
-PLANES, PEERS = 16, 8
-ROWS, SOURCES = 64, 4
+Z, ROW, REP = ("zh", "zl"), "x", ("yl", "core")
+PLANES, SIDES, PEERS = 16, 2, 4
+ROWS, SOURCES = 64, 2
 KERNEL_VMEM = 24 * 1024 * 1024
 
 
@@ -29,16 +29,15 @@
     scale_ref[...] = lax.rsqrt(mean_square + epsilon)
     gained = hidden * gain_ref[...]
     low = lax.broadcasted_iota(jnp.int32, (hidden.shape[0], 128), 1) < 64
-    for pair in range(PLANES // 2):
-        for tile in range(PEERS // 2):
-            start = pair * 1024 + tile * 128
-            first = gained[:, start : start + 128]
-            second = gained[:, start + 512 : start + 640]
-            columns = slice(pair * 128, pair * 128 + 128)
+    for z in range(PLANES):
+        for pair in range(PEERS // 2):
+            start = z * 512 + pair * 128
+            first, second = gained[:, start : start + 128], gained[:, start + 256 : start + 384]
+            columns = slice(z * 128, z * 128 + 128)
             even = jnp.where(low, first, pltpu.roll(second, 64, 1))
             odd = jnp.where(low, pltpu.roll(first, 64, 1), second)
-            packed_ref[2 * tile, :, columns] = even.astype(jnp.bfloat16)
-            packed_ref[2 * tile + 1, :, columns] = odd.astype(jnp.bfloat16)
+            packed_ref[2 * pair, :, columns] = even.astype(jnp.bfloat16)
+            packed_ref[2 * pair + 1, :, columns] = odd.astype(jnp.bfloat16)
 
 
 def pack(hidden, gain):
@@ -70,44 +69,47 @@
 HELD = (0, -1, 1, 2)
 
 
-def project_kernel(residue_ref, tokens_ref, *refs):
+def project_kernel(place_ref, tokens_ref, *refs):
     held_refs, (out_ref, weight) = refs[: len(HELD)], refs[len(HELD) :]
 
     @pl.when(pl.program_id(0) == 0)
     def _():
         for held_ref, above in zip(held_refs, HELD, strict=True):
-            residue = lax.rem(residue_ref[0] + above + STEPS, STEPS)
+            residue = lax.rem(place_ref[0] + above + STEPS, STEPS)
             for at in range(PLANES // STEPS):
-                rows = pl.ds(pl.multiple_of((at * STEPS + residue) * 64, 64), 64)
-                weight[rows, :] = held_ref[at * 64 : at * 64 + 64, :]
+                for nth in range(SIDES):
+                    side = place_ref[1] if nth == 0 else 1 - place_ref[1]
+                    start = (at * STEPS + residue) * 128 + side * 64
+                    given = (at * SIDES + nth) * 64
+                    weight[pl.ds(pl.multiple_of(start, 64), 64), :] = held_ref[given : given + 64, :]
 
     tokens = tokens_ref[...].reshape(-1, tokens_ref.shape[-1])
     product = jnp.dot(tokens, weight[...], preferred_element_type=jnp.float32)
     out_ref[...] = product.astype(jnp.bfloat16).reshape(out_ref.shape)
 
 
-def project(residue, tokens, held):
-    peers, rows, features = tokens.shape
+def project(place, tokens, held):
+    sources, rows, features = tokens.shape
     width = held[0].shape[1]
-    whole = [pl.BlockSpec(part.shape, lambda i, residue: (0, 0)) for part in held]
+    whole = [pl.BlockSpec(part.shape, lambda i, place: (0, 0)) for part in held]
     return pl.pallas_call(
         project_kernel,
         grid_spec=pltpu.PrefetchScalarGridSpec(
             num_scalar_prefetch=1,
-            grid=(peers // SOURCES,),
-            in_specs=[pl.BlockSpec((SOURCES, rows, features), lambda i, residue: (i, 0, 0)), *whole],
-            out_specs=pl.BlockSpec((SOURCES, rows, width), lambda i, residue: (i, 0, 0)),
+            grid=(sources // SOURCES,),
+            in_specs=[pl.BlockSpec((SOURCES, rows, features), lambda i, place: (i, 0, 0)), *whole],
+            out_specs=pl.BlockSpec((SOURCES, rows, width), lambda i, place: (i, 0, 0)),
             scratch_shapes=[pltpu.VMEM((features, width), jnp.bfloat16)],
         ),
-        out_shape=pltpu.HBM((peers, rows, width), jnp.bfloat16),
+        out_shape=pltpu.HBM((sources, rows, width), jnp.bfloat16),
         compiler_params=pltpu.CompilerParams(vmem_limit_bytes=KERNEL_VMEM),
         cost_estimate=pl.CostEstimate(
-            flops=2 * peers * rows * features * width,
-            bytes_accessed=2 * (peers * rows * (features + width) + features * width),
+            flops=2 * sources * rows * features * width,
+            bytes_accessed=2 * (sources * rows * (features + width) + features * width),
             transcendentals=0,
         ),
         name="project_keys",
-    )(residue, tokens, *held)
+    )(place, tokens, *held)
 
 
 def moved(block, target):
@@ -123,9 +125,11 @@
     inner_layer = lax.dynamic_index_in_dim(inner_params[0], layer_idx, 0, keepdims=False)
     pseudo_grad = (outer_layer - inner_layer.astype(jnp.float32)).astype(jnp.bfloat16)
 
+    block = key_weight[0]
+    block = jnp.concatenate([block, lax.ppermute(block, "yh", [(0, 1), (1, 0)])], axis=0)
     packed, scale = pack(hidden_in[0], norm_gain[None])
-    packed, block = lax.optimization_barrier((packed, key_weight[0]))
-    tokens = lax.all_to_all(packed, PLANE, 0, 0, tiled=True)
+    packed, block, pseudo_grad = lax.optimization_barrier((packed, block, pseudo_grad))
+    tokens = lax.all_to_all(packed, ROW, 0, 0, tiled=True)
     own = lax.all_gather(block, "zh", axis=0, tiled=True)
     own, pseudo_grad = lax.optimization_barrier((own, pseudo_grad))
     held = (
@@ -138,10 +142,10 @@
     for other in range(1, replicas):
         pairs = [(replica, replica ^ other) for replica in range(replicas)]
         others.append(lax.ppermute(pseudo_grad, REP, pairs))
-    residue = lax.axis_index("zl").astype(jnp.int32)[None]
-    partial = project(residue, tokens, held)
+    place = jnp.stack([lax.axis_index(axis).astype(jnp.int32) for axis in ("zl", "yh")])
+    partial = project(place, tokens, held)
     partial, layer_idx, others = lax.optimization_barrier((partial, layer_idx, others))
-    partial = lax.all_to_all(partial, PLANE, 0, 0, tiled=True)
+    partial = lax.all_to_all(partial, ROW, 0, 0, tiled=True)
     outer_layer = lax.dynamic_index_in_dim(outer_params, layer_idx, 0, keepdims=False)
     moment_layer = lax.dynamic_index_in_dim(outer_moment, layer_idx, 0, keepdims=False)
     inner_layer = lax.dynamic_index_in_dim(inner_params[0], layer_idx, 0, keepdims=False)

time: 96.3 us -> 98.2 us (1.020)
  waiting for transfers between devices: 21 us -> 11.7 us
  starting transfers between devices: 33.9 us -> 39.4 us
  blocking collectives: 24.9 us -> 29.6 us
    all_to_all x2, waiting for transfers between devices: 21 us -> 8.15 us  [the longest x1 8.15 us: shards(): partial = lax.all_to_all(partial, ROW, 0, 0, tiled=True)]
    all_to_all x2, starting transfers between devices: 14.7 us -> 8.3 us  [the longest x1 4.27 us: shards(): partial = lax.all_to_all(partial, ROW, 0, 0, tiled=True)]
    ppermute x0 -> x1, starting transfers between devices: none -> 5.65 us  [shards(): lax.ppermute(block, 'yh', [(0, 1), (1, 0)])]
    ppermute x3, starting transfers between devices: 10.6 us -> 15.4 us  [shards(): others.append(lax.ppermute(pseudo_grad, REP, pairs))]
    all_gather x1, blocking collectives: 24.9 us -> 29.6 us  [shards(): own = lax.all_gather(block, 'zh', axis=0, tiled=True)]
    ppermute x3, waiting for transfers between devices: 0.01 us -> 3.58 us  [moved(): lax.ppermute(block, Z, [(z, target(z) % PLANES) for z in range(PLANES)])]
    ppermute x3, starting transfers between devices: 8.56 us -> 10.1 us  [moved(): lax.ppermute(block, Z, [(z, target(z) % PLANES) for z in range(PLANES)])]
    unnamed x4 -> x6, local copies, waits for them, and re-layouts: 2.64 us -> 2.64 us
  transfers between devices with their start and end apart: 8 -> 9, of which waited for: 1 -> 2; matrix products, arithmetic and copies ran while one was open for 4% -> 3% of each run, Pallas kernels for 4% -> 8%
where the time goes in v11:
time: 98.2 us; the launch traced here: 96.8 us
  starting transfers between devices  39.4 us (40%)
  blocking collectives  29.6 us (30%)
  waiting for transfers between devices  11.7 us (12%)
  Pallas kernels  8.13 us (8%)
  other arithmetic  3.77 us (4%)
  local copies, waits for them, and re-layouts  2.64 us (3%)
  between operations  1.41 us (1%)
    all_gather x1, blocking collectives, shards(): own = lax.all_gather(block, 'zh', axis=0, tiled=True)  29.6 us
    ppermute x3, starting transfers between devices, shards(): others.append(lax.ppermute(pseudo_grad, REP, pairs))  15.4 us
    ppermute x3, starting transfers between devices, moved(): lax.ppermute(block, Z, [(z, target(z) % PLANES) for z in range(PLANES)])  10.1 us
    all_to_all x1, waiting for transfers between devices, shards(): partial = lax.all_to_all(partial, ROW, 0, 0, tiled=True)  8.15 us
    ppermute x1, starting transfers between devices, shards(): lax.ppermute(block, 'yh', [(0, 1), (1, 0)])  5.65 us
    pallas_call x1, Pallas kernels, project(): pl.pallas_call(project_kernel, grid_spec=pltpu.PrefetchScalarGridSpec(num...  4.95 us
    all_to_all x1, starting transfers between devices, shards(): partial = lax.all_to_all(partial, ROW, 0, 0, tiled=True)  4.27 us
    all_to_all x1, starting transfers between devices, shards(): tokens = lax.all_to_all(packed, ROW, 0, 0, tiled=True)  4.02 us
  transfers between devices with their start and end apart: 9, of which 2 were waited for; matrix products, arithmetic and copies ran while one was open for 3% of the time, Pallas kernels for 8%

profile of v11, /device:TPU:1, one launch (start us, length us, event | category | flops | bytes accessed | tf_op | source)
XLA Modules:
  0.0 96.8 jit_solution(13305216170937114618)
XLA Ops:
  0.6 5.7 %collective-permute-start = (bf16[64,512]{1,0:T(8,128)(2,1)}, bf16[64,512]{1,0:T(8,128)(2,1)S(1)}, u32[]{:S(2)}, u32[]{:S(2)}) collective-permute-start(bf16[64,512]{1,0:T(8,128)(2,1)} %bitcast.34), channel_id=1, source_target_pairs={{0,4},{4,0},{1,5},{5,1},{2,6},{6,2},{3,7},{7,3},{8,12},{12,8},{9,1... | collective-permute-start | bytes 196616 | tf_op jit(solution)/shard_map/ppermute | solution.py:129
  6.9 0.0 copy-start
  6.9 1.9 %copy-done = bf16[1,192,8192]{2,1,0:T(8,128)(2,1)S(1)} copy-done((bf16[1,192,8192]{2,1,0:T(8,128)(2,1)S(1)}, bf16[1,192,8192]{2,1,0:T(8,128)(2,1)}, u32[]{:S(2)}) %copy-start) | copy-done | bytes 3145752
  8.8 0.0 copy-start.1
  8.8 0.8 copy-done.1
  9.6 0.0 copy-start.2
  9.6 3.2 %pack_hidden.1 = (bf16[4,192,2048]{2,1,0:T(8,128)(2,1)}, f32[192,1]{1,0:T(8,128)S(1)}) custom-call(bf16[192,8192]{1,0:T(8,128)(2,1)S(1)} %bitcast.32, f32[1,8192]{1,0:T(1,128)S(1)} %bitcast.33), custom_call_target="tpu_custom_call" | custom-call | flops 6291456 | bytes 6291456 | tf_op jit(solution)/shard_map/pack_hidden/pallas_call | solution.py:45
  12.8 0.9 fusion.3
  13.7 0.0 collective-permute-done
  13.7 0.0 copy-done.2
  13.7 4.0 %all-to-all-start = ((bf16[4,192,2048]{2,1,0:T(8,128)(2,1)}), bf16[4,192,2048]{2,1,0:T(8,128)(2,1)S(1)}, u32[]{:S(2)}, u32[]{:S(2)}) async-start(bf16[4,192,2048]{2,1,0:T(8,128)(2,1)} %get-tuple-element.17), calls=%async_computation | async-start | bytes 6291456 | tf_op jit(solution)/shard_map/all_to_all | solution.py:132
  17.8 29.6 %all_gather.3.refs_0_ = bf16[512,512]{1,0:T(8,128)(2,1)} all-gather(bf16[128,512]{1,0:T(8,128)(2,1)S(1)} %pad_maximum_fusion), channel_id=1, replica_groups=mesh['yl'=2,'core'=2,'zh'=4,'zl'=4,'yh'=2,'x'=4] {'zh'}, dimensions={0}, use_global_device_ids=true | all-gather | bytes 655360 | tf_op jit(solution)/shard_map/all_gather | solution.py:133
  47.4 4.6 %collective-permute-start.3 = (bf16[512,512]{1,0:T(8,128)(2,1)}, bf16[512,512]{1,0:T(8,128)(2,1)}, u32[]{:S(2)}, u32[]{:S(2)}) collective-permute-start(bf16[512,512]{1,0:T(8,128)(2,1)} %all_gather.3.refs_0_), channel_id=1, source_target_pairs={{0,16},{8,120},{16,32},{24,8},{32,48},{40,24},{48,64},{56,40},{64,... | collective-permute-start | bytes 1572872 | tf_op jit(solution)/shard_map/ppermute | solution.py:116
  52.0 2.5 %collective-permute-start.2 = (bf16[512,512]{1,0:T(8,128)(2,1)}, bf16[512,512]{1,0:T(8,128)(2,1)}, u32[]{:S(2)}, u32[]{:S(2)}) collective-permute-start(bf16[512,512]{1,0:T(8,128)(2,1)} %all_gather.3.refs_0_), channel_id=1, source_target_pairs={{0,120},{8,0},{16,8},{24,16},{32,24},{40,32},{48,40},{56,48},{64,5... | collective-permute-start | bytes 1572872 | tf_op jit(solution)/shard_map/ppermute | solution.py:116
  54.4 3.1 %collective-permute-start.1 = (bf16[512,512]{1,0:T(8,128)(2,1)}, bf16[512,512]{1,0:T(8,128)(2,1)}, u32[]{:S(2)}, u32[]{:S(2)}) collective-permute-start(bf16[512,512]{1,0:T(8,128)(2,1)} %all_gather.3.refs_0_), channel_id=1, source_target_pairs={{0,8},{8,16},{16,24},{24,32},{32,40},{40,48},{48,56},{56,64},{64,7... | collective-permute-start | bytes 1572872 | tf_op jit(solution)/shard_map/ppermute | solution.py:116
  57.5 0.1 pad_add_fusion.place_ref
  57.6 6.7 %collective-permute-start.6 = (bf16[64,512]{1,0:T(8,128)(2,1)S(1)}, bf16[64,512]{1,0:T(8,128)(2,1)S(1)}, u32[]{:S(2)}, u32[]{:S(2)}) collective-permute-start(bf16[64,512]{1,0:T(8,128)(2,1)S(1)} %fusion.3), channel_id=1, source_target_pairs={{0,384},{128,256},{256,128},{384,0},{1,385},{129,257},{257,129},{3... | collective-permute-start | bytes 196616 | tf_op jit(solution)/shard_map/ppermute | solution.py:144
  64.3 3.0 %collective-permute-start.5 = (bf16[64,512]{1,0:T(8,128)(2,1)S(1)}, bf16[64,512]{1,0:T(8,128)(2,1)S(1)}, u32[]{:S(2)}, u32[]{:S(2)}) collective-permute-start(bf16[64,512]{1,0:T(8,128)(2,1)S(1)} %fusion.3), channel_id=1, source_target_pairs={{0,256},{128,384},{256,0},{384,128},{1,257},{129,385},{257,1},{385... | collective-permute-start | bytes 196616 | tf_op jit(solution)/shard_map/ppermute | solution.py:144
  67.3 0.0 collective-permute-done.3.refs_3_
  67.3 5.7 %collective-permute-start.4 = (bf16[64,512]{1,0:T(8,128)(2,1)S(1)}, bf16[64,512]{1,0:T(8,128)(2,1)S(1)}, u32[]{:S(2)}, u32[]{:S(2)}) collective-permute-start(bf16[64,512]{1,0:T(8,128)(2,1)S(1)} %fusion.3), channel_id=1, source_target_pairs={{0,128},{128,0},{256,384},{384,256},{1,129},{129,1},{257,385},{385... | collective-permute-start | bytes 196616 | tf_op jit(solution)/shard_map/ppermute | solution.py:144
  73.0 3.6 %collective-permute-done.2.refs_2_ = bf16[512,512]{1,0:T(8,128)(2,1)} collective-permute-done((bf16[512,512]{1,0:T(8,128)(2,1)}, bf16[512,512]{1,0:T(8,128)(2,1)}, u32[]{:S(2)}, u32[]{:S(2)}) %collective-permute-start.2) | collective-permute-done | bytes 524320 | tf_op jit(solution)/shard_map/ppermute | solution.py:116
  76.6 0.0 collective-permute-done.1.refs_1_
  76.6 0.0 all-to-all-done.tokens_ref
  76.6 4.9 %project_keys.1 = bf16[4,192,512]{2,1,0:T(8,128)(2,1)} custom-call(s32[2]{0:T(128)S(1)} %pad_add_fusion.place_ref, bf16[4,192,2048]{2,1,0:T(8,128)(2,1)S(1)} %all-to-all-done.tokens_ref, bf16[512,512]{1,0:T(8,128)(2,1)} %all_gather.3.refs_0_, bf16[512,512]{1,0:T(8,128)(2,1)} %collective-permute-done.1.refs_1_, ...), custom_call_target="tpu_custom_call" | custom-call | flops 1610612736 | bytes 6029312 | tf_op jit(solution)/shard_map/project_keys/pallas_call | solution.py:95
  81.5 0.0 collective-permute-done.6
  81.5 0.0 collective-permute-done.5
  81.5 0.0 collective-permute-done.4
  81.6 4.3 %all-to-all-start.1 = ((bf16[4,192,512]{2,1,0:T(8,128)(2,1)}), bf16[4,192,512]{2,1,0:T(8,128)(2,1)S(1)}, u32[]{:S(2)}, u32[]{:S(2)}) async-start(bf16[4,192,512]{2,1,0:T(8,128)(2,1)} %project_keys.1), calls=%async_computation.1 | async-start | bytes 1572864 | tf_op jit(solution)/shard_map/all_to_all | solution.py:148
  85.8 0.1 reduce
  85.9 1.8 %fusion.4 = (bf16[1,64,512]{2,1,0:T(8,128)(2,1)}, f32[64,512]{1,0:T(8,128)}, f32[64,512]{1,0:T(8,128)}) fusion(bf16[1,7,64,512]{3,2,1,0:T(8,128)(2,1)} %param.13, s32[]{:T(128)S(6)} %select_n.12, bf16[64,512]{1,0:T(8,128)(2,1)S(1)} %collective-permute-done.6, bf16[64,512]{1,0:T(8,128)(2,1)S(1)} %collective-permute-done.5, ...), kind=kLoop, calls=%fused_computation.12 | loop fusion | flops 589824 | bytes 917508 | tf_op jit(solution)/shard_map/broadcast_in_dim | solution.py:158
  87.7 8.1 %all-to-all-done.1 = bf16[4,192,512]{2,1,0:T(8,128)(2,1)S(1)} async-done(((bf16[4,192,512]{2,1,0:T(8,128)(2,1)}), bf16[4,192,512]{2,1,0:T(8,128)(2,1)S(1)}, u32[]{:S(2)}, u32[]{:S(2)}) %all-to-all-start.1) | async-done | bytes 786464 | tf_op jit(solution)/shard_map/all_to_all | solution.py:148
  95.9 0.1 convert_reduce_fusion
  96.0 0.8 fusion
  (1 shorter events, 0.0 us)
Async XLA Ops:
  0.6 13.1 %collective-permute-start = (bf16[64,512]{1,0:T(8,128)(2,1)}, bf16[64,512]{1,0:T(8,128)(2,1)S(1)}, u32[]{:S(2)}, u32[]{:S(2)}) collective-permute-start(bf16[64,512]{1,0:T(8,128)(2,1)} %bitcast.34), channel_id=1, source_target_pairs={{0,4},{4,0},{1,5},{5,1},{2,6},{6,2},{3,7},{7,3},{8,12},{12,8},{9,1... | collective-permute-start | bytes 196616 | tf_op jit(solution)/shard_map/ppermute | solution.py:129
  6.9 1.9 %copy-start = (bf16[1,192,8192]{2,1,0:T(8,128)(2,1)S(1)}, bf16[1,192,8192]{2,1,0:T(8,128)(2,1)}, u32[]{:S(2)}) copy-start(bf16[1,192,8192]{2,1,0:T(8,128)(2,1)} %param.7) | copy-start | bytes 9437188
  8.8 0.8 copy-start.1
  9.6 4.1 %copy-start.2 = (bf16[1,64,512]{2,1,0:T(8,128)(2,1)S(1)}, bf16[1,64,512]{2,1,0:T(8,128)(2,1)}, u32[]{:S(2)}) copy-start(bf16[1,64,512]{2,1,0:T(8,128)(2,1)} %param.9) | copy-start | bytes 196612
  13.7 62.8 %all-to-all-start = ((bf16[4,192,2048]{2,1,0:T(8,128)(2,1)}), bf16[4,192,2048]{2,1,0:T(8,128)(2,1)S(1)}, u32[]{:S(2)}, u32[]{:S(2)}) async-start(bf16[4,192,2048]{2,1,0:T(8,128)(2,1)} %get-tuple-element.17), calls=%async_computation | async-start | bytes 6291456 | tf_op jit(solution)/shard_map/all_to_all | solution.py:132
  47.4 19.9 %collective-permute-start.3 = (bf16[512,512]{1,0:T(8,128)(2,1)}, bf16[512,512]{1,0:T(8,128)(2,1)}, u32[]{:S(2)}, u32[]{:S(2)}) collective-permute-start(bf16[512,512]{1,0:T(8,128)(2,1)} %all_gather.3.refs_0_), channel_id=1, source_target_pairs={{0,16},{8,120},{16,32},{24,8},{32,48},{40,24},{48,64},{56,40},{64,... | collective-permute-start | bytes 1572872 | tf_op jit(solution)/shard_map/ppermute | solution.py:116
  52.0 24.6 %collective-permute-start.2 = (bf16[512,512]{1,0:T(8,128)(2,1)}, bf16[512,512]{1,0:T(8,128)(2,1)}, u32[]{:S(2)}, u32[]{:S(2)}) collective-permute-start(bf16[512,512]{1,0:T(8,128)(2,1)} %all_gather.3.refs_0_), channel_id=1, source_target_pairs={{0,120},{8,0},{16,8},{24,16},{32,24},{40,32},{48,40},{56,48},{64,5... | collective-permute-start | bytes 1572872 | tf_op jit(solution)/shard_map/ppermute | solution.py:116
  54.4 22.1 %collective-permute-start.1 = (bf16[512,512]{1,0:T(8,128)(2,1)}, bf16[512,512]{1,0:T(8,128)(2,1)}, u32[]{:S(2)}, u32[]{:S(2)}) collective-permute-start(bf16[512,512]{1,0:T(8,128)(2,1)} %all_gather.3.refs_0_), channel_id=1, source_target_pairs={{0,8},{8,16},{16,24},{24,32},{32,40},{40,48},{48,56},{56,64},{64,7... | collective-permute-start | bytes 1572872 | tf_op jit(solution)/shard_map/ppermute | solution.py:116
  57.6 23.9 %collective-permute-start.6 = (bf16[64,512]{1,0:T(8,128)(2,1)S(1)}, bf16[64,512]{1,0:T(8,128)(2,1)S(1)}, u32[]{:S(2)}, u32[]{:S(2)}) collective-permute-start(bf16[64,512]{1,0:T(8,128)(2,1)S(1)} %fusion.3), channel_id=1, source_target_pairs={{0,384},{128,256},{256,128},{384,0},{1,385},{129,257},{257,129},{3... | collective-permute-start | bytes 196616 | tf_op jit(solution)/shard_map/ppermute | solution.py:144
  64.3 17.2 %collective-permute-start.5 = (bf16[64,512]{1,0:T(8,128)(2,1)S(1)}, bf16[64,512]{1,0:T(8,128)(2,1)S(1)}, u32[]{:S(2)}, u32[]{:S(2)}) collective-permute-start(bf16[64,512]{1,0:T(8,128)(2,1)S(1)} %fusion.3), channel_id=1, source_target_pairs={{0,256},{128,384},{256,0},{384,128},{1,257},{129,385},{257,1},{385... | collective-permute-start | bytes 196616 | tf_op jit(solution)/shard_map/ppermute | solution.py:144
  67.3 14.2 %collective-permute-start.4 = (bf16[64,512]{1,0:T(8,128)(2,1)S(1)}, bf16[64,512]{1,0:T(8,128)(2,1)S(1)}, u32[]{:S(2)}, u32[]{:S(2)}) collective-permute-start(bf16[64,512]{1,0:T(8,128)(2,1)S(1)} %fusion.3), channel_id=1, source_target_pairs={{0,128},{128,0},{256,384},{384,256},{1,129},{129,1},{257,385},{385... | collective-permute-start | bytes 196616 | tf_op jit(solution)/shard_map/ppermute | solution.py:144
  81.6 14.3 %all-to-all-start.1 = ((bf16[4,192,512]{2,1,0:T(8,128)(2,1)}), bf16[4,192,512]{2,1,0:T(8,128)(2,1)S(1)}, u32[]{:S(2)}, u32[]{:S(2)}) async-start(bf16[4,192,512]{2,1,0:T(8,128)(2,1)} %project_keys.1), calls=%async_computation.1 | async-start | bytes 1572864 | tf_op jit(solution)/shard_map/all_to_all | solution.py:148

commit v12 on v11

--- a/solution.py
+++ b/solution.py
@@ -66,7 +66,7 @@
 
 
 STEPS = 4
-HELD = (0, -1, 1, 2)
+HELD = tuple((above, side) for side in range(SIDES) for above in (0, 2, -1, 1))
 
 
 def project_kernel(place_ref, tokens_ref, *refs):
@@ -74,14 +74,13 @@
 
     @pl.when(pl.program_id(0) == 0)
     def _():
-        for held_ref, above in zip(held_refs, HELD, strict=True):
+        for held_ref, (above, other) in zip(held_refs, HELD, strict=True):
             residue = lax.rem(place_ref[0] + above + STEPS, STEPS)
+            side = 1 - place_ref[1] if other else place_ref[1]
             for at in range(PLANES // STEPS):
-                for nth in range(SIDES):
-                    side = place_ref[1] if nth == 0 else 1 - place_ref[1]
-                    start = (at * STEPS + residue) * 128 + side * 64
-                    given = (at * SIDES + nth) * 64
-                    weight[pl.ds(pl.multiple_of(start, 64), 64), :] = held_ref[given : given + 64, :]
+                start = (at * STEPS + residue) * 128 + side * 64
+                rows = pl.ds(pl.multiple_of(start, 64), 64)
+                weight[rows, :] = held_ref[at * 64 : at * 64 + 64, :]
 
     tokens = tokens_ref[...].reshape(-1, tokens_ref.shape[-1])
     product = jnp.dot(tokens, weight[...], preferred_element_type=jnp.float32)
@@ -125,19 +124,18 @@
     inner_layer = lax.dynamic_index_in_dim(inner_params[0], layer_idx, 0, keepdims=False)
     pseudo_grad = (outer_layer - inner_layer.astype(jnp.float32)).astype(jnp.bfloat16)
 
-    block = key_weight[0]
-    block = jnp.concatenate([block, lax.ppermute(block, "yh", [(0, 1), (1, 0)])], axis=0)
     packed, scale = pack(hidden_in[0], norm_gain[None])
-    packed, block, pseudo_grad = lax.optimization_barrier((packed, block, pseudo_grad))
+    packed, block, pseudo_grad = lax.optimization_barrier((packed, key_weight[0], pseudo_grad))
     tokens = lax.all_to_all(packed, ROW, 0, 0, tiled=True)
     own = lax.all_gather(block, "zh", axis=0, tiled=True)
-    own, pseudo_grad = lax.optimization_barrier((own, pseudo_grad))
-    held = (
+    held = [
         own,
+        moved(own, lambda z: z + 2 if z % 2 == 0 else z - 2),
         moved(own, lambda z: z + 1),
         moved(own, lambda z: z - 1),
-        moved(own, lambda z: z + 2 if z % 2 == 0 else z - 2),
-    )
+    ]
+    held += [lax.ppermute(part, "yh", [(0, 1), (1, 0)]) for part in held]
+    own, pseudo_grad = lax.optimization_barrier((held[3], pseudo_grad))
     others = []
     for other in range(1, replicas):
         pairs = [(replica, replica ^ other) for replica in range(replicas)]

time: 98.2 us -> 99.2 us (1.010)
  the two profiles are of different devices: /device:TPU:1 before, /device:TPU:32 now
where the time goes in v12:
time: 99.2 us; the launch traced here: 98.5 us
  starting transfers between devices  42.8 us (43%)
  blocking collectives  25.9 us (26%)
  waiting for transfers between devices  13.1 us (13%)
  Pallas kernels  8.05 us (8%)
  other arithmetic  4.53 us (5%)
  local copies, waits for them, and re-layouts  2.64 us (3%)
  between operations  1.44 us (1%)
    all_gather x1, blocking collectives, shards(): own = lax.all_gather(block, 'zh', axis=0, tiled=True)  25.9 us
    ppermute x4, starting transfers between devices, shards(): held += [lax.ppermute(part, 'yh', [(0, 1), (1, 0)]) for part in held]  14.7 us
    ppermute x3, starting transfers between devices, moved(): lax.ppermute(block, Z, [(z, target(z) % PLANES) for z in range(PLANES)])  11.2 us
    ppermute x3, starting transfers between devices, shards(): others.append(lax.ppermute(pseudo_grad, REP, pairs))  7.58 us
    all_to_all x1, waiting for transfers between devices, shards(): partial = lax.all_to_all(partial, ROW, 0, 0, tiled=True)  7.45 us
    ppermute x4, waiting for transfers between devices, shards(): held += [lax.ppermute(part, 'yh', [(0, 1), (1, 0)]) for part in held]  5.67 us
    all_to_all x1, starting transfers between devices, shards(): partial = lax.all_to_all(partial, ROW, 0, 0, tiled=True)  4.96 us
    pallas_call x1, Pallas kernels, project(): pl.pallas_call(project_kernel, grid_spec=pltpu.PrefetchScalarGridSpec(num...  4.88 us
  transfers between devices with their start and end apart: 12, of which 3 were waited for; matrix products, arithmetic and copies ran while one was open for 2% of the time, Pallas kernels for 5%

profile of v12, /device:TPU:32, one launch (start us, length us, event | category | flops | bytes accessed | tf_op | source)
XLA Modules:
  0.0 98.5 jit_solution(15890435327326196060)
XLA Ops:
  1.3 0.0 copy-start
  1.3 1.9 %copy-done = bf16[1,192,8192]{2,1,0:T(8,128)(2,1)S(1)} copy-done((bf16[1,192,8192]{2,1,0:T(8,128)(2,1)S(1)}, bf16[1,192,8192]{2,1,0:T(8,128)(2,1)}, u32[]{:S(2)}) %copy-start) | copy-done | bytes 3145752
  3.2 0.0 copy-start.1
  3.2 0.8 copy-done.1
  3.9 3.2 %pack_hidden.1 = (bf16[4,192,2048]{2,1,0:T(8,128)(2,1)}, f32[192,1]{1,0:T(8,128)S(1)}) custom-call(bf16[192,8192]{1,0:T(8,128)(2,1)S(1)} %bitcast.32, f32[1,8192]{1,0:T(1,128)S(1)} %bitcast.33), custom_call_target="tpu_custom_call" | custom-call | flops 6291456 | bytes 6291456 | tf_op jit(solution)/shard_map/pack_hidden/pallas_call | solution.py:45
  7.1 1.5 %fusion.3 = bf16[64,512]{1,0:T(8,128)(2,1)} fusion(f32[7,64,512]{2,1,0:T(8,128)} %param.11, s32[]{:T(128)S(6)} %select_n.11, bf16[1,7,64,512]{3,2,1,0:T(8,128)(2,1)} %param.13), kind=kLoop, calls=%fused_computation.7 | loop fusion | flops 98304 | bytes 262148 | tf_op jit(solution)/shard_map/convert_element_type | solution.py:125
  8.6 4.3 %all-to-all-start = ((bf16[4,192,2048]{2,1,0:T(8,128)(2,1)}), bf16[4,192,2048]{2,1,0:T(8,128)(2,1)S(1)}, u32[]{:S(2)}, u32[]{:S(2)}) async-start(bf16[4,192,2048]{2,1,0:T(8,128)(2,1)} %get-tuple-element.16), calls=%async_computation | async-start | bytes 6291456 | tf_op jit(solution)/shard_map/all_to_all | solution.py:129
  12.9 25.9 %all_gather.3.refs_0_ = bf16[256,512]{1,0:T(8,128)(2,1)S(1)} all-gather(bf16[64,512]{1,0:T(8,128)(2,1)} %bitcast.34), channel_id=1, replica_groups=mesh['yl'=2,'core'=2,'zh'=4,'zl'=4,'yh'=2,'x'=4] {'zh'}, dimensions={0}, use_global_device_ids=true | all-gather | bytes 327680 | tf_op jit(solution)/shard_map/all_gather | solution.py:130
  38.8 2.8 %collective-permute-start.2 = (bf16[256,512]{1,0:T(8,128)(2,1)S(1)}, bf16[256,512]{1,0:T(8,128)(2,1)}, u32[]{:S(2)}, u32[]{:S(2)}) collective-permute-start(bf16[256,512]{1,0:T(8,128)(2,1)S(1)} %all_gather.3.refs_0_), channel_id=1, source_target_pairs={{0,120},{8,0},{16,8},{24,16},{32,24},{40,32},{48,40},{56,48},{64,5... | collective-permute-start | bytes 786440 | tf_op jit(solution)/shard_map/ppermute | solution.py:115
  41.7 3.0 %collective-permute-start.1 = (bf16[256,512]{1,0:T(8,128)(2,1)S(1)}, bf16[256,512]{1,0:T(8,128)(2,1)}, u32[]{:S(2)}, u32[]{:S(2)}) collective-permute-start(bf16[256,512]{1,0:T(8,128)(2,1)S(1)} %all_gather.3.refs_0_), channel_id=1, source_target_pairs={{0,8},{8,16},{16,24},{24,32},{32,40},{40,48},{48,56},{56,64},{64,7... | collective-permute-start | bytes 786440 | tf_op jit(solution)/shard_map/ppermute | solution.py:115
  44.7 5.4 %collective-permute-start = (bf16[256,512]{1,0:T(8,128)(2,1)S(1)}, bf16[256,512]{1,0:T(8,128)(2,1)}, u32[]{:S(2)}, u32[]{:S(2)}) collective-permute-start(bf16[256,512]{1,0:T(8,128)(2,1)S(1)} %all_gather.3.refs_0_), channel_id=1, source_target_pairs={{0,16},{8,120},{16,32},{24,8},{32,48},{40,24},{48,64},{56,40},{64,... | collective-permute-start | bytes 786440 | tf_op jit(solution)/shard_map/ppermute | solution.py:115
  50.1 5.1 %collective-permute-start.3 = (bf16[256,512]{1,0:T(8,128)(2,1)S(1)}, bf16[256,512]{1,0:T(8,128)(2,1)}, u32[]{:S(2)}, u32[]{:S(2)}) collective-permute-start(bf16[256,512]{1,0:T(8,128)(2,1)S(1)} %all_gather.3.refs_0_), channel_id=1, source_target_pairs={{0,4},{4,0},{1,5},{5,1},{2,6},{6,2},{3,7},{7,3},{8,12},{12,8},{9,1... | collective-permute-start | bytes 786440 | tf_op jit(solution)/shard_map/ppermute | solution.py:137
  55.2 0.0 collective-permute-done.2.refs_3_
  55.2 2.2 %collective-permute-start.6 = (bf16[256,512]{1,0:T(8,128)(2,1)}, bf16[256,512]{1,0:T(8,128)(2,1)}, u32[]{:S(2)}, u32[]{:S(2)}) collective-permute-start(bf16[256,512]{1,0:T(8,128)(2,1)} %collective-permute-done.2.refs_3_), channel_id=1, source_target_pairs={{0,4},{4,0},{1,5},{5,1},{2,6},{6,2},{3,7},{7,3},{8,12},{12,8},{9,1... | collective-permute-start | bytes 786440 | tf_op jit(solution)/shard_map/ppermute | solution.py:137
  57.5 0.0 collective-permute-done.1.refs_2_
  57.5 5.1 %collective-permute-start.5 = (bf16[256,512]{1,0:T(8,128)(2,1)}, bf16[256,512]{1,0:T(8,128)(2,1)}, u32[]{:S(2)}, u32[]{:S(2)}) collective-permute-start(bf16[256,512]{1,0:T(8,128)(2,1)} %collective-permute-done.1.refs_2_), channel_id=1, source_target_pairs={{0,4},{4,0},{1,5},{5,1},{2,6},{6,2},{3,7},{7,3},{8,12},{12,8},{9,1... | collective-permute-start | bytes 786440 | tf_op jit(solution)/shard_map/ppermute | solution.py:137
  62.6 0.0 collective-permute-done.refs_1_
  62.6 2.2 %collective-permute-start.4 = (bf16[256,512]{1,0:T(8,128)(2,1)}, bf16[256,512]{1,0:T(8,128)(2,1)}, u32[]{:S(2)}, u32[]{:S(2)}) collective-permute-start(bf16[256,512]{1,0:T(8,128)(2,1)} %collective-permute-done.refs_1_), channel_id=1, source_target_pairs={{0,4},{4,0},{1,5},{5,1},{2,6},{6,2},{3,7},{7,3},{8,12},{12,8},{9,1... | collective-permute-start | bytes 786440 | tf_op jit(solution)/shard_map/ppermute | solution.py:137
  64.8 0.1 pad_add_fusion.place_ref
  64.9 1.9 %collective-permute-start.9 = (bf16[64,512]{1,0:T(8,128)(2,1)}, bf16[64,512]{1,0:T(8,128)(2,1)}, u32[]{:S(2)}, u32[]{:S(2)}) collective-permute-start(bf16[64,512]{1,0:T(8,128)(2,1)} %fusion.3), channel_id=1, source_target_pairs={{0,384},{128,256},{256,128},{384,0},{1,385},{129,257},{257,129},{3... | collective-permute-start | bytes 196616 | tf_op jit(solution)/shard_map/ppermute | solution.py:142
  66.8 0.0 collective-permute-done.3.refs_4_
  66.9 3.5 %collective-permute-start.8 = (bf16[64,512]{1,0:T(8,128)(2,1)}, bf16[64,512]{1,0:T(8,128)(2,1)}, u32[]{:S(2)}, u32[]{:S(2)}) collective-permute-start(bf16[64,512]{1,0:T(8,128)(2,1)} %fusion.3), channel_id=1, source_target_pairs={{0,256},{128,384},{256,0},{384,128},{1,257},{129,385},{257,1},{385... | collective-permute-start | bytes 196616 | tf_op jit(solution)/shard_map/ppermute | solution.py:142
  70.3 0.0 collective-permute-done.6.refs_7_
  70.4 2.2 %collective-permute-start.7 = (bf16[64,512]{1,0:T(8,128)(2,1)}, bf16[64,512]{1,0:T(8,128)(2,1)}, u32[]{:S(2)}, u32[]{:S(2)}) collective-permute-start(bf16[64,512]{1,0:T(8,128)(2,1)} %fusion.3), channel_id=1, source_target_pairs={{0,128},{128,0},{256,384},{384,256},{1,129},{129,1},{257,385},{385... | collective-permute-start | bytes 196616 | tf_op jit(solution)/shard_map/ppermute | solution.py:142
  72.5 1.4 %collective-permute-done.5.refs_6_ = bf16[256,512]{1,0:T(8,128)(2,1)} collective-permute-done((bf16[256,512]{1,0:T(8,128)(2,1)}, bf16[256,512]{1,0:T(8,128)(2,1)}, u32[]{:S(2)}, u32[]{:S(2)}) %collective-permute-start.5) | collective-permute-done | bytes 262176 | tf_op jit(solution)/shard_map/ppermute | solution.py:137
  73.9 4.3 %collective-permute-done.4.refs_5_ = bf16[256,512]{1,0:T(8,128)(2,1)} collective-permute-done((bf16[256,512]{1,0:T(8,128)(2,1)}, bf16[256,512]{1,0:T(8,128)(2,1)}, u32[]{:S(2)}, u32[]{:S(2)}) %collective-permute-start.4) | collective-permute-done | bytes 262176 | tf_op jit(solution)/shard_map/ppermute | solution.py:137
  78.2 0.0 all-to-all-done.tokens_ref
  78.2 4.9 %project_keys.1 = bf16[4,192,512]{2,1,0:T(8,128)(2,1)} custom-call(s32[2]{0:T(128)S(1)} %pad_add_fusion.place_ref, bf16[4,192,2048]{2,1,0:T(8,128)(2,1)S(1)} %all-to-all-done.tokens_ref, bf16[256,512]{1,0:T(8,128)(2,1)S(1)} %all_gather.3.refs_0_, bf16[256,512]{1,0:T(8,128)(2,1)} %collective-permute-done.refs_1_, ...), custom_call_target="tpu_custom_call" | custom-call | flops 1610612736 | bytes 6029312 | tf_op jit(solution)/shard_map/project_keys/pallas_call | solution.py:94
  83.1 0.0 collective-permute-done.9
  83.1 0.0 collective-permute-done.8
  83.1 0.0 collective-permute-done.7
  83.1 5.0 %all-to-all-start.1 = ((bf16[4,192,512]{2,1,0:T(8,128)(2,1)}), bf16[4,192,512]{2,1,0:T(8,128)(2,1)S(1)}, u32[]{:S(2)}, u32[]{:S(2)}) async-start(bf16[4,192,512]{2,1,0:T(8,128)(2,1)} %project_keys.1), calls=%async_computation.1 | async-start | bytes 1572864 | tf_op jit(solution)/shard_map/all_to_all | solution.py:146
  88.1 0.1 reduce
  88.2 1.9 %fusion.4 = (bf16[1,64,512]{2,1,0:T(8,128)(2,1)}, f32[64,512]{1,0:T(8,128)}, f32[64,512]{1,0:T(8,128)}) fusion(bf16[1,7,64,512]{3,2,1,0:T(8,128)(2,1)} %param.13, s32[]{:T(128)S(6)} %select_n.12, bf16[64,512]{1,0:T(8,128)(2,1)} %collective-permute-done.9, bf16[64,512]{1,0:T(8,128)(2,1)} %collective-permute-done.8, ...), kind=kLoop, calls=%fused_computation.11 | loop fusion | flops 589824 | bytes 917508 | tf_op jit(solution)/shard_map/broadcast_in_dim | solution.py:156
  90.1 7.5 %all-to-all-done.1 = bf16[4,192,512]{2,1,0:T(8,128)(2,1)S(1)} async-done(((bf16[4,192,512]{2,1,0:T(8,128)(2,1)}), bf16[4,192,512]{2,1,0:T(8,128)(2,1)S(1)}, u32[]{:S(2)}, u32[]{:S(2)}) %all-to-all-start.1) | async-done | bytes 786464 | tf_op jit(solution)/shard_map/all_to_all | solution.py:146
  97.6 0.1 convert_reduce_fusion
  97.7 0.8 fusion
Async XLA Ops:
  1.3 1.9 %copy-start = (bf16[1,192,8192]{2,1,0:T(8,128)(2,1)S(1)}, bf16[1,192,8192]{2,1,0:T(8,128)(2,1)}, u32[]{:S(2)}) copy-start(bf16[1,192,8192]{2,1,0:T(8,128)(2,1)} %param.7) | copy-start | bytes 9437188
  3.2 0.8 copy-start.1
  8.6 69.6 %all-to-all-start = ((bf16[4,192,2048]{2,1,0:T(8,128)(2,1)}), bf16[4,192,2048]{2,1,0:T(8,128)(2,1)S(1)}, u32[]{:S(2)}, u32[]{:S(2)}) async-start(bf16[4,192,2048]{2,1,0:T(8,128)(2,1)} %get-tuple-element.16), calls=%async_computation | async-start | bytes 6291456 | tf_op jit(solution)/shard_map/all_to_all | solution.py:129
  38.8 16.4 %collective-permute-start.2 = (bf16[256,512]{1,0:T(8,128)(2,1)S(1)}, bf16[256,512]{1,0:T(8,128)(2,1)}, u32[]{:S(2)}, u32[]{:S(2)}) collective-permute-start(bf16[256,512]{1,0:T(8,128)(2,1)S(1)} %all_gather.3.refs_0_), channel_id=1, source_target_pairs={{0,120},{8,0},{16,8},{24,16},{32,24},{40,32},{48,40},{56,48},{64,5... | collective-permute-start | bytes 786440 | tf_op jit(solution)/shard_map/ppermute | solution.py:115
  41.7 15.8 %collective-permute-start.1 = (bf16[256,512]{1,0:T(8,128)(2,1)S(1)}, bf16[256,512]{1,0:T(8,128)(2,1)}, u32[]{:S(2)}, u32[]{:S(2)}) collective-permute-start(bf16[256,512]{1,0:T(8,128)(2,1)S(1)} %all_gather.3.refs_0_), channel_id=1, source_target_pairs={{0,8},{8,16},{16,24},{24,32},{32,40},{40,48},{48,56},{56,64},{64,7... | collective-permute-start | bytes 786440 | tf_op jit(solution)/shard_map/ppermute | solution.py:115
  44.7 17.9 %collective-permute-start = (bf16[256,512]{1,0:T(8,128)(2,1)S(1)}, bf16[256,512]{1,0:T(8,128)(2,1)}, u32[]{:S(2)}, u32[]{:S(2)}) collective-permute-start(bf16[256,512]{1,0:T(8,128)(2,1)S(1)} %all_gather.3.refs_0_), channel_id=1, source_target_pairs={{0,16},{8,120},{16,32},{24,8},{32,48},{40,24},{48,64},{56,40},{64,... | collective-permute-start | bytes 786440 | tf_op jit(solution)/shard_map/ppermute | solution.py:115
  50.1 16.8 %collective-permute-start.3 = (bf16[256,512]{1,0:T(8,128)(2,1)S(1)}, bf16[256,512]{1,0:T(8,128)(2,1)}, u32[]{:S(2)}, u32[]{:S(2)}) collective-permute-start(bf16[256,512]{1,0:T(8,128)(2,1)S(1)} %all_gather.3.refs_0_), channel_id=1, source_target_pairs={{0,4},{4,0},{1,5},{5,1},{2,6},{6,2},{3,7},{7,3},{8,12},{12,8},{9,1... | collective-permute-start | bytes 786440 | tf_op jit(solution)/shard_map/ppermute | solution.py:137
  55.2 15.1 %collective-permute-start.6 = (bf16[256,512]{1,0:T(8,128)(2,1)}, bf16[256,512]{1,0:T(8,128)(2,1)}, u32[]{:S(2)}, u32[]{:S(2)}) collective-permute-start(bf16[256,512]{1,0:T(8,128)(2,1)} %collective-permute-done.2.refs_3_), channel_id=1, source_target_pairs={{0,4},{4,0},{1,5},{5,1},{2,6},{6,2},{3,7},{7,3},{8,12},{12,8},{9,1... | collective-permute-start | bytes 786440 | tf_op jit(solution)/shard_map/ppermute | solution.py:137
  57.5 16.4 %collective-permute-start.5 = (bf16[256,512]{1,0:T(8,128)(2,1)}, bf16[256,512]{1,0:T(8,128)(2,1)}, u32[]{:S(2)}, u32[]{:S(2)}) collective-permute-start(bf16[256,512]{1,0:T(8,128)(2,1)} %collective-permute-done.1.refs_2_), channel_id=1, source_target_pairs={{0,4},{4,0},{1,5},{5,1},{2,6},{6,2},{3,7},{7,3},{8,12},{12,8},{9,1... | collective-permute-start | bytes 786440 | tf_op jit(solution)/shard_map/ppermute | solution.py:137
  62.6 15.6 %collective-permute-start.4 = (bf16[256,512]{1,0:T(8,128)(2,1)}, bf16[256,512]{1,0:T(8,128)(2,1)}, u32[]{:S(2)}, u32[]{:S(2)}) collective-permute-start(bf16[256,512]{1,0:T(8,128)(2,1)} %collective-permute-done.refs_1_), channel_id=1, source_target_pairs={{0,4},{4,0},{1,5},{5,1},{2,6},{6,2},{3,7},{7,3},{8,12},{12,8},{9,1... | collective-permute-start | bytes 786440 | tf_op jit(solution)/shard_map/ppermute | solution.py:137
  64.9 18.2 %collective-permute-start.9 = (bf16[64,512]{1,0:T(8,128)(2,1)}, bf16[64,512]{1,0:T(8,128)(2,1)}, u32[]{:S(2)}, u32[]{:S(2)}) collective-permute-start(bf16[64,512]{1,0:T(8,128)(2,1)} %fusion.3), channel_id=1, source_target_pairs={{0,384},{128,256},{256,128},{384,0},{1,385},{129,257},{257,129},{3... | collective-permute-start | bytes 196616 | tf_op jit(solution)/shard_map/ppermute | solution.py:142
  66.9 16.3 %collective-permute-start.8 = (bf16[64,512]{1,0:T(8,128)(2,1)}, bf16[64,512]{1,0:T(8,128)(2,1)}, u32[]{:S(2)}, u32[]{:S(2)}) collective-permute-start(bf16[64,512]{1,0:T(8,128)(2,1)} %fusion.3), channel_id=1, source_target_pairs={{0,256},{128,384},{256,0},{384,128},{1,257},{129,385},{257,1},{385... | collective-permute-start | bytes 196616 | tf_op jit(solution)/shard_map/ppermute | solution.py:142
  70.4 12.8 %collective-permute-start.7 = (bf16[64,512]{1,0:T(8,128)(2,1)}, bf16[64,512]{1,0:T(8,128)(2,1)}, u32[]{:S(2)}, u32[]{:S(2)}) collective-permute-start(bf16[64,512]{1,0:T(8,128)(2,1)} %fusion.3), channel_id=1, source_target_pairs={{0,128},{128,0},{256,384},{384,256},{1,129},{129,1},{257,385},{385... | collective-permute-start | bytes 196616 | tf_op jit(solution)/shard_map/ppermute | solution.py:142
  83.1 14.4 %all-to-all-start.1 = ((bf16[4,192,512]{2,1,0:T(8,128)(2,1)}), bf16[4,192,512]{2,1,0:T(8,128)(2,1)S(1)}, u32[]{:S(2)}, u32[]{:S(2)}) async-start(bf16[4,192,512]{2,1,0:T(8,128)(2,1)} %project_keys.1), calls=%async_computation.1 | async-start | bytes 1572864 | tf_op jit(solution)/shard_map/all_to_all | solution.py:146

commit v13 on v12

--- a/solution.py
+++ b/solution.py
@@ -119,13 +119,8 @@
     hidden_in, norm_gain, key_weight, fragment_index, outer_params, outer_moment, inner_params
 ):
     replicas = 4
-    layer_idx = fragment_index[0]
-    outer_layer = lax.dynamic_index_in_dim(outer_params, layer_idx, 0, keepdims=False)
-    inner_layer = lax.dynamic_index_in_dim(inner_params[0], layer_idx, 0, keepdims=False)
-    pseudo_grad = (outer_layer - inner_layer.astype(jnp.float32)).astype(jnp.bfloat16)
-
     packed, scale = pack(hidden_in[0], norm_gain[None])
-    packed, block, pseudo_grad = lax.optimization_barrier((packed, key_weight[0], pseudo_grad))
+    packed, block = lax.optimization_barrier((packed, key_weight[0]))
     tokens = lax.all_to_all(packed, ROW, 0, 0, tiled=True)
     own = lax.all_gather(block, "zh", axis=0, tiled=True)
     held = [
@@ -135,15 +130,19 @@
         moved(own, lambda z: z - 1),
     ]
     held += [lax.ppermute(part, "yh", [(0, 1), (1, 0)]) for part in held]
-    own, pseudo_grad = lax.optimization_barrier((held[3], pseudo_grad))
+    held[1], fragment_index = lax.optimization_barrier((held[1], fragment_index))
+    layer_idx = fragment_index[0]
+    outer_layer = lax.dynamic_index_in_dim(outer_params, layer_idx, 0, keepdims=False)
+    inner_layer = lax.dynamic_index_in_dim(inner_params[0], layer_idx, 0, keepdims=False)
+    pseudo_grad = (outer_layer - inner_layer.astype(jnp.float32)).astype(jnp.bfloat16)
+    place = jnp.stack([lax.axis_index(axis).astype(jnp.int32) for axis in ("zl", "yh")])
+    partial = project(place, tokens, held)
+    partial, layer_idx, pseudo_grad = lax.optimization_barrier((partial, layer_idx, pseudo_grad))
+    partial = lax.all_to_all(partial, ROW, 0, 0, tiled=True)
     others = []
     for other in range(1, replicas):
         pairs = [(replica, replica ^ other) for replica in range(replicas)]
         others.append(lax.ppermute(pseudo_grad, REP, pairs))
-    place = jnp.stack([lax.axis_index(axis).astype(jnp.int32) for axis in ("zl", "yh")])
-    partial = project(place, tokens, held)
-    partial, layer_idx, others = lax.optimization_barrier((partial, layer_idx, others))
-    partial = lax.all_to_all(partial, ROW, 0, 0, tiled=True)
     outer_layer = lax.dynamic_index_in_dim(outer_params, layer_idx, 0, keepdims=False)
     moment_layer = lax.dynamic_index_in_dim(outer_moment, layer_idx, 0, keepdims=False)
     inner_layer = lax.dynamic_index_in_dim(inner_params[0], layer_idx, 0, keepdims=False)

time: 99.2 us -> 97.6 us (0.984)
  the two profiles are of different devices: /device:TPU:32 before, /device:TPU:1 now
where the time goes in v13:
time: 97.6 us; the launch traced here: 95.7 us
  starting transfers between devices  42 us (43%)
  blocking collectives  24.6 us (25%)
  waiting for transfers between devices  12.6 us (13%)
  Pallas kernels  8.05 us (8%)
  other arithmetic  4.43 us (5%)
  local copies, waits for them, and re-layouts  2.64 us (3%)
  between operations  1.43 us (1%)
    all_gather x1, blocking collectives, shards(): own = lax.all_gather(block, 'zh', axis=0, tiled=True)  24.6 us
    ppermute x4, starting transfers between devices, shards(): held += [lax.ppermute(part, 'yh', [(0, 1), (1, 0)]) for part in held]  13.9 us
    ppermute x4, waiting for transfers between devices, shards(): held += [lax.ppermute(part, 'yh', [(0, 1), (1, 0)]) for part in held]  11.3 us
    ppermute x3, starting transfers between devices, shards(): others.append(lax.ppermute(pseudo_grad, REP, pairs))  10.4 us
    ppermute x3, starting transfers between devices, moved(): lax.ppermute(block, Z, [(z, target(z) % PLANES) for z in range(PLANES)])  8.56 us
    pallas_call x1, Pallas kernels, project(): pl.pallas_call(project_kernel, grid_spec=pltpu.PrefetchScalarGridSpec(num...  4.88 us
    all_to_all x1, starting transfers between devices, shards(): tokens = lax.all_to_all(packed, ROW, 0, 0, tiled=True)  4.84 us
    all_to_all x1, starting transfers between devices, shards(): partial = lax.all_to_all(partial, ROW, 0, 0, tiled=True)  4.22 us
  transfers between devices with their start and end apart: 12, of which 4 were waited for; matrix products, arithmetic and copies ran while one was open for 4% of the time, Pallas kernels for 0%

profile of v13, /device:TPU:1, one launch (start us, length us, event | category | flops | bytes accessed | tf_op | source)
XLA Modules:
  0.0 95.7 jit_solution(9773207243943029003)
XLA Ops:
  0.6 0.0 copy-start
  0.6 1.9 %copy-done = bf16[1,192,8192]{2,1,0:T(8,128)(2,1)S(1)} copy-done((bf16[1,192,8192]{2,1,0:T(8,128)(2,1)S(1)}, bf16[1,192,8192]{2,1,0:T(8,128)(2,1)}, u32[]{:S(2)}) %copy-start) | copy-done | bytes 3145752
  2.5 0.0 copy-start.1
  2.5 0.8 copy-done.1
  3.3 3.2 %pack_hidden.1 = (bf16[4,192,2048]{2,1,0:T(8,128)(2,1)}, f32[192,1]{1,0:T(8,128)S(1)}) custom-call(bf16[192,8192]{1,0:T(8,128)(2,1)S(1)} %bitcast.32, f32[1,8192]{1,0:T(1,128)S(1)} %bitcast.33), custom_call_target="tpu_custom_call" | custom-call | flops 6291456 | bytes 6291456 | tf_op jit(solution)/shard_map/pack_hidden/pallas_call | solution.py:45
  6.4 4.8 %all-to-all-start = ((bf16[4,192,2048]{2,1,0:T(8,128)(2,1)}), bf16[4,192,2048]{2,1,0:T(8,128)(2,1)S(1)}, u32[]{:S(2)}, u32[]{:S(2)}) async-start(bf16[4,192,2048]{2,1,0:T(8,128)(2,1)} %get-tuple-element.14), calls=%async_computation | async-start | bytes 6291456 | tf_op jit(solution)/shard_map/all_to_all | solution.py:124
  11.3 24.6 %all_gather.3.refs_0_ = bf16[256,512]{1,0:T(8,128)(2,1)S(1)} all-gather(bf16[64,512]{1,0:T(8,128)(2,1)} %bitcast.34), channel_id=1, replica_groups=mesh['yl'=2,'core'=2,'zh'=4,'zl'=4,'yh'=2,'x'=4] {'zh'}, dimensions={0}, use_global_device_ids=true | all-gather | bytes 327680 | tf_op jit(solution)/shard_map/all_gather | solution.py:125
  35.9 2.9 %collective-permute-start.2 = (bf16[256,512]{1,0:T(8,128)(2,1)S(1)}, bf16[256,512]{1,0:T(8,128)(2,1)}, u32[]{:S(2)}, u32[]{:S(2)}) collective-permute-start(bf16[256,512]{1,0:T(8,128)(2,1)S(1)} %all_gather.3.refs_0_), channel_id=1, source_target_pairs={{0,120},{8,0},{16,8},{24,16},{32,24},{40,32},{48,40},{56,48},{64,5... | collective-permute-start | bytes 786440 | tf_op jit(solution)/shard_map/ppermute | solution.py:115
  38.8 2.3 %collective-permute-start.1 = (bf16[256,512]{1,0:T(8,128)(2,1)S(1)}, bf16[256,512]{1,0:T(8,128)(2,1)}, u32[]{:S(2)}, u32[]{:S(2)}) collective-permute-start(bf16[256,512]{1,0:T(8,128)(2,1)S(1)} %all_gather.3.refs_0_), channel_id=1, source_target_pairs={{0,8},{8,16},{16,24},{24,32},{32,40},{40,48},{48,56},{56,64},{64,7... | collective-permute-start | bytes 786440 | tf_op jit(solution)/shard_map/ppermute | solution.py:115
  41.2 3.3 %collective-permute-start = (bf16[256,512]{1,0:T(8,128)(2,1)S(1)}, bf16[256,512]{1,0:T(8,128)(2,1)}, u32[]{:S(2)}, u32[]{:S(2)}) collective-permute-start(bf16[256,512]{1,0:T(8,128)(2,1)S(1)} %all_gather.3.refs_0_), channel_id=1, source_target_pairs={{0,16},{8,120},{16,32},{24,8},{32,48},{40,24},{48,64},{56,40},{64,... | collective-permute-start | bytes 786440 | tf_op jit(solution)/shard_map/ppermute | solution.py:115
  44.5 4.8 %collective-permute-start.3 = (bf16[256,512]{1,0:T(8,128)(2,1)S(1)}, bf16[256,512]{1,0:T(8,128)(2,1)}, u32[]{:S(2)}, u32[]{:S(2)}) collective-permute-start(bf16[256,512]{1,0:T(8,128)(2,1)S(1)} %all_gather.3.refs_0_), channel_id=1, source_target_pairs={{0,4},{4,0},{1,5},{5,1},{2,6},{6,2},{3,7},{7,3},{8,12},{12,8},{9,1... | collective-permute-start | bytes 786440 | tf_op jit(solution)/shard_map/ppermute | solution.py:132
  49.3 0.0 collective-permute-done.2.refs_3_
  49.3 2.0 %collective-permute-start.6 = (bf16[256,512]{1,0:T(8,128)(2,1)}, bf16[256,512]{1,0:T(8,128)(2,1)}, u32[]{:S(2)}, u32[]{:S(2)}) collective-permute-start(bf16[256,512]{1,0:T(8,128)(2,1)} %collective-permute-done.2.refs_3_), channel_id=1, source_target_pairs={{0,4},{4,0},{1,5},{5,1},{2,6},{6,2},{3,7},{7,3},{8,12},{12,8},{9,1... | collective-permute-start | bytes 786440 | tf_op jit(solution)/shard_map/ppermute | solution.py:132
  51.3 0.0 collective-permute-done.1.refs_2_
  51.3 4.8 %collective-permute-start.5 = (bf16[256,512]{1,0:T(8,128)(2,1)}, bf16[256,512]{1,0:T(8,128)(2,1)}, u32[]{:S(2)}, u32[]{:S(2)}) collective-permute-start(bf16[256,512]{1,0:T(8,128)(2,1)} %collective-permute-done.1.refs_2_), channel_id=1, source_target_pairs={{0,4},{4,0},{1,5},{5,1},{2,6},{6,2},{3,7},{7,3},{8,12},{12,8},{9,1... | collective-permute-start | bytes 786440 | tf_op jit(solution)/shard_map/ppermute | solution.py:132
  56.1 0.0 collective-permute-done.refs_1_
  56.1 2.3 %collective-permute-start.4 = (bf16[256,512]{1,0:T(8,128)(2,1)}, bf16[256,512]{1,0:T(8,128)(2,1)}, u32[]{:S(2)}, u32[]{:S(2)}) collective-permute-start(bf16[256,512]{1,0:T(8,128)(2,1)} %collective-permute-done.refs_1_), channel_id=1, source_target_pairs={{0,4},{4,0},{1,5},{5,1},{2,6},{6,2},{3,7},{7,3},{8,12},{12,8},{9,1... | collective-permute-start | bytes 786440 | tf_op jit(solution)/shard_map/ppermute | solution.py:132
  59.1 0.1 pad_add_fusion.place_ref
  59.2 1.5 %fusion.3 = bf16[64,512]{1,0:T(8,128)(2,1)} fusion(f32[7,64,512]{2,1,0:T(8,128)} %param.11, s32[]{:T(128)S(6)} %select_n.11, bf16[1,7,64,512]{3,2,1,0:T(8,128)(2,1)} %param.13), kind=kLoop, calls=%fused_computation.7 | loop fusion | flops 98304 | bytes 262148 | tf_op jit(solution)/shard_map/convert_element_type | solution.py:137
  60.7 0.0 collective-permute-done.3.refs_4_
  60.7 0.1 collective-permute-done.6.refs_7_
  60.8 5.6 %collective-permute-done.5.refs_6_ = bf16[256,512]{1,0:T(8,128)(2,1)} collective-permute-done((bf16[256,512]{1,0:T(8,128)(2,1)}, bf16[256,512]{1,0:T(8,128)(2,1)}, u32[]{:S(2)}, u32[]{:S(2)}) %collective-permute-start.5) | collective-permute-done | bytes 262176 | tf_op jit(solution)/shard_map/ppermute | solution.py:132
  66.4 5.6 %collective-permute-done.4.refs_5_ = bf16[256,512]{1,0:T(8,128)(2,1)} collective-permute-done((bf16[256,512]{1,0:T(8,128)(2,1)}, bf16[256,512]{1,0:T(8,128)(2,1)}, u32[]{:S(2)}, u32[]{:S(2)}) %collective-permute-start.4) | collective-permute-done | bytes 262176 | tf_op jit(solution)/shard_map/ppermute | solution.py:132
  72.0 0.0 all-to-all-done.tokens_ref
  72.0 4.9 %project_keys.1 = bf16[4,192,512]{2,1,0:T(8,128)(2,1)} custom-call(s32[2]{0:T(128)S(1)} %pad_add_fusion.place_ref, bf16[4,192,2048]{2,1,0:T(8,128)(2,1)S(1)} %all-to-all-done.tokens_ref, bf16[256,512]{1,0:T(8,128)(2,1)S(1)} %all_gather.3.refs_0_, bf16[256,512]{1,0:T(8,128)(2,1)} %collective-permute-done.refs_1_, ...), custom_call_target="tpu_custom_call" | custom-call | flops 1610612736 | bytes 6029312 | tf_op jit(solution)/shard_map/project_keys/pallas_call | solution.py:94
  76.9 4.2 %all-to-all-start.1 = ((bf16[4,192,512]{2,1,0:T(8,128)(2,1)}), bf16[4,192,512]{2,1,0:T(8,128)(2,1)S(1)}, u32[]{:S(2)}, u32[]{:S(2)}) async-start(bf16[4,192,512]{2,1,0:T(8,128)(2,1)} %project_keys.1), calls=%async_computation.1 | async-start | bytes 1572864 | tf_op jit(solution)/shard_map/all_to_all | solution.py:141
  81.1 6.2 %collective-permute-start.9 = (bf16[64,512]{1,0:T(8,128)(2,1)}, bf16[64,512]{1,0:T(8,128)(2,1)S(1)}, u32[]{:S(2)}, u32[]{:S(2)}) collective-permute-start(bf16[64,512]{1,0:T(8,128)(2,1)} %fusion.3), channel_id=1, source_target_pairs={{0,384},{128,256},{256,128},{384,0},{1,385},{129,257},{257,129},{3... | collective-permute-start | bytes 196616 | tf_op jit(solution)/shard_map/ppermute | solution.py:145
  87.4 2.2 %collective-permute-start.8 = (bf16[64,512]{1,0:T(8,128)(2,1)}, bf16[64,512]{1,0:T(8,128)(2,1)S(1)}, u32[]{:S(2)}, u32[]{:S(2)}) collective-permute-start(bf16[64,512]{1,0:T(8,128)(2,1)} %fusion.3), channel_id=1, source_target_pairs={{0,256},{128,384},{256,0},{384,128},{1,257},{129,385},{257,1},{385... | collective-permute-start | bytes 196616 | tf_op jit(solution)/shard_map/ppermute | solution.py:145
  89.6 2.0 %collective-permute-start.7 = (bf16[64,512]{1,0:T(8,128)(2,1)}, bf16[64,512]{1,0:T(8,128)(2,1)S(1)}, u32[]{:S(2)}, u32[]{:S(2)}) collective-permute-start(bf16[64,512]{1,0:T(8,128)(2,1)} %fusion.3), channel_id=1, source_target_pairs={{0,128},{128,0},{256,384},{384,256},{1,129},{129,1},{257,385},{385... | collective-permute-start | bytes 196616 | tf_op jit(solution)/shard_map/ppermute | solution.py:145
  91.6 0.1 reduce
  91.7 0.0 collective-permute-done.9
  91.7 1.3 %collective-permute-done.8 = bf16[64,512]{1,0:T(8,128)(2,1)S(1)} collective-permute-done((bf16[64,512]{1,0:T(8,128)(2,1)}, bf16[64,512]{1,0:T(8,128)(2,1)S(1)}, u32[]{:S(2)}, u32[]{:S(2)}) %collective-permute-start.8) | collective-permute-done | bytes 65568 | tf_op jit(solution)/shard_map/ppermute | solution.py:145
  93.0 0.0 collective-permute-done.7
  93.0 1.8 %fusion.4 = (bf16[1,64,512]{2,1,0:T(8,128)(2,1)}, f32[64,512]{1,0:T(8,128)}, f32[64,512]{1,0:T(8,128)}) fusion(bf16[1,7,64,512]{3,2,1,0:T(8,128)(2,1)} %param.13, s32[]{:T(128)S(6)} %select_n.12, bf16[64,512]{1,0:T(8,128)(2,1)S(1)} %collective-permute-done.9, bf16[64,512]{1,0:T(8,128)(2,1)S(1)} %collective-permute-done.8, ...), kind=kLoop, calls=%fused_computation.11 | loop fusion | flops 589824 | bytes 917508 | tf_op jit(solution)/shard_map/broadcast_in_dim | solution.py:155
  94.8 0.0 all-to-all-done.1
  94.8 0.1 convert_reduce_fusion
  94.9 0.8 fusion
Async XLA Ops:
  0.6 1.9 %copy-start = (bf16[1,192,8192]{2,1,0:T(8,128)(2,1)S(1)}, bf16[1,192,8192]{2,1,0:T(8,128)(2,1)}, u32[]{:S(2)}) copy-start(bf16[1,192,8192]{2,1,0:T(8,128)(2,1)} %param.7) | copy-start | bytes 9437188
  2.5 0.8 copy-start.1
  6.4 65.6 %all-to-all-start = ((bf16[4,192,2048]{2,1,0:T(8,128)(2,1)}), bf16[4,192,2048]{2,1,0:T(8,128)(2,1)S(1)}, u32[]{:S(2)}, u32[]{:S(2)}) async-start(bf16[4,192,2048]{2,1,0:T(8,128)(2,1)} %get-tuple-element.14), calls=%async_computation | async-start | bytes 6291456 | tf_op jit(solution)/shard_map/all_to_all | solution.py:124
  35.9 13.4 %collective-permute-start.2 = (bf16[256,512]{1,0:T(8,128)(2,1)S(1)}, bf16[256,512]{1,0:T(8,128)(2,1)}, u32[]{:S(2)}, u32[]{:S(2)}) collective-permute-start(bf16[256,512]{1,0:T(8,128)(2,1)S(1)} %all_gather.3.refs_0_), channel_id=1, source_target_pairs={{0,120},{8,0},{16,8},{24,16},{32,24},{40,32},{48,40},{56,48},{64,5... | collective-permute-start | bytes 786440 | tf_op jit(solution)/shard_map/ppermute | solution.py:115
  38.8 12.5 %collective-permute-start.1 = (bf16[256,512]{1,0:T(8,128)(2,1)S(1)}, bf16[256,512]{1,0:T(8,128)(2,1)}, u32[]{:S(2)}, u32[]{:S(2)}) collective-permute-start(bf16[256,512]{1,0:T(8,128)(2,1)S(1)} %all_gather.3.refs_0_), channel_id=1, source_target_pairs={{0,8},{8,16},{16,24},{24,32},{32,40},{40,48},{48,56},{56,64},{64,7... | collective-permute-start | bytes 786440 | tf_op jit(solution)/shard_map/ppermute | solution.py:115
  41.2 15.0 %collective-permute-start = (bf16[256,512]{1,0:T(8,128)(2,1)S(1)}, bf16[256,512]{1,0:T(8,128)(2,1)}, u32[]{:S(2)}, u32[]{:S(2)}) collective-permute-start(bf16[256,512]{1,0:T(8,128)(2,1)S(1)} %all_gather.3.refs_0_), channel_id=1, source_target_pairs={{0,16},{8,120},{16,32},{24,8},{32,48},{40,24},{48,64},{56,40},{64,... | collective-permute-start | bytes 786440 | tf_op jit(solution)/shard_map/ppermute | solution.py:115
  44.5 16.2 %collective-permute-start.3 = (bf16[256,512]{1,0:T(8,128)(2,1)S(1)}, bf16[256,512]{1,0:T(8,128)(2,1)}, u32[]{:S(2)}, u32[]{:S(2)}) collective-permute-start(bf16[256,512]{1,0:T(8,128)(2,1)S(1)} %all_gather.3.refs_0_), channel_id=1, source_target_pairs={{0,4},{4,0},{1,5},{5,1},{2,6},{6,2},{3,7},{7,3},{8,12},{12,8},{9,1... | collective-permute-start | bytes 786440 | tf_op jit(solution)/shard_map/ppermute | solution.py:132
  49.3 11.5 %collective-permute-start.6 = (bf16[256,512]{1,0:T(8,128)(2,1)}, bf16[256,512]{1,0:T(8,128)(2,1)}, u32[]{:S(2)}, u32[]{:S(2)}) collective-permute-start(bf16[256,512]{1,0:T(8,128)(2,1)} %collective-permute-done.2.refs_3_), channel_id=1, source_target_pairs={{0,4},{4,0},{1,5},{5,1},{2,6},{6,2},{3,7},{7,3},{8,12},{12,8},{9,1... | collective-permute-start | bytes 786440 | tf_op jit(solution)/shard_map/ppermute | solution.py:132
  51.3 15.1 %collective-permute-start.5 = (bf16[256,512]{1,0:T(8,128)(2,1)}, bf16[256,512]{1,0:T(8,128)(2,1)}, u32[]{:S(2)}, u32[]{:S(2)}) collective-permute-start(bf16[256,512]{1,0:T(8,128)(2,1)} %collective-permute-done.1.refs_2_), channel_id=1, source_target_pairs={{0,4},{4,0},{1,5},{5,1},{2,6},{6,2},{3,7},{7,3},{8,12},{12,8},{9,1... | collective-permute-start | bytes 786440 | tf_op jit(solution)/shard_map/ppermute | solution.py:132
  56.1 15.9 %collective-permute-start.4 = (bf16[256,512]{1,0:T(8,128)(2,1)}, bf16[256,512]{1,0:T(8,128)(2,1)}, u32[]{:S(2)}, u32[]{:S(2)}) collective-permute-start(bf16[256,512]{1,0:T(8,128)(2,1)} %collective-permute-done.refs_1_), channel_id=1, source_target_pairs={{0,4},{4,0},{1,5},{5,1},{2,6},{6,2},{3,7},{7,3},{8,12},{12,8},{9,1... | collective-permute-start | bytes 786440 | tf_op jit(solution)/shard_map/ppermute | solution.py:132
  76.9 17.9 %all-to-all-start.1 = ((bf16[4,192,512]{2,1,0:T(8,128)(2,1)}), bf16[4,192,512]{2,1,0:T(8,128)(2,1)S(1)}, u32[]{:S(2)}, u32[]{:S(2)}) async-start(bf16[4,192,512]{2,1,0:T(8,128)(2,1)} %project_keys.1), calls=%async_computation.1 | async-start | bytes 1572864 | tf_op jit(solution)/shard_map/all_to_all | solution.py:141
  81.1 10.6 %collective-permute-start.9 = (bf16[64,512]{1,0:T(8,128)(2,1)}, bf16[64,512]{1,0:T(8,128)(2,1)S(1)}, u32[]{:S(2)}, u32[]{:S(2)}) collective-permute-start(bf16[64,512]{1,0:T(8,128)(2,1)} %fusion.3), channel_id=1, source_target_pairs={{0,384},{128,256},{256,128},{384,0},{1,385},{129,257},{257,129},{3... | collective-permute-start | bytes 196616 | tf_op jit(solution)/shard_map/ppermute | solution.py:145
  87.4 5.6 %collective-permute-start.8 = (bf16[64,512]{1,0:T(8,128)(2,1)}, bf16[64,512]{1,0:T(8,128)(2,1)S(1)}, u32[]{:S(2)}, u32[]{:S(2)}) collective-permute-start(bf16[64,512]{1,0:T(8,128)(2,1)} %fusion.3), channel_id=1, source_target_pairs={{0,256},{128,384},{256,0},{384,128},{1,257},{129,385},{257,1},{385... | collective-permute-start | bytes 196616 | tf_op jit(solution)/shard_map/ppermute | solution.py:145
  89.6 3.4 %collective-permute-start.7 = (bf16[64,512]{1,0:T(8,128)(2,1)}, bf16[64,512]{1,0:T(8,128)(2,1)S(1)}, u32[]{:S(2)}, u32[]{:S(2)}) collective-permute-start(bf16[64,512]{1,0:T(8,128)(2,1)} %fusion.3), channel_id=1, source_target_pairs={{0,128},{128,0},{256,384},{384,256},{1,129},{129,1},{257,385},{385... | collective-permute-start | bytes 196616 | tf_op jit(solution)/shard_map/ppermute | solution.py:145

commit v14 on v7

--- a/solution.py
+++ b/solution.py
@@ -67,7 +67,7 @@
 
 
 STEPS = 4
-HELD = (0, -1, 1, 2)
+HELD = (0, 2, -1, 1)
 
 
 def project_kernel(residue_ref, tokens_ref, *refs):
@@ -124,23 +124,27 @@
     own = lax.all_gather(block, "zh", axis=0, tiled=True)
     held = (
         own,
+        moved(own, lambda z: z + 2 if z % 2 == 0 else z - 2),
         moved(own, lambda z: z + 1),
         moved(own, lambda z: z - 1),
-        moved(own, lambda z: z + 2 if z % 2 == 0 else z - 2),
     )
+    _, fragment_index = lax.optimization_barrier((own, fragment_index))
+    layer_idx = fragment_index[0]
+    outer_layer = lax.dynamic_index_in_dim(outer_params, layer_idx, 0, keepdims=False)
+    inner_layer = lax.dynamic_index_in_dim(inner_params[0], layer_idx, 0, keepdims=False)
+    pseudo_grad = (outer_layer - inner_layer.astype(jnp.float32)).astype(jnp.bfloat16)
+    others = []
+    for other in range(1, replicas):
+        pairs = [(replica, replica ^ other) for replica in range(replicas)]
+        others.append(lax.ppermute(pseudo_grad, REP, pairs))
     residue = lax.axis_index("zl").astype(jnp.int32)[None]
     partial = project(residue, tokens, held)
-    partial, fragment_index = lax.optimization_barrier((partial, fragment_index))
+    partial, layer_idx, others = lax.optimization_barrier((partial, layer_idx, others))
     partial = lax.all_to_all(partial, PLANE, 0, 0, tiled=True)
-    layer_idx = fragment_index[0]
     outer_layer = lax.dynamic_index_in_dim(outer_params, layer_idx, 0, keepdims=False)
     moment_layer = lax.dynamic_index_in_dim(outer_moment, layer_idx, 0, keepdims=False)
     inner_layer = lax.dynamic_index_in_dim(inner_params[0], layer_idx, 0, keepdims=False)
-    pseudo_grad = (outer_layer - inner_layer.astype(jnp.float32)).astype(jnp.bfloat16)
-    summed = pseudo_grad.astype(jnp.float32)
-    for other in range(1, replicas):
-        pairs = [(replica, replica ^ other) for replica in range(replicas)]
-        summed += lax.ppermute(pseudo_grad, REP, pairs).astype(jnp.float32)
+    summed = pseudo_grad.astype(jnp.float32) + sum(part.astype(jnp.float32) for part in others)
     new_outer, new_moment = outer_update(summed / replicas, outer_layer, moment_layer)
     mixed_inner = (
         mix_keep * inner_layer.astype(jnp.float32) + (1.0 - mix_keep) * new_outer

time: 93.4 us -> 97.2 us (1.041)
  the two profiles are of different devices: /device:TPU:464 before, /device:TPU:1 now
where the time goes in v14:
time: 97.2 us; the launch traced here: 96.6 us
  starting transfers between devices  34.8 us (36%)
  blocking collectives  24.9 us (26%)
  waiting for transfers between devices  21 us (22%)
  Pallas kernels  7.33 us (8%)
  other arithmetic  4.57 us (5%)
  local copies, waits for them, and re-layouts  2.64 us (3%)
  between operations  1.4 us (1%)
    all_gather x1, blocking collectives, shards(): own = lax.all_gather(block, 'zh', axis=0, tiled=True)  24.9 us
    all_to_all x1, waiting for transfers between devices, shards(): partial = lax.all_to_all(partial, PLANE, 0, 0, tiled=True)  21 us
    ppermute x3, starting transfers between devices, shards(): others.append(lax.ppermute(pseudo_grad, REP, pairs))  10.9 us
    ppermute x3, starting transfers between devices, moved(): lax.ppermute(block, Z, [(z, target(z) % PLANES) for z in range(PLANES)])  9.77 us
    all_to_all x1, starting transfers between devices, shards(): tokens = lax.all_to_all(packed, PLANE, 0, 0, tiled=True)  7.48 us
    all_to_all x1, starting transfers between devices, shards(): partial = lax.all_to_all(partial, PLANE, 0, 0, tiled=True)  6.65 us
    pallas_call x1, Pallas kernels, project(): pl.pallas_call(project_kernel, grid_spec=pltpu.PrefetchScalarGridSpec(num...  4.1 us
    pallas_call x1, Pallas kernels, pack(): pl.pallas_call(pack_kernel, grid=(tokens // ROWS,), in_specs=[pl.BlockSpe...  3.23 us
  transfers between devices with their start and end apart: 8, of which 1 were waited for; matrix products, arithmetic and copies ran while one was open for 4% of the time, Pallas kernels for 4%

profile of v14, /device:TPU:1, one launch (start us, length us, event | category | flops | bytes accessed | tf_op | source)
XLA Modules:
  0.0 96.6 jit_solution(15254678964658719790)
XLA Ops:
  0.6 0.0 copy-start
  0.6 1.9 %copy-done = bf16[1,192,8192]{2,1,0:T(8,128)(2,1)S(1)} copy-done((bf16[1,192,8192]{2,1,0:T(8,128)(2,1)S(1)}, bf16[1,192,8192]{2,1,0:T(8,128)(2,1)}, u32[]{:S(2)}) %copy-start) | copy-done | bytes 3145752
  2.5 0.0 copy-start.1
  2.5 0.8 copy-done.1
  3.3 3.2 %pack_hidden.1 = (bf16[8,192,1024]{2,1,0:T(8,128)(2,1)}, f32[192,1]{1,0:T(8,128)S(1)}) custom-call(bf16[192,8192]{1,0:T(8,128)(2,1)S(1)} %bitcast.31, f32[1,8192]{1,0:T(1,128)S(1)} %bitcast.32), custom_call_target="tpu_custom_call" | custom-call | flops 6291456 | bytes 6291456 | tf_op jit(solution)/shard_map/pack_hidden/pallas_call | solution.py:46
  6.5 7.5 %all-to-all-start = ((bf16[8,192,1024]{2,1,0:T(8,128)(2,1)}), bf16[8,192,1024]{2,1,0:T(8,128)(2,1)S(1)}, u32[]{:S(2)}, u32[]{:S(2)}) async-start(bf16[8,192,1024]{2,1,0:T(8,128)(2,1)} %get-tuple-element.15), calls=%async_computation | async-start | bytes 6291456 | tf_op jit(solution)/shard_map/all_to_all | solution.py:123
  14.0 24.9 %all_gather.3.refs_0_ = bf16[256,512]{1,0:T(8,128)(2,1)S(1)} all-gather(bf16[64,512]{1,0:T(8,128)(2,1)} %bitcast.33), channel_id=1, replica_groups=mesh['yl'=2,'core'=2,'zh'=4,'zl'=4,'yh'=2,'x'=4] {'zh'}, dimensions={0}, use_global_device_ids=true | all-gather | bytes 327680 | tf_op jit(solution)/shard_map/all_gather | solution.py:124
  38.9 3.3 %collective-permute-start = (bf16[256,512]{1,0:T(8,128)(2,1)S(1)}, bf16[256,512]{1,0:T(8,128)(2,1)}, u32[]{:S(2)}, u32[]{:S(2)}) collective-permute-start(bf16[256,512]{1,0:T(8,128)(2,1)S(1)} %all_gather.3.refs_0_), channel_id=1, source_target_pairs={{0,16},{8,120},{16,32},{24,8},{32,48},{40,24},{48,64},{56,40},{64,... | collective-permute-start | bytes 786440 | tf_op jit(solution)/shard_map/ppermute | solution.py:114
  42.2 2.5 %collective-permute-start.1 = (bf16[256,512]{1,0:T(8,128)(2,1)S(1)}, bf16[256,512]{1,0:T(8,128)(2,1)}, u32[]{:S(2)}, u32[]{:S(2)}) collective-permute-start(bf16[256,512]{1,0:T(8,128)(2,1)S(1)} %all_gather.3.refs_0_), channel_id=1, source_target_pairs={{0,8},{8,16},{16,24},{24,32},{32,40},{40,48},{48,56},{56,64},{64,7... | collective-permute-start | bytes 786440 | tf_op jit(solution)/shard_map/ppermute | solution.py:114
  44.6 4.0 %collective-permute-start.2 = (bf16[256,512]{1,0:T(8,128)(2,1)S(1)}, bf16[256,512]{1,0:T(8,128)(2,1)}, u32[]{:S(2)}, u32[]{:S(2)}) collective-permute-start(bf16[256,512]{1,0:T(8,128)(2,1)S(1)} %all_gather.3.refs_0_), channel_id=1, source_target_pairs={{0,120},{8,0},{16,8},{24,16},{32,24},{40,32},{48,40},{56,48},{64,5... | collective-permute-start | bytes 786440 | tf_op jit(solution)/shard_map/ppermute | solution.py:114
  49.3 1.6 %fusion.3 = bf16[64,512]{1,0:T(8,128)(2,1)} fusion(f32[7,64,512]{2,1,0:T(8,128)} %param.11, s32[]{:T(128)S(6)} %select_n.11, bf16[1,7,64,512]{3,2,1,0:T(8,128)(2,1)} %param.13), kind=kLoop, calls=%fused_computation.7 | loop fusion | flops 98304 | bytes 262148 | tf_op jit(solution)/shard_map/convert_element_type | solution.py:135
  50.9 5.4 %collective-permute-start.3 = (bf16[64,512]{1,0:T(8,128)(2,1)}, bf16[64,512]{1,0:T(8,128)(2,1)}, u32[]{:S(2)}, u32[]{:S(2)}) collective-permute-start(bf16[64,512]{1,0:T(8,128)(2,1)} %fusion.3), channel_id=1, source_target_pairs={{0,128},{128,0},{256,384},{384,256},{1,129},{129,1},{257,385},{385... | collective-permute-start | bytes 196616 | tf_op jit(solution)/shard_map/ppermute | solution.py:139
  56.3 2.3 %collective-permute-start.4 = (bf16[64,512]{1,0:T(8,128)(2,1)}, bf16[64,512]{1,0:T(8,128)(2,1)}, u32[]{:S(2)}, u32[]{:S(2)}) collective-permute-start(bf16[64,512]{1,0:T(8,128)(2,1)} %fusion.3), channel_id=1, source_target_pairs={{0,256},{128,384},{256,0},{384,128},{1,257},{129,385},{257,1},{385... | collective-permute-start | bytes 196616 | tf_op jit(solution)/shard_map/ppermute | solution.py:139
  58.6 0.0 collective-permute-done.refs_1_
  58.6 3.2 %collective-permute-start.5 = (bf16[64,512]{1,0:T(8,128)(2,1)}, bf16[64,512]{1,0:T(8,128)(2,1)}, u32[]{:S(2)}, u32[]{:S(2)}) collective-permute-start(bf16[64,512]{1,0:T(8,128)(2,1)} %fusion.3), channel_id=1, source_target_pairs={{0,384},{128,256},{256,128},{384,0},{1,385},{129,257},{257,129},{3... | collective-permute-start | bytes 196616 | tf_op jit(solution)/shard_map/ppermute | solution.py:139
  61.8 0.0 collective-permute-done.1.refs_2_
  61.8 0.0 collective-permute-done.2.refs_3_
  61.8 0.0 all-to-all-done.tokens_ref
  61.8 4.1 %project_keys.1 = bf16[8,192,512]{2,1,0:T(8,128)(2,1)} custom-call(s32[1]{0:T(128)} %bitcast.residue_ref, bf16[8,192,1024]{2,1,0:T(8,128)(2,1)S(1)} %all-to-all-done.tokens_ref, bf16[256,512]{1,0:T(8,128)(2,1)S(1)} %all_gather.3.refs_0_, bf16[256,512]{1,0:T(8,128)(2,1)} %collective-permute-done.refs_1_, bf16[256,512]{1,0:T(8,128)(2,1)} %collective-permute-done.1.refs_2_, ...), custom_call_target="tpu_custom_call" | custom-call | flops 1610612736 | bytes 5767168 | tf_op jit(solution)/shard_map/project_keys/pallas_call | solution.py:93
  65.9 0.0 collective-permute-done.3
  65.9 0.0 collective-permute-done.4
  66.0 0.0 collective-permute-done.5
  66.0 6.6 %all-to-all-start.1 = ((bf16[8,192,512]{2,1,0:T(8,128)(2,1)}), bf16[8,192,512]{2,1,0:T(8,128)(2,1)S(1)}, u32[]{:S(2)}, u32[]{:S(2)}) async-start(bf16[8,192,512]{2,1,0:T(8,128)(2,1)} %project_keys.1), calls=%async_computation.1 | async-start | bytes 3145728 | tf_op jit(solution)/shard_map/all_to_all | solution.py:143
  72.6 0.1 reduce
  72.7 1.9 %fusion.4 = (bf16[1,64,512]{2,1,0:T(8,128)(2,1)}, f32[64,512]{1,0:T(8,128)}, f32[64,512]{1,0:T(8,128)}) fusion(bf16[1,7,64,512]{3,2,1,0:T(8,128)(2,1)} %param.13, s32[]{:T(128)S(6)} %select_n.12, bf16[64,512]{1,0:T(8,128)(2,1)} %collective-permute-done.5, bf16[64,512]{1,0:T(8,128)(2,1)} %collective-permute-done.4, ...), kind=kLoop, calls=%fused_computation.11 | loop fusion | flops 589824 | bytes 917508 | tf_op jit(solution)/shard_map/broadcast_in_dim | solution.py:153
  74.6 21.0 %all-to-all-done.1 = bf16[8,192,512]{2,1,0:T(8,128)(2,1)S(1)} async-done(((bf16[8,192,512]{2,1,0:T(8,128)(2,1)}), bf16[8,192,512]{2,1,0:T(8,128)(2,1)S(1)}, u32[]{:S(2)}, u32[]{:S(2)}) %all-to-all-start.1) | async-done | bytes 1572896 | tf_op jit(solution)/shard_map/all_to_all | solution.py:143
  95.6 0.2 convert_reduce_fusion
  95.8 0.8 fusion
Async XLA Ops:
  0.6 1.9 %copy-start = (bf16[1,192,8192]{2,1,0:T(8,128)(2,1)S(1)}, bf16[1,192,8192]{2,1,0:T(8,128)(2,1)}, u32[]{:S(2)}) copy-start(bf16[1,192,8192]{2,1,0:T(8,128)(2,1)} %param.7) | copy-start | bytes 9437188
  2.5 0.8 copy-start.1
  6.5 55.3 %all-to-all-start = ((bf16[8,192,1024]{2,1,0:T(8,128)(2,1)}), bf16[8,192,1024]{2,1,0:T(8,128)(2,1)S(1)}, u32[]{:S(2)}, u32[]{:S(2)}) async-start(bf16[8,192,1024]{2,1,0:T(8,128)(2,1)} %get-tuple-element.15), calls=%async_computation | async-start | bytes 6291456 | tf_op jit(solution)/shard_map/all_to_all | solution.py:123
  38.9 19.8 %collective-permute-start = (bf16[256,512]{1,0:T(8,128)(2,1)S(1)}, bf16[256,512]{1,0:T(8,128)(2,1)}, u32[]{:S(2)}, u32[]{:S(2)}) collective-permute-start(bf16[256,512]{1,0:T(8,128)(2,1)S(1)} %all_gather.3.refs_0_), channel_id=1, source_target_pairs={{0,16},{8,120},{16,32},{24,8},{32,48},{40,24},{48,64},{56,40},{64,... | collective-permute-start | bytes 786440 | tf_op jit(solution)/shard_map/ppermute | solution.py:114
  42.2 19.6 %collective-permute-start.1 = (bf16[256,512]{1,0:T(8,128)(2,1)S(1)}, bf16[256,512]{1,0:T(8,128)(2,1)}, u32[]{:S(2)}, u32[]{:S(2)}) collective-permute-start(bf16[256,512]{1,0:T(8,128)(2,1)S(1)} %all_gather.3.refs_0_), channel_id=1, source_target_pairs={{0,8},{8,16},{16,24},{24,32},{32,40},{40,48},{48,56},{56,64},{64,7... | collective-permute-start | bytes 786440 | tf_op jit(solution)/shard_map/ppermute | solution.py:114
  44.6 17.2 %collective-permute-start.2 = (bf16[256,512]{1,0:T(8,128)(2,1)S(1)}, bf16[256,512]{1,0:T(8,128)(2,1)}, u32[]{:S(2)}, u32[]{:S(2)}) collective-permute-start(bf16[256,512]{1,0:T(8,128)(2,1)S(1)} %all_gather.3.refs_0_), channel_id=1, source_target_pairs={{0,120},{8,0},{16,8},{24,16},{32,24},{40,32},{48,40},{56,48},{64,5... | collective-permute-start | bytes 786440 | tf_op jit(solution)/shard_map/ppermute | solution.py:114
  50.9 15.1 %collective-permute-start.3 = (bf16[64,512]{1,0:T(8,128)(2,1)}, bf16[64,512]{1,0:T(8,128)(2,1)}, u32[]{:S(2)}, u32[]{:S(2)}) collective-permute-start(bf16[64,512]{1,0:T(8,128)(2,1)} %fusion.3), channel_id=1, source_target_pairs={{0,128},{128,0},{256,384},{384,256},{1,129},{129,1},{257,385},{385... | collective-permute-start | bytes 196616 | tf_op jit(solution)/shard_map/ppermute | solution.py:139
  56.3 9.6 %collective-permute-start.4 = (bf16[64,512]{1,0:T(8,128)(2,1)}, bf16[64,512]{1,0:T(8,128)(2,1)}, u32[]{:S(2)}, u32[]{:S(2)}) collective-permute-start(bf16[64,512]{1,0:T(8,128)(2,1)} %fusion.3), channel_id=1, source_target_pairs={{0,256},{128,384},{256,0},{384,128},{1,257},{129,385},{257,1},{385... | collective-permute-start | bytes 196616 | tf_op jit(solution)/shard_map/ppermute | solution.py:139
  58.6 7.3 %collective-permute-start.5 = (bf16[64,512]{1,0:T(8,128)(2,1)}, bf16[64,512]{1,0:T(8,128)(2,1)}, u32[]{:S(2)}, u32[]{:S(2)}) collective-permute-start(bf16[64,512]{1,0:T(8,128)(2,1)} %fusion.3), channel_id=1, source_target_pairs={{0,384},{128,256},{256,128},{384,0},{1,385},{129,257},{257,129},{3... | collective-permute-start | bytes 196616 | tf_op jit(solution)/shard_map/ppermute | solution.py:139
  66.0 29.6 %all-to-all-start.1 = ((bf16[8,192,512]{2,1,0:T(8,128)(2,1)}), bf16[8,192,512]{2,1,0:T(8,128)(2,1)S(1)}, u32[]{:S(2)}, u32[]{:S(2)}) async-start(bf16[8,192,512]{2,1,0:T(8,128)(2,1)} %project_keys.1), calls=%async_computation.1 | async-start | bytes 3145728 | tf_op jit(solution)/shard_map/all_to_all | solution.py:143

commit v15 on v7

--- a/solution.py
+++ b/solution.py
@@ -12,8 +12,8 @@
 
 Z, PLANE, REP = ("zh", "zl"), ("yh", "x"), ("yl", "core")
 PLANES, PEERS = 16, 8
-ROWS, SOURCES = 64, 4
-KERNEL_VMEM = 24 * 1024 * 1024
+ROWS, SOURCES = 96, 4
+PACK_VMEM, PROJECT_VMEM = 60 * 1024 * 1024, 24 * 1024 * 1024
 
 
 def outer_update(averaged, outer_layer, moment_layer):
@@ -58,7 +58,7 @@
             pltpu.HBM((PEERS, tokens, features // PEERS), jnp.bfloat16),
             jax.ShapeDtypeStruct((tokens, 1), jnp.float32),
         ],
-        compiler_params=pltpu.CompilerParams(vmem_limit_bytes=KERNEL_VMEM),
+        compiler_params=pltpu.CompilerParams(vmem_limit_bytes=PACK_VMEM),
         cost_estimate=pl.CostEstimate(
             flops=4 * tokens * features, bytes_accessed=4 * tokens * features, transcendentals=tokens
         ),
@@ -67,7 +67,7 @@
 
 
 STEPS = 4
-HELD = (0, -1, 1, 2)
+HELD = (0, 2, -1, 1)
 
 
 def project_kernel(residue_ref, tokens_ref, *refs):
@@ -100,7 +100,7 @@
             scratch_shapes=[pltpu.VMEM((features, width), jnp.bfloat16)],
         ),
         out_shape=pltpu.HBM((peers, rows, width), jnp.bfloat16),
-        compiler_params=pltpu.CompilerParams(vmem_limit_bytes=KERNEL_VMEM),
+        compiler_params=pltpu.CompilerParams(vmem_limit_bytes=PROJECT_VMEM),
         cost_estimate=pl.CostEstimate(
             flops=2 * peers * rows * features * width,
             bytes_accessed=2 * (peers * rows * (features + width) + features * width),
@@ -124,9 +124,9 @@
     own = lax.all_gather(block, "zh", axis=0, tiled=True)
     held = (
         own,
+        moved(own, lambda z: z + 2 if z % 2 == 0 else z - 2),
         moved(own, lambda z: z + 1),
         moved(own, lambda z: z - 1),
-        moved(own, lambda z: z + 2 if z % 2 == 0 else z - 2),
     )
     residue = lax.axis_index("zl").astype(jnp.int32)[None]
     partial = project(residue, tokens, held)

time: 93.4 us -> 92.2 us (0.987)
  the two profiles are of different devices: /device:TPU:464 before, /device:TPU:400 now
where the time goes in v15:
time: 92.2 us; the launch traced here: 91.7 us
  starting transfers between devices  39.5 us (43%)
  blocking collectives  19.4 us (21%)
  waiting for transfers between devices  19.1 us (21%)
  Pallas kernels  8.54 us (9%)
  other arithmetic  3.79 us (4%)
  between operations  1.37 us (1%)
    all_gather x1, blocking collectives, shards(): own = lax.all_gather(block, 'zh', axis=0, tiled=True)  19.4 us
    all_to_all x1, starting transfers between devices, shards(): partial = lax.all_to_all(partial, PLANE, 0, 0, tiled=True)  15 us
    ppermute x3, waiting for transfers between devices, shards(): summed += lax.ppermute(pseudo_grad, REP, pairs).astype(jnp.float32)  11.3 us
    ppermute x3, starting transfers between devices, moved(): lax.ppermute(block, Z, [(z, target(z) % PLANES) for z in range(PLANES)])  9.45 us
    ppermute x3, starting transfers between devices, shards(): summed += lax.ppermute(pseudo_grad, REP, pairs).astype(jnp.float32)  7.59 us
    all_to_all x1, starting transfers between devices, shards(): tokens = lax.all_to_all(packed, PLANE, 0, 0, tiled=True)  7.4 us
    ppermute x3, waiting for transfers between devices, moved(): lax.ppermute(block, Z, [(z, target(z) % PLANES) for z in range(PLANES)])  5.15 us
    pallas_call x1, Pallas kernels, pack(): pl.pallas_call(pack_kernel, grid=(tokens // ROWS,), in_specs=[pl.BlockSpe...  4.47 us
  transfers between devices with their start and end apart: 8, of which 5 were waited for; matrix products, arithmetic and copies ran while one was open for 3% of the time, Pallas kernels for 0%

profile of v15, /device:TPU:400, one launch (start us, length us, event | category | flops | bytes accessed | tf_op | source)
XLA Modules:
  0.0 91.7 jit_solution(5334515789168686785)
XLA Ops:
  0.6 4.5 %pack_hidden.1 = (bf16[8,192,1024]{2,1,0:T(8,128)(2,1)}, f32[192,1]{1,0:T(8,128)}) custom-call(bf16[192,8192]{1,0:T(8,128)(2,1)} %bitcast.25, f32[1,8192]{1,0:T(1,128)} %bitcast.27), custom_call_target="tpu_custom_call" | custom-call | flops 6291456 | bytes 6291456 | tf_op jit(solution)/shard_map/pack_hidden/pallas_call | solution.py:46
  5.1 0.0 copy-start.1
  5.1 7.4 %all-to-all-start = ((bf16[8,192,1024]{2,1,0:T(8,128)(2,1)}), bf16[8,192,1024]{2,1,0:T(8,128)(2,1)S(1)}, u32[]{:S(2)}, u32[]{:S(2)}) async-start(bf16[8,192,1024]{2,1,0:T(8,128)(2,1)} %get-tuple-element.11), calls=%async_computation | async-start | bytes 6291456 | tf_op jit(solution)/shard_map/all_to_all | solution.py:123
  12.5 0.0 copy-done.1
  12.5 19.4 %all_gather.3.refs_0_ = bf16[256,512]{1,0:T(8,128)(2,1)S(1)} all-gather(bf16[64,512]{1,0:T(8,128)(2,1)S(1)} %bitcast.26), channel_id=1, replica_groups=mesh['yl'=2,'core'=2,'zh'=4,'zl'=4,'yh'=2,'x'=4] {'zh'}, dimensions={0}, use_global_device_ids=true | all-gather | bytes 327680 | tf_op jit(solution)/shard_map/all_gather | solution.py:124
  31.9 2.4 %collective-permute-start = (bf16[256,512]{1,0:T(8,128)(2,1)S(1)}, bf16[256,512]{1,0:T(8,128)(2,1)}, u32[]{:S(2)}, u32[]{:S(2)}) collective-permute-start(bf16[256,512]{1,0:T(8,128)(2,1)S(1)} %all_gather.3.refs_0_), channel_id=1, source_target_pairs={{0,16},{8,120},{16,32},{24,8},{32,48},{40,24},{48,64},{56,40},{64,... | collective-permute-start | bytes 786440 | tf_op jit(solution)/shard_map/ppermute | solution.py:114
  34.3 3.4 %collective-permute-start.1 = (bf16[256,512]{1,0:T(8,128)(2,1)S(1)}, bf16[256,512]{1,0:T(8,128)(2,1)}, u32[]{:S(2)}, u32[]{:S(2)}) collective-permute-start(bf16[256,512]{1,0:T(8,128)(2,1)S(1)} %all_gather.3.refs_0_), channel_id=1, source_target_pairs={{0,8},{8,16},{16,24},{24,32},{32,40},{40,48},{48,56},{56,64},{64,7... | collective-permute-start | bytes 786440 | tf_op jit(solution)/shard_map/ppermute | solution.py:114
  37.8 3.6 %collective-permute-start.2 = (bf16[256,512]{1,0:T(8,128)(2,1)S(1)}, bf16[256,512]{1,0:T(8,128)(2,1)}, u32[]{:S(2)}, u32[]{:S(2)}) collective-permute-start(bf16[256,512]{1,0:T(8,128)(2,1)S(1)} %all_gather.3.refs_0_), channel_id=1, source_target_pairs={{0,120},{8,0},{16,8},{24,16},{32,24},{40,32},{48,40},{56,48},{64,5... | collective-permute-start | bytes 786440 | tf_op jit(solution)/shard_map/ppermute | solution.py:114
  41.4 2.4 %collective-permute-done.refs_1_ = bf16[256,512]{1,0:T(8,128)(2,1)} collective-permute-done((bf16[256,512]{1,0:T(8,128)(2,1)S(1)}, bf16[256,512]{1,0:T(8,128)(2,1)}, u32[]{:S(2)}, u32[]{:S(2)}) %collective-permute-start) | collective-permute-done | bytes 262176 | tf_op jit(solution)/shard_map/ppermute | solution.py:114
  43.8 2.7 %collective-permute-done.1.refs_2_ = bf16[256,512]{1,0:T(8,128)(2,1)} collective-permute-done((bf16[256,512]{1,0:T(8,128)(2,1)S(1)}, bf16[256,512]{1,0:T(8,128)(2,1)}, u32[]{:S(2)}, u32[]{:S(2)}) %collective-permute-start.1) | collective-permute-done | bytes 262176 | tf_op jit(solution)/shard_map/ppermute | solution.py:114
  46.5 0.0 collective-permute-done.2.refs_3_
  46.5 2.7 %all-to-all-done.tokens_ref = bf16[8,192,1024]{2,1,0:T(8,128)(2,1)S(1)} async-done(((bf16[8,192,1024]{2,1,0:T(8,128)(2,1)}), bf16[8,192,1024]{2,1,0:T(8,128)(2,1)S(1)}, u32[]{:S(2)}, u32[]{:S(2)}) %all-to-all-start) | async-done | bytes 3145760 | tf_op jit(solution)/shard_map/all_to_all | solution.py:123
  49.2 4.1 %project_keys.1 = bf16[8,192,512]{2,1,0:T(8,128)(2,1)} custom-call(s32[1]{0:T(128)} %bitcast.residue_ref, bf16[8,192,1024]{2,1,0:T(8,128)(2,1)S(1)} %all-to-all-done.tokens_ref, bf16[256,512]{1,0:T(8,128)(2,1)S(1)} %all_gather.3.refs_0_, bf16[256,512]{1,0:T(8,128)(2,1)} %collective-permute-done.refs_1_, bf16[256,512]{1,0:T(8,128)(2,1)} %collective-permute-done.1.refs_2_, ...), custom_call_target="tpu_custom_call" | custom-call | flops 1610612736 | bytes 5767168 | tf_op jit(solution)/shard_map/project_keys/pallas_call | solution.py:93
  53.3 0.0 copy-start
  53.3 15.0 %all-to-all-start.1 = ((bf16[8,192,512]{2,1,0:T(8,128)(2,1)}), bf16[8,192,512]{2,1,0:T(8,128)(2,1)S(1)}, u32[]{:S(2)}, u32[]{:S(2)}) async-start(bf16[8,192,512]{2,1,0:T(8,128)(2,1)} %project_keys.1), calls=%async_computation.1 | async-start | bytes 3145728 | tf_op jit(solution)/shard_map/all_to_all | solution.py:134
  69.0 0.9 %fusion.1 = bf16[64,512]{1,0:T(8,128)(2,1)S(1)} fusion(f32[7,64,512]{2,1,0:T(8,128)} %param.11, s32[]{:T(128)S(6)} %select_n.7, bf16[1,7,64,512]{3,2,1,0:T(8,128)(2,1)} %param.13), kind=kLoop, calls=%fused_computation.5 | loop fusion | flops 98304 | bytes 262148 | tf_op jit(solution)/shard_map/convert_element_type | solution.py:139
  69.9 1.9 %collective-permute-start.5 = (bf16[64,512]{1,0:T(8,128)(2,1)S(1)}, bf16[64,512]{1,0:T(8,128)(2,1)S(1)}, u32[]{:S(2)}, u32[]{:S(2)}) collective-permute-start(bf16[64,512]{1,0:T(8,128)(2,1)S(1)} %fusion.1), channel_id=1, source_target_pairs={{0,384},{128,256},{256,128},{384,0},{1,385},{129,257},{257,129},{3... | collective-permute-start | bytes 196616 | tf_op jit(solution)/shard_map/ppermute | solution.py:143
  71.8 3.2 %collective-permute-start.4 = (bf16[64,512]{1,0:T(8,128)(2,1)S(1)}, bf16[64,512]{1,0:T(8,128)(2,1)S(1)}, u32[]{:S(2)}, u32[]{:S(2)}) collective-permute-start(bf16[64,512]{1,0:T(8,128)(2,1)S(1)} %fusion.1), channel_id=1, source_target_pairs={{0,256},{128,384},{256,0},{384,128},{1,257},{129,385},{257,1},{385... | collective-permute-start | bytes 196616 | tf_op jit(solution)/shard_map/ppermute | solution.py:143
  75.0 2.5 %collective-permute-start.3 = (bf16[64,512]{1,0:T(8,128)(2,1)S(1)}, bf16[64,512]{1,0:T(8,128)(2,1)S(1)}, u32[]{:S(2)}, u32[]{:S(2)}) collective-permute-start(bf16[64,512]{1,0:T(8,128)(2,1)S(1)} %fusion.1), channel_id=1, source_target_pairs={{0,128},{128,0},{256,384},{384,256},{1,129},{129,1},{257,385},{385... | collective-permute-start | bytes 196616 | tf_op jit(solution)/shard_map/ppermute | solution.py:143
  77.5 0.0 copy-done
  77.5 0.1 reduce
  77.6 8.9 %collective-permute-done.5 = bf16[64,512]{1,0:T(8,128)(2,1)S(1)} collective-permute-done((bf16[64,512]{1,0:T(8,128)(2,1)S(1)}, bf16[64,512]{1,0:T(8,128)(2,1)S(1)}, u32[]{:S(2)}, u32[]{:S(2)}) %collective-permute-start.5) | collective-permute-done | bytes 65568 | tf_op jit(solution)/shard_map/ppermute | solution.py:143
  86.5 2.4 %collective-permute-done.4 = bf16[64,512]{1,0:T(8,128)(2,1)S(1)} collective-permute-done((bf16[64,512]{1,0:T(8,128)(2,1)S(1)}, bf16[64,512]{1,0:T(8,128)(2,1)S(1)}, u32[]{:S(2)}, u32[]{:S(2)}) %collective-permute-start.4) | collective-permute-done | bytes 65568 | tf_op jit(solution)/shard_map/ppermute | solution.py:143
  88.9 0.0 collective-permute-done.3
  88.9 1.8 %fusion.4 = (bf16[1,64,512]{2,1,0:T(8,128)(2,1)}, f32[64,512]{1,0:T(8,128)}, f32[64,512]{1,0:T(8,128)}) fusion(bf16[1,7,64,512]{3,2,1,0:T(8,128)(2,1)} %param.13, s32[]{:T(128)S(6)} %select_n.7, bf16[64,512]{1,0:T(8,128)(2,1)S(1)} %collective-permute-done.5, bf16[64,512]{1,0:T(8,128)(2,1)S(1)} %collective-permute-done.4, ...), kind=kLoop, calls=%fused_computation.11 | loop fusion | flops 589824 | bytes 917508 | tf_op jit(solution)/shard_map/broadcast_in_dim | solution.py:149
  90.7 0.0 all-to-all-done.1
  90.7 0.2 convert_reduce_fusion
  90.9 0.8 fusion
Async XLA Ops:
  5.1 7.4 %copy-start.1 = (bf16[1,64,512]{2,1,0:T(8,128)(2,1)S(1)}, bf16[1,64,512]{2,1,0:T(8,128)(2,1)}, u32[]{:S(2)}) copy-start(bf16[1,64,512]{2,1,0:T(8,128)(2,1)} %param.9) | copy-start | bytes 196612
  5.1 44.1 %all-to-all-start = ((bf16[8,192,1024]{2,1,0:T(8,128)(2,1)}), bf16[8,192,1024]{2,1,0:T(8,128)(2,1)S(1)}, u32[]{:S(2)}, u32[]{:S(2)}) async-start(bf16[8,192,1024]{2,1,0:T(8,128)(2,1)} %get-tuple-element.11), calls=%async_computation | async-start | bytes 6291456 | tf_op jit(solution)/shard_map/all_to_all | solution.py:123
  31.9 11.9 %collective-permute-start = (bf16[256,512]{1,0:T(8,128)(2,1)S(1)}, bf16[256,512]{1,0:T(8,128)(2,1)}, u32[]{:S(2)}, u32[]{:S(2)}) collective-permute-start(bf16[256,512]{1,0:T(8,128)(2,1)S(1)} %all_gather.3.refs_0_), channel_id=1, source_target_pairs={{0,16},{8,120},{16,32},{24,8},{32,48},{40,24},{48,64},{56,40},{64,... | collective-permute-start | bytes 786440 | tf_op jit(solution)/shard_map/ppermute | solution.py:114
  34.3 12.2 %collective-permute-start.1 = (bf16[256,512]{1,0:T(8,128)(2,1)S(1)}, bf16[256,512]{1,0:T(8,128)(2,1)}, u32[]{:S(2)}, u32[]{:S(2)}) collective-permute-start(bf16[256,512]{1,0:T(8,128)(2,1)S(1)} %all_gather.3.refs_0_), channel_id=1, source_target_pairs={{0,8},{8,16},{16,24},{24,32},{32,40},{40,48},{48,56},{56,64},{64,7... | collective-permute-start | bytes 786440 | tf_op jit(solution)/shard_map/ppermute | solution.py:114
  37.8 8.8 %collective-permute-start.2 = (bf16[256,512]{1,0:T(8,128)(2,1)S(1)}, bf16[256,512]{1,0:T(8,128)(2,1)}, u32[]{:S(2)}, u32[]{:S(2)}) collective-permute-start(bf16[256,512]{1,0:T(8,128)(2,1)S(1)} %all_gather.3.refs_0_), channel_id=1, source_target_pairs={{0,120},{8,0},{16,8},{24,16},{32,24},{40,32},{48,40},{56,48},{64,5... | collective-permute-start | bytes 786440 | tf_op jit(solution)/shard_map/ppermute | solution.py:114
  53.3 24.2 %copy-start = (f32[192,1]{1,0:T(8,128)S(1)}, f32[192,1]{1,0:T(8,128)}, u32[]{:S(2)}) copy-start(f32[192,1]{1,0:T(8,128)} %get-tuple-element.14) | copy-start | bytes 2308
  53.3 37.4 %all-to-all-start.1 = ((bf16[8,192,512]{2,1,0:T(8,128)(2,1)}), bf16[8,192,512]{2,1,0:T(8,128)(2,1)S(1)}, u32[]{:S(2)}, u32[]{:S(2)}) async-start(bf16[8,192,512]{2,1,0:T(8,128)(2,1)} %project_keys.1), calls=%async_computation.1 | async-start | bytes 3145728 | tf_op jit(solution)/shard_map/all_to_all | solution.py:134
  69.9 16.6 %collective-permute-start.5 = (bf16[64,512]{1,0:T(8,128)(2,1)S(1)}, bf16[64,512]{1,0:T(8,128)(2,1)S(1)}, u32[]{:S(2)}, u32[]{:S(2)}) collective-permute-start(bf16[64,512]{1,0:T(8,128)(2,1)S(1)} %fusion.1), channel_id=1, source_target_pairs={{0,384},{128,256},{256,128},{384,0},{1,385},{129,257},{257,129},{3... | collective-permute-start | bytes 196616 | tf_op jit(solution)/shard_map/ppermute | solution.py:143
  71.8 17.1 %collective-permute-start.4 = (bf16[64,512]{1,0:T(8,128)(2,1)S(1)}, bf16[64,512]{1,0:T(8,128)(2,1)S(1)}, u32[]{:S(2)}, u32[]{:S(2)}) collective-permute-start(bf16[64,512]{1,0:T(8,128)(2,1)S(1)} %fusion.1), channel_id=1, source_target_pairs={{0,256},{128,384},{256,0},{384,128},{1,257},{129,385},{257,1},{385... | collective-permute-start | bytes 196616 | tf_op jit(solution)/shard_map/ppermute | solution.py:143
  75.0 13.9 %collective-permute-start.3 = (bf16[64,512]{1,0:T(8,128)(2,1)S(1)}, bf16[64,512]{1,0:T(8,128)(2,1)S(1)}, u32[]{:S(2)}, u32[]{:S(2)}) collective-permute-start(bf16[64,512]{1,0:T(8,128)(2,1)S(1)} %fusion.1), channel_id=1, source_target_pairs={{0,128},{128,0},{256,384},{384,256},{1,129},{129,1},{257,385},{385... | collective-permute-start | bytes 196616 | tf_op jit(solution)/shard_map/ppermute | solution.py:143

commit v16 on v15

--- a/solution.py
+++ b/solution.py
@@ -67,7 +67,7 @@
 
 
 STEPS = 4
-HELD = (0, 2, -1, 1)
+HELD = (0, 1, -1, 2)
 
 
 def project_kernel(residue_ref, tokens_ref, *refs):
@@ -124,19 +124,22 @@
     own = lax.all_gather(block, "zh", axis=0, tiled=True)
     held = (
         own,
+        moved(own, lambda z: z - 1),
+        moved(own, lambda z: z + 1),
         moved(own, lambda z: z + 2 if z % 2 == 0 else z - 2),
-        moved(own, lambda z: z + 1),
-        moved(own, lambda z: z - 1),
     )
+    _, fragment_index = lax.optimization_barrier((own, fragment_index))
+    layer_idx = fragment_index[0]
+    outer_layer = lax.dynamic_index_in_dim(outer_params, layer_idx, 0, keepdims=False)
+    inner_layer = lax.dynamic_index_in_dim(inner_params[0], layer_idx, 0, keepdims=False)
+    pseudo_grad = (outer_layer - inner_layer.astype(jnp.float32)).astype(jnp.bfloat16)
     residue = lax.axis_index("zl").astype(jnp.int32)[None]
     partial = project(residue, tokens, held)
-    partial, fragment_index = lax.optimization_barrier((partial, fragment_index))
+    partial, layer_idx, pseudo_grad = lax.optimization_barrier((partial, layer_idx, pseudo_grad))
     partial = lax.all_to_all(partial, PLANE, 0, 0, tiled=True)
-    layer_idx = fragment_index[0]
     outer_layer = lax.dynamic_index_in_dim(outer_params, layer_idx, 0, keepdims=False)
     moment_layer = lax.dynamic_index_in_dim(outer_moment, layer_idx, 0, keepdims=False)
     inner_layer = lax.dynamic_index_in_dim(inner_params[0], layer_idx, 0, keepdims=False)
-    pseudo_grad = (outer_layer - inner_layer.astype(jnp.float32)).astype(jnp.bfloat16)
     summed = pseudo_grad.astype(jnp.float32)
     for other in range(1, replicas):
         pairs = [(replica, replica ^ other) for replica in range(replicas)]

time: 92.2 us -> 92.2 us (level)
    ppermute x3, waiting for transfers between devices: 11.3 us -> 12.9 us  [shards(): summed += lax.ppermute(pseudo_grad, REP, pairs).astype(jnp.float32)]
    ppermute x3, waiting for transfers between devices: 5.15 us -> 3.57 us  [moved(): lax.ppermute(block, Z, [(z, target(z) % PLANES) for z in range(PLANES)])]
where the time goes in v16:
time: 92.2 us; the launch traced here: 91.7 us
  starting transfers between devices  39.5 us (43%)
  blocking collectives  19.4 us (21%)
  waiting for transfers between devices  19.1 us (21%)
  Pallas kernels  8.54 us (9%)
  other arithmetic  3.79 us (4%)
  between operations  1.37 us (1%)
    all_gather x1, blocking collectives, shards(): own = lax.all_gather(block, 'zh', axis=0, tiled=True)  19.4 us
    all_to_all x1, starting transfers between devices, shards(): partial = lax.all_to_all(partial, PLANE, 0, 0, tiled=True)  15 us
    ppermute x3, waiting for transfers between devices, shards(): summed += lax.ppermute(pseudo_grad, REP, pairs).astype(jnp.float32)  12.9 us
    ppermute x3, starting transfers between devices, moved(): lax.ppermute(block, Z, [(z, target(z) % PLANES) for z in range(PLANES)])  9.45 us
    ppermute x3, starting transfers between devices, shards(): summed += lax.ppermute(pseudo_grad, REP, pairs).astype(jnp.float32)  7.57 us
    all_to_all x1, starting transfers between devices, shards(): tokens = lax.all_to_all(packed, PLANE, 0, 0, tiled=True)  7.4 us
    pallas_call x1, Pallas kernels, pack(): pl.pallas_call(pack_kernel, grid=(tokens // ROWS,), in_specs=[pl.BlockSpe...  4.47 us
    pallas_call x1, Pallas kernels, project(): pl.pallas_call(project_kernel, grid_spec=pltpu.PrefetchScalarGridSpec(num...  4.07 us
  transfers between devices with their start and end apart: 8, of which 5 were waited for; matrix products, arithmetic and copies ran while one was open for 3% of the time, Pallas kernels for 0%

profile of v16, /device:TPU:400, one launch (start us, length us, event | category | flops | bytes accessed | tf_op | source)
XLA Modules:
  0.0 91.7 jit_solution(540318877316050580)
XLA Ops:
  0.6 4.5 %pack_hidden.1 = (bf16[8,192,1024]{2,1,0:T(8,128)(2,1)}, f32[192,1]{1,0:T(8,128)}) custom-call(bf16[192,8192]{1,0:T(8,128)(2,1)} %bitcast.31, f32[1,8192]{1,0:T(1,128)} %bitcast.33), custom_call_target="tpu_custom_call" | custom-call | flops 6291456 | bytes 6291456 | tf_op jit(solution)/shard_map/pack_hidden/pallas_call | solution.py:46
  5.1 0.0 copy-start.1
  5.1 7.4 %all-to-all-start = ((bf16[8,192,1024]{2,1,0:T(8,128)(2,1)}), bf16[8,192,1024]{2,1,0:T(8,128)(2,1)S(1)}, u32[]{:S(2)}, u32[]{:S(2)}) async-start(bf16[8,192,1024]{2,1,0:T(8,128)(2,1)} %get-tuple-element.13), calls=%async_computation | async-start | bytes 6291456 | tf_op jit(solution)/shard_map/all_to_all | solution.py:123
  12.5 0.0 copy-done.1
  12.5 19.4 %all_gather.3.refs_0_ = bf16[256,512]{1,0:T(8,128)(2,1)S(1)} all-gather(bf16[64,512]{1,0:T(8,128)(2,1)S(1)} %bitcast.32), channel_id=1, replica_groups=mesh['yl'=2,'core'=2,'zh'=4,'zl'=4,'yh'=2,'x'=4] {'zh'}, dimensions={0}, use_global_device_ids=true | all-gather | bytes 327680 | tf_op jit(solution)/shard_map/all_gather | solution.py:124
  31.9 2.4 %collective-permute-start.2 = (bf16[256,512]{1,0:T(8,128)(2,1)S(1)}, bf16[256,512]{1,0:T(8,128)(2,1)}, u32[]{:S(2)}, u32[]{:S(2)}) collective-permute-start(bf16[256,512]{1,0:T(8,128)(2,1)S(1)} %all_gather.3.refs_0_), channel_id=1, source_target_pairs={{0,16},{8,120},{16,32},{24,8},{32,48},{40,24},{48,64},{56,40},{64,... | collective-permute-start | bytes 786440 | tf_op jit(solution)/shard_map/ppermute | solution.py:114
  34.3 3.4 %collective-permute-start.1 = (bf16[256,512]{1,0:T(8,128)(2,1)S(1)}, bf16[256,512]{1,0:T(8,128)(2,1)}, u32[]{:S(2)}, u32[]{:S(2)}) collective-permute-start(bf16[256,512]{1,0:T(8,128)(2,1)S(1)} %all_gather.3.refs_0_), channel_id=1, source_target_pairs={{0,8},{8,16},{16,24},{24,32},{32,40},{40,48},{48,56},{56,64},{64,7... | collective-permute-start | bytes 786440 | tf_op jit(solution)/shard_map/ppermute | solution.py:114
  37.8 3.6 %collective-permute-start = (bf16[256,512]{1,0:T(8,128)(2,1)S(1)}, bf16[256,512]{1,0:T(8,128)(2,1)}, u32[]{:S(2)}, u32[]{:S(2)}) collective-permute-start(bf16[256,512]{1,0:T(8,128)(2,1)S(1)} %all_gather.3.refs_0_), channel_id=1, source_target_pairs={{0,120},{8,0},{16,8},{24,16},{32,24},{40,32},{48,40},{56,48},{64,5... | collective-permute-start | bytes 786440 | tf_op jit(solution)/shard_map/ppermute | solution.py:114
  42.0 0.9 %fusion.3 = bf16[64,512]{1,0:T(8,128)(2,1)S(1)} fusion(f32[7,64,512]{2,1,0:T(8,128)} %param.11, s32[]{:T(128)S(6)} %select_n.11, bf16[1,7,64,512]{3,2,1,0:T(8,128)(2,1)} %param.13), kind=kLoop, calls=%fused_computation.7 | loop fusion | flops 98304 | bytes 262148 | tf_op jit(solution)/shard_map/convert_element_type | solution.py:135
  43.0 0.9 collective-permute-done.2.refs_3_
  43.8 2.7 %collective-permute-done.1.refs_2_ = bf16[256,512]{1,0:T(8,128)(2,1)} collective-permute-done((bf16[256,512]{1,0:T(8,128)(2,1)S(1)}, bf16[256,512]{1,0:T(8,128)(2,1)}, u32[]{:S(2)}, u32[]{:S(2)}) %collective-permute-start.1) | collective-permute-done | bytes 262176 | tf_op jit(solution)/shard_map/ppermute | solution.py:114
  46.5 0.0 collective-permute-done.refs_1_
  46.5 2.7 %all-to-all-done.tokens_ref = bf16[8,192,1024]{2,1,0:T(8,128)(2,1)S(1)} async-done(((bf16[8,192,1024]{2,1,0:T(8,128)(2,1)}), bf16[8,192,1024]{2,1,0:T(8,128)(2,1)S(1)}, u32[]{:S(2)}, u32[]{:S(2)}) %all-to-all-start) | async-done | bytes 3145760 | tf_op jit(solution)/shard_map/all_to_all | solution.py:123
  49.2 4.1 %project_keys.1 = bf16[8,192,512]{2,1,0:T(8,128)(2,1)} custom-call(s32[1]{0:T(128)} %bitcast.residue_ref, bf16[8,192,1024]{2,1,0:T(8,128)(2,1)S(1)} %all-to-all-done.tokens_ref, bf16[256,512]{1,0:T(8,128)(2,1)S(1)} %all_gather.3.refs_0_, bf16[256,512]{1,0:T(8,128)(2,1)} %collective-permute-done.refs_1_, bf16[256,512]{1,0:T(8,128)(2,1)} %collective-permute-done.1.refs_2_, ...), custom_call_target="tpu_custom_call" | custom-call | flops 1610612736 | bytes 5767168 | tf_op jit(solution)/shard_map/project_keys/pallas_call | solution.py:93
  53.3 0.0 copy-start
  53.3 15.0 %all-to-all-start.1 = ((bf16[8,192,512]{2,1,0:T(8,128)(2,1)}), bf16[8,192,512]{2,1,0:T(8,128)(2,1)S(1)}, u32[]{:S(2)}, u32[]{:S(2)}) async-start(bf16[8,192,512]{2,1,0:T(8,128)(2,1)} %project_keys.1), calls=%async_computation.1 | async-start | bytes 3145728 | tf_op jit(solution)/shard_map/all_to_all | solution.py:139
  68.3 1.9 %collective-permute-start.5 = (bf16[64,512]{1,0:T(8,128)(2,1)S(1)}, bf16[64,512]{1,0:T(8,128)(2,1)S(1)}, u32[]{:S(2)}, u32[]{:S(2)}) collective-permute-start(bf16[64,512]{1,0:T(8,128)(2,1)S(1)} %fusion.3), channel_id=1, source_target_pairs={{0,384},{128,256},{256,128},{384,0},{1,385},{129,257},{257,129},{3... | collective-permute-start | bytes 196616 | tf_op jit(solution)/shard_map/ppermute | solution.py:146
  70.2 3.2 %collective-permute-start.4 = (bf16[64,512]{1,0:T(8,128)(2,1)S(1)}, bf16[64,512]{1,0:T(8,128)(2,1)S(1)}, u32[]{:S(2)}, u32[]{:S(2)}) collective-permute-start(bf16[64,512]{1,0:T(8,128)(2,1)S(1)} %fusion.3), channel_id=1, source_target_pairs={{0,256},{128,384},{256,0},{384,128},{1,257},{129,385},{257,1},{385... | collective-permute-start | bytes 196616 | tf_op jit(solution)/shard_map/ppermute | solution.py:146
  73.4 2.5 %collective-permute-start.3 = (bf16[64,512]{1,0:T(8,128)(2,1)S(1)}, bf16[64,512]{1,0:T(8,128)(2,1)S(1)}, u32[]{:S(2)}, u32[]{:S(2)}) collective-permute-start(bf16[64,512]{1,0:T(8,128)(2,1)S(1)} %fusion.3), channel_id=1, source_target_pairs={{0,128},{128,0},{256,384},{384,256},{1,129},{129,1},{257,385},{385... | collective-permute-start | bytes 196616 | tf_op jit(solution)/shard_map/ppermute | solution.py:146
  75.9 0.0 copy-done
  75.9 0.1 reduce
  76.1 10.5 %collective-permute-done.5 = bf16[64,512]{1,0:T(8,128)(2,1)S(1)} collective-permute-done((bf16[64,512]{1,0:T(8,128)(2,1)S(1)}, bf16[64,512]{1,0:T(8,128)(2,1)S(1)}, u32[]{:S(2)}, u32[]{:S(2)}) %collective-permute-start.5) | collective-permute-done | bytes 65568 | tf_op jit(solution)/shard_map/ppermute | solution.py:146
  86.5 2.4 %collective-permute-done.4 = bf16[64,512]{1,0:T(8,128)(2,1)S(1)} collective-permute-done((bf16[64,512]{1,0:T(8,128)(2,1)S(1)}, bf16[64,512]{1,0:T(8,128)(2,1)S(1)}, u32[]{:S(2)}, u32[]{:S(2)}) %collective-permute-start.4) | collective-permute-done | bytes 65568 | tf_op jit(solution)/shard_map/ppermute | solution.py:146
  88.9 0.0 collective-permute-done.3
  88.9 1.8 %fusion.4 = (bf16[1,64,512]{2,1,0:T(8,128)(2,1)}, f32[64,512]{1,0:T(8,128)}, f32[64,512]{1,0:T(8,128)}) fusion(bf16[1,7,64,512]{3,2,1,0:T(8,128)(2,1)} %param.13, s32[]{:T(128)S(6)} %select_n.12, bf16[64,512]{1,0:T(8,128)(2,1)S(1)} %collective-permute-done.5, bf16[64,512]{1,0:T(8,128)(2,1)S(1)} %collective-permute-done.4, ...), kind=kLoop, calls=%fused_computation.11 | loop fusion | flops 589824 | bytes 917508 | tf_op jit(solution)/shard_map/broadcast_in_dim | solution.py:152
  90.7 0.0 all-to-all-done.1
  90.7 0.2 convert_reduce_fusion
  90.9 0.8 fusion
Async XLA Ops:
  5.1 7.4 %copy-start.1 = (bf16[1,64,512]{2,1,0:T(8,128)(2,1)S(1)}, bf16[1,64,512]{2,1,0:T(8,128)(2,1)}, u32[]{:S(2)}) copy-start(bf16[1,64,512]{2,1,0:T(8,128)(2,1)} %param.9) | copy-start | bytes 196612
  5.1 44.1 %all-to-all-start = ((bf16[8,192,1024]{2,1,0:T(8,128)(2,1)}), bf16[8,192,1024]{2,1,0:T(8,128)(2,1)S(1)}, u32[]{:S(2)}, u32[]{:S(2)}) async-start(bf16[8,192,1024]{2,1,0:T(8,128)(2,1)} %get-tuple-element.13), calls=%async_computation | async-start | bytes 6291456 | tf_op jit(solution)/shard_map/all_to_all | solution.py:123
  31.9 11.9 %collective-permute-start.2 = (bf16[256,512]{1,0:T(8,128)(2,1)S(1)}, bf16[256,512]{1,0:T(8,128)(2,1)}, u32[]{:S(2)}, u32[]{:S(2)}) collective-permute-start(bf16[256,512]{1,0:T(8,128)(2,1)S(1)} %all_gather.3.refs_0_), channel_id=1, source_target_pairs={{0,16},{8,120},{16,32},{24,8},{32,48},{40,24},{48,64},{56,40},{64,... | collective-permute-start | bytes 786440 | tf_op jit(solution)/shard_map/ppermute | solution.py:114
  34.3 12.2 %collective-permute-start.1 = (bf16[256,512]{1,0:T(8,128)(2,1)S(1)}, bf16[256,512]{1,0:T(8,128)(2,1)}, u32[]{:S(2)}, u32[]{:S(2)}) collective-permute-start(bf16[256,512]{1,0:T(8,128)(2,1)S(1)} %all_gather.3.refs_0_), channel_id=1, source_target_pairs={{0,8},{8,16},{16,24},{24,32},{32,40},{40,48},{48,56},{56,64},{64,7... | collective-permute-start | bytes 786440 | tf_op jit(solution)/shard_map/ppermute | solution.py:114
  37.8 8.8 %collective-permute-start = (bf16[256,512]{1,0:T(8,128)(2,1)S(1)}, bf16[256,512]{1,0:T(8,128)(2,1)}, u32[]{:S(2)}, u32[]{:S(2)}) collective-permute-start(bf16[256,512]{1,0:T(8,128)(2,1)S(1)} %all_gather.3.refs_0_), channel_id=1, source_target_pairs={{0,120},{8,0},{16,8},{24,16},{32,24},{40,32},{48,40},{56,48},{64,5... | collective-permute-start | bytes 786440 | tf_op jit(solution)/shard_map/ppermute | solution.py:114
  53.3 22.7 %copy-start = (f32[192,1]{1,0:T(8,128)S(1)}, f32[192,1]{1,0:T(8,128)}, u32[]{:S(2)}) copy-start(f32[192,1]{1,0:T(8,128)} %get-tuple-element.17) | copy-start | bytes 2308
  53.3 37.4 %all-to-all-start.1 = ((bf16[8,192,512]{2,1,0:T(8,128)(2,1)}), bf16[8,192,512]{2,1,0:T(8,128)(2,1)S(1)}, u32[]{:S(2)}, u32[]{:S(2)}) async-start(bf16[8,192,512]{2,1,0:T(8,128)(2,1)} %project_keys.1), calls=%async_computation.1 | async-start | bytes 3145728 | tf_op jit(solution)/shard_map/all_to_all | solution.py:139
  68.3 18.2 %collective-permute-start.5 = (bf16[64,512]{1,0:T(8,128)(2,1)S(1)}, bf16[64,512]{1,0:T(8,128)(2,1)S(1)}, u32[]{:S(2)}, u32[]{:S(2)}) collective-permute-start(bf16[64,512]{1,0:T(8,128)(2,1)S(1)} %fusion.3), channel_id=1, source_target_pairs={{0,384},{128,256},{256,128},{384,0},{1,385},{129,257},{257,129},{3... | collective-permute-start | bytes 196616 | tf_op jit(solution)/shard_map/ppermute | solution.py:146
  70.2 18.7 %collective-permute-start.4 = (bf16[64,512]{1,0:T(8,128)(2,1)S(1)}, bf16[64,512]{1,0:T(8,128)(2,1)S(1)}, u32[]{:S(2)}, u32[]{:S(2)}) collective-permute-start(bf16[64,512]{1,0:T(8,128)(2,1)S(1)} %fusion.3), channel_id=1, source_target_pairs={{0,256},{128,384},{256,0},{384,128},{1,257},{129,385},{257,1},{385... | collective-permute-start | bytes 196616 | tf_op jit(solution)/shard_map/ppermute | solution.py:146
  73.4 15.5 %collective-permute-start.3 = (bf16[64,512]{1,0:T(8,128)(2,1)S(1)}, bf16[64,512]{1,0:T(8,128)(2,1)S(1)}, u32[]{:S(2)}, u32[]{:S(2)}) collective-permute-start(bf16[64,512]{1,0:T(8,128)(2,1)S(1)} %fusion.3), channel_id=1, source_target_pairs={{0,128},{128,0},{256,384},{384,256},{1,129},{129,1},{257,385},{385... | collective-permute-start | bytes 196616 | tf_op jit(solution)/shard_map/ppermute | solution.py:146

commit v17 on v16

--- a/solution.py
+++ b/solution.py
@@ -140,10 +140,11 @@
     outer_layer = lax.dynamic_index_in_dim(outer_params, layer_idx, 0, keepdims=False)
     moment_layer = lax.dynamic_index_in_dim(outer_moment, layer_idx, 0, keepdims=False)
     inner_layer = lax.dynamic_index_in_dim(inner_params[0], layer_idx, 0, keepdims=False)
-    summed = pseudo_grad.astype(jnp.float32)
+    parts = [pseudo_grad.astype(jnp.float32)]
     for other in range(1, replicas):
         pairs = [(replica, replica ^ other) for replica in range(replicas)]
-        summed += lax.ppermute(pseudo_grad, REP, pairs).astype(jnp.float32)
+        parts.append(lax.ppermute(pseudo_grad, REP, pairs).astype(jnp.float32))
+    summed = (parts[0] + parts[1]) + (parts[2] + parts[3])
     new_outer, new_moment = outer_update(summed / replicas, outer_layer, moment_layer)
     mixed_inner = (
         mix_keep * inner_layer.astype(jnp.float32) + (1.0 - mix_keep) * new_outer

time: 92.2 us -> 92.2 us (level)
  no operation moved by 1% of the time
where the time goes in v17:
time: 92.2 us; the launch traced here: 91.7 us
  starting transfers between devices  39.5 us (43%)
  blocking collectives  19.4 us (21%)
  waiting for transfers between devices  19.1 us (21%)
  Pallas kernels  8.54 us (9%)
  other arithmetic  3.79 us (4%)
  between operations  1.37 us (1%)
    all_gather x1, blocking collectives, shards(): own = lax.all_gather(block, 'zh', axis=0, tiled=True)  19.4 us
    all_to_all x1, starting transfers between devices, shards(): partial = lax.all_to_all(partial, PLANE, 0, 0, tiled=True)  15 us
    ppermute x3, waiting for transfers between devices, shards(): parts.append(lax.ppermute(pseudo_grad, REP, pairs).astype(jnp.float32))  12.9 us
    ppermute x3, starting transfers between devices, moved(): lax.ppermute(block, Z, [(z, target(z) % PLANES) for z in range(PLANES)])  9.45 us
    ppermute x3, starting transfers between devices, shards(): parts.append(lax.ppermute(pseudo_grad, REP, pairs).astype(jnp.float32))  7.57 us
    all_to_all x1, starting transfers between devices, shards(): tokens = lax.all_to_all(packed, PLANE, 0, 0, tiled=True)  7.4 us
    pallas_call x1, Pallas kernels, pack(): pl.pallas_call(pack_kernel, grid=(tokens // ROWS,), in_specs=[pl.BlockSpe...  4.47 us
    pallas_call x1, Pallas kernels, project(): pl.pallas_call(project_kernel, grid_spec=pltpu.PrefetchScalarGridSpec(num...  4.07 us
  transfers between devices with their start and end apart: 8, of which 5 were waited for; matrix products, arithmetic and copies ran while one was open for 3% of the time, Pallas kernels for 0%

profile of v17, /device:TPU:400, one launch (start us, length us, event | category | flops | bytes accessed | tf_op | source)
XLA Modules:
  0.0 91.7 jit_solution(14539812382178318177)
XLA Ops:
  0.6 4.5 %pack_hidden.1 = (bf16[8,192,1024]{2,1,0:T(8,128)(2,1)}, f32[192,1]{1,0:T(8,128)}) custom-call(bf16[192,8192]{1,0:T(8,128)(2,1)} %bitcast.31, f32[1,8192]{1,0:T(1,128)} %bitcast.33), custom_call_target="tpu_custom_call" | custom-call | flops 6291456 | bytes 6291456 | tf_op jit(solution)/shard_map/pack_hidden/pallas_call | solution.py:46
  5.1 0.0 copy-start.1
  5.1 7.4 %all-to-all-start = ((bf16[8,192,1024]{2,1,0:T(8,128)(2,1)}), bf16[8,192,1024]{2,1,0:T(8,128)(2,1)S(1)}, u32[]{:S(2)}, u32[]{:S(2)}) async-start(bf16[8,192,1024]{2,1,0:T(8,128)(2,1)} %get-tuple-element.13), calls=%async_computation | async-start | bytes 6291456 | tf_op jit(solution)/shard_map/all_to_all | solution.py:123
  12.5 0.0 copy-done.1
  12.5 19.4 %all_gather.3.refs_0_ = bf16[256,512]{1,0:T(8,128)(2,1)S(1)} all-gather(bf16[64,512]{1,0:T(8,128)(2,1)S(1)} %bitcast.32), channel_id=1, replica_groups=mesh['yl'=2,'core'=2,'zh'=4,'zl'=4,'yh'=2,'x'=4] {'zh'}, dimensions={0}, use_global_device_ids=true | all-gather | bytes 327680 | tf_op jit(solution)/shard_map/all_gather | solution.py:124
  31.9 2.4 %collective-permute-start.2 = (bf16[256,512]{1,0:T(8,128)(2,1)S(1)}, bf16[256,512]{1,0:T(8,128)(2,1)}, u32[]{:S(2)}, u32[]{:S(2)}) collective-permute-start(bf16[256,512]{1,0:T(8,128)(2,1)S(1)} %all_gather.3.refs_0_), channel_id=1, source_target_pairs={{0,16},{8,120},{16,32},{24,8},{32,48},{40,24},{48,64},{56,40},{64,... | collective-permute-start | bytes 786440 | tf_op jit(solution)/shard_map/ppermute | solution.py:114
  34.3 3.4 %collective-permute-start.1 = (bf16[256,512]{1,0:T(8,128)(2,1)S(1)}, bf16[256,512]{1,0:T(8,128)(2,1)}, u32[]{:S(2)}, u32[]{:S(2)}) collective-permute-start(bf16[256,512]{1,0:T(8,128)(2,1)S(1)} %all_gather.3.refs_0_), channel_id=1, source_target_pairs={{0,8},{8,16},{16,24},{24,32},{32,40},{40,48},{48,56},{56,64},{64,7... | collective-permute-start | bytes 786440 | tf_op jit(solution)/shard_map/ppermute | solution.py:114
  37.8 3.6 %collective-permute-start = (bf16[256,512]{1,0:T(8,128)(2,1)S(1)}, bf16[256,512]{1,0:T(8,128)(2,1)}, u32[]{:S(2)}, u32[]{:S(2)}) collective-permute-start(bf16[256,512]{1,0:T(8,128)(2,1)S(1)} %all_gather.3.refs_0_), channel_id=1, source_target_pairs={{0,120},{8,0},{16,8},{24,16},{32,24},{40,32},{48,40},{56,48},{64,5... | collective-permute-start | bytes 786440 | tf_op jit(solution)/shard_map/ppermute | solution.py:114
  42.0 0.9 %fusion.3 = bf16[64,512]{1,0:T(8,128)(2,1)S(1)} fusion(f32[7,64,512]{2,1,0:T(8,128)} %param.11, s32[]{:T(128)S(6)} %select_n.11, bf16[1,7,64,512]{3,2,1,0:T(8,128)(2,1)} %param.13), kind=kLoop, calls=%fused_computation.7 | loop fusion | flops 98304 | bytes 262148 | tf_op jit(solution)/shard_map/convert_element_type | solution.py:135
  43.0 0.9 collective-permute-done.2.refs_3_
  43.8 2.7 %collective-permute-done.1.refs_2_ = bf16[256,512]{1,0:T(8,128)(2,1)} collective-permute-done((bf16[256,512]{1,0:T(8,128)(2,1)S(1)}, bf16[256,512]{1,0:T(8,128)(2,1)}, u32[]{:S(2)}, u32[]{:S(2)}) %collective-permute-start.1) | collective-permute-done | bytes 262176 | tf_op jit(solution)/shard_map/ppermute | solution.py:114
  46.5 0.0 collective-permute-done.refs_1_
  46.5 2.7 %all-to-all-done.tokens_ref = bf16[8,192,1024]{2,1,0:T(8,128)(2,1)S(1)} async-done(((bf16[8,192,1024]{2,1,0:T(8,128)(2,1)}), bf16[8,192,1024]{2,1,0:T(8,128)(2,1)S(1)}, u32[]{:S(2)}, u32[]{:S(2)}) %all-to-all-start) | async-done | bytes 3145760 | tf_op jit(solution)/shard_map/all_to_all | solution.py:123
  49.2 4.1 %project_keys.1 = bf16[8,192,512]{2,1,0:T(8,128)(2,1)} custom-call(s32[1]{0:T(128)} %bitcast.residue_ref, bf16[8,192,1024]{2,1,0:T(8,128)(2,1)S(1)} %all-to-all-done.tokens_ref, bf16[256,512]{1,0:T(8,128)(2,1)S(1)} %all_gather.3.refs_0_, bf16[256,512]{1,0:T(8,128)(2,1)} %collective-permute-done.refs_1_, bf16[256,512]{1,0:T(8,128)(2,1)} %collective-permute-done.1.refs_2_, ...), custom_call_target="tpu_custom_call" | custom-call | flops 1610612736 | bytes 5767168 | tf_op jit(solution)/shard_map/project_keys/pallas_call | solution.py:93
  53.3 0.0 copy-start
  53.3 15.0 %all-to-all-start.1 = ((bf16[8,192,512]{2,1,0:T(8,128)(2,1)}), bf16[8,192,512]{2,1,0:T(8,128)(2,1)S(1)}, u32[]{:S(2)}, u32[]{:S(2)}) async-start(bf16[8,192,512]{2,1,0:T(8,128)(2,1)} %project_keys.1), calls=%async_computation.1 | async-start | bytes 3145728 | tf_op jit(solution)/shard_map/all_to_all | solution.py:139
  68.3 1.9 %collective-permute-start.5 = (bf16[64,512]{1,0:T(8,128)(2,1)S(1)}, bf16[64,512]{1,0:T(8,128)(2,1)S(1)}, u32[]{:S(2)}, u32[]{:S(2)}) collective-permute-start(bf16[64,512]{1,0:T(8,128)(2,1)S(1)} %fusion.3), channel_id=1, source_target_pairs={{0,384},{128,256},{256,128},{384,0},{1,385},{129,257},{257,129},{3... | collective-permute-start | bytes 196616 | tf_op jit(solution)/shard_map/ppermute | solution.py:146
  70.2 3.2 %collective-permute-start.4 = (bf16[64,512]{1,0:T(8,128)(2,1)S(1)}, bf16[64,512]{1,0:T(8,128)(2,1)S(1)}, u32[]{:S(2)}, u32[]{:S(2)}) collective-permute-start(bf16[64,512]{1,0:T(8,128)(2,1)S(1)} %fusion.3), channel_id=1, source_target_pairs={{0,256},{128,384},{256,0},{384,128},{1,257},{129,385},{257,1},{385... | collective-permute-start | bytes 196616 | tf_op jit(solution)/shard_map/ppermute | solution.py:146
  73.4 2.5 %collective-permute-start.3 = (bf16[64,512]{1,0:T(8,128)(2,1)S(1)}, bf16[64,512]{1,0:T(8,128)(2,1)S(1)}, u32[]{:S(2)}, u32[]{:S(2)}) collective-permute-start(bf16[64,512]{1,0:T(8,128)(2,1)S(1)} %fusion.3), channel_id=1, source_target_pairs={{0,128},{128,0},{256,384},{384,256},{1,129},{129,1},{257,385},{385... | collective-permute-start | bytes 196616 | tf_op jit(solution)/shard_map/ppermute | solution.py:146
  75.9 0.0 copy-done
  75.9 0.1 reduce
  76.1 10.5 %collective-permute-done.5 = bf16[64,512]{1,0:T(8,128)(2,1)S(1)} collective-permute-done((bf16[64,512]{1,0:T(8,128)(2,1)S(1)}, bf16[64,512]{1,0:T(8,128)(2,1)S(1)}, u32[]{:S(2)}, u32[]{:S(2)}) %collective-permute-start.5) | collective-permute-done | bytes 65568 | tf_op jit(solution)/shard_map/ppermute | solution.py:146
  86.5 2.4 %collective-permute-done.4 = bf16[64,512]{1,0:T(8,128)(2,1)S(1)} collective-permute-done((bf16[64,512]{1,0:T(8,128)(2,1)S(1)}, bf16[64,512]{1,0:T(8,128)(2,1)S(1)}, u32[]{:S(2)}, u32[]{:S(2)}) %collective-permute-start.4) | collective-permute-done | bytes 65568 | tf_op jit(solution)/shard_map/ppermute | solution.py:146
  88.9 0.0 collective-permute-done.3
  88.9 1.8 %fusion.4 = (bf16[1,64,512]{2,1,0:T(8,128)(2,1)}, f32[64,512]{1,0:T(8,128)}, f32[64,512]{1,0:T(8,128)}) fusion(bf16[1,7,64,512]{3,2,1,0:T(8,128)(2,1)} %param.13, s32[]{:T(128)S(6)} %select_n.12, bf16[64,512]{1,0:T(8,128)(2,1)S(1)} %collective-permute-done.5, bf16[64,512]{1,0:T(8,128)(2,1)S(1)} %collective-permute-done.4, ...), kind=kLoop, calls=%fused_computation.11 | loop fusion | flops 589824 | bytes 917508 | tf_op jit(solution)/shard_map/broadcast_in_dim | solution.py:153
  90.7 0.0 all-to-all-done.1
  90.7 0.2 convert_reduce_fusion
  90.9 0.8 fusion
Async XLA Ops:
  5.1 7.4 %copy-start.1 = (bf16[1,64,512]{2,1,0:T(8,128)(2,1)S(1)}, bf16[1,64,512]{2,1,0:T(8,128)(2,1)}, u32[]{:S(2)}) copy-start(bf16[1,64,512]{2,1,0:T(8,128)(2,1)} %param.9) | copy-start | bytes 196612
  5.1 44.1 %all-to-all-start = ((bf16[8,192,1024]{2,1,0:T(8,128)(2,1)}), bf16[8,192,1024]{2,1,0:T(8,128)(2,1)S(1)}, u32[]{:S(2)}, u32[]{:S(2)}) async-start(bf16[8,192,1024]{2,1,0:T(8,128)(2,1)} %get-tuple-element.13), calls=%async_computation | async-start | bytes 6291456 | tf_op jit(solution)/shard_map/all_to_all | solution.py:123
  31.9 11.9 %collective-permute-start.2 = (bf16[256,512]{1,0:T(8,128)(2,1)S(1)}, bf16[256,512]{1,0:T(8,128)(2,1)}, u32[]{:S(2)}, u32[]{:S(2)}) collective-permute-start(bf16[256,512]{1,0:T(8,128)(2,1)S(1)} %all_gather.3.refs_0_), channel_id=1, source_target_pairs={{0,16},{8,120},{16,32},{24,8},{32,48},{40,24},{48,64},{56,40},{64,... | collective-permute-start | bytes 786440 | tf_op jit(solution)/shard_map/ppermute | solution.py:114
  34.3 12.2 %collective-permute-start.1 = (bf16[256,512]{1,0:T(8,128)(2,1)S(1)}, bf16[256,512]{1,0:T(8,128)(2,1)}, u32[]{:S(2)}, u32[]{:S(2)}) collective-permute-start(bf16[256,512]{1,0:T(8,128)(2,1)S(1)} %all_gather.3.refs_0_), channel_id=1, source_target_pairs={{0,8},{8,16},{16,24},{24,32},{32,40},{40,48},{48,56},{56,64},{64,7... | collective-permute-start | bytes 786440 | tf_op jit(solution)/shard_map/ppermute | solution.py:114
  37.8 8.8 %collective-permute-start = (bf16[256,512]{1,0:T(8,128)(2,1)S(1)}, bf16[256,512]{1,0:T(8,128)(2,1)}, u32[]{:S(2)}, u32[]{:S(2)}) collective-permute-start(bf16[256,512]{1,0:T(8,128)(2,1)S(1)} %all_gather.3.refs_0_), channel_id=1, source_target_pairs={{0,120},{8,0},{16,8},{24,16},{32,24},{40,32},{48,40},{56,48},{64,5... | collective-permute-start | bytes 786440 | tf_op jit(solution)/shard_map/ppermute | solution.py:114
  53.3 22.7 %copy-start = (f32[192,1]{1,0:T(8,128)S(1)}, f32[192,1]{1,0:T(8,128)}, u32[]{:S(2)}) copy-start(f32[192,1]{1,0:T(8,128)} %get-tuple-element.17) | copy-start | bytes 2308
  53.3 37.4 %all-to-all-start.1 = ((bf16[8,192,512]{2,1,0:T(8,128)(2,1)}), bf16[8,192,512]{2,1,0:T(8,128)(2,1)S(1)}, u32[]{:S(2)}, u32[]{:S(2)}) async-start(bf16[8,192,512]{2,1,0:T(8,128)(2,1)} %project_keys.1), calls=%async_computation.1 | async-start | bytes 3145728 | tf_op jit(solution)/shard_map/all_to_all | solution.py:139
  68.3 18.2 %collective-permute-start.5 = (bf16[64,512]{1,0:T(8,128)(2,1)S(1)}, bf16[64,512]{1,0:T(8,128)(2,1)S(1)}, u32[]{:S(2)}, u32[]{:S(2)}) collective-permute-start(bf16[64,512]{1,0:T(8,128)(2,1)S(1)} %fusion.3), channel_id=1, source_target_pairs={{0,384},{128,256},{256,128},{384,0},{1,385},{129,257},{257,129},{3... | collective-permute-start | bytes 196616 | tf_op jit(solution)/shard_map/ppermute | solution.py:146
  70.2 18.7 %collective-permute-start.4 = (bf16[64,512]{1,0:T(8,128)(2,1)S(1)}, bf16[64,512]{1,0:T(8,128)(2,1)S(1)}, u32[]{:S(2)}, u32[]{:S(2)}) collective-permute-start(bf16[64,512]{1,0:T(8,128)(2,1)S(1)} %fusion.3), channel_id=1, source_target_pairs={{0,256},{128,384},{256,0},{384,128},{1,257},{129,385},{257,1},{385... | collective-permute-start | bytes 196616 | tf_op jit(solution)/shard_map/ppermute | solution.py:146
  73.4 15.5 %collective-permute-start.3 = (bf16[64,512]{1,0:T(8,128)(2,1)S(1)}, bf16[64,512]{1,0:T(8,128)(2,1)S(1)}, u32[]{:S(2)}, u32[]{:S(2)}) collective-permute-start(bf16[64,512]{1,0:T(8,128)(2,1)S(1)} %fusion.3), channel_id=1, source_target_pairs={{0,128},{128,0},{256,384},{384,256},{1,129},{129,1},{257,385},{385... | collective-permute-start | bytes 196616 | tf_op jit(solution)/shard_map/ppermute | solution.py:146

commit v18 on v16

--- a/solution.py
+++ b/solution.py
@@ -114,6 +114,10 @@
     return lax.ppermute(block, Z, [(z, target(z) % PLANES) for z in range(PLANES)])
 
 
+def swapped(block, axis):
+    return lax.ppermute(block, axis, [(0, 1), (1, 0)])
+
+
 def shards(
     hidden_in, norm_gain, key_weight, fragment_index, outer_params, outer_moment, inner_params
 ):
@@ -122,28 +126,30 @@
     packed, block = lax.optimization_barrier((packed, key_weight[0]))
     tokens = lax.all_to_all(packed, PLANE, 0, 0, tiled=True)
     own = lax.all_gather(block, "zh", axis=0, tiled=True)
-    held = (
+    held = [
         own,
         moved(own, lambda z: z - 1),
         moved(own, lambda z: z + 1),
         moved(own, lambda z: z + 2 if z % 2 == 0 else z - 2),
-    )
-    _, fragment_index = lax.optimization_barrier((own, fragment_index))
+    ]
+    held[0], fragment_index = lax.optimization_barrier((own, fragment_index))
     layer_idx = fragment_index[0]
     outer_layer = lax.dynamic_index_in_dim(outer_params, layer_idx, 0, keepdims=False)
     inner_layer = lax.dynamic_index_in_dim(inner_params[0], layer_idx, 0, keepdims=False)
     pseudo_grad = (outer_layer - inner_layer.astype(jnp.float32)).astype(jnp.bfloat16)
+    pair_sum = pseudo_grad.astype(jnp.float32) + swapped(pseudo_grad, "core").astype(jnp.float32)
+    pair_sum = pair_sum.astype(jnp.bfloat16)
+    other_sum = swapped(pair_sum, "yl")
     residue = lax.axis_index("zl").astype(jnp.int32)[None]
     partial = project(residue, tokens, held)
-    partial, layer_idx, pseudo_grad = lax.optimization_barrier((partial, layer_idx, pseudo_grad))
+    partial, layer_idx, pair_sum, other_sum = lax.optimization_barrier(
+        (partial, layer_idx, pair_sum, other_sum)
+    )
     partial = lax.all_to_all(partial, PLANE, 0, 0, tiled=True)
     outer_layer = lax.dynamic_index_in_dim(outer_params, layer_idx, 0, keepdims=False)
     moment_layer = lax.dynamic_index_in_dim(outer_moment, layer_idx, 0, keepdims=False)
     inner_layer = lax.dynamic_index_in_dim(inner_params[0], layer_idx, 0, keepdims=False)
-    summed = pseudo_grad.astype(jnp.float32)
-    for other in range(1, replicas):
-        pairs = [(replica, replica ^ other) for replica in range(replicas)]
-        summed += lax.ppermute(pseudo_grad, REP, pairs).astype(jnp.float32)
+    summed = pair_sum.astype(jnp.float32) + other_sum.astype(jnp.float32)
     new_outer, new_moment = outer_update(summed / replicas, outer_layer, moment_layer)
     mixed_inner = (
         mix_keep * inner_layer.astype(jnp.float32) + (1.0 - mix_keep) * new_outer

time: 92.2 us -> 95 us (1.030)
  the two profiles are of different devices: /device:TPU:400 before, /device:TPU:1 now
where the time goes in v18:
time: 95 us; the launch traced here: 94.4 us
  starting transfers between devices  30.6 us (32%)
  waiting for transfers between devices  26.7 us (28%)
  blocking collectives  22.5 us (24%)
  Pallas kernels  8.55 us (9%)
  other arithmetic  4.64 us (5%)
  between operations  1.38 us (1%)
    all_gather x1, blocking collectives, shards(): own = lax.all_gather(block, 'zh', axis=0, tiled=True)  22.5 us
    all_to_all x1, waiting for transfers between devices, shards(): partial = lax.all_to_all(partial, PLANE, 0, 0, tiled=True)  21 us
    ppermute x3, starting transfers between devices, moved(): lax.ppermute(block, Z, [(z, target(z) % PLANES) for z in range(PLANES)])  8.46 us
    all_to_all x1, starting transfers between devices, shards(): tokens = lax.all_to_all(packed, PLANE, 0, 0, tiled=True)  7.61 us
    all_to_all x1, starting transfers between devices, shards(): partial = lax.all_to_all(partial, PLANE, 0, 0, tiled=True)  7.28 us
    ppermute x2, starting transfers between devices, swapped(): return lax.ppermute(block, axis, [(0, 1), (1, 0)])  7.27 us
    ppermute x3, waiting for transfers between devices, moved(): lax.ppermute(block, Z, [(z, target(z) % PLANES) for z in range(PLANES)])  5.74 us
    pallas_call x1, Pallas kernels, pack(): pl.pallas_call(pack_kernel, grid=(tokens // ROWS,), in_specs=[pl.BlockSpe...  4.48 us
  transfers between devices with their start and end apart: 7, of which 2 were waited for; matrix products, arithmetic and copies ran while one was open for 4% of the time, Pallas kernels for 4%

profile of v18, /device:TPU:1, one launch (start us, length us, event | category | flops | bytes accessed | tf_op | source)
XLA Modules:
  0.0 94.4 jit_solution(16882177970584504847)
XLA Ops:
  0.6 4.5 %pack_hidden.1 = (bf16[8,192,1024]{2,1,0:T(8,128)(2,1)}, f32[192,1]{1,0:T(8,128)}) custom-call(bf16[192,8192]{1,0:T(8,128)(2,1)} %bitcast.31, f32[1,8192]{1,0:T(1,128)} %bitcast.33), custom_call_target="tpu_custom_call" | custom-call | flops 6291456 | bytes 6291456 | tf_op jit(solution)/shard_map/pack_hidden/pallas_call | solution.py:46
  5.1 0.0 copy-start.1
  5.1 7.6 %all-to-all-start = ((bf16[8,192,1024]{2,1,0:T(8,128)(2,1)}), bf16[8,192,1024]{2,1,0:T(8,128)(2,1)S(1)}, u32[]{:S(2)}, u32[]{:S(2)}) async-start(bf16[8,192,1024]{2,1,0:T(8,128)(2,1)} %get-tuple-element.15), calls=%async_computation | async-start | bytes 6291456 | tf_op jit(solution)/shard_map/all_to_all | solution.py:127
  13.4 0.9 fusion.3
  14.3 5.0 %collective-permute-start.3 = (bf16[64,512]{1,0:T(8,128)(2,1)S(1)}, bf16[64,512]{1,0:T(8,128)(2,1)}, u32[]{:S(2)}, u32[]{:S(2)}) collective-permute-start(bf16[64,512]{1,0:T(8,128)(2,1)S(1)} %fusion.3), channel_id=1, source_target_pairs={{0,128},{128,0},{1,129},{129,1},{2,130},{130,2},{3,131},{131,3},{4... | collective-permute-start | bytes 196616 | tf_op jit(solution)/shard_map/ppermute | solution.py:118
  19.3 0.0 copy-done.1
  19.3 22.5 %all_gather.3.refs_0_ = bf16[256,512]{1,0:T(8,128)(2,1)S(1)} all-gather(bf16[64,512]{1,0:T(8,128)(2,1)S(1)} %bitcast.32), channel_id=1, replica_groups=mesh['yl'=2,'core'=2,'zh'=4,'zl'=4,'yh'=2,'x'=4] {'zh'}, dimensions={0}, use_global_device_ids=true | all-gather | bytes 327680 | tf_op jit(solution)/shard_map/all_gather | solution.py:128
  41.8 3.3 %collective-permute-start = (bf16[256,512]{1,0:T(8,128)(2,1)S(1)}, bf16[256,512]{1,0:T(8,128)(2,1)}, u32[]{:S(2)}, u32[]{:S(2)}) collective-permute-start(bf16[256,512]{1,0:T(8,128)(2,1)S(1)} %all_gather.3.refs_0_), channel_id=1, source_target_pairs={{0,120},{8,0},{16,8},{24,16},{32,24},{40,32},{48,40},{56,48},{64,5... | collective-permute-start | bytes 786440 | tf_op jit(solution)/shard_map/ppermute | solution.py:114
  45.1 2.0 %collective-permute-start.1 = (bf16[256,512]{1,0:T(8,128)(2,1)S(1)}, bf16[256,512]{1,0:T(8,128)(2,1)}, u32[]{:S(2)}, u32[]{:S(2)}) collective-permute-start(bf16[256,512]{1,0:T(8,128)(2,1)S(1)} %all_gather.3.refs_0_), channel_id=1, source_target_pairs={{0,8},{8,16},{16,24},{24,32},{32,40},{40,48},{48,56},{56,64},{64,7... | collective-permute-start | bytes 786440 | tf_op jit(solution)/shard_map/ppermute | solution.py:114
  47.1 3.2 %collective-permute-start.2 = (bf16[256,512]{1,0:T(8,128)(2,1)S(1)}, bf16[256,512]{1,0:T(8,128)(2,1)}, u32[]{:S(2)}, u32[]{:S(2)}) collective-permute-start(bf16[256,512]{1,0:T(8,128)(2,1)S(1)} %all_gather.3.refs_0_), channel_id=1, source_target_pairs={{0,16},{8,120},{16,32},{24,8},{32,48},{40,24},{48,64},{56,40},{64,... | collective-permute-start | bytes 786440 | tf_op jit(solution)/shard_map/ppermute | solution.py:114
  50.3 0.0 collective-permute-done.3
  50.3 0.9 add_convert_fusion
  51.1 2.3 %collective-permute-start.4 = (bf16[64,512]{1,0:T(8,128)(2,1)S(1)}, bf16[64,512]{1,0:T(8,128)(2,1)S(1)}, u32[]{:S(2)}, u32[]{:S(2)}) collective-permute-start(bf16[64,512]{1,0:T(8,128)(2,1)S(1)} %add_convert_fusion), channel_id=1, source_target_pairs={{0,256},{256,0},{1,257},{257,1},{2,258},{258,2},{3,259},{259,3},{4... | collective-permute-start | bytes 196616 | tf_op jit(solution)/shard_map/ppermute | solution.py:118
  53.5 0.0 collective-permute-done.refs_1_
  53.5 0.0 collective-permute-done.1.refs_2_
  53.5 5.7 %collective-permute-done.2.refs_3_ = bf16[256,512]{1,0:T(8,128)(2,1)} collective-permute-done((bf16[256,512]{1,0:T(8,128)(2,1)S(1)}, bf16[256,512]{1,0:T(8,128)(2,1)}, u32[]{:S(2)}, u32[]{:S(2)}) %collective-permute-start.2) | collective-permute-done | bytes 262176 | tf_op jit(solution)/shard_map/ppermute | solution.py:114
  59.2 0.0 all-to-all-done.tokens_ref
  59.2 4.1 %project_keys.1 = bf16[8,192,512]{2,1,0:T(8,128)(2,1)} custom-call(s32[1]{0:T(128)} %bitcast.residue_ref, bf16[8,192,1024]{2,1,0:T(8,128)(2,1)S(1)} %all-to-all-done.tokens_ref, bf16[256,512]{1,0:T(8,128)(2,1)S(1)} %all_gather.3.refs_0_, bf16[256,512]{1,0:T(8,128)(2,1)} %collective-permute-done.refs_1_, bf16[256,512]{1,0:T(8,128)(2,1)} %collective-permute-done.1.refs_2_, ...), custom_call_target="tpu_custom_call" | custom-call | flops 1610612736 | bytes 5767168 | tf_op jit(solution)/shard_map/project_keys/pallas_call | solution.py:93
  63.3 0.0 copy-start
  63.3 0.0 collective-permute-done.4
  63.3 7.3 %all-to-all-start.1 = ((bf16[8,192,512]{2,1,0:T(8,128)(2,1)}), bf16[8,192,512]{2,1,0:T(8,128)(2,1)S(1)}, u32[]{:S(2)}, u32[]{:S(2)}) async-start(bf16[8,192,512]{2,1,0:T(8,128)(2,1)} %project_keys.1), calls=%async_computation.1 | async-start | bytes 3145728 | tf_op jit(solution)/shard_map/all_to_all | solution.py:148
  70.6 0.0 copy-done
  70.6 0.1 reduce
  70.7 1.8 %fusion.4 = (bf16[1,64,512]{2,1,0:T(8,128)(2,1)}, f32[64,512]{1,0:T(8,128)}, f32[64,512]{1,0:T(8,128)}) fusion(bf16[1,7,64,512]{3,2,1,0:T(8,128)(2,1)} %param.13, s32[]{:T(128)S(6)} %select_n.12, bf16[64,512]{1,0:T(8,128)(2,1)S(1)} %collective-permute-done.4, bf16[64,512]{1,0:T(8,128)(2,1)S(1)} %add_convert_fusion, f32[7,64,512]{2,1,0:T(8,128)} %param.11, ...), kind=kLoop, calls=%fused_computation.12 | loop fusion | flops 458752 | bytes 786436 | tf_op jit(solution)/shard_map/broadcast_in_dim | solution.py:158
  72.4 21.0 %all-to-all-done.1 = bf16[8,192,512]{2,1,0:T(8,128)(2,1)S(1)} async-done(((bf16[8,192,512]{2,1,0:T(8,128)(2,1)}), bf16[8,192,512]{2,1,0:T(8,128)(2,1)S(1)}, u32[]{:S(2)}, u32[]{:S(2)}) %all-to-all-start.1) | async-done | bytes 1572896 | tf_op jit(solution)/shard_map/all_to_all | solution.py:148
  93.4 0.2 convert_reduce_fusion
  93.7 0.8 fusion
Async XLA Ops:
  5.1 14.2 %copy-start.1 = (bf16[1,64,512]{2,1,0:T(8,128)(2,1)S(1)}, bf16[1,64,512]{2,1,0:T(8,128)(2,1)}, u32[]{:S(2)}) copy-start(bf16[1,64,512]{2,1,0:T(8,128)(2,1)} %param.9) | copy-start | bytes 196612
  5.1 54.1 %all-to-all-start = ((bf16[8,192,1024]{2,1,0:T(8,128)(2,1)}), bf16[8,192,1024]{2,1,0:T(8,128)(2,1)S(1)}, u32[]{:S(2)}, u32[]{:S(2)}) async-start(bf16[8,192,1024]{2,1,0:T(8,128)(2,1)} %get-tuple-element.15), calls=%async_computation | async-start | bytes 6291456 | tf_op jit(solution)/shard_map/all_to_all | solution.py:127
  14.3 36.0 %collective-permute-start.3 = (bf16[64,512]{1,0:T(8,128)(2,1)S(1)}, bf16[64,512]{1,0:T(8,128)(2,1)}, u32[]{:S(2)}, u32[]{:S(2)}) collective-permute-start(bf16[64,512]{1,0:T(8,128)(2,1)S(1)} %fusion.3), channel_id=1, source_target_pairs={{0,128},{128,0},{1,129},{129,1},{2,130},{130,2},{3,131},{131,3},{4... | collective-permute-start | bytes 196616 | tf_op jit(solution)/shard_map/ppermute | solution.py:118
  41.8 11.7 %collective-permute-start = (bf16[256,512]{1,0:T(8,128)(2,1)S(1)}, bf16[256,512]{1,0:T(8,128)(2,1)}, u32[]{:S(2)}, u32[]{:S(2)}) collective-permute-start(bf16[256,512]{1,0:T(8,128)(2,1)S(1)} %all_gather.3.refs_0_), channel_id=1, source_target_pairs={{0,120},{8,0},{16,8},{24,16},{32,24},{40,32},{48,40},{56,48},{64,5... | collective-permute-start | bytes 786440 | tf_op jit(solution)/shard_map/ppermute | solution.py:114
  45.1 8.4 %collective-permute-start.1 = (bf16[256,512]{1,0:T(8,128)(2,1)S(1)}, bf16[256,512]{1,0:T(8,128)(2,1)}, u32[]{:S(2)}, u32[]{:S(2)}) collective-permute-start(bf16[256,512]{1,0:T(8,128)(2,1)S(1)} %all_gather.3.refs_0_), channel_id=1, source_target_pairs={{0,8},{8,16},{16,24},{24,32},{32,40},{40,48},{48,56},{56,64},{64,7... | collective-permute-start | bytes 786440 | tf_op jit(solution)/shard_map/ppermute | solution.py:114
  47.1 12.1 %collective-permute-start.2 = (bf16[256,512]{1,0:T(8,128)(2,1)S(1)}, bf16[256,512]{1,0:T(8,128)(2,1)}, u32[]{:S(2)}, u32[]{:S(2)}) collective-permute-start(bf16[256,512]{1,0:T(8,128)(2,1)S(1)} %all_gather.3.refs_0_), channel_id=1, source_target_pairs={{0,16},{8,120},{16,32},{24,8},{32,48},{40,24},{48,64},{56,40},{64,... | collective-permute-start | bytes 786440 | tf_op jit(solution)/shard_map/ppermute | solution.py:114
  51.1 12.1 %collective-permute-start.4 = (bf16[64,512]{1,0:T(8,128)(2,1)S(1)}, bf16[64,512]{1,0:T(8,128)(2,1)S(1)}, u32[]{:S(2)}, u32[]{:S(2)}) collective-permute-start(bf16[64,512]{1,0:T(8,128)(2,1)S(1)} %add_convert_fusion), channel_id=1, source_target_pairs={{0,256},{256,0},{1,257},{257,1},{2,258},{258,2},{3,259},{259,3},{4... | collective-permute-start | bytes 196616 | tf_op jit(solution)/shard_map/ppermute | solution.py:118
  63.3 7.3 %copy-start = (f32[192,1]{1,0:T(8,128)S(1)}, f32[192,1]{1,0:T(8,128)}, u32[]{:S(2)}) copy-start(f32[192,1]{1,0:T(8,128)} %get-tuple-element.20) | copy-start | bytes 2308
  63.3 30.2 %all-to-all-start.1 = ((bf16[8,192,512]{2,1,0:T(8,128)(2,1)}), bf16[8,192,512]{2,1,0:T(8,128)(2,1)S(1)}, u32[]{:S(2)}, u32[]{:S(2)}) async-start(bf16[8,192,512]{2,1,0:T(8,128)(2,1)} %project_keys.1), calls=%async_computation.1 | async-start | bytes 3145728 | tf_op jit(solution)/shard_map/all_to_all | solution.py:148

commit v19 on v16

--- a/solution.py
+++ b/solution.py
@@ -140,10 +140,8 @@
     outer_layer = lax.dynamic_index_in_dim(outer_params, layer_idx, 0, keepdims=False)
     moment_layer = lax.dynamic_index_in_dim(outer_moment, layer_idx, 0, keepdims=False)
     inner_layer = lax.dynamic_index_in_dim(inner_params[0], layer_idx, 0, keepdims=False)
-    summed = pseudo_grad.astype(jnp.float32)
-    for other in range(1, replicas):
-        pairs = [(replica, replica ^ other) for replica in range(replicas)]
-        summed += lax.ppermute(pseudo_grad, REP, pairs).astype(jnp.float32)
+    every = lax.all_gather(pseudo_grad, REP, axis=0, tiled=False).astype(jnp.float32)
+    summed = (every[0] + every[1]) + (every[2] + every[3])
     new_outer, new_moment = outer_update(summed / replicas, outer_layer, moment_layer)
     mixed_inner = (
         mix_keep * inner_layer.astype(jnp.float32) + (1.0 - mix_keep) * new_outer

time: 92.2 us -> 93.8 us (1.017)
  the two profiles are of different devices: /device:TPU:400 before, /device:TPU:467 now
where the time goes in v19:
time: 93.8 us; the launch traced here: 93.3 us
  blocking collectives  38.5 us (41%)
  starting transfers between devices  24.4 us (26%)
  waiting for transfers between devices  15 us (16%)
  Pallas kernels  8.56 us (9%)
  other arithmetic  5.46 us (6%)
  between operations  1.35 us (1%)
    all_gather x1, blocking collectives, shards(): lax.all_gather(pseudo_grad, REP, axis=0, tiled=False).astype(jnp.float32)  22.2 us
    all_gather x1, blocking collectives, shards(): own = lax.all_gather(block, 'zh', axis=0, tiled=True)  16.2 us
    all_to_all x1, waiting for transfers between devices, shards(): tokens = lax.all_to_all(packed, PLANE, 0, 0, tiled=True)  11.2 us
    ppermute x3, starting transfers between devices, moved(): lax.ppermute(block, Z, [(z, target(z) % PLANES) for z in range(PLANES)])  9.31 us
    all_to_all x1, starting transfers between devices, shards(): partial = lax.all_to_all(partial, PLANE, 0, 0, tiled=True)  8.3 us
    all_to_all x1, starting transfers between devices, shards(): tokens = lax.all_to_all(packed, PLANE, 0, 0, tiled=True)  6.81 us
    pallas_call x1, Pallas kernels, pack(): pl.pallas_call(pack_kernel, grid=(tokens // ROWS,), in_specs=[pl.BlockSpe...  4.51 us
    pallas_call x1, Pallas kernels, project(): pl.pallas_call(project_kernel, grid_spec=pltpu.PrefetchScalarGridSpec(num...  4.05 us
  transfers between devices with their start and end apart: 5, of which 3 were waited for; matrix products, arithmetic and copies ran while one was open for 5% of the time, Pallas kernels for 0%

profile of v19, /device:TPU:467, one launch (start us, length us, event | category | flops | bytes accessed | tf_op | source)
XLA Modules:
  0.0 93.3 jit_solution(15477891591415086128)
XLA Ops:
  0.6 4.5 %pack_hidden.1 = (bf16[8,192,1024]{2,1,0:T(8,128)(2,1)}, f32[192,1]{1,0:T(8,128)}) custom-call(bf16[192,8192]{1,0:T(8,128)(2,1)} %bitcast.41, f32[1,8192]{1,0:T(1,128)} %bitcast.43), custom_call_target="tpu_custom_call" | custom-call | flops 6291456 | bytes 6291456 | tf_op jit(solution)/shard_map/pack_hidden/pallas_call | solution.py:46
  5.1 0.0 copy-start.1
  5.1 6.8 %all-to-all-start = ((bf16[8,192,1024]{2,1,0:T(8,128)(2,1)}), bf16[8,192,1024]{2,1,0:T(8,128)(2,1)S(1)}, u32[]{:S(2)}, u32[]{:S(2)}) async-start(bf16[8,192,1024]{2,1,0:T(8,128)(2,1)} %get-tuple-element.13), calls=%async_computation | async-start | bytes 6291456 | tf_op jit(solution)/shard_map/all_to_all | solution.py:123
  11.9 0.0 copy-done.1
  11.9 16.2 %all_gather.9.refs_0_ = bf16[256,512]{1,0:T(8,128)(2,1)S(1)} all-gather(bf16[64,512]{1,0:T(8,128)(2,1)S(1)} %bitcast.42), channel_id=1, replica_groups=mesh['yl'=2,'core'=2,'zh'=4,'zl'=4,'yh'=2,'x'=4] {'zh'}, dimensions={0}, use_global_device_ids=true | all-gather | bytes 327680 | tf_op jit(solution)/shard_map/all_gather | solution.py:124
  28.2 4.0 %collective-permute-start.2 = (bf16[256,512]{1,0:T(8,128)(2,1)S(1)}, bf16[256,512]{1,0:T(8,128)(2,1)}, u32[]{:S(2)}, u32[]{:S(2)}) collective-permute-start(bf16[256,512]{1,0:T(8,128)(2,1)S(1)} %all_gather.9.refs_0_), channel_id=1, source_target_pairs={{0,16},{8,120},{16,32},{24,8},{32,48},{40,24},{48,64},{56,40},{64,... | collective-permute-start | bytes 786440 | tf_op jit(solution)/shard_map/ppermute | solution.py:114
  32.2 1.9 %collective-permute-start.1 = (bf16[256,512]{1,0:T(8,128)(2,1)S(1)}, bf16[256,512]{1,0:T(8,128)(2,1)}, u32[]{:S(2)}, u32[]{:S(2)}) collective-permute-start(bf16[256,512]{1,0:T(8,128)(2,1)S(1)} %all_gather.9.refs_0_), channel_id=1, source_target_pairs={{0,8},{8,16},{16,24},{24,32},{32,40},{40,48},{48,56},{56,64},{64,7... | collective-permute-start | bytes 786440 | tf_op jit(solution)/shard_map/ppermute | solution.py:114
  34.2 3.4 %collective-permute-start = (bf16[256,512]{1,0:T(8,128)(2,1)S(1)}, bf16[256,512]{1,0:T(8,128)(2,1)}, u32[]{:S(2)}, u32[]{:S(2)}) collective-permute-start(bf16[256,512]{1,0:T(8,128)(2,1)S(1)} %all_gather.9.refs_0_), channel_id=1, source_target_pairs={{0,120},{8,0},{16,8},{24,16},{32,24},{40,32},{48,40},{56,48},{64,5... | collective-permute-start | bytes 786440 | tf_op jit(solution)/shard_map/ppermute | solution.py:114
  38.2 0.9 fusion.5
  39.1 0.0 collective-permute-done.2.refs_3_
  39.1 3.6 %collective-permute-done.1.refs_2_ = bf16[256,512]{1,0:T(8,128)(2,1)} collective-permute-done((bf16[256,512]{1,0:T(8,128)(2,1)S(1)}, bf16[256,512]{1,0:T(8,128)(2,1)}, u32[]{:S(2)}, u32[]{:S(2)}) %collective-permute-start.1) | collective-permute-done | bytes 262176 | tf_op jit(solution)/shard_map/ppermute | solution.py:114
  42.7 0.2 collective-permute-done.refs_1_
  42.9 11.2 %all-to-all-done.tokens_ref = bf16[8,192,1024]{2,1,0:T(8,128)(2,1)S(1)} async-done(((bf16[8,192,1024]{2,1,0:T(8,128)(2,1)}), bf16[8,192,1024]{2,1,0:T(8,128)(2,1)S(1)}, u32[]{:S(2)}, u32[]{:S(2)}) %all-to-all-start) | async-done | bytes 3145760 | tf_op jit(solution)/shard_map/all_to_all | solution.py:123
  54.2 4.1 %project_keys.1 = bf16[8,192,512]{2,1,0:T(8,128)(2,1)} custom-call(s32[1]{0:T(128)} %bitcast.residue_ref, bf16[8,192,1024]{2,1,0:T(8,128)(2,1)S(1)} %all-to-all-done.tokens_ref, bf16[256,512]{1,0:T(8,128)(2,1)S(1)} %all_gather.9.refs_0_, bf16[256,512]{1,0:T(8,128)(2,1)} %collective-permute-done.refs_1_, bf16[256,512]{1,0:T(8,128)(2,1)} %collective-permute-done.1.refs_2_, ...), custom_call_target="tpu_custom_call" | custom-call | flops 1610612736 | bytes 5767168 | tf_op jit(solution)/shard_map/project_keys/pallas_call | solution.py:93
  58.2 0.0 copy-start
  58.2 8.3 %all-to-all-start.1 = ((bf16[8,192,512]{2,1,0:T(8,128)(2,1)}), bf16[8,192,512]{2,1,0:T(8,128)(2,1)S(1)}, u32[]{:S(2)}, u32[]{:S(2)}) async-start(bf16[8,192,512]{2,1,0:T(8,128)(2,1)} %project_keys.1), calls=%async_computation.1 | async-start | bytes 3145728 | tf_op jit(solution)/shard_map/all_to_all | solution.py:139
  66.5 0.0 copy-done
  66.5 0.1 reduce
  66.6 22.2 %all-gather = bf16[256,512]{1,0:T(8,128)(2,1)S(1)} all-gather(bf16[64,512]{1,0:T(8,128)(2,1)S(1)} %fusion.5), channel_id=2, replica_groups=mesh['yl'=2,'core'=2,'zh'=4,'zl'=4,'yh'=2,'x'=4] {'yl','core'}, dimensions={0}, use_global_device_ids=true | all-gather | bytes 327680 | tf_op jit(solution)/shard_map/all_gather | solution.py:143
  88.9 0.1 convert_element_type.53
  88.9 1.7 %fusion.4 = (bf16[1,64,512]{2,1,0:T(8,128)(2,1)}, f32[64,512]{1,0:T(8,128)S(1)}) fusion(f32[7,64,512]{2,1,0:T(8,128)} %param.11, s32[]{:T(128)S(6)} %select_n.12, f32[7,64,512]{2,1,0:T(8,128)} %param.12, bf16[1,7,64,512]{3,2,1,0:T(8,128)(2,1)} %param.13, f32[256,512]{1,0:T(8,128)S(1)} %convert_element_type.53), kind=kLoop, calls=%fused_computation.9 | loop fusion | flops 458752 | bytes 1048580 | tf_op jit(solution)/shard_map/convert_element_type | solution.py:148
  90.6 1.7 %bitcast_subtract_fusion = (f32[64,512]{1,0:T(8,128)}, f32[64,512]{1,0:T(8,128)}) fusion(f32[64,512]{1,0:T(8,128)S(1)} %get-tuple-element.21, f32[7,64,512]{2,1,0:T(8,128)} %param.11, s32[]{:T(128)S(6)} %select_n.12, f32[7,64,512]{2,1,0:T(8,128)} %param.12), kind=kLoop, calls=%fused_computation.18 | loop fusion | flops 196608 | bytes 655364 | tf_op jit(solution)/shard_map/sub | solution.py:21
  92.3 0.0 all-to-all-done.1
  92.3 0.2 convert_reduce_fusion
  92.5 0.8 fusion
Async XLA Ops:
  5.1 6.8 %copy-start.1 = (bf16[1,64,512]{2,1,0:T(8,128)(2,1)S(1)}, bf16[1,64,512]{2,1,0:T(8,128)(2,1)}, u32[]{:S(2)}) copy-start(bf16[1,64,512]{2,1,0:T(8,128)(2,1)} %param.9) | copy-start | bytes 196612
  5.1 49.0 %all-to-all-start = ((bf16[8,192,1024]{2,1,0:T(8,128)(2,1)}), bf16[8,192,1024]{2,1,0:T(8,128)(2,1)S(1)}, u32[]{:S(2)}, u32[]{:S(2)}) async-start(bf16[8,192,1024]{2,1,0:T(8,128)(2,1)} %get-tuple-element.13), calls=%async_computation | async-start | bytes 6291456 | tf_op jit(solution)/shard_map/all_to_all | solution.py:123
  28.2 10.9 %collective-permute-start.2 = (bf16[256,512]{1,0:T(8,128)(2,1)S(1)}, bf16[256,512]{1,0:T(8,128)(2,1)}, u32[]{:S(2)}, u32[]{:S(2)}) collective-permute-start(bf16[256,512]{1,0:T(8,128)(2,1)S(1)} %all_gather.9.refs_0_), channel_id=1, source_target_pairs={{0,16},{8,120},{16,32},{24,8},{32,48},{40,24},{48,64},{56,40},{64,... | collective-permute-start | bytes 786440 | tf_op jit(solution)/shard_map/ppermute | solution.py:114
  32.2 10.5 %collective-permute-start.1 = (bf16[256,512]{1,0:T(8,128)(2,1)S(1)}, bf16[256,512]{1,0:T(8,128)(2,1)}, u32[]{:S(2)}, u32[]{:S(2)}) collective-permute-start(bf16[256,512]{1,0:T(8,128)(2,1)S(1)} %all_gather.9.refs_0_), channel_id=1, source_target_pairs={{0,8},{8,16},{16,24},{24,32},{32,40},{40,48},{48,56},{56,64},{64,7... | collective-permute-start | bytes 786440 | tf_op jit(solution)/shard_map/ppermute | solution.py:114
  34.2 8.8 %collective-permute-start = (bf16[256,512]{1,0:T(8,128)(2,1)S(1)}, bf16[256,512]{1,0:T(8,128)(2,1)}, u32[]{:S(2)}, u32[]{:S(2)}) collective-permute-start(bf16[256,512]{1,0:T(8,128)(2,1)S(1)} %all_gather.9.refs_0_), channel_id=1, source_target_pairs={{0,120},{8,0},{16,8},{24,16},{32,24},{40,32},{48,40},{56,48},{64,5... | collective-permute-start | bytes 786440 | tf_op jit(solution)/shard_map/ppermute | solution.py:114
  58.2 8.3 %copy-start = (f32[192,1]{1,0:T(8,128)S(1)}, f32[192,1]{1,0:T(8,128)}, u32[]{:S(2)}) copy-start(f32[192,1]{1,0:T(8,128)} %get-tuple-element.17) | copy-start | bytes 2308
  58.2 34.1 %all-to-all-start.1 = ((bf16[8,192,512]{2,1,0:T(8,128)(2,1)}), bf16[8,192,512]{2,1,0:T(8,128)(2,1)S(1)}, u32[]{:S(2)}, u32[]{:S(2)}) async-start(bf16[8,192,512]{2,1,0:T(8,128)(2,1)} %project_keys.1), calls=%async_computation.1 | async-start | bytes 3145728 | tf_op jit(solution)/shard_map/all_to_all | solution.py:139
